TPU v7x, 32 devices: a whole 2x2x4 slice. The times are simulated.
32 devices in a mesh: ctx: 8 (over y, x, core), head: 4 (over z).
Axes of the slice: x: 2, y: 2, z: 4, core: 2. Of those that a mesh axis runs over, the one named last changes fastest.
Arguments:
- tokens: bfloat16 [2048, 2048], P('ctx'), may hold values from -6 to 6
- qkv_weight: bfloat16 [2048, 3, 16, 128], P(None, None, 'head'), may hold values from -0.125 to 0.125
- small_weight: bfloat16 [2048, 16, 15], P(None, 'head'), may hold values from -0.125 to 0.125
- head_param: float32 [16, 2], P('head'), as said below
- norm_gain: float32 [128], replicated, may hold values from 0.1 to 1.9
- out_weight: bfloat16 [16, 128, 2048], P('head'), may hold values from -0.125 to 0.125
- grad_out: bfloat16 [2048, 2048], P('ctx'), may hold values from -6 to 6
Outputs:
- layer_out: bfloat16 [2048, 2048], P('ctx', 'head')
- grad_tokens: bfloat16 [2048, 2048], P('ctx', 'head')
Inputs may be any that keep to these rules, and one draw needn't show every extreme that they name: `head_param`: column 0 holds each head's decay rate, positive; column 1 a bias added before the write strength's sigmoid.
All inputs are finite; a program needn't handle non-finite values.
Results may differ from a plain program's by a relative error of at most 0.017.
Values may be sent and summed in bfloat16 or wider, within the bound.
No kernel may reach another device: no remote copies, remote signals or barrier semaphores. Data moves between devices by JAX's collectives and lax.ppermute only.
A program may use at most 128 MiB of HBM per device.

v0:
```python
import jax
import jax.numpy as jnp
from jax import lax
from jax.sharding import PartitionSpec as P

BLOCK = 64


def mat_mul(left, right):
    return jnp.matmul(left, right, precision=lax.Precision.HIGHEST)


def flip_last(array_in):
    return jnp.swapaxes(array_in, -1, -2)


def unit_scale(values):
    return values * lax.rsqrt(jnp.sum(values * values, -1, keepdims=True) + 1e-06)


def block_pieces(q_in, k_in, v_in, beta_w, decay_log):
    length = q_in.shape[-2]
    cum_log = jnp.cumsum(decay_log, axis=-1)
    row_id = lax.broadcasted_iota(jnp.int32, (length, length), 0)
    col_id = lax.broadcasted_iota(jnp.int32, (length, length), 1)
    inclusive = row_id >= col_id
    strict = row_id > col_id
    spread = cum_log[..., :, None] - cum_log[..., None, :]
    decay_mat = jnp.where(inclusive, jnp.exp(jnp.where(inclusive, spread, 0.0)), 0.0)
    key_gram = mat_mul(k_in, flip_last(k_in))
    lower_part = jnp.where(strict, beta_w[..., :, None] * decay_mat * key_gram, 0.0)
    system = lower_part + jnp.eye(length, dtype=jnp.float32)
    growth = jnp.exp(cum_log)
    right_side = jnp.concatenate(
        [beta_w[..., None] * v_in, (beta_w * growth)[..., None] * k_in], -1
    )
    solved = jax.scipy.linalg.solve_triangular(system, right_side, lower=True, unit_diagonal=True)
    value_dim = v_in.shape[-1]
    new_values = solved[..., :value_dim]
    key_mix = solved[..., value_dim:]
    scores = mat_mul(q_in, flip_last(k_in)) * decay_mat
    intra_out = mat_mul(scores, new_values)
    query_mix = growth[..., None] * q_in - mat_mul(scores, key_mix)
    tail_decay = jnp.exp(cum_log[..., -1:] - cum_log)
    tail_keys = tail_decay[..., None] * k_in
    eye_key = jnp.eye(k_in.shape[-1], dtype=jnp.float32)
    transit = jnp.exp(cum_log[..., -1])[..., None, None] * eye_key - mat_mul(
        flip_last(key_mix), tail_keys
    )
    own_state = mat_mul(flip_last(new_values), tail_keys)
    return (intra_out, query_mix, transit, own_state)


def butterfly(transit, own_state):
    total_count = transit.shape[0]
    eye_key = jnp.eye(transit.shape[-1], dtype=jnp.float32)
    prefix = jnp.broadcast_to(eye_key, transit.shape)
    block_a = transit
    block_u = own_state
    found_all = []
    block_len = 1
    while block_len < total_count:
        pair_count = total_count // (2 * block_len)
        split_a = block_a.reshape((pair_count, 2) + block_a.shape[1:])
        split_u = block_u.reshape((pair_count, 2) + block_u.shape[1:])
        split_p = prefix.reshape((pair_count, 2, block_len) + prefix.shape[1:])
        low_a = split_a[:, 0]
        high_a = split_a[:, 1]
        low_u = split_u[:, 0]
        high_u = split_u[:, 1]
        upper_p = split_p[:, 1]
        arriving = mat_mul(low_u[:, None], upper_p)
        moved_p = mat_mul(low_a[:, None], upper_p)
        found_all.append(
            jnp.stack([jnp.zeros_like(arriving), arriving], 1).reshape(own_state.shape)
        )
        prefix = jnp.stack([split_p[:, 0], moved_p], 1).reshape(prefix.shape)
        block_a = mat_mul(low_a, high_a)
        block_u = mat_mul(low_u, high_a) + high_u
        block_len = block_len * 2
    return (found_all, prefix, block_a[0], block_u[0])


def pick_levels(stack_all, position):
    total_count = stack_all.shape[0]
    block_a = stack_all[:, 0]
    block_u = stack_all[:, 1]
    eye_key = jnp.eye(block_a.shape[-1], dtype=jnp.float32)
    prefix = jnp.broadcast_to(eye_key, block_a.shape[1:])
    found_all = []
    block_len = 1
    while block_len < total_count:
        pair_count = total_count // (2 * block_len)
        split_a = block_a.reshape((pair_count, 2) + block_a.shape[1:])
        split_u = block_u.reshape((pair_count, 2) + block_u.shape[1:])
        pair_no = position // (2 * block_len)
        is_upper = position // block_len % 2 == 1
        low_a = lax.dynamic_index_in_dim(split_a[:, 0], pair_no, 0, keepdims=False)
        low_u = lax.dynamic_index_in_dim(split_u[:, 0], pair_no, 0, keepdims=False)
        found_all.append(jnp.where(is_upper, mat_mul(low_u, prefix), 0.0))
        prefix = jnp.where(is_upper, mat_mul(low_a, prefix), prefix)
        block_a = mat_mul(split_a[:, 0], split_a[:, 1])
        block_u = mat_mul(split_u[:, 0], split_a[:, 1]) + split_u[:, 1]
        block_len = block_len * 2
    return tuple(found_all)


def on_device(tokens, qkv_weight, small_weight, head_param, norm_gain, out_weight, grad_out):
    row_count = tokens.shape[0]
    model_width = tokens.shape[1]
    head_count = qkv_weight.shape[2]
    head_dim = qkv_weight.shape[3]
    extra_cols = small_weight.shape[2]
    levels_n = extra_cols - 2
    block_count = row_count // BLOCK
    index_ctx = lax.axis_index("ctx")
    shard_bits = lax.axis_size("ctx").bit_length() - 1
    local_bits = block_count.bit_length() - 1
    flat_qkv = qkv_weight.reshape(model_width, 3 * head_count * head_dim)
    flat_small = small_weight.reshape(model_width, head_count * extra_cols)
    flat_out = out_weight.reshape(head_count * head_dim, model_width)
    proj = jnp.dot(tokens, flat_qkv, preferred_element_type=jnp.float32).reshape(
        row_count, 3, head_count, head_dim
    )
    gate_pre = jnp.dot(tokens, flat_small, preferred_element_type=jnp.float32).reshape(
        row_count, head_count, extra_cols
    )

    def to_blocks(tensor):
        return jnp.swapaxes(tensor.reshape((block_count, BLOCK) + tensor.shape[1:]), 1, 2)

    def section_local(q_raw, k_raw, v_raw, gate_in):
        gate_blk = to_blocks(gate_in)
        beta_w = jax.nn.sigmoid(gate_blk[..., levels_n + 1] + head_param[:, 1][None, :, None])
        decay_log = -head_param[:, 0][None, :, None] * jax.nn.sigmoid(gate_blk[..., levels_n])
        weights = jax.nn.softplus(gate_blk[..., :levels_n])
        intra_out, query_mix, transit, own_state = block_pieces(
            to_blocks(unit_scale(q_raw)),
            to_blocks(unit_scale(k_raw)),
            to_blocks(v_raw),
            beta_w,
            decay_log,
        )
        found_all, prefix, block_a, block_u = butterfly(transit, own_state)
        local_out = weights[..., 0:1] * intra_out
        for level_no in range(len(found_all)):
            local_out = local_out + weights[..., level_no + 1 : level_no + 2] * mat_mul(
                query_mix, flip_last(found_all[level_no])
            )
        query_hat = mat_mul(query_mix, flip_last(prefix))
        far_weights = weights[..., local_bits + 1 : local_bits + 1 + shard_bits]
        return (jnp.stack([block_a, block_u], 0), (local_out, query_hat, far_weights))

    def section_out(local_out, query_hat, far_weights, incoming):
        summed = local_out
        for level_no in range(len(incoming)):
            summed = summed + far_weights[..., level_no : level_no + 1] * mat_mul(
                query_hat, flip_last(incoming[level_no])[None]
            )
        return summed * lax.rsqrt(jnp.mean(summed * summed, -1, keepdims=True) + 1e-06) * norm_gain

    (summary, carried), pull_local = jax.vjp(
        section_local, proj[:, 0], proj[:, 1], proj[:, 2], gate_pre
    )
    gathered = lax.all_gather(summary[None].astype(jnp.bfloat16), "ctx", axis=0, tiled=True).astype(
        jnp.float32
    )

    def from_gathered(stack_all):
        return pick_levels(stack_all, index_ctx)

    incoming, pull_cross = jax.vjp(from_gathered, gathered)
    normed, pull_out = jax.vjp(section_out, carried[0], carried[1], carried[2], incoming)
    normed_low = (
        jnp.swapaxes(normed, 1, 2)
        .reshape((row_count,) + normed.shape[1:2] + normed.shape[3:])
        .reshape(row_count, head_count * head_dim)
        .astype(jnp.bfloat16)
    )
    out_part = jnp.dot(normed_low, flat_out, preferred_element_type=jnp.float32)
    layer_out = lax.psum_scatter(
        out_part.astype(jnp.bfloat16), "head", scatter_dimension=1, tiled=True
    )
    grad_normed = jnp.dot(grad_out, flat_out.T, preferred_element_type=jnp.float32)
    grad_normed = to_blocks(grad_normed.reshape(row_count, head_count, head_dim))
    grad_local, grad_hat, grad_far, grad_incoming = pull_out(grad_normed)
    (grad_gathered,) = pull_cross(grad_incoming)
    grad_summary = lax.psum_scatter(
        grad_gathered.astype(jnp.bfloat16), "ctx", scatter_dimension=0, tiled=True
    ).astype(jnp.float32)[0]
    grad_q, grad_k, grad_v, grad_gate = pull_local((grad_summary, (grad_local, grad_hat, grad_far)))
    grad_proj = (
        jnp.stack([grad_q, grad_k, grad_v], 1)
        .astype(jnp.bfloat16)
        .reshape(row_count, 3 * head_count * head_dim)
    )
    grad_small = grad_gate.astype(jnp.bfloat16).reshape(row_count, head_count * extra_cols)
    grad_part = jnp.dot(grad_proj, flat_qkv.T, preferred_element_type=jnp.float32)
    grad_part = grad_part + jnp.dot(grad_small, flat_small.T, preferred_element_type=jnp.float32)
    grad_tokens = lax.psum_scatter(
        grad_part.astype(jnp.bfloat16), "head", scatter_dimension=1, tiled=True
    )
    return (layer_out, grad_tokens)


def solution(mesh):
    placed = (
        P("ctx", None),
        P(None, None, "head", None),
        P(None, "head", None),
        P("head", None),
        P(),
        P("head", None, None),
        P("ctx", None),
    )
    return jax.shard_map(
        on_device,
        mesh=mesh,
        in_specs=placed,
        out_specs=(P("ctx", "head"), P("ctx", "head")),
        check_vma=False,
    )
```

profile of v0, /device:TPU:0, one launch (start us, length us, event | category | flops | bytes accessed | tf_op | source)
XLA Modules:
  0.0 392.2 jit_solution(7382804241769528324)
XLA Ops:
  7.2 11.1 %reshape.453 = bf16[2048,1536]{1,0:T(8,128)(2,1)} reshape(bf16[2048,3,4,128]{3,2,1,0:T(4,128)(2,1)} %param.8) | data formatting | bytes 12582912 | tf_op jit(solution)/shard_map/reshape | solution.py:119
  18.4 8.7 %copy.523 = bf16[1536,2048]{1,0:T(8,128)(2,1)} copy(bf16[1536,2048]{0,1:T(8,128)(2,1)} %bitcast.757) | data formatting | bytes 12582912 | tf_op jit(solution)/shard_map/dot_general | solution.py:122
  27.0 4.3 %fusion.49 = f32[256,3,4,128]{3,0,2,1:T(8,128)S(1)} fusion(bf16[3,4,128,2048]{3,2,1,0:T(8,128)(2,1)} %bitcast.811, bf16[256,2048]{1,0:T(8,128)(2,1)} %param.7), kind=kOutput, calls=%fused_computation.107 | convolution fusion | flops 1610612736 | bytes 8912896 | tf_op jit(solution)/shard_map/dot_general | solution.py:122
  53.3 2.2 add_bitcast_fusion.1
  55.5 79.6 %custom-call.10 = f32[4,4,1,64,64]{3,4,2,1,0:T(8,128)S(1)} custom-call(f32[4,4,1,64,64]{4,3,2,1,0:T(8,128)} %add_bitcast_fusion.1), custom_call_target="InvertDiagBlocksLowerTriangular" | custom-call | tf_op jit(solution)/shard_map/jvp(jit(_solve_triangular))/vmap(vmap())/triangular_solve | solution.py:37
  135.3 2.4 fusion.45
  137.7 2.1 fusion.150
  139.8 2.2 convolution_subtract_fusion
  186.5 2.1 convolution_bitcast_fusion.12
  192.3 2.1 fusion.319
  194.5 2.9 fusion.318
  197.4 3.1 fusion.317
  207.6 2.2 fusion.78
  236.7 2.1 fusion.86
  242.2 2.6 copy.621
  255.6 3.2 fusion.142
  271.0 2.5 fusion.132
  273.5 3.0 fusion.139
  278.4 2.7 add_bitcast_fusion
  282.2 3.7 fusion.15
  288.4 2.3 fusion.75
  299.7 2.1 convolution_add_fusion.1
  301.8 2.1 convolution_add_fusion.2
  307.2 2.0 fusion.155
  314.1 2.6 convolution_add_fusion.3
  321.2 2.8 copy.651
  324.1 5.4 %reduce_window_sum.26 = f32[4,4,64,1]{3,2,1,0:T(8,128)} reduce-window(f32[4,4,64,1]{3,2,1,0:T(8,128)S(1)} %copy.651, f32[]{:T(128)} %constant.158.clone.1), window={size=1x1x64x1 pad=0_0x0_0x0_63x0_0}, to_apply=%region_22.23 | reduce-window | flops 64512 | bytes 8196 | tf_op jit(solution)/shard_map/transpose(jvp(jit(cumsum)))/reduce_window_sum | solution.py:23
  329.5 2.7 copy.652
  333.7 3.2 fusion.51
  340.8 3.0 fusion.20
  349.7 5.6 %fusion.8 = bf16[256,2048]{1,0:T(8,128)(2,1)} fusion(f32[256,2048]{1,0:T(8,128)S(1)} %convolution_bitcast_fusion, bf16[2048,3,4,128]{3,2,1,0:T(4,128)(2,1)} %param.8, bf16[256,1,4,128]{3,0,2,1:T(8,128)(2,1)S(1)} %bitcast.827, bf16[256,1,4,128]{3,0,2,1:T(8,128)(2,1)S(1)} %get-tuple-element.50, bf16[256,1,4,128]{3,0,2,1:T(8,128)(2,1)S(1)} %get-tuple-element.49), kind=kOutput, calls=%fused_computation.10 | convolution fusion | flops 1612447744 | bytes 10223616 | tf_op jit(solution)/shard_map/dot_general | solution.py:198
  355.4 30.0 %reduce-scatter.8.cloned.1.call-done = bf16[256,512]{1,0:T(8,128)(2,1)} async-done(((bf16[256,2048]{1,0:T(8,128)(2,1)}), bf16[256,512]{1,0:T(8,128)(2,1)}) %reduce-scatter.8.cloned.1.call-update) | async-done | bytes 262160 | tf_op jit(solution)/shard_map/reduce_scatter | solution.py:200
  (485 shorter events, 166.7 us)
Async XLA Ops:
  7.2 200.3 %copy-start = (bf16[4,128,2048]{2,1,0:T(8,128)(2,1)S(1)}, bf16[4,128,2048]{2,1,0:T(8,128)(2,1)}, u32[]{:S(2)}) copy-start(bf16[4,128,2048]{2,1,0:T(8,128)(2,1)} %param.12) | copy-start | bytes 6291460
  7.2 193.3 %all-gather.2.cloned.1.call-start = ((), (), s32[]{:S(2)}) async-start(), calls=%async_computation.3 | async-start | bytes 2359296 | tf_op jit(solution)/shard_map/all_gather | solution.py:165
  32.2 15.4 %copy-start.105 = (f32[256,4]{0,1:T(4,128)}, f32[256,4]{0,1:T(4,128)S(1)}, u32[]{:S(2)}) copy-start(f32[256,4]{0,1:T(4,128)S(1)} %get-tuple-element.5) | copy-start | bytes 12292
  33.1 19.2 %copy-start.67 = (f32[256,1,4,128]{3,0,2,1:T(8,128)}, f32[256,1,4,128]{3,0,2,1:T(8,128)S(1)}, u32[]{:S(2)}) copy-start(f32[256,1,4,128]{3,0,2,1:T(8,128)S(1)} %get-tuple-element.52) | copy-start | bytes 1572868
  33.9 19.5 %copy-start.95 = (pred[64,64]{1,0:T(8,128)(4,1)}, pred[64,64]{1,0:T(8,128)(4,1)S(1)}, u32[]{:S(2)}) copy-start(pred[64,64]{1,0:T(8,128)(4,1)S(1)} %iota_compare_fusion.3) | copy-start | bytes 12292
  34.5 6.4 %copy-start.131 = (f32[4]{0:T(128)}, f32[4]{0:T(128)S(1)}, u32[]{:S(2)}) copy-start(f32[4]{0:T(128)S(1)} %get-tuple-element.71) | copy-start | bytes 52
  34.5 9.3 %copy-start.129 = (f32[4]{0:T(128)}, f32[4]{0:T(128)S(1)}, u32[]{:S(2)}) copy-start(f32[4]{0:T(128)S(1)} %get-tuple-element.70) | copy-start | bytes 52
  51.6 83.6 %copy-start.128 = (f32[4,4]{1,0:T(4,128)S(1)}, f32[4,4]{1,0:T(4,128)}, u32[]{:S(2)}) copy-start(f32[4,4]{1,0:T(4,128)} %slice_bitcast_fusion.62) | copy-start | bytes 196
  52.3 85.3 %copy-start.97 = (pred[64,64]{1,0:T(8,128)(4,1)}, pred[64,64]{1,0:T(8,128)(4,1)S(1)}, u32[]{:S(2)}) copy-start(pred[64,64]{1,0:T(8,128)(4,1)S(1)} %iota_compare_fusion.4) | copy-start | bytes 12292
  135.2 4.6 %copy-start.54 = (f32[4,4,1,64,64]{3,4,2,1,0:T(8,128)}, f32[4,4,1,64,64]{3,4,2,1,0:T(8,128)S(1)}, u32[]{:S(2)}) copy-start(f32[4,4,1,64,64]{3,4,2,1,0:T(8,128)S(1)} %custom-call.10) | copy-start | bytes 786436
  142.7 8.2 %copy-start.17 = (f32[1,2,4,128,128]{4,3,2,1,0:T(8,128)}, f32[1,2,4,128,128]{4,3,2,1,0:T(8,128)S(1)}, u32[]{:S(2)}) copy-start(f32[1,2,4,128,128]{4,3,2,1,0:T(8,128)S(1)} %convolution_bitcast_fusion.10) | copy-start | bytes 1572868
  142.7 5.7 %copy-start.103 = (f32[256,4]{0,1:T(4,128)S(1)}, f32[256,4]{0,1:T(4,128)}, u32[]{:S(2)}) copy-start(f32[256,4]{0,1:T(4,128)} %get-tuple-element.4) | copy-start | bytes 12292
  145.3 140.6 %reduce-scatter.6.cloned.1.call-start = ((), (), s32[]{:S(2)}) async-start(), calls=%async_computation.5 | async-start | bytes 2359296 | tf_op jit(solution)/shard_map/reduce_scatter | solution.py:188
  186.4 8.0 %copy-start.41 = (f32[1,2,2,4,128,128]{5,4,3,2,1,0:T(8,128)}, f32[1,2,2,4,128,128]{5,4,3,2,1,0:T(8,128)S(1)}, u32[]{:S(2)}) copy-start(f32[1,2,2,4,128,128]{5,4,3,2,1,0:T(8,128)S(1)} %stack.27.clone) | copy-start | bytes 3145732
  188.6 8.8 %copy-start.35 = (f32[2,2,1,4,128,128]{5,4,3,1,0,2:T(8,128)}, f32[2,2,1,4,128,128]{5,4,3,1,0,2:T(8,128)S(1)}, u32[]{:S(2)}) copy-start(f32[2,2,1,4,128,128]{5,4,3,1,0,2:T(8,128)S(1)} %stack.25.clone) | copy-start | bytes 3145732
  189.8 4.7 %copy-start.10 = (f32[4,4,64,64]{3,2,1,0:T(8,128)}, f32[4,4,64,64]{3,2,1,0:T(8,128)S(1)}, u32[]{:S(2)}) copy-start(f32[4,4,64,64]{3,2,1,0:T(8,128)S(1)} %fusion.111) | copy-start | bytes 786436
  192.3 5.1 %copy-start.5 = (f32[4,4,64,128]{3,2,1,0:T(8,128)}, f32[4,4,64,128]{3,2,1,0:T(8,128)S(1)}, u32[]{:S(2)}) copy-start(f32[4,4,64,128]{3,2,1,0:T(8,128)S(1)} %convolution_subtract_fusion.1) | copy-start | bytes 1572868
  205.8 4.7 %copy-start.26 = (f32[4,4,64,128]{3,2,0,1:T(8,128)}, f32[4,4,64,128]{3,2,0,1:T(8,128)S(1)}, u32[]{:S(2)}) copy-start(f32[4,4,64,128]{3,2,0,1:T(8,128)S(1)} %fusion.182) | copy-start | bytes 1572868
  211.9 15.7 %copy-start.58 = (f32[4,4,64,128]{3,2,0,1:T(8,128)}, f32[4,4,64,128]{3,2,0,1:T(8,128)S(1)}, u32[]{:S(2)}) copy-start(f32[4,4,64,128]{3,2,0,1:T(8,128)S(1)} %get-tuple-element.20) | copy-start | bytes 1572868
  212.2 8.1 %copy-start.60 = (f32[4,4,64,128]{3,2,0,1:T(8,128)}, f32[4,4,64,128]{3,2,0,1:T(8,128)S(1)}, u32[]{:S(2)}) copy-start(f32[4,4,64,128]{3,2,0,1:T(8,128)S(1)} %get-tuple-element.61) | copy-start | bytes 1572868
  231.9 123.5 %reduce-scatter.4.cloned.1.call-start = ((), (), s32[]{:S(2)}) async-start(), calls=%async_computation.4 | async-start | bytes 1310720 | tf_op jit(solution)/shard_map/reduce_scatter | solution.py:181
  232.0 4.6 %copy-start.76 = (f32[4,4,64,128]{3,2,1,0:T(8,128)S(1)}, f32[4,4,64,128]{3,2,1,0:T(8,128)}, u32[]{:S(2)}) copy-start(f32[4,4,64,128]{3,2,1,0:T(8,128)} %get-tuple-element.22) | copy-start | bytes 1572868
  255.6 4.6 %copy-start.38 = (f32[4,4,128,128]{3,2,1,0:T(8,128)S(1)}, f32[4,4,128,128]{3,2,1,0:T(8,128)}, u32[]{:S(2)}) copy-start(f32[4,4,128,128]{3,2,1,0:T(8,128)} %copy-done.37) | copy-start | bytes 3145732
  255.6 5.6 %copy-start.62 = (f32[1,2,4,128,128]{4,3,2,1,0:T(8,128)S(1)}, f32[1,2,4,128,128]{4,3,2,1,0:T(8,128)}, u32[]{:S(2)}) copy-start(f32[1,2,4,128,128]{4,3,2,1,0:T(8,128)} %copy-done.61) | copy-start | bytes 1572868
  267.2 6.3 %copy-start.47 = (f32[4,4,64,128]{3,2,1,0:T(8,128)}, f32[4,4,64,128]{3,2,1,0:T(8,128)S(1)}, u32[]{:S(2)}) copy-start(f32[4,4,64,128]{3,2,1,0:T(8,128)S(1)} %get-tuple-element.75) | copy-start | bytes 1572868
  271.0 5.5 %copy-start.82 = (bf16[4,64,4,128]{3,2,1,0:T(4,128)(2,1)S(1)}, bf16[4,64,4,128]{3,2,1,0:T(4,128)(2,1)}, u32[]{:S(2)}) copy-start(bf16[4,64,4,128]{3,2,1,0:T(4,128)(2,1)} %copy.576) | copy-start | bytes 786436
  278.3 107.1 %reduce-scatter.8.cloned.1.call-start = ((), (), s32[]{:S(2)}) async-start(), calls=%async_computation.6 | async-start | bytes 1310720 | tf_op jit(solution)/shard_map/reduce_scatter | solution.py:200
  285.9 4.9 %copy-start.52 = (f32[4,4,128,128]{3,2,1,0:T(8,128)S(1)}, f32[4,4,128,128]{3,2,1,0:T(8,128)}, u32[]{:S(2)}) copy-start(f32[4,4,128,128]{3,2,1,0:T(8,128)} %copy-done.51) | copy-start | bytes 3145732
  319.3 13.1 %copy-start.130 = (f32[4]{0:T(128)S(1)}, f32[4]{0:T(128)}, u32[]{:S(2)}) copy-start(f32[4]{0:T(128)} %copy-done.129) | copy-start | bytes 52
  319.3 13.1 %copy-start.132 = (f32[4]{0:T(128)S(1)}, f32[4]{0:T(128)}, u32[]{:S(2)}) copy-start(f32[4]{0:T(128)} %copy-done.131) | copy-start | bytes 52
  333.7 7.0 %copy-start.89 = (f32[4,64,4]{2,0,1:T(4,128)S(1)}, f32[4,64,4]{2,0,1:T(4,128)}, u32[]{:S(2)}) copy-start(f32[4,64,4]{2,0,1:T(4,128)} %get-tuple-element.63) | copy-start | bytes 12292
  333.7 7.1 %copy-start.34 = (f32[256,1,4,128]{3,0,2,1:T(8,128)S(1)}, f32[256,1,4,128]{3,0,2,1:T(8,128)}, u32[]{:S(2)}) copy-start(f32[256,1,4,128]{3,0,2,1:T(8,128)} %get-tuple-element.51) | copy-start | bytes 1572868
  (109 other events, 271.4 us)
Sparse Core Ops, SparseCore 0:
  145.4 30.5 all-gather.1
  232.0 43.9 reduce-scatter.5
  279.0 29.2 reduce-scatter.3
  355.5 29.8 reduce-scatter.7
where the time goes:
time: 399 us; the launch traced here: 392 us
  other arithmetic  126 us (32%)
  matrix products  124 us (31%)
  local copies, waits for them, and re-layouts  95.2 us (24%)
  waiting for transfers between devices  30.1 us (8%)
  between operations  16.5 us (4%)
    dot_general x80, matrix products, mat_mul(): return jnp.matmul(left, right, precision=lax.Precision.HIGHEST)  101 us
    another operation x5, other arithmetic, block_pieces(): jax.scipy.linalg.solve_triangular(system, right_side, lower=True, unit_di...  83.1 us
    reduce_scatter x1, waiting for transfers between devices, on_device(): lax.psum_scatter(grad_part.astype(jnp.bfloat16), 'head', scatter_dimensio...  30 us
    mul x9, local copies, waits for them, and re-layouts, section_out(): far_weights[..., level_no:level_no + 1]  14.3 us
    reshape x1, local copies, waits for them, and re-layouts, on_device(): flat_qkv = qkv_weight.reshape(model_width, 3 * head_count * head_dim)  11.1 us
    dot_general x1, local copies, waits for them, and re-layouts, on_device(): jnp.dot(tokens, flat_qkv, preferred_element_type=jnp.float32)  8.66 us
    mul x6, local copies, waits for them, and re-layouts, section_local(): weights[..., level_no + 1:level_no + 2]  8.37 us
  transfers between devices with their start and end apart: 4, of which 1 were waited for; matrix products, arithmetic and copies ran while one was open for 44% of the time, Pallas kernels for 0%

commit v1 on v0

v1 whole, which is shorter than its diff:
```python
import functools

import jax
import jax.numpy as jnp
from jax import lax
from jax.experimental import pallas as pl
from jax.experimental.pallas import tpu as pltpu
from jax.sharding import PartitionSpec as P

BLOCK = 64
LANES = 128
EPS = 1e-06
VMEM_BYTES = 58 * 1024 * 1024
F32 = jnp.float32
BF16 = jnp.bfloat16
WHOLE = pl.BlockSpec(memory_space=pltpu.VMEM)
SCALARS = pl.BlockSpec(memory_space=pltpu.SMEM)
PARAMS = pltpu.CompilerParams(vmem_limit_bytes=VMEM_BYTES)


def contract(left, right, dim_left, dim_right):
    return lax.dot_general(
        left.astype(BF16),
        right.astype(BF16),
        (((dim_left,), (dim_right,)), ((), ())),
        preferred_element_type=F32,
    )


def mm(left, right):
    return contract(left, right, 1, 0)


def mm_nt(left, right):
    return contract(left, right, 1, 1)


def mm_tn(left, right):
    return contract(left, right, 0, 0)


def split(values):
    high = values.astype(BF16)
    return high, (values - high.astype(F32)).astype(BF16)


def mm_nt_fine(left, right):
    left_high, left_low = split(left)
    right_high, right_low = split(right)
    return mm_nt(left_high, right_high) + (mm_nt(left_low, right_high) + mm_nt(left_high, right_low))


def mm_full(left, right):
    return jnp.dot(left, right, precision=lax.Precision.HIGHEST, preferred_element_type=F32)


def pair_ids(count):
    row_id = lax.broadcasted_iota(jnp.int32, (count, count), 0)
    col_id = lax.broadcasted_iota(jnp.int32, (count, count), 1)
    return row_id, col_id


def row_sum(values):
    return jnp.sum(values, 1, keepdims=True)


def col_sum(values):
    return jnp.sum(values, 0, keepdims=True)


def lane_of(rows):
    return lax.broadcasted_iota(jnp.int32, (rows, LANES), 1)


def decay_of(pack, pack_t, col, inclusive):
    spread = pack[:, col : col + 1] - pack_t[col : col + 1, :]
    return jnp.where(inclusive, jnp.exp(jnp.minimum(spread, 0.0)), 0.0)


def level_mix(pack, head, heads, bits, apart):
    block_bit = BLOCK.bit_length() - 1
    mix = pack[:, head : head + 1]
    mixed = jnp.broadcast_to(mix, apart.shape)
    for level in range(1, bits + 1):
        col = level * heads + head
        here = (apart >> (block_bit + level - 1)) >= 1
        mixed = jnp.where(here, pack[:, col : col + 1], mixed)
    return mixed


def project_body(
    sizes, hp_ref, tokens_ref, w_ref, small_ref, wr_ref, qkv_ref, gate_ref, pack_ref, pack_t_ref,
    trans_ref, mixed_ref, pair_ref, wide, acc, gate_acc
):
    heads, levels, steps = sizes
    step = pl.program_id(0)
    rows = tokens_ref.shape[0]
    depth = tokens_ref.shape[1]
    cols = 3 * heads
    wide[...] = w_ref[...].astype(F32)
    for col in range(cols):
        part = wide[pl.ds(col, depth, stride=cols), :]
        wr_ref[:, col * LANES : (col + 1) * LANES] = part.astype(BF16)
    own = jnp.dot(tokens_ref[...], wr_ref[...], preferred_element_type=F32)
    own_gate = mm_nt(tokens_ref[...], small_ref[...])

    @pl.when(step == 0)
    def _():
        acc[...] = own
        gate_acc[...] = own_gate

    @pl.when(step > 0)
    def _():
        acc[...] += own
        gate_acc[...] += own_gate

    @pl.when(step == steps - 1)
    def _():
        local_summary(
            heads, levels, hp_ref, acc, gate_acc, qkv_ref, gate_ref, pack_ref, pack_t_ref,
            trans_ref, mixed_ref, pair_ref
        )


def local_summary(
    heads, levels, hp_ref, acc, gate_acc, qkv_ref, gate_ref, pack_ref, pack_t_ref, trans_ref,
    mixed_ref, pair_ref
):
    rows = acc.shape[0]
    decay_col = levels * heads
    beta_col = decay_col + heads
    norm_col = beta_col + heads
    gate = gate_acc[...]
    gate_ref[...] = gate
    lane = lane_of(rows)
    lane_row = lane_of(1)
    rate = jnp.zeros((1, LANES), F32)
    bias = jnp.zeros((1, LANES), F32)
    for head in range(heads):
        rate = jnp.where(lane_row == decay_col + head, hp_ref[head, 0], rate)
        bias = jnp.where(lane_row == beta_col + head, hp_ref[head, 1], bias)
    switch = jax.nn.sigmoid(gate + bias)
    lam = jnp.maximum(gate, 0.0) + jnp.log1p(jnp.exp(-jnp.abs(gate)))
    row_id, col_id = pair_ids(rows)
    inclusive = row_id >= col_id
    strict = row_id > col_id
    apart = row_id ^ col_id
    cum = mm_full(inclusive.astype(F32), -rate * switch)
    pack = jnp.where(lane < decay_col, lam, jnp.where(lane < beta_col, cum, switch))
    q_all, k_all, v_all = [], [], []
    for head in range(heads):
        for part in range(2):
            col = (part * heads + head) * LANES
            raw = acc[:, col : col + LANES]
            scale = lax.rsqrt(row_sum(raw * raw) + EPS)
            unit = raw * scale
            qkv_ref[part, head] = unit
            pack = jnp.where(lane == norm_col + part * heads + head, scale, pack)
            if part == 1:
                k_all.append(unit)
        col = (2 * heads + head) * LANES
        v_all.append(acc[:, col : col + LANES])
        qkv_ref[2, head] = v_all[head]
    pack_ref[...] = pack
    pack_t = pack.T
    pack_t_ref[...] = pack_t
    eye = (row_id == col_id).astype(F32)
    lower_all, trans_all = [], []
    for head in range(heads):
        decay = decay_of(pack, pack_t, decay_col + head, inclusive)
        beta = pack[:, beta_col + head : beta_col + head + 1]
        gram = mm_nt(k_all[head], k_all[head])
        lower = jnp.where(strict, beta * decay * gram, 0.0)
        lower_all.append(lower)
        trans_all.append((eye - jnp.where(apart == 1, lower, 0.0)).astype(BF16))
    for bit in range(1, rows.bit_length() - 1):
        here = (apart >> bit) == 1
        for head in range(heads):
            trans = trans_all[head]
            edge = jnp.where(here, lower_all[head], 0.0)
            trans_all[head] = trans - mm(mm(trans, edge), trans).astype(BF16)
    for head in range(heads):
        trans = trans_all[head]
        lower = lower_all[head]
        high = lower.astype(BF16)
        rest = eye - trans.astype(F32) - mm(high, trans) - mm(lower - high.astype(F32), trans)
        trans_all[head] = (trans.astype(F32) + mm(trans, rest)).astype(BF16)
        trans_ref[head] = trans_all[head]
    eye_key = eye[:LANES, :LANES]
    for head in range(heads):
        cum_col = pack[:, decay_col + head : decay_col + head + 1]
        beta = pack[:, beta_col + head : beta_col + head + 1]
        last = cum_col[rows - 1 : rows, :]
        tail = jnp.exp(last - cum_col) * k_all[head]
        mixed = mm_tn(trans_all[head], tail)
        mixed_ref[head] = mixed
        grown = (beta * jnp.exp(cum_col)) * k_all[head]
        pair_ref[head, :LANES] = (jnp.exp(last) * eye_key - mm_tn(grown, mixed)).astype(BF16)
        pair_ref[head, LANES:] = mm_tn(beta * v_all[head], mixed).astype(BF16)


def project(tokens, flat_w, small_t, head_param, heads, levels):
    rows, width = tokens.shape
    steps = 4
    depth = width // steps
    cols = 3 * heads
    key = flat_w.shape[1]
    fixed = lambda *shape: pl.BlockSpec(shape, lambda step: (0,) * len(shape))
    out_shape = (
        jax.ShapeDtypeStruct((width, cols * key), BF16),
        jax.ShapeDtypeStruct((3, heads, rows, key), F32),
        jax.ShapeDtypeStruct((rows, LANES), F32),
        jax.ShapeDtypeStruct((rows, LANES), F32),
        jax.ShapeDtypeStruct((LANES, rows), F32),
        jax.ShapeDtypeStruct((heads, rows, rows), BF16),
        jax.ShapeDtypeStruct((heads, rows, key), F32),
        jax.ShapeDtypeStruct((heads, 2 * key, key), BF16),
    )
    out_specs = (pl.BlockSpec((depth, cols * key), lambda step: (step, 0)),) + tuple(
        fixed(*shape.shape) for shape in out_shape[1:]
    )
    return pl.pallas_call(
        functools.partial(project_body, (heads, levels, steps)),
        grid=(steps,),
        out_shape=out_shape,
        in_specs=[
            SCALARS,
            pl.BlockSpec((rows, depth), lambda step: (0, step)),
            pl.BlockSpec((depth * cols, key), lambda step: (step, 0)),
            pl.BlockSpec((LANES, depth), lambda step: (0, step)),
        ],
        out_specs=out_specs,
        scratch_shapes=[
            pltpu.VMEM((depth * cols, key), F32),
            pltpu.VMEM((rows, cols * key), F32),
            pltpu.VMEM((rows, LANES), F32),
        ],
        compiler_params=PARAMS,
        name="project",
    )(head_param, tokens, flat_w, small_t)


def local_body(sizes, qkv_ref, pack_ref, pack_t_ref, trans_ref, attn_ref, local_ref, hat_ref):
    heads, levels, bits = sizes
    rows = pack_ref.shape[0]
    decay_col = levels * heads
    beta_col = decay_col + heads
    pack = pack_ref[...]
    pack_t = pack_t_ref[...]
    row_id, col_id = pair_ids(rows)
    inclusive = row_id >= col_id
    apart = row_id ^ col_id
    for head in range(heads):
        q_in, k_in, v_in = qkv_ref[0, head], qkv_ref[1, head], qkv_ref[2, head]
        decay = decay_of(pack, pack_t, decay_col + head, inclusive)
        scores = mm_nt_fine(q_in, k_in) * decay
        attn = mm(scores, trans_ref[head])
        attn_ref[head] = attn.astype(BF16)
        attn = attn * pack_t[beta_col + head : beta_col + head + 1, :]
        mix = level_mix(pack, head, heads, bits, apart)
        growth = jnp.exp(pack[:, decay_col + head : decay_col + head + 1])
        local_ref[head] = mm(attn * mix, v_in)
        hat_ref[head] = growth * q_in - mm(attn, growth * k_in)


def local_part(qkv, pack, pack_t, trans, levels, bits):
    heads, rows, key = qkv.shape[1:]
    return pl.pallas_call(
        functools.partial(local_body, (heads, levels, bits)),
        out_shape=(
            jax.ShapeDtypeStruct((heads, rows, rows), BF16),
            jax.ShapeDtypeStruct((heads, rows, key), F32),
            jax.ShapeDtypeStruct((heads, rows, key), F32),
        ),
        in_specs=[WHOLE] * 4,
        out_specs=(WHOLE,) * 3,
        compiler_params=PARAMS,
        name="local_part",
    )(qkv, pack, pack_t, trans)


def join_body(bit, place_ref, own_ref, other_ref, out_ref):
    heads = own_ref.shape[0]
    key = own_ref.shape[2]
    upper = ((place_ref[0] >> bit) & 1) == 1
    for head in range(heads):
        own, other = own_ref[head], other_ref[head]
        low = jnp.where(upper, other, own)
        high = jnp.where(upper, own, other)
        moved = mm(low, high[:key])
        out_ref[head, :key] = moved[:key].astype(BF16)
        out_ref[head, key:] = (moved[key:] + high[key:].astype(F32)).astype(BF16)


def join(bit, place, own, other):
    return pl.pallas_call(
        functools.partial(join_body, bit),
        out_shape=jax.ShapeDtypeStruct(own.shape, BF16),
        in_specs=[SCALARS, WHOLE, WHOLE],
        out_specs=WHOLE,
        compiler_params=PARAMS,
        name="join",
    )(place, own, other)


def cross_body(sizes, place_ref, gain_ref, pack_ref, local_ref, hat_ref, grad_ref, *refs):
    heads, bits, far = sizes
    others = refs[:far]
    normed_ref, dout_ref, dhat_ref, dfar_ref = refs[far : far + 4]
    sends = refs[far + 4 :]
    rows = pack_ref.shape[0]
    key = hat_ref.shape[2]
    place = place_ref[0]
    pack = pack_ref[...]
    gain = gain_ref[...]
    lane = lane_of(rows)
    dfar = jnp.zeros((rows, LANES), F32)
    eye_key = jnp.where(pair_ids(key)[0] == pair_ids(key)[1], 1.0, 0.0).astype(BF16)
    uppers = [((place >> bit) & 1) == 1 for bit in range(far)]
    for head in range(heads):
        prefix = eye_key
        prefixes, found = [], []
        for bit in range(far):
            prefixes.append(prefix)
            moved = mm(others[bit][head], prefix)
            found.append(jnp.where(uppers[bit], moved[key:], 0.0).astype(BF16))
            prefix = jnp.where(uppers[bit], moved[:key].astype(BF16), prefix)
        hat = hat_ref[head].astype(BF16)
        summed = local_ref[head]
        reached, weights = [], []
        for bit in range(far):
            col = (bits + 1 + bit) * heads + head
            weights.append(pack[:, col : col + 1])
            reached.append(mm_nt(hat, found[bit]))
            summed = summed + weights[bit] * reached[bit]
        scale = lax.rsqrt(jnp.mean(summed * summed, -1, keepdims=True) + EPS)
        unit = summed * scale
        normed_ref[:, head * key : (head + 1) * key] = (unit * gain).astype(BF16)
        pulled = grad_ref[:, head * key : (head + 1) * key] * gain
        dout = scale * (pulled - unit * jnp.mean(pulled * unit, -1, keepdims=True))
        dout_ref[head] = dout
        dhat = jnp.zeros((rows, key), F32)
        dfound = []
        for bit in range(far):
            col = (bits + 1 + bit) * heads + head
            dfar = jnp.where(lane == col, row_sum(dout * reached[bit]), dfar)
            spread = (weights[bit] * dout).astype(BF16)
            dhat = dhat + mm(spread, found[bit])
            dfound.append(mm_tn(spread, hat))
        dhat_ref[head] = dhat
        dprefix = jnp.zeros((key, key), F32)
        for bit in reversed(range(far)):
            dfree = jnp.where(uppers[bit], dfound[bit], 0.0)
            if bit == far - 1:
                sends[bit][head] = mm_nt(dfree, prefixes[bit]).astype(BF16)
                if bit > 0:
                    dprefix = mm_tn(others[bit][head, key:], dfree)
            else:
                both = jnp.concatenate([jnp.where(uppers[bit], dprefix, 0.0), dfree], 0)
                sends[bit][head] = mm_nt(both, prefixes[bit]).astype(BF16)
                if bit > 0:
                    moved = mm_tn(others[bit][head], both)
                    dprefix = jnp.where(uppers[bit], moved, dprefix)
    dfar_ref[...] = dfar


def cross(place, gain, pack, local_out, hat, grad_normed, others, bits):
    heads, rows, key = hat.shape
    far = len(others)
    sends = tuple(
        jax.ShapeDtypeStruct((heads, (1 if bit == far - 1 else 2) * key, key), BF16)
        for bit in range(far)
    )
    out_shape = (
        jax.ShapeDtypeStruct((rows, heads * key), BF16),
        jax.ShapeDtypeStruct((heads, rows, key), F32),
        jax.ShapeDtypeStruct((heads, rows, key), F32),
        jax.ShapeDtypeStruct((rows, LANES), F32),
    ) + sends
    return pl.pallas_call(
        functools.partial(cross_body, (heads, bits, far)),
        out_shape=out_shape,
        in_specs=[SCALARS] + [WHOLE] * (5 + far),
        out_specs=(WHOLE,) * len(out_shape),
        compiler_params=PARAMS,
        name="cross",
    )(place, gain, pack, local_out, hat, grad_normed, *others)


def spread_body(count, place_ref, left_ref, right_ref, *out_refs):
    size = out_refs[0].shape[1]
    for shift in range(count):
        dest = lax.rem(place_ref[1] + shift, count)
        cols = pl.ds(pl.multiple_of(dest * size, size), size)
        out_refs[shift][...] = jnp.dot(
            left_ref[...], right_ref[:, cols], preferred_element_type=F32
        ).astype(BF16)


def spread_out(place, left, right, count):
    size = right.shape[1] // count
    return pl.pallas_call(
        functools.partial(spread_body, count),
        out_shape=(jax.ShapeDtypeStruct((left.shape[0], size), BF16),) * count,
        in_specs=[SCALARS, WHOLE, WHOLE],
        out_specs=(WHOLE,) * count,
        compiler_params=PARAMS,
        name="spread_out",
    )(place, left, right)


def lower_pull(dlower, beta, decay, gram, strict, k_in):
    dlower = jnp.where(strict, dlower, 0.0)
    shaped = dlower * decay
    dbeta = row_sum(shaped * gram)
    dgram = shaped * beta
    both = dgram * gram
    dkey = mm(dgram, k_in) + mm_tn(dgram, k_in)
    return dbeta, row_sum(both), col_sum(both), dkey


def pull_body(
    sizes, qkv_ref, pack_ref, pack_t_ref, trans_ref, attn_ref, dout_ref, dhat_ref,
    dqkv_ref, dgrown_ref, dcol_ref, drow_ref
):
    heads, levels, bits = sizes
    rows = pack_ref.shape[0]
    decay_col = levels * heads
    beta_col = decay_col + heads
    block_bit = BLOCK.bit_length() - 1
    pack = pack_ref[...]
    pack_t = pack_t_ref[...]
    row_id, col_id = pair_ids(rows)
    inclusive = row_id >= col_id
    strict = row_id > col_id
    apart = row_id ^ col_id
    lane = lane_of(rows)
    dcol = jnp.zeros((rows, LANES), F32)
    dbeta_rows, dcum_rows = [], []
    for head in range(heads):
        q_in, k_in, v_in = qkv_ref[0, head], qkv_ref[1, head], qkv_ref[2, head]
        decay = decay_of(pack, pack_t, decay_col + head, inclusive)
        beta = pack[:, beta_col + head : beta_col + head + 1]
        beta_row = pack_t[beta_col + head : beta_col + head + 1, :]
        growth = jnp.exp(pack[:, decay_col + head : decay_col + head + 1])
        mix = level_mix(pack, head, heads, bits, apart)
        attn_low = attn_ref[head]
        attn0 = attn_low.astype(F32)
        attn = attn0 * beta_row
        dout = dout_ref[head].astype(BF16)
        dhat = dhat_ref[head]
        gram = mm_nt(k_in, k_in)
        scores = mm_nt(q_in, k_in) * decay
        rest = dout_ref[head] - dout.astype(F32)
        dprod = mm_nt(dout, v_in) + mm_nt(rest, v_in)
        dv = mm_tn(attn * mix, dout)
        touched = dprod * attn
        for level in range(bits + 1):
            if level == 0:
                here = (apart >> block_bit) == 0
            else:
                here = (apart >> (block_bit + level - 1)) == 1
            dcol = jnp.where(
                lane == level * heads + head, row_sum(jnp.where(here, touched, 0.0)), dcol
            )
        dattn = dprod * mix - mm_nt(dhat, growth * k_in)
        dattn0 = dattn * beta_row
        dbeta_rows.append(col_sum(dattn * attn0))
        dscore = mm_nt(dattn0, trans_ref[head])
        dlower = -mm_tn(attn_low, dscore)
        dgrown = -beta * mm_tn(attn_low, dhat)
        dprobs = dscore * decay
        dq = growth * dhat + mm(dprobs, k_in)
        dk = mm_tn(dprobs, q_in)
        shift = dscore * scores
        dbeta, dcum_col, dcum_row, dk_lower = lower_pull(dlower, beta, decay, gram, strict, k_in)
        dcum_col = dcum_col + row_sum(shift) + growth * row_sum(q_in * dhat)
        dcum_rows.append(-dcum_row - col_sum(shift))
        dqkv_ref[0, head] = dq
        dqkv_ref[1, head] = dk + dk_lower
        dqkv_ref[2, head] = dv
        dgrown_ref[head] = dgrown
        dcol = jnp.where(lane == beta_col + head, dbeta, dcol)
        dcol = jnp.where(lane == decay_col + head, dcum_col, dcol)
    dcol_ref[...] = dcol
    drow_ref[...] = jnp.concatenate(dcum_rows + dbeta_rows, 0)


def pull_local(qkv, pack, pack_t, trans, attn, dout, dhat, levels, bits):
    heads, rows, key = qkv.shape[1:]
    out_shape = (
        jax.ShapeDtypeStruct((3, heads, rows, key), F32),
        jax.ShapeDtypeStruct((heads, rows, key), F32),
        jax.ShapeDtypeStruct((rows, LANES), F32),
        jax.ShapeDtypeStruct((2 * heads, rows), F32),
    )
    return pl.pallas_call(
        functools.partial(pull_body, (heads, levels, bits)),
        out_shape=out_shape,
        in_specs=[WHOLE] * 7,
        out_specs=(WHOLE,) * len(out_shape),
        compiler_params=PARAMS,
        name="pull_local",
    )(qkv, pack, pack_t, trans, attn, dout, dhat)


def finish_body(sizes, place_ref, hp_ref, *refs):
    heads, levels, far, count = sizes
    (qkv_ref, gate_ref, pack_ref, pack_t_ref, trans_ref, mixed_ref, dqkv_ref, dgrown_ref,
     dcol_ref, drow_ref, dfar_ref, small_ref, wr_ref) = refs[:13]
    others = refs[13 : 13 + far]
    arrived = refs[13 + far : 13 + 2 * far]
    out_refs = refs[13 + 2 * far : 13 + 2 * far + count]
    dproj, wr, sem = refs[13 + 2 * far + count :]
    rows = pack_ref.shape[0]
    key = qkv_ref.shape[3]
    fetch = pltpu.make_async_copy(wr_ref, wr, sem)
    fetch.start()
    decay_col = levels * heads
    beta_col = decay_col + heads
    norm_col = beta_col + heads
    place = place_ref[0]
    uppers = [((place >> bit) & 1) == 1 for bit in range(far)]
    pack = pack_ref[...]
    pack_t = pack_t_ref[...]
    row_id, col_id = pair_ids(rows)
    inclusive = row_id >= col_id
    strict = row_id > col_id
    lane = lane_of(rows)
    last_row = lax.broadcasted_iota(jnp.int32, (rows, 1), 0) == rows - 1
    eye_key = (pair_ids(key)[0] == pair_ids(key)[1]).astype(F32)
    dcol = jnp.where(lane < decay_col, dcol_ref[...] + dfar_ref[...], dcol_ref[...])
    dcum_rows, dcum_cols = [], []
    for head in range(heads):
        q_in, k_in, v_in = qkv_ref[0, head], qkv_ref[1, head], qkv_ref[2, head]
        decay = decay_of(pack, pack_t, decay_col + head, inclusive)
        beta = pack[:, beta_col + head : beta_col + head + 1]
        cum_col = pack[:, decay_col + head : decay_col + head + 1]
        growth = jnp.exp(cum_col)
        last = cum_col[rows - 1 : rows, :]
        tail = jnp.exp(last - cum_col)
        gram = mm_nt(k_in, k_in)
        dpair = jnp.zeros((2 * key, key), F32)
        for bit in reversed(range(far)):
            other = others[bit][head]
            if bit == far - 1:
                got = jnp.concatenate(
                    [jnp.zeros((key, key), F32), arrived[bit][head].astype(F32)], 0
                )
                dpair = jnp.where(uppers[bit], 0.0, got)
            else:
                as_low = mm_nt(dpair, other[:key]) + arrived[bit][head].astype(F32)
                as_high = jnp.concatenate([mm_tn(other, dpair), dpair[key:]], 0)
                dpair = jnp.where(uppers[bit], as_high, as_low)
        mixed = mixed_ref[head]
        grown = growth * k_in
        dmixed = mm(v_in, dpair[key:]) - mm(grown, dpair[:key])
        moved = mm_nt(beta * mixed, dpair)
        dgrown = dgrown_ref[head] - moved[:, :key]
        dv = dqkv_ref[2, head] + moved[:, key:]
        dbeta_more = row_sum(mixed * dmixed)
        dtail = mm(trans_ref[head], beta * dmixed)
        dbeta, dcum_col, dcum_row, dk_lower = lower_pull(
            -mm_nt(mixed, dtail), beta, decay, gram, strict, k_in
        )
        dcum_rows.append(-dcum_row)
        tail_pull = tail * row_sum(k_in * dtail)
        at_last = col_sum(tail_pull) + jnp.exp(last) * col_sum(row_sum(dpair[:key] * eye_key))
        dcum_col = dcum_col + growth * row_sum(k_in * dgrown) - tail_pull
        dcum_col = dcum_col + jnp.where(last_row, at_last, 0.0)
        dk = dqkv_ref[1, head] + dk_lower + growth * dgrown + tail * dtail
        dq = dqkv_ref[0, head]
        dcol = dcol + jnp.where(lane == beta_col + head, dbeta + dbeta_more, 0.0)
        dcol = dcol + jnp.where(lane == decay_col + head, dcum_col, 0.0)
        for part, unit, dunit in ((0, q_in, dq), (1, k_in, dk)):
            at = norm_col + part * heads + head
            scale = pack[:, at : at + 1]
            back = scale * (dunit - unit * row_sum(unit * dunit))
            col = (part * heads + head) * key
            dproj[:, col : col + key] = back.astype(BF16)
        col = (2 * heads + head) * key
        dproj[:, col : col + key] = dv.astype(BF16)
    drow = drow_ref[...]
    drow = drow + jnp.concatenate(dcum_rows + [jnp.zeros((heads, rows), F32)], 0)
    drow = jnp.concatenate(
        [jnp.zeros((decay_col, rows), F32), drow,
         jnp.zeros((LANES - norm_col, rows), F32)], 0
    )
    dcol = dcol + drow.T
    lane_row = lane_of(1)
    rate = jnp.zeros((1, LANES), F32)
    bias = jnp.zeros((1, LANES), F32)
    for head in range(heads):
        rate = jnp.where(lane_row == decay_col + head, hp_ref[head, 0], rate)
        bias = jnp.where(lane_row == beta_col + head, hp_ref[head, 1], bias)
    switch = jax.nn.sigmoid(gate_ref[...] + bias)
    dlog = mm_full((row_id <= col_id).astype(F32), dcol)
    slope = switch * (1.0 - switch)
    dgate = jnp.where(
        lane < decay_col,
        dcol * switch,
        jnp.where(lane < beta_col, -rate * dlog * slope, dcol * slope),
    )
    dgate = jnp.where(lane < norm_col, dgate, 0.0).astype(BF16)
    fetch.wait()
    size = out_refs[0].shape[1]
    for shift in range(count):
        dest = lax.rem(place_ref[1] + shift, count)
        span = pl.ds(pl.multiple_of(dest * size, size), size)
        part = mm_nt(dproj[...], wr[span, :]) + mm(dgate, small_ref[:, span])
        out_refs[shift][...] = part.astype(BF16)


def finish(place, head_param, arrays, wr, others, arrived, levels, count):
    heads, rows, key = arrays[0].shape[1:]
    width = wr.shape[0]
    far = len(others)
    return pl.pallas_call(
        functools.partial(finish_body, (heads, levels, far, count)),
        out_shape=(jax.ShapeDtypeStruct((rows, width // count), BF16),) * count,
        in_specs=[SCALARS, SCALARS]
        + [WHOLE] * len(arrays)
        + [pl.BlockSpec(memory_space=pl.ANY)]
        + [WHOLE] * (2 * far),
        out_specs=(WHOLE,) * count,
        scratch_shapes=[
            pltpu.VMEM((rows, wr.shape[1]), BF16),
            pltpu.VMEM(wr.shape, BF16),
            pltpu.SemaphoreType.DMA,
        ],
        compiler_params=PARAMS,
        name="finish",
    )(place, head_param, *arrays, wr, *others, *arrived)


def swap(value, axis, bit):
    size = lax.axis_size(axis)
    return lax.ppermute(value, axis, [(at, at ^ (1 << bit)) for at in range(size)])


def scatter_sum(parts, axis):
    count = lax.axis_size(axis)
    total = parts[0].astype(F32)
    for shift in range(1, count):
        got = lax.ppermute(parts[shift], axis, [(at, (at + shift) % count) for at in range(count)])
        total = total + got.astype(F32)
    return total.astype(BF16)


def on_device(tokens, qkv_weight, small_weight, head_param, norm_gain, out_weight, grad_out):
    rows, width = tokens.shape
    heads, key = qkv_weight.shape[2:]
    cols = small_weight.shape[2]
    levels = cols - 2
    bits = (rows // BLOCK).bit_length() - 1
    far = lax.axis_size("ctx").bit_length() - 1
    count = lax.axis_size("head")
    place = jnp.stack([lax.axis_index("ctx"), lax.axis_index("head")]).astype(jnp.int32)
    flat_w = qkv_weight.reshape(width * 3 * heads, key)
    small_t = jnp.transpose(small_weight, (2, 1, 0)).reshape(cols * heads, width)
    small_t = jnp.pad(small_t, ((0, LANES - cols * heads), (0, 0)))
    flat_out = out_weight.reshape(heads * key, width)
    gain = norm_gain.reshape(1, key)

    wr, qkv, gate, pack, pack_t, trans, mixed, pair = project(
        tokens, flat_w, small_t, head_param, heads, levels
    )
    attn, local_out, hat = local_part(qkv, pack, pack_t, trans, levels, bits)
    grad_normed = lax.dot_general(
        grad_out, flat_out, (((1,), (1,)), ((), ())), preferred_element_type=F32
    )
    others = []
    for bit in range(far):
        others.append(swap(pair, "ctx", bit))
        if bit < far - 1:
            pair = join(bit, place, pair, others[bit])
    normed, dout, dhat, dfar, *sends = cross(
        place, gain, pack, local_out, hat, grad_normed, others, bits
    )
    arrived = []
    for bit in range(far):
        got = [swap(value, "ctx", bit) for value in sends]
        arrived.append(got[0])
        sends = [
            (mine.astype(F32) + more.astype(F32)).astype(BF16)
            for mine, more in zip(sends[1:], got[1:])
        ]
    layer_out = scatter_sum(spread_out(place, normed, flat_out, count), "head")
    dqkv, dgrown, dcol, drow = pull_local(
        qkv, pack, pack_t, trans, attn, dout, dhat, levels, bits
    )
    arrays = (qkv, gate, pack, pack_t, trans, mixed, dqkv, dgrown, dcol, drow, dfar, small_t)
    parts = finish(place, head_param, arrays, wr, others, arrived, levels, count)
    return layer_out, scatter_sum(parts, "head")


def solution(mesh):
    placed = (
        P("ctx", None),
        P(None, None, "head", None),
        P(None, "head", None),
        P("head", None),
        P(),
        P("head", None, None),
        P("ctx", None),
    )
    return jax.shard_map(
        on_device,
        mesh=mesh,
        in_specs=placed,
        out_specs=(P("ctx", "head"), P("ctx", "head")),
        check_vma=False,
    )
```

time: 399 us -> 114 us (0.29)
  the two profiles are of different devices: /device:TPU:0 before, /device:TPU:8 now
where the time goes in v1:
time: 114 us; the launch traced here: 113 us
  Pallas kernels  52.5 us (46%)
  waiting for transfers between devices  32.1 us (28%)
  starting transfers between devices  16.7 us (15%)
  local copies, waits for them, and re-layouts  6.1 us (5%)
  other arithmetic  3.38 us (3%)
  matrix products  1.62 us (1%)
    ppermute x6, waiting for transfers between devices, scatter_sum(): lax.ppermute(parts[shift], axis, [(at, (at + shift) % count) for at in ra...  20.1 us
    pallas_call x1, Pallas kernels, project(): pl.pallas_call(functools.partial(project_body, (heads, levels, steps)), g...  13.8 us
    ppermute x9, waiting for transfers between devices, swap(): lax.ppermute(value, axis, [(at, at ^ 1 << bit) for at in range(size)])  12 us
    pallas_call x1, Pallas kernels, finish(): pl.pallas_call(functools.partial(finish_body, (heads, levels, far, count)...  11.1 us
    pallas_call x1, Pallas kernels, pull_local(): pl.pallas_call(functools.partial(pull_body, (heads, levels, bits)), out_s...  8.67 us
    ppermute x6, starting transfers between devices, scatter_sum(): lax.ppermute(parts[shift], axis, [(at, (at + shift) % count) for at in ra...  8.38 us
    ppermute x9, starting transfers between devices, swap(): lax.ppermute(value, axis, [(at, at ^ 1 << bit) for at in range(size)])  8.35 us
    pallas_call x1, Pallas kernels, cross(): pl.pallas_call(functools.partial(cross_body, (heads, bits, far)), out_sha...  7.61 us
  transfers between devices with their start and end apart: 15, of which 7 were waited for; matrix products, arithmetic and copies ran while one was open for 3% of the time, Pallas kernels for 24%

profile of v1, /device:TPU:8, one launch (start us, length us, event | category | flops | bytes accessed | tf_op | source)
XLA Modules:
  0.0 113.2 jit_solution(2884095572758262228)
XLA Ops:
  0.6 1.4 %copy.9.hp_ref = f32[4,2]{1,0:T(4,128)} copy(f32[4,2]{0,1:T(2,128)} %param.10) | data formatting | bytes 64 | tf_op args[3]
  2.0 1.0 reshape.18
  3.0 0.8 pad.4.small_ref.refs_11_
  3.9 13.8 %project.1 = (bf16[2048,1536]{1,0:T(8,128)(2,1)}, f32[3,4,256,128]{3,2,1,0:T(8,128)}, f32[256,128]{1,0:T(8,128)}, f32[256,128]{1,0:T(8,128)}, f32[128,256]{1,0:T...) custom-call(f32[4,2]{1,0:T(4,128)} %copy.9.hp_ref, ...), custom_call_target="tpu_custom_call" | custom-call | tf_op jit(solution)/shard_map/project/pallas_call | solution.py:222
  18.4 1.1 collective-permute-done.other_ref.refs_0_.refs_13_
  19.5 0.7 copy-done.1
  20.2 2.0 %join.2.own_ref = bf16[4,256,128]{2,1,0:T(8,128)(2,1)} custom-call(s32[2]{0:T(128)} %pad_add_fusion.place_ref, bf16[4,256,128]{2,1,0:T(8,128)(2,1)} %get-tuple-element.38.own_ref, bf16[4,256,128]{2,1,0:T(8,128)(2,1)} %copy-done.1), custom_call_target="tpu_custom_call" | custom-call | tf_op jit(solution)/shard_map/join/pallas_call | solution.py:296
  22.2 1.5 %collective-permute-start.1 = (bf16[4,256,128]{2,1,0:T(8,128)(2,1)}, bf16[4,256,128]{2,1,0:T(8,128)(2,1)S(1)}, u32[]{:S(2)}, u32[]{:S(2)}) collective-permute-start(bf16[4,256,128]{2,1,0:T(8,128)(2,1)} %join.2.own_ref), channel_id=1, source_target_pairs={{0,8},{4,12},{8,0},{12,4},{16,24},{20,28},{24,16},{28,20},{1,9},{5... | collective-permute-start | bytes 786440 | tf_op jit(solution)/shard_map/ppermute | solution.py:638
  23.7 4.2 %local_part.1 = (bf16[4,256,256]{2,1,0:T(8,128)(2,1)}, f32[4,256,128]{2,1,0:T(8,128)}, f32[4,256,128]{2,1,0:T(8,128)}) custom-call(f32[3,4,256,128]{3,2,1,0:T(8,128)} %get-tuple-element.33.qkv_ref.refs_0_, f32[256,128]{1,0:T(8,128)} %get-tuple-element.32.pack_ref.refs_2_, f32[128,256]{1,0:T(8,128)} %get-tuple-element.34.pack_t_ref.refs_3_, ...), custom_call_target="tpu_custom_call" | custom-call | tf_op jit(solution)/shard_map/local_part/pallas_call | solution.py:268
  27.9 2.9 %collective-permute-done.1.other_ref.refs_1_.refs_14_ = bf16[4,256,128]{2,1,0:T(8,128)(2,1)S(1)} collective-permute-done((bf16[4,256,128]{2,1,0:T(8,128)(2,1)}, bf16[4,256,128]{2,1,0:T(8,128)(2,1)S(1)}, u32[]{:S(2)}, u32[]{:S(2)}) %collective-permute-start.1) | collective-permute-done | bytes 262176 | tf_op jit(solution)/shard_map/ppermute | solution.py:638
  30.8 0.7 copy-done.2
  31.5 2.0 %join.3 = bf16[4,256,128]{2,1,0:T(8,128)(2,1)} custom-call(s32[2]{0:T(128)} %pad_add_fusion.place_ref, bf16[4,256,128]{2,1,0:T(8,128)(2,1)} %join.2.own_ref, bf16[4,256,128]{2,1,0:T(8,128)(2,1)} %copy-done.2), custom_call_target="tpu_custom_call" | custom-call | tf_op jit(solution)/shard_map/join/pallas_call | solution.py:296
  33.5 1.5 %collective-permute-start.2 = (bf16[4,256,128]{2,1,0:T(8,128)(2,1)}, bf16[4,256,128]{2,1,0:T(8,128)(2,1)S(1)}, u32[]{:S(2)}, u32[]{:S(2)}) collective-permute-start(bf16[4,256,128]{2,1,0:T(8,128)(2,1)} %join.3), channel_id=1, source_target_pairs={{0,16},{4,20},{8,24},{12,28},{16,0},{20,4},{24,8},{28,12},{1,17},{... | collective-permute-start | bytes 786440 | tf_op jit(solution)/shard_map/ppermute | solution.py:638
  35.0 1.6 %fusion.grad_ref = f32[256,512]{1,0:T(8,128)} fusion(bf16[256,2048]{1,0:T(8,128)(2,1)S(1)} %copy-done, bf16[512,2048]{1,0:T(8,128)(2,1)S(1)} %bitcast.10), kind=kOutput, calls=%fused_computation.6 | convolution fusion | flops 536870912 | bytes 3670016 | tf_op jit(solution)/shard_map/dot_general | solution.py:669
  36.6 4.6 %collective-permute-done.2.refs_2_.refs_15_ = bf16[4,256,128]{2,1,0:T(8,128)(2,1)S(1)} collective-permute-done((bf16[4,256,128]{2,1,0:T(8,128)(2,1)}, bf16[4,256,128]{2,1,0:T(8,128)(2,1)S(1)}, u32[]{:S(2)}, u32[]{:S(2)}) %collective-permute-start.2) | collective-permute-done | bytes 262176 | tf_op jit(solution)/shard_map/ppermute | solution.py:638
  41.9 7.6 %cross.1 = (bf16[256,512]{1,0:T(8,128)(2,1)}, f32[4,256,128]{2,1,0:T(8,128)}, f32[4,256,128]{2,1,0:T(8,128)}, f32[256,128]{1,0:T(8,128)}, bf16[4,256,128]{2,1,0:...) custom-call(s32[2]{0:T(128)} %pad_add_fusion.place_ref, f32[1,128]{1,0:T(1,128)} %bitcast.12, ...), custom_call_target="tpu_custom_call" | custom-call | tf_op jit(solution)/shard_map/cross/pallas_call | solution.py:380
  50.2 3.1 %spread_out.1 = (bf16[256,512]{1,0:T(8,128)(2,1)}, bf16[256,512]{1,0:T(8,128)(2,1)}, bf16[256,512]{1,0:T(8,128)(2,1)}, bf16[256,512]{1,0:T(8,128)(2,1)}) custom-call(s32[2]{0:T(128)} %pad_add_fusion.place_ref, bf16[256,512]{1,0:T(8,128)(2,1)} %get-tuple-element.39.left_ref, bf16[512,2048]{1,0:T(8,128)(2,1)} %bitcast.9), custom_call_target="tpu_custom_call" | custom-call | tf_op jit(solution)/shard_map/spread_out/pallas_call | solution.py:402
  53.3 1.6 %collective-permute-start.3 = (bf16[256,512]{1,0:T(8,128)(2,1)}, bf16[256,512]{1,0:T(8,128)(2,1)S(1)}, u32[]{:S(2)}, u32[]{:S(2)}) collective-permute-start(bf16[256,512]{1,0:T(8,128)(2,1)} %get-tuple-element.41), channel_id=1, source_target_pairs={{0,1},{1,2},{2,3},{3,0},{4,5},{5,6},{6,7},{7,4},{8,9},{9,10},{10,1... | collective-permute-start | bytes 786440 | tf_op jit(solution)/shard_map/ppermute | solution.py:645
  54.9 1.3 %collective-permute-start.4 = (bf16[256,512]{1,0:T(8,128)(2,1)}, bf16[256,512]{1,0:T(8,128)(2,1)S(1)}, u32[]{:S(2)}, u32[]{:S(2)}) collective-permute-start(bf16[256,512]{1,0:T(8,128)(2,1)} %get-tuple-element.42), channel_id=1, source_target_pairs={{0,2},{1,3},{2,0},{3,1},{4,6},{5,7},{6,4},{7,5},{8,10},{9,11},{10,... | collective-permute-start | bytes 786440 | tf_op jit(solution)/shard_map/ppermute | solution.py:645
  56.2 1.7 %collective-permute-start.5 = (bf16[256,512]{1,0:T(8,128)(2,1)}, bf16[256,512]{1,0:T(8,128)(2,1)S(1)}, u32[]{:S(2)}, u32[]{:S(2)}) collective-permute-start(bf16[256,512]{1,0:T(8,128)(2,1)} %get-tuple-element.43), channel_id=1, source_target_pairs={{0,3},{1,0},{2,1},{3,2},{4,7},{5,4},{6,5},{7,6},{8,11},{9,8},{10,9... | collective-permute-start | bytes 786440 | tf_op jit(solution)/shard_map/ppermute | solution.py:645
  58.0 1.6 %collective-permute-start.10 = (bf16[4,128,128]{2,1,0:T(8,128)(2,1)S(1)}, bf16[4,128,128]{2,1,0:T(8,128)(2,1)S(1)}, u32[]{:S(2)}, u32[]{:S(2)}) collective-permute-start(bf16[4,128,128]{2,1,0:T(8,128)(2,1)S(1)} %add_convert_fusion.4), channel_id=1, source_target_pairs={{0,8},{4,12},{8,0},{12,4},{16,24},{20,28},{24,16},{28,20},{1,9},{5... | collective-permute-start | bytes 393224 | tf_op jit(solution)/shard_map/ppermute | solution.py:638
  59.6 3.4 %collective-permute-done.10 = bf16[4,128,128]{2,1,0:T(8,128)(2,1)S(1)} collective-permute-done((bf16[4,128,128]{2,1,0:T(8,128)(2,1)S(1)}, bf16[4,128,128]{2,1,0:T(8,128)(2,1)S(1)}, u32[]{:S(2)}, u32[]{:S(2)}) %collective-permute-start.10) | collective-permute-done | bytes 131104 | tf_op jit(solution)/shard_map/ppermute | solution.py:638
  63.0 1.5 %collective-permute-start.8 = (bf16[4,256,128]{2,1,0:T(8,128)(2,1)S(1)}, bf16[4,256,128]{2,1,0:T(8,128)(2,1)S(1)}, u32[]{:S(2)}, u32[]{:S(2)}) collective-permute-start(bf16[4,256,128]{2,1,0:T(8,128)(2,1)S(1)} %add_convert_fusion.1), channel_id=1, source_target_pairs={{0,8},{4,12},{8,0},{12,4},{16,24},{20,28},{24,16},{28,20},{1,9},{5... | collective-permute-start | bytes 786440 | tf_op jit(solution)/shard_map/ppermute | solution.py:638
  64.6 1.6 %collective-permute-start.11 = (bf16[4,128,128]{2,1,0:T(8,128)(2,1)S(1)}, bf16[4,128,128]{2,1,0:T(8,128)(2,1)S(1)}, u32[]{:S(2)}, u32[]{:S(2)}) collective-permute-start(bf16[4,128,128]{2,1,0:T(8,128)(2,1)S(1)} %add_convert_fusion.3), channel_id=1, source_target_pairs={{0,16},{4,20},{8,24},{12,28},{16,0},{20,4},{24,8},{28,12},{1,17},{... | collective-permute-start | bytes 393224 | tf_op jit(solution)/shard_map/ppermute | solution.py:638
  66.2 8.7 %pull_local.1 = (f32[3,4,256,128]{3,2,1,0:T(8,128)}, f32[4,256,128]{2,1,0:T(8,128)}, f32[256,128]{1,0:T(8,128)}, f32[8,256]{1,0:T(8,128)}) custom-call(f32[3,4,256,128]{3,2,1,0:T(8,128)} %get-tuple-element.33.qkv_ref.refs_0_, f32[256,128]{1,0:T(8,128)} %get-tuple-element.32.pack_ref.refs_2_, f32[128,256]{1,0:T(8,128)} %get-tuple-element.34.pack_t_ref.refs_3_, ...), custom_call_target="tpu_custom_call" | custom-call | tf_op jit(solution)/shard_map/pull_local/pallas_call | solution.py:497
  75.6 11.1 %finish.1 = (bf16[256,512]{1,0:T(8,128)(2,1)}, bf16[256,512]{1,0:T(8,128)(2,1)}, bf16[256,512]{1,0:T(8,128)(2,1)}, bf16[256,512]{1,0:T(8,128)(2,1)}) custom-call(s32[2]{0:T(128)} %pad_add_fusion.place_ref, f32[4,2]{1,0:T(4,128)} %copy.9.hp_ref, f32[3,4,256,128]{3,2,1,0:T(8,128)} %get-tuple-element.33.qkv_ref.refs_0_, f32[256,128]{1,0:T(8,128)} %get-tuple-element.44.refs_1_, ...), custom_call_target="tpu_custom_call" | custom-call | tf_op jit(solution)/shard_map/finish/pallas_call | solution.py:618
  87.0 3.4 %collective-permute-start.13 = (bf16[256,512]{1,0:T(8,128)(2,1)}, bf16[256,512]{1,0:T(8,128)(2,1)S(1)}, u32[]{:S(2)}, u32[]{:S(2)}) collective-permute-start(bf16[256,512]{1,0:T(8,128)(2,1)} %get-tuple-element.60), channel_id=1, source_target_pairs={{0,2},{1,3},{2,0},{3,1},{4,6},{5,7},{6,4},{7,5},{8,10},{9,11},{10,... | collective-permute-start | bytes 786440 | tf_op jit(solution)/shard_map/ppermute | solution.py:645
  90.5 0.8 add_convert_fusion.2
  91.4 13.7 %collective-permute-done.12 = bf16[256,512]{1,0:T(8,128)(2,1)S(1)} collective-permute-done((bf16[256,512]{1,0:T(8,128)(2,1)}, bf16[256,512]{1,0:T(8,128)(2,1)S(1)}, u32[]{:S(2)}, u32[]{:S(2)}) %collective-permute-start.12) | collective-permute-done | bytes 262176 | tf_op jit(solution)/shard_map/ppermute | solution.py:645
  105.0 3.1 %collective-permute-done.13 = bf16[256,512]{1,0:T(8,128)(2,1)S(1)} collective-permute-done((bf16[256,512]{1,0:T(8,128)(2,1)}, bf16[256,512]{1,0:T(8,128)(2,1)S(1)}, u32[]{:S(2)}, u32[]{:S(2)}) %collective-permute-start.13) | collective-permute-done | bytes 262176 | tf_op jit(solution)/shard_map/ppermute | solution.py:645
  108.1 3.3 %collective-permute-done.14 = bf16[256,512]{1,0:T(8,128)(2,1)S(1)} collective-permute-done((bf16[256,512]{1,0:T(8,128)(2,1)}, bf16[256,512]{1,0:T(8,128)(2,1)S(1)}, u32[]{:S(2)}, u32[]{:S(2)}) %collective-permute-start.14) | collective-permute-done | bytes 262176 | tf_op jit(solution)/shard_map/ppermute | solution.py:645
  111.4 1.8 %add_convert_fusion = bf16[256,512]{1,0:T(8,128)(2,1)} fusion(bf16[256,512]{1,0:T(8,128)(2,1)S(1)} %collective-permute-done.14, bf16[256,512]{1,0:T(8,128)(2,1)S(1)} %collective-permute-done.13, bf16[256,512]{1,0:T(8,128)(2,1)S(1)} %collective-permute-done.12, bf16[256,512]{1,0:T(8,128)(2,1)} %get-tuple-element.58), kind=kLoop, calls=%fused_computation | loop fusion | flops 1048576 | bytes 1310720 | tf_op jit(solution)/shard_map/convert_element_type | solution.py:647
  (38 shorter events, 3.3 us)
Async XLA Ops:
  0.6 34.4 %copy-start = (bf16[256,2048]{1,0:T(8,128)(2,1)S(1)}, bf16[256,2048]{1,0:T(8,128)(2,1)}, u32[]{:S(2)}) copy-start(bf16[256,2048]{1,0:T(8,128)(2,1)} %param.13) | copy-start | bytes 3145732
  17.7 17.3 %copy-start.3 = (bf16[4,128,2048]{2,1,0:T(8,128)(2,1)S(1)}, bf16[4,128,2048]{2,1,0:T(8,128)(2,1)}, u32[]{:S(2)}) copy-start(bf16[4,128,2048]{2,1,0:T(8,128)(2,1)} %param.12) | copy-start | bytes 6291460
  17.7 1.8 %collective-permute-start = (bf16[4,256,128]{2,1,0:T(8,128)(2,1)}, bf16[4,256,128]{2,1,0:T(8,128)(2,1)S(1)}, u32[]{:S(2)}, u32[]{:S(2)}) collective-permute-start(bf16[4,256,128]{2,1,0:T(8,128)(2,1)} %get-tuple-element.38.own_ref), channel_id=1, source_target_pairs={{0,4},{4,0},{8,12},{12,8},{16,20},{20,16},{24,28},{28,24},{1,5},{5... | collective-permute-start | bytes 786440 | tf_op jit(solution)/shard_map/ppermute | solution.py:638
  19.5 0.7 copy-start.1
  22.2 8.6 %collective-permute-start.1 = (bf16[4,256,128]{2,1,0:T(8,128)(2,1)}, bf16[4,256,128]{2,1,0:T(8,128)(2,1)S(1)}, u32[]{:S(2)}, u32[]{:S(2)}) collective-permute-start(bf16[4,256,128]{2,1,0:T(8,128)(2,1)} %join.2.own_ref), channel_id=1, source_target_pairs={{0,8},{4,12},{8,0},{12,4},{16,24},{20,28},{24,16},{28,20},{1,9},{5... | collective-permute-start | bytes 786440 | tf_op jit(solution)/shard_map/ppermute | solution.py:638
  30.8 0.7 copy-start.2
  33.5 7.7 %collective-permute-start.2 = (bf16[4,256,128]{2,1,0:T(8,128)(2,1)}, bf16[4,256,128]{2,1,0:T(8,128)(2,1)S(1)}, u32[]{:S(2)}, u32[]{:S(2)}) collective-permute-start(bf16[4,256,128]{2,1,0:T(8,128)(2,1)} %join.3), channel_id=1, source_target_pairs={{0,16},{4,20},{8,24},{12,28},{16,0},{20,4},{24,8},{28,12},{1,17},{... | collective-permute-start | bytes 786440 | tf_op jit(solution)/shard_map/ppermute | solution.py:638
  41.2 0.7 copy-start.4
  49.5 8.4 %copy-start.10 = (bf16[4,128,128]{2,1,0:T(8,128)(2,1)S(1)}, bf16[4,128,128]{2,1,0:T(8,128)(2,1)}, u32[]{:S(2)}) copy-start(bf16[4,128,128]{2,1,0:T(8,128)(2,1)} %get-tuple-element.57) | copy-start | bytes 393220
  49.5 10.0 %copy-start.7 = (bf16[4,256,128]{2,1,0:T(8,128)(2,1)S(1)}, bf16[4,256,128]{2,1,0:T(8,128)(2,1)}, u32[]{:S(2)}) copy-start(bf16[4,256,128]{2,1,0:T(8,128)(2,1)} %get-tuple-element.56) | copy-start | bytes 786436
  49.5 6.7 %collective-permute-start.9 = (bf16[4,128,128]{2,1,0:T(8,128)(2,1)}, bf16[4,128,128]{2,1,0:T(8,128)(2,1)S(1)}, u32[]{:S(2)}, u32[]{:S(2)}) collective-permute-start(bf16[4,128,128]{2,1,0:T(8,128)(2,1)} %get-tuple-element.57), channel_id=1, source_target_pairs={{0,4},{4,0},{8,12},{12,8},{16,20},{20,16},{24,28},{28,24},{1,5},{5... | collective-permute-start | bytes 393224 | tf_op jit(solution)/shard_map/ppermute | solution.py:638
  49.6 8.4 %collective-permute-start.7 = (bf16[4,256,128]{2,1,0:T(8,128)(2,1)}, bf16[4,256,128]{2,1,0:T(8,128)(2,1)S(1)}, u32[]{:S(2)}, u32[]{:S(2)}) collective-permute-start(bf16[4,256,128]{2,1,0:T(8,128)(2,1)} %get-tuple-element.56), channel_id=1, source_target_pairs={{0,4},{4,0},{8,12},{12,8},{16,20},{20,16},{24,28},{28,24},{1,5},{5... | collective-permute-start | bytes 786440 | tf_op jit(solution)/shard_map/ppermute | solution.py:638
  50.1 14.5 %collective-permute-start.6 = (bf16[4,256,128]{2,1,0:T(8,128)(2,1)}, bf16[4,256,128]{2,1,0:T(8,128)(2,1)S(1)}, u32[]{:S(2)}, u32[]{:S(2)}) collective-permute-start(bf16[4,256,128]{2,1,0:T(8,128)(2,1)} %get-tuple-element.55), channel_id=1, source_target_pairs={{0,4},{4,0},{8,12},{12,8},{16,20},{20,16},{24,28},{28,24},{1,5},{5... | collective-permute-start | bytes 786440 | tf_op jit(solution)/shard_map/ppermute | solution.py:638
  53.3 37.2 %collective-permute-start.3 = (bf16[256,512]{1,0:T(8,128)(2,1)}, bf16[256,512]{1,0:T(8,128)(2,1)S(1)}, u32[]{:S(2)}, u32[]{:S(2)}) collective-permute-start(bf16[256,512]{1,0:T(8,128)(2,1)} %get-tuple-element.41), channel_id=1, source_target_pairs={{0,1},{1,2},{2,3},{3,0},{4,5},{5,6},{6,7},{7,4},{8,9},{9,10},{10,1... | collective-permute-start | bytes 786440 | tf_op jit(solution)/shard_map/ppermute | solution.py:645
  54.9 35.6 %collective-permute-start.4 = (bf16[256,512]{1,0:T(8,128)(2,1)}, bf16[256,512]{1,0:T(8,128)(2,1)S(1)}, u32[]{:S(2)}, u32[]{:S(2)}) collective-permute-start(bf16[256,512]{1,0:T(8,128)(2,1)} %get-tuple-element.42), channel_id=1, source_target_pairs={{0,2},{1,3},{2,0},{3,1},{4,6},{5,7},{6,4},{7,5},{8,10},{9,11},{10,... | collective-permute-start | bytes 786440 | tf_op jit(solution)/shard_map/ppermute | solution.py:645
  56.2 34.3 %collective-permute-start.5 = (bf16[256,512]{1,0:T(8,128)(2,1)}, bf16[256,512]{1,0:T(8,128)(2,1)S(1)}, u32[]{:S(2)}, u32[]{:S(2)}) collective-permute-start(bf16[256,512]{1,0:T(8,128)(2,1)} %get-tuple-element.43), channel_id=1, source_target_pairs={{0,3},{1,0},{2,1},{3,2},{4,7},{5,4},{6,5},{7,6},{8,11},{9,8},{10,9... | collective-permute-start | bytes 786440 | tf_op jit(solution)/shard_map/ppermute | solution.py:645
  58.0 5.1 %collective-permute-start.10 = (bf16[4,128,128]{2,1,0:T(8,128)(2,1)S(1)}, bf16[4,128,128]{2,1,0:T(8,128)(2,1)S(1)}, u32[]{:S(2)}, u32[]{:S(2)}) collective-permute-start(bf16[4,128,128]{2,1,0:T(8,128)(2,1)S(1)} %add_convert_fusion.4), channel_id=1, source_target_pairs={{0,8},{4,12},{8,0},{12,4},{16,24},{20,28},{24,16},{28,20},{1,9},{5... | collective-permute-start | bytes 393224 | tf_op jit(solution)/shard_map/ppermute | solution.py:638
  63.0 11.8 %collective-permute-start.8 = (bf16[4,256,128]{2,1,0:T(8,128)(2,1)S(1)}, bf16[4,256,128]{2,1,0:T(8,128)(2,1)S(1)}, u32[]{:S(2)}, u32[]{:S(2)}) collective-permute-start(bf16[4,256,128]{2,1,0:T(8,128)(2,1)S(1)} %add_convert_fusion.1), channel_id=1, source_target_pairs={{0,8},{4,12},{8,0},{12,4},{16,24},{20,28},{24,16},{28,20},{1,9},{5... | collective-permute-start | bytes 786440 | tf_op jit(solution)/shard_map/ppermute | solution.py:638
  64.6 10.3 %copy-start.6 = (bf16[4,256,128]{2,1,0:T(8,128)(2,1)}, bf16[4,256,128]{2,1,0:T(8,128)(2,1)S(1)}, u32[]{:S(2)}) copy-start(bf16[4,256,128]{2,1,0:T(8,128)(2,1)S(1)} %collective-permute-done.6.refs_16_) | copy-start | bytes 786436
  64.6 10.3 %collective-permute-start.11 = (bf16[4,128,128]{2,1,0:T(8,128)(2,1)S(1)}, bf16[4,128,128]{2,1,0:T(8,128)(2,1)S(1)}, u32[]{:S(2)}, u32[]{:S(2)}) collective-permute-start(bf16[4,128,128]{2,1,0:T(8,128)(2,1)S(1)} %add_convert_fusion.3), channel_id=1, source_target_pairs={{0,16},{4,20},{8,24},{12,28},{16,0},{20,4},{24,8},{28,12},{1,17},{... | collective-permute-start | bytes 393224 | tf_op jit(solution)/shard_map/ppermute | solution.py:638
  74.8 0.7 copy-start.9
  74.9 0.8 copy-start.8
  75.6 14.9 %copy-start.5 = (bf16[256,512]{1,0:T(8,128)(2,1)S(1)}, bf16[256,512]{1,0:T(8,128)(2,1)}, u32[]{:S(2)}) copy-start(bf16[256,512]{1,0:T(8,128)(2,1)} %get-tuple-element.40) | copy-start | bytes 786436
  86.7 18.3 %collective-permute-start.12 = (bf16[256,512]{1,0:T(8,128)(2,1)}, bf16[256,512]{1,0:T(8,128)(2,1)S(1)}, u32[]{:S(2)}, u32[]{:S(2)}) collective-permute-start(bf16[256,512]{1,0:T(8,128)(2,1)} %get-tuple-element.59), channel_id=1, source_target_pairs={{0,1},{1,2},{2,3},{3,0},{4,5},{5,6},{6,7},{7,4},{8,9},{9,10},{10,1... | collective-permute-start | bytes 786440 | tf_op jit(solution)/shard_map/ppermute | solution.py:645
  87.0 21.1 %collective-permute-start.13 = (bf16[256,512]{1,0:T(8,128)(2,1)}, bf16[256,512]{1,0:T(8,128)(2,1)S(1)}, u32[]{:S(2)}, u32[]{:S(2)}) collective-permute-start(bf16[256,512]{1,0:T(8,128)(2,1)} %get-tuple-element.60), channel_id=1, source_target_pairs={{0,2},{1,3},{2,0},{3,1},{4,6},{5,7},{6,4},{7,5},{8,10},{9,11},{10,... | collective-permute-start | bytes 786440 | tf_op jit(solution)/shard_map/ppermute | solution.py:645
  90.5 20.9 %collective-permute-start.14 = (bf16[256,512]{1,0:T(8,128)(2,1)}, bf16[256,512]{1,0:T(8,128)(2,1)S(1)}, u32[]{:S(2)}, u32[]{:S(2)}) collective-permute-start(bf16[256,512]{1,0:T(8,128)(2,1)} %get-tuple-element.61), channel_id=1, source_target_pairs={{0,3},{1,0},{2,1},{3,2},{4,7},{5,4},{6,5},{7,6},{8,11},{9,8},{10,9... | collective-permute-start | bytes 786440 | tf_op jit(solution)/shard_map/ppermute | solution.py:645

commit v2 on v1

v2 whole, which is shorter than its diff:
```python
import functools

import jax
import jax.numpy as jnp
from jax import lax
from jax.experimental import pallas as pl
from jax.experimental.pallas import tpu as pltpu
from jax.sharding import PartitionSpec as P

BLOCK = 64
LANES = 128
EPS = 1e-06
VMEM_BYTES = 28 * 1024 * 1024
F32 = jnp.float32
BF16 = jnp.bfloat16
WHOLE = pl.BlockSpec(memory_space=pltpu.VMEM)
SCALARS = pl.BlockSpec(memory_space=pltpu.SMEM)
PARAMS = pltpu.CompilerParams(vmem_limit_bytes=VMEM_BYTES)


def contract(left, right, dim_left, dim_right):
    return lax.dot_general(
        left.astype(BF16),
        right.astype(BF16),
        (((dim_left,), (dim_right,)), ((), ())),
        preferred_element_type=F32,
    )


def mm(left, right):
    return contract(left, right, 1, 0)


def mm_nt(left, right):
    return contract(left, right, 1, 1)


def mm_tn(left, right):
    return contract(left, right, 0, 0)


def split(values):
    high = values.astype(BF16)
    return high, (values - high.astype(F32)).astype(BF16)


def mm_nt_fine(left, right):
    left_high, left_low = split(left)
    right_high, right_low = split(right)
    return mm_nt(left_high, right_high) + (mm_nt(left_low, right_high) + mm_nt(left_high, right_low))


def mm_full(left, right):
    return jnp.dot(left, right, precision=lax.Precision.HIGHEST, preferred_element_type=F32)


def pair_ids(count):
    row_id = lax.broadcasted_iota(jnp.int32, (count, count), 0)
    col_id = lax.broadcasted_iota(jnp.int32, (count, count), 1)
    return row_id, col_id


def row_sum(values):
    return jnp.sum(values, 1, keepdims=True)


def col_sum(values):
    return jnp.sum(values, 0, keepdims=True)


def lane_of(rows):
    return lax.broadcasted_iota(jnp.int32, (rows, LANES), 1)


def decay_of(pack, pack_t, col, inclusive):
    spread = pack[:, col : col + 1] - pack_t[col : col + 1, :]
    return jnp.where(inclusive, jnp.exp(jnp.minimum(spread, 0.0)), 0.0)


def kept(shape, dtype):
    return pltpu.VMEM(shape, dtype)


def pin(values):
    return [pltpu.with_memory_space_constraint(value, pltpu.VMEM) for value in values]


def local_call(body, name, out_shape, scalars, arrays, scratch=(), remote=()):
    return pl.pallas_call(
        body,
        out_shape=tuple(out_shape),
        in_specs=[SCALARS] * len(scalars)
        + [WHOLE] * len(arrays)
        + [pl.BlockSpec(memory_space=pl.ANY)] * len(remote),
        out_specs=(WHOLE,) * len(out_shape),
        scratch_shapes=list(scratch),
        compiler_params=PARAMS,
        name=name,
    )(*scalars, *pin(arrays), *remote)


def column(pack, at):
    return pack[:, at : at + 1]


def level_mix(pack, head, heads, bits, apart):
    block_bit = BLOCK.bit_length() - 1
    mixed = jnp.broadcast_to(column(pack, head), apart.shape)
    for level in range(1, bits + 1):
        here = (apart >> (block_bit + level - 1)) >= 1
        mixed = jnp.where(here, column(pack, level * heads + head), mixed)
    return mixed


def head_rows(hp_ref, heads, decay_col, beta_col):
    lane_row = lane_of(1)
    rate = jnp.zeros((1, LANES), F32)
    bias = jnp.zeros((1, LANES), F32)
    for head in range(heads):
        rate = jnp.where(lane_row == decay_col + head, hp_ref[0, head], rate)
        bias = jnp.where(lane_row == beta_col + head, hp_ref[1, head], bias)
    return rate, bias


def project_body(sizes, hp_ref, tokens_hbm, w_hbm, small_hbm, *refs):
    heads, levels, chunks = sizes
    (wr_ref, small_ref, qkv_ref, gate_ref, pack_ref, pack_t_ref, trans_ref, mixed_t_ref,
     decay_ref, base_ref, lower_ref, pair_ref) = refs[:12]
    tokens, wide_in, wide_even, wide_odd, small_in, small_wide, acc, sems = refs[12:]
    rows, width = tokens.shape
    depth = width // chunks
    cols = 3 * heads
    fetch_tokens = pltpu.make_async_copy(tokens_hbm, tokens, sems.at[chunks])
    fetch_small = pltpu.make_async_copy(small_hbm, small_in, sems.at[chunks + 1])
    fetches = []
    for chunk in range(chunks):
        span = pl.ds(chunk * depth * cols, depth * cols)
        fetches.append(
            pltpu.make_async_copy(w_hbm.at[span, :], wide_in.at[span, :], sems.at[chunk])
        )
    fetches[0].start()
    fetch_tokens.start()
    fetch_small.start()
    for fetch in fetches[1:]:
        fetch.start()
    for chunk in range(chunks):
        fetches[chunk].wait()
        at = chunk * depth
        wide = wide_odd if chunk % 2 else wide_even
        wide[...] = wide_in[at * cols : (at + depth) * cols, :].astype(F32)
        for col in range(cols):
            part = wide[pl.ds(col, depth, stride=cols), :]
            wr_ref[at : at + depth, col * LANES : (col + 1) * LANES] = part.astype(BF16)
        if chunk == 0:
            fetch_tokens.wait()
        own = jnp.dot(
            tokens[:, at : at + depth], wr_ref[at : at + depth, :], preferred_element_type=F32
        )
        if chunk == 0:
            acc[...] = own
        else:
            acc[...] += own
    fetch_small.wait()
    small_rows = small_in.shape[0] * heads
    for level in range(small_in.shape[0]):
        small_wide[level * heads : (level + 1) * heads, :] = small_in[level].astype(F32)
    small_wide[small_rows:, :] = jnp.zeros((LANES - small_rows, width), F32)
    small_ref[...] = small_wide[...].astype(BF16)
    gate = mm_nt(tokens[...], small_ref[...])
    decay_col = levels * heads
    beta_col = decay_col + heads
    norm_col = beta_col + heads
    gate_ref[...] = gate
    lane = lane_of(rows)
    rate, bias = head_rows(hp_ref, heads, decay_col, beta_col)
    switch = jax.nn.sigmoid(gate + bias)
    lam = jnp.maximum(gate, 0.0) + jnp.log1p(jnp.exp(-jnp.abs(gate)))
    row_id, col_id = pair_ids(rows)
    inclusive = row_id >= col_id
    strict = row_id > col_id
    apart = row_id ^ col_id
    cum = mm_full(inclusive.astype(F32), -rate * switch)
    pack = jnp.where(lane < decay_col, lam, jnp.where(lane < beta_col, cum, switch))
    k_all, v_all = [], []
    for head in range(heads):
        for part in range(2):
            col = (part * heads + head) * LANES
            raw = acc[:, col : col + LANES]
            scale = lax.rsqrt(row_sum(raw * raw) + EPS)
            unit = raw * scale
            qkv_ref[part, head] = unit
            pack = jnp.where(lane == norm_col + part * heads + head, scale, pack)
            if part == 1:
                k_all.append(unit)
        col = (2 * heads + head) * LANES
        v_all.append(acc[:, col : col + LANES])
        qkv_ref[2, head] = v_all[head]
    pack_ref[...] = pack
    pack_t = pack.T
    pack_t_ref[...] = pack_t
    eye = (row_id == col_id).astype(F32)
    lower_all, trans_all = [], []
    for head in range(heads):
        decay = decay_of(pack, pack_t, decay_col + head, inclusive)
        decay_ref[head] = decay
        gram = mm_nt(k_all[head], k_all[head])
        base = jnp.where(strict, decay * gram, 0.0)
        base_ref[head] = base
        lower = column(pack, beta_col + head) * base
        lower_ref[head] = lower
        lower_all.append(lower)
        trans_all.append((eye - jnp.where(apart == 1, lower, 0.0)).astype(BF16))
    for bit in range(1, rows.bit_length() - 1):
        here = (apart >> bit) == 1
        edge = [jnp.where(here, lower, 0.0) for lower in lower_all]
        half = [mm(trans, part) for trans, part in zip(trans_all, edge)]
        trans_all = [
            trans - mm(part, trans).astype(BF16) for trans, part in zip(trans_all, half)
        ]
    rest_all = []
    for trans, lower in zip(trans_all, lower_all):
        high, low = split(lower)
        rest_all.append(eye - trans.astype(F32) - mm(high, trans) - mm(low, trans))
    trans_all = [
        (trans.astype(F32) + mm(trans, rest)).astype(BF16)
        for trans, rest in zip(trans_all, rest_all)
    ]
    mixed_all = []
    for head in range(heads):
        trans_ref[head] = trans_all[head]
        cum_row = pack_t[decay_col + head : decay_col + head + 1, :]
        tail_t = k_all[head].T * jnp.exp(cum_row[:, rows - 1 :] - cum_row)
        mixed_all.append(mm(tail_t, trans_all[head]))
    eye_key = eye[:LANES, :LANES]
    for head in range(heads):
        mixed_t_ref[head] = mixed_all[head]
        cum_col = column(pack, decay_col + head)
        beta = column(pack, beta_col + head)
        grown = (beta * jnp.exp(cum_col)) * k_all[head]
        both = jnp.concatenate([-grown, beta * v_all[head]], 1)
        pair = mm(mixed_all[head], both)
        last = jnp.exp(cum_col[rows - 1 : rows, :])
        pair_ref[head, :, :LANES] = (last * eye_key + pair[:, :LANES]).astype(BF16)
        pair_ref[head, :, LANES:] = pair[:, LANES:].astype(BF16)


def project(tokens, flat_w, small, head_param, heads, levels):
    rows, width = tokens.shape
    chunks = 8
    cols = 3 * heads
    key = flat_w.shape[1]
    square = (heads, rows, rows)
    out_shape = (
        kept((width, cols * key), BF16),
        kept((LANES, width), BF16),
        kept((3, heads, rows, key), F32),
        kept((rows, LANES), F32),
        kept((rows, LANES), F32),
        kept((LANES, rows), F32),
        kept(square, BF16),
        kept((heads, key, rows), F32),
        kept(square, F32),
        kept(square, F32),
        kept(square, F32),
        kept((heads, key, 2 * key), BF16),
    )
    scratch = [
        pltpu.VMEM(tokens.shape, BF16),
        pltpu.VMEM(flat_w.shape, BF16),
        pltpu.VMEM((width // chunks * cols, key), F32),
        pltpu.VMEM((width // chunks * cols, key), F32),
        pltpu.VMEM(small.shape, BF16),
        pltpu.VMEM((LANES, width), F32),
        pltpu.VMEM((rows, cols * key), F32),
        pltpu.SemaphoreType.DMA((chunks + 2,)),
    ]
    return local_call(
        functools.partial(project_body, (heads, levels, chunks)), "project", out_shape,
        [head_param], [], scratch, [tokens, flat_w, small],
    )


def local_body(sizes, qkv_ref, pack_ref, pack_t_ref, trans_ref, mixed_t_ref, decay_ref, *outs):
    heads, levels, bits = sizes
    (attn_ref, attn_t_ref, prod_t_ref, scores_ref, mix_ref, mixed_ref, local_ref, hat_ref,
     hat_t_ref) = outs
    rows = pack_ref.shape[0]
    decay_col = levels * heads
    beta_col = decay_col + heads
    pack = pack_ref[...]
    pack_t = pack_t_ref[...]
    row_id, col_id = pair_ids(rows)
    apart = row_id ^ col_id
    for head in range(heads):
        scores = mm_nt_fine(qkv_ref[0, head], qkv_ref[1, head]) * decay_ref[head]
        scores_ref[head] = scores.astype(BF16)
        mix_ref[head] = level_mix(pack, head, heads, bits, apart)
        mixed_ref[head] = mixed_t_ref[head].T.astype(BF16)
    for head in range(heads):
        attn = mm(scores_ref[head], trans_ref[head])
        attn_ref[head] = attn.astype(BF16)
        attn_t_ref[head] = attn.T.astype(BF16)
        attn = attn * pack_t[beta_col + head : beta_col + head + 1, :]
        prod = attn * mix_ref[head]
        prod_t_ref[head] = prod.T.astype(BF16)
        growth = jnp.exp(column(pack, decay_col + head))
        local_ref[head] = mm(prod, qkv_ref[2, head])
        hat = growth * qkv_ref[0, head] - mm(attn, growth * qkv_ref[1, head])
        hat_ref[head] = hat.astype(BF16)
        hat_t_ref[head] = hat.T.astype(BF16)


def local_part(qkv, pack, pack_t, trans, mixed_t, decay, levels, bits):
    heads, rows, key = qkv.shape[1:]
    square = (heads, rows, rows)
    out_shape = (
        kept(square, BF16),
        kept(square, BF16),
        kept(square, BF16),
        kept(square, BF16),
        kept(square, F32),
        kept((heads, rows, key), BF16),
        kept((heads, rows, key), F32),
        kept((heads, rows, key), BF16),
        kept((heads, key, rows), BF16),
    )
    return local_call(
        functools.partial(local_body, (heads, levels, bits)), "local_part", out_shape,
        [], [qkv, pack, pack_t, trans, mixed_t, decay],
    )


def join_pair(upper, own, other):
    key = own.shape[0]
    low = jnp.where(upper, other, own)
    high = jnp.where(upper, own, other)
    moved = mm(high[:, :key], low)
    late = jnp.concatenate([jnp.zeros((key, key), F32), high[:, key:].astype(F32)], 1)
    return (moved + late).astype(BF16)


def join_body(bit, place_ref, own_ref, other_ref, out_ref):
    upper = ((place_ref[0] >> bit) & 1) == 1
    for head in range(own_ref.shape[0]):
        out_ref[head] = join_pair(upper, own_ref[head], other_ref[head])


def join(bit, place, own, other):
    return local_call(
        functools.partial(join_body, bit), "join", [kept(own.shape, BF16)], [place], [own, other]
    )[0]


def gather_node(head, bit, first, near, uppers):
    if bit == 0:
        return near[first][head]
    own = gather_node(head, bit - 1, first, near, uppers)
    other = gather_node(head, bit - 1, first ^ (1 << (bit - 1)), near, uppers)
    return join_pair(uppers[bit], own, other)


def cross_body(sizes, place_ref, gain_ref, pack_ref, local_ref, hat_ref, hat_t_ref, grad_ref, *refs):
    heads, bits, far, near_count = sizes
    first_ref = refs[0]
    near = (None,) + refs[1 : near_count + 1]
    refs = refs[near_count + 1 :]
    normed_ref, dout_ref, dhat_ref, dfar_ref = refs[:4]
    nodes = refs[4 : 4 + far - 2]
    sends = refs[4 + max(far - 2, 0) :]
    rows = pack_ref.shape[0]
    key = hat_ref.shape[2]
    place = place_ref[0]
    pack = pack_ref[...]
    gain = gain_ref[...]
    lane = lane_of(rows)
    all_heads = range(heads)
    uppers = [((place >> bit) & 1) == 1 for bit in range(far)]
    others = []
    for bit in range(far):
        if bit == 0:
            others.append([first_ref[head] for head in all_heads])
        elif bit == 1:
            others.append([near[1][head] for head in all_heads])
        else:
            others.append(
                [gather_node(head, bit - 1, 1 << (bit - 1), near, uppers) for head in all_heads]
            )
            for head in all_heads:
                nodes[bit - 2][head] = others[bit][head]
    eye_key = jnp.where(pair_ids(key)[0] == pair_ids(key)[1], 1.0, 0.0).astype(BF16)
    prefix = [eye_key for head in all_heads]
    prefixes, found = [], []
    for bit in range(far):
        prefixes.append(prefix)
        moved = [mm(prefix[head], others[bit][head]) for head in all_heads]
        found.append([jnp.where(uppers[bit], m[:, key:], 0.0).astype(BF16) for m in moved])
        prefix = [
            jnp.where(uppers[bit], moved[head][:, :key].astype(BF16), prefix[head])
            for head in all_heads
        ]
    found = [jnp.concatenate([found[bit][head] for bit in range(far)], 1) for head in all_heads]
    reached = [mm(hat_ref[head], found[head]) for head in all_heads]
    dfar = jnp.zeros((rows, LANES), F32)
    spread = []
    for head in all_heads:
        summed = local_ref[head]
        weights, parts = [], []
        for bit in range(far):
            weights.append(column(pack, (bits + 1 + bit) * heads + head))
            parts.append(reached[head][:, bit * key : (bit + 1) * key])
            summed = summed + weights[bit] * parts[bit]
        scale = lax.rsqrt(jnp.mean(summed * summed, -1, keepdims=True) + EPS)
        unit = summed * scale
        normed_ref[:, head * key : (head + 1) * key] = (unit * gain).astype(BF16)
        pulled = grad_ref[:, head * key : (head + 1) * key] * gain
        dout = scale * (pulled - unit * jnp.mean(pulled * unit, -1, keepdims=True))
        dout_ref[head] = dout
        for bit in range(far):
            col = (bits + 1 + bit) * heads + head
            dfar = jnp.where(lane == col, row_sum(dout * parts[bit]), dfar)
        spread.append(
            jnp.concatenate([(weights[bit] * dout).astype(BF16) for bit in range(far)], 1)
        )
    dfar_ref[...] = dfar
    dfound = [mm(hat_t_ref[head], spread[head]) for head in all_heads]
    for head in all_heads:
        dhat_ref[head] = mm_nt(spread[head], found[head])
    dprefix = [jnp.zeros((key, key), F32) for head in all_heads]
    for bit in reversed(range(far)):
        dfree = [
            jnp.where(uppers[bit], d[:, bit * key : (bit + 1) * key], 0.0) for d in dfound
        ]
        both = [
            jnp.concatenate([jnp.where(uppers[bit], dprefix[head], 0.0), dfree[head]], 1)
            for head in all_heads
        ]
        for head in all_heads:
            if bit == far - 1:
                sends[bit][head] = mm_tn(prefixes[bit][head], dfree[head]).astype(BF16)
            else:
                sends[bit][head] = mm_tn(prefixes[bit][head], both[head]).astype(BF16)
        if bit > 0:
            moved = [mm_nt(both[head], others[bit][head]) for head in all_heads]
            dprefix = [
                jnp.where(uppers[bit], moved[head], dprefix[head]) for head in all_heads
            ]


def cross(place, gain, pack, local_out, hat, hat_t, grad_normed, first, near, bits, far):
    heads, rows, key = hat.shape
    nodes = tuple(kept(first.shape, BF16) for bit in range(2, far))
    sends = tuple(
        kept((heads, key, (1 if bit == far - 1 else 2) * key), BF16) for bit in range(far)
    )
    out_shape = (
        kept((rows, heads * key), BF16),
        kept((heads, rows, key), F32),
        kept((heads, rows, key), F32),
        kept((rows, LANES), F32),
    ) + nodes + sends
    got = local_call(
        functools.partial(cross_body, (heads, bits, far, len(near))), "cross", out_shape,
        [place], [gain, pack, local_out, hat, hat_t, grad_normed, first, *near],
    )
    return got[:4], got[4 : 4 + len(nodes)], got[4 + len(nodes) :]


def spread_body(count, place_ref, left_ref, right_ref, *out_refs):
    size = out_refs[0].shape[1]
    for shift in range(count):
        dest = lax.rem(place_ref[1] + shift, count)
        cols = pl.ds(pl.multiple_of(dest * size, size), size)
        out_refs[shift][...] = jnp.dot(
            left_ref[...], right_ref[:, cols], preferred_element_type=F32
        ).astype(BF16)


def spread_out(place, left, right, count):
    out = kept((left.shape[0], right.shape[1] // count), BF16)
    return local_call(
        functools.partial(spread_body, count), "spread_out", [out] * count, [place], [left, right]
    )


def add_body(*refs):
    count = len(refs) // 3
    for at in range(count):
        left, right = refs[at][...].astype(F32), refs[count + at][...].astype(F32)
        refs[2 * count + at][...] = (left + right).astype(BF16)


def add_all(left, right):
    out_shape = [kept(value.shape, BF16) for value in left]
    return local_call(add_body, "add_all", out_shape, [], [*left, *right])


def lower_pull(dlower, base, lower, beta, decay, strict, k_in):
    dlower = jnp.where(strict, dlower, 0.0)
    dbeta = row_sum(dlower * base)
    dgram = dlower * (beta * decay)
    dkey = mm(dgram, k_in) + mm_tn(dgram, k_in)
    return dbeta, beta * dbeta, col_sum(dlower * lower), dkey


def pull_body(sizes, *refs):
    heads, levels, bits = sizes
    (qkv_ref, pack_ref, pack_t_ref, trans_ref, attn_ref, attn_t_ref, prod_t_ref, scores_ref,
     mix_ref, decay_ref, base_ref, lower_ref, dout_ref, dhat_ref) = refs[:14]
    dqkv_ref, dgrown_ref, dcol_ref, drow_ref = refs[14:]
    rows = pack_ref.shape[0]
    decay_col = levels * heads
    beta_col = decay_col + heads
    block_bit = BLOCK.bit_length() - 1
    pack = pack_ref[...]
    pack_t = pack_t_ref[...]
    row_id, col_id = pair_ids(rows)
    strict = row_id > col_id
    apart = row_id ^ col_id
    lane = lane_of(rows)
    all_heads = range(heads)
    dcol = jnp.zeros((rows, LANES), F32)
    dbeta_rows, dcum_rows, dattn_all = [], [], []
    for head in all_heads:
        high, low = split(dout_ref[head])
        v_in = qkv_ref[2, head].astype(BF16)
        dprod = mm_nt(high, v_in) + mm_nt(low, v_in)
        dqkv_ref[2, head] = mm(prod_t_ref[head], high)
        beta_row = pack_t[beta_col + head : beta_col + head + 1, :]
        growth = jnp.exp(column(pack, decay_col + head))
        attn0 = attn_ref[head].astype(F32)
        touched = dprod * (attn0 * beta_row)
        for level in range(bits + 1):
            if level == 0:
                here = (apart >> block_bit) == 0
            else:
                here = (apart >> (block_bit + level - 1)) == 1
            dcol = jnp.where(
                lane == level * heads + head, row_sum(jnp.where(here, touched, 0.0)), dcol
            )
        dattn = dprod * mix_ref[head] - mm_nt(dhat_ref[head], growth * qkv_ref[1, head])
        dbeta_rows.append(col_sum(dattn * attn0))
        dattn_all.append((dattn * beta_row).astype(BF16))
    dscore_all = [mm_nt(dattn_all[head], trans_ref[head]) for head in all_heads]
    moved_all = []
    for head in all_heads:
        both = jnp.concatenate(
            [dscore_all[head].astype(BF16), dhat_ref[head].astype(BF16)], 1
        )
        moved_all.append(mm(attn_t_ref[head], both))
    for head in all_heads:
        q_in, k_in = qkv_ref[0, head], qkv_ref[1, head]
        beta = column(pack, beta_col + head)
        growth = jnp.exp(column(pack, decay_col + head))
        dscore = dscore_all[head]
        dprobs = dscore * decay_ref[head]
        shift = dscore * scores_ref[head].astype(F32)
        dgrown_ref[head] = -beta * moved_all[head][:, rows:]
        dbeta, dcum_col, dcum_row, dk_lower = lower_pull(
            -moved_all[head][:, :rows], base_ref[head], lower_ref[head], beta, decay_ref[head],
            strict, k_in
        )
        dhat = dhat_ref[head]
        dqkv_ref[0, head] = growth * dhat + mm(dprobs, k_in)
        dqkv_ref[1, head] = mm_tn(dprobs, q_in) + dk_lower
        dcum_col = dcum_col + row_sum(shift) + growth * row_sum(q_in * dhat)
        dcum_rows.append(-dcum_row - col_sum(shift))
        dcol = jnp.where(lane == beta_col + head, dbeta, dcol)
        dcol = jnp.where(lane == decay_col + head, dcum_col, dcol)
    dcol_ref[...] = dcol
    drow_ref[...] = jnp.concatenate(dcum_rows + dbeta_rows, 0)


def pull_local(arrays, levels, bits):
    heads, rows, key = arrays[0].shape[1:]
    out_shape = (
        kept((3, heads, rows, key), F32),
        kept((heads, rows, key), F32),
        kept((rows, LANES), F32),
        kept((2 * heads, rows), F32),
    )
    return local_call(
        functools.partial(pull_body, (heads, levels, bits)), "pull_local", out_shape, [], arrays
    )


def finish_body(sizes, place_ref, hp_ref, *refs):
    heads, levels, far, count, arrived_counts = sizes
    (qkv_ref, gate_ref, pack_ref, trans_ref, mixed_ref, decay_ref, base_ref, lower_ref,
     dqkv_ref, dgrown_ref, dcol_ref, drow_ref, dfar_ref, small_ref, wr_ref) = refs[:15]
    others = refs[15 : 15 + far]
    refs = refs[15 + far :]
    arrived = []
    for found in arrived_counts:
        arrived.append(refs[:found])
        refs = refs[found:]
    out_refs = refs[:count]
    (dproj,) = refs[count:]
    rows = pack_ref.shape[0]
    key = qkv_ref.shape[3]
    decay_col = levels * heads
    beta_col = decay_col + heads
    norm_col = beta_col + heads
    place = place_ref[0]
    all_heads = range(heads)
    uppers = [((place >> bit) & 1) == 1 for bit in range(far)]
    pack = pack_ref[...]
    row_id, col_id = pair_ids(rows)
    strict = row_id > col_id
    lane = lane_of(rows)
    last_row = lax.broadcasted_iota(jnp.int32, (rows, 1), 0) == rows - 1
    eye_key = (pair_ids(key)[0] == pair_ids(key)[1]).astype(F32)
    dpair = [jnp.zeros((key, 2 * key), F32) for head in all_heads]
    for bit in reversed(range(far)):
        for head in all_heads:
            got = arrived[bit][0][head].astype(F32)
            for more in arrived[bit][1:]:
                got = got + more[head].astype(F32)
            other = others[bit][head]
            if bit == far - 1:
                got = jnp.concatenate([jnp.zeros((key, key), F32), got], 1)
                dpair[head] = jnp.where(uppers[bit], 0.0, got)
            else:
                as_low = mm_tn(other[:, :key], dpair[head]) + got
                as_high = mm_nt(dpair[head], other)
                as_high = jnp.concatenate([as_high, dpair[head][:, key:]], 1)
                dpair[head] = jnp.where(uppers[bit], as_high, as_low)
    moved_all, dmixed_all = [], []
    for head in all_heads:
        beta = column(pack, beta_col + head)
        growth = jnp.exp(column(pack, decay_col + head))
        both = jnp.concatenate([-growth * qkv_ref[1, head], qkv_ref[2, head]], 1)
        dmixed_all.append(mm_nt(both, dpair[head]))
        moved_all.append(mm(beta * mixed_ref[head].astype(F32), dpair[head]))
    dtail_all = [
        mm(trans_ref[head], column(pack, beta_col + head) * dmixed_all[head])
        for head in all_heads
    ]
    dlower_all = [-mm_nt(mixed_ref[head], dtail_all[head]) for head in all_heads]
    dcol = jnp.where(lane < decay_col, dcol_ref[...] + dfar_ref[...], dcol_ref[...])
    dcum_rows = []
    for head in all_heads:
        q_in, k_in = qkv_ref[0, head], qkv_ref[1, head]
        beta = column(pack, beta_col + head)
        cum_col = column(pack, decay_col + head)
        growth = jnp.exp(cum_col)
        last = cum_col[rows - 1 : rows, :]
        tail = jnp.exp(last - cum_col)
        dgrown = dgrown_ref[head] - moved_all[head][:, :key]
        dv = dqkv_ref[2, head] + moved_all[head][:, key:]
        dbeta_more = row_sum(mixed_ref[head].astype(F32) * dmixed_all[head])
        dtail = dtail_all[head]
        dbeta, dcum_col, dcum_row, dk_lower = lower_pull(
            dlower_all[head], base_ref[head], lower_ref[head], beta, decay_ref[head], strict, k_in
        )
        dcum_rows.append(-dcum_row)
        tail_pull = tail * row_sum(k_in * dtail)
        trace = col_sum(row_sum(dpair[head][:, :key] * eye_key))
        at_last = col_sum(tail_pull) + jnp.exp(last) * trace
        dcum_col = dcum_col + growth * row_sum(k_in * dgrown) - tail_pull
        dcum_col = dcum_col + jnp.where(last_row, at_last, 0.0)
        dk = dqkv_ref[1, head] + dk_lower + growth * dgrown + tail * dtail
        dq = dqkv_ref[0, head]
        dcol = dcol + jnp.where(lane == beta_col + head, dbeta + dbeta_more, 0.0)
        dcol = dcol + jnp.where(lane == decay_col + head, dcum_col, 0.0)
        for part, unit, dunit in ((0, q_in, dq), (1, k_in, dk)):
            scale = column(pack, norm_col + part * heads + head)
            back = scale * (dunit - unit * row_sum(unit * dunit))
            col = (part * heads + head) * key
            dproj[:, col : col + key] = back.astype(BF16)
        col = (2 * heads + head) * key
        dproj[:, col : col + key] = dv.astype(BF16)
    drow = drow_ref[...]
    drow = drow + jnp.concatenate(dcum_rows + [jnp.zeros((heads, rows), F32)], 0)
    drow = jnp.concatenate(
        [jnp.zeros((decay_col, rows), F32), drow,
         jnp.zeros((LANES - norm_col, rows), F32)], 0
    )
    dcol = dcol + drow.T
    rate, bias = head_rows(hp_ref, heads, decay_col, beta_col)
    switch = jax.nn.sigmoid(gate_ref[...] + bias)
    dlog = mm_full((row_id <= col_id).astype(F32), dcol)
    slope = switch * (1.0 - switch)
    dgate = jnp.where(
        lane < decay_col,
        dcol * switch,
        jnp.where(lane < beta_col, -rate * dlog * slope, dcol * slope),
    )
    dgate = jnp.where(lane < norm_col, dgate, 0.0).astype(BF16)
    size = out_refs[0].shape[1]
    for shift in range(count):
        dest = lax.rem(place_ref[1] + shift, count)
        span = pl.ds(pl.multiple_of(dest * size, size), size)
        part = mm_nt(dproj[...], wr_ref[span, :]) + mm(dgate, small_ref[:, span])
        out_refs[shift][...] = part.astype(BF16)


def finish(place, head_param, arrays, others, arrived, levels, count):
    rows = arrays[0].shape[2]
    width, cols = arrays[-1].shape
    far = len(others)
    counts = tuple(len(group) for group in arrived)
    heads = arrays[0].shape[1]
    flat = [value for group in arrived for value in group]
    return local_call(
        functools.partial(finish_body, (heads, levels, far, count, counts)), "finish",
        [kept((rows, width // count), BF16)] * count,
        [place, head_param], [*arrays, *others, *flat], [pltpu.VMEM((rows, cols), BF16)],
    )


def swap(value, axis, mask):
    size = lax.axis_size(axis)
    return lax.ppermute(value, axis, [(at, at ^ mask) for at in range(size)])


def scatter_sum(parts, axis):
    count = lax.axis_size(axis)
    total = parts[0].astype(F32)
    for shift in range(1, count):
        got = lax.ppermute(parts[shift], axis, [(at, (at + shift) % count) for at in range(count)])
        total = total + got.astype(F32)
    return total.astype(BF16)


def on_device(tokens, qkv_weight, small_weight, head_param, norm_gain, out_weight, grad_out):
    rows, width = tokens.shape
    heads, key = qkv_weight.shape[2:]
    levels = small_weight.shape[2] - 2
    bits = (rows // BLOCK).bit_length() - 1
    size = lax.axis_size("ctx")
    far = size.bit_length() - 1
    count = lax.axis_size("head")
    place = jnp.stack([lax.axis_index("ctx"), lax.axis_index("head")]).astype(jnp.int32)
    flat_w = qkv_weight.reshape(width * 3 * heads, key)
    small = jnp.transpose(small_weight, (2, 1, 0))
    rates = head_param.T
    flat_out = out_weight.reshape(heads * key, width)
    gain = norm_gain.reshape(1, key)

    (wr, small_t, qkv, gate, pack, pack_t, trans, mixed_t, decay, base, lower, pair) = project(
        tokens, flat_w, small, rates, heads, levels
    )
    first = swap(pair, "ctx", 1)
    node = join(0, place, pair, first)
    near = [swap(node, "ctx", 2 * at) for at in range(1, size // 2)]
    (attn, attn_t, prod_t, scores, mix, mixed, local_out, hat, hat_t) = local_part(
        qkv, pack, pack_t, trans, mixed_t, decay, levels, bits
    )
    grad_normed = lax.dot_general(
        grad_out, flat_out, (((1,), (1,)), ((), ())), preferred_element_type=F32
    )
    (normed, dout, dhat, dfar), nodes, sends = cross(
        place, gain, pack, local_out, hat, hat_t, grad_normed, first, near, bits, far
    )
    others = [first, near[0], *nodes]
    got = [swap(value, "ctx", 1) for value in sends]
    arrived = [[got[0]]]
    sums = add_all(sends[1:], got[1:])
    for bit in range(1, far):
        half = 1 << (bit - 1)
        arrived.append([swap(sums[bit - 1], "ctx", 2 * at) for at in range(half, 2 * half)])
    layer_out = scatter_sum(spread_out(place, normed, flat_out, count), "head")
    dqkv, dgrown, dcol, drow = pull_local(
        [qkv, pack, pack_t, trans, attn, attn_t, prod_t, scores, mix, decay, base, lower, dout,
         dhat],
        levels, bits,
    )
    arrays = [qkv, gate, pack, trans, mixed, decay, base, lower, dqkv, dgrown, dcol, drow, dfar,
              small_t, wr]
    parts = finish(place, rates, arrays, others, arrived, levels, count)
    return layer_out, scatter_sum(parts, "head")


def solution(mesh):
    placed = (
        P("ctx", None),
        P(None, None, "head", None),
        P(None, "head", None),
        P("head", None),
        P(),
        P("head", None, None),
        P("ctx", None),
    )
    return jax.shard_map(
        on_device,
        mesh=mesh,
        in_specs=placed,
        out_specs=(P("ctx", "head"), P("ctx", "head")),
        check_vma=False,
    )
```

time: 114 us -> 106 us (0.930)
  the two profiles are of different devices: /device:TPU:8 before, /device:TPU:9 now
where the time goes in v2:
time: 106 us
  waiting for transfers between devices  41.7 us (39%)
  Pallas kernels  29 us (27%)
  local copies, waits for them, and re-layouts  17.5 us (17%)
  starting transfers between devices  14.5 us (14%)
  other arithmetic  1.75 us (2%)
    pallas_call x8, Pallas kernels, local_call(): pl.pallas_call(body, out_shape=tuple(out_shape), in_specs=[SCALARS] * len...  29 us
    ppermute x6, waiting for transfers between devices, scatter_sum(): lax.ppermute(parts[shift], axis, [(at, (at + shift) % count) for at in ra...  28.9 us
    unnamed x54, local copies, waits for them, and re-layouts  17.5 us
    ppermute x10, waiting for transfers between devices, swap(): return lax.ppermute(value, axis, [(at, at ^ mask) for at in range(size)])  12.8 us
    ppermute x6, starting transfers between devices, scatter_sum(): lax.ppermute(parts[shift], axis, [(at, (at + shift) % count) for at in ra...  7.29 us
    ppermute x10, starting transfers between devices, swap(): return lax.ppermute(value, axis, [(at, at ^ mask) for at in range(size)])  7.22 us
  transfers between devices with their start and end apart: 16, of which 9 were waited for; matrix products, arithmetic and copies ran while one was open for 2% of the time, Pallas kernels for 13%

profile of v2, /device:TPU:9, one launch (start us, length us, event | category | flops | bytes accessed | tf_op | source)
XLA Modules:
  0.0 106.0 jit_solution(4278246086069517023)
XLA Ops:
  0.7 2.9 %copy-done.5 = bf16[2048,3,4,128]{3,2,1,0:T(4,128)(2,1)S(1)} copy-done((bf16[2048,3,4,128]{3,2,1,0:T(4,128)(2,1)S(1)}, bf16[2048,3,4,128]{3,2,1,0:T(4,128)(2,1)}, u32[]{:S(2)}) %copy-start.5) | copy-done | bytes 6291480
  3.5 1.2 %copy-done.11 = bf16[256,2048]{1,0:T(8,128)(2,1)S(1)} copy-done((bf16[256,2048]{1,0:T(8,128)(2,1)S(1)}, bf16[256,2048]{1,0:T(8,128)(2,1)}, u32[]{:S(2)}) %copy-start.11) | copy-done | bytes 1048600
  4.7 0.9 copy-done.19
  6.4 10.6 %project.1 = (bf16[2048,1536]{1,0:T(8,128)(2,1)S(1)}, bf16[128,2048]{1,0:T(8,128)(2,1)S(1)}, f32[3,4,256,128]{3,2,1,0:T(8,128)S(1)}, f32[256,128]{1,0:T(8,128)S(...) custom-call(f32[2,4]{1,0:T(2,128)S(1)} %bitcast.15, ...), custom_call_target="tpu_custom_call" | custom-call | tf_op jit(solution)/shard_map/project/pallas_call | solution.py:89
  17.0 1.0 copy-done.1
  18.0 2.7 %copy-done.4 = bf16[2048,1536]{1,0:T(8,128)(2,1)} copy-done((bf16[2048,1536]{1,0:T(8,128)(2,1)}, bf16[2048,1536]{1,0:T(8,128)(2,1)S(1)}, u32[]{:S(2)}) %copy-start.4) | copy-done | bytes 6291480
  20.7 1.0 copy-done.6
  21.7 1.0 copy-done.8
  26.2 1.2 %copy-done.2 = f32[4,256,256]{2,1,0:T(8,128)S(1)} copy-done((f32[4,256,256]{2,1,0:T(8,128)S(1)}, f32[4,256,256]{2,1,0:T(8,128)}, u32[]{:S(2)}) %copy-start.2) | copy-done | bytes 1048600
  28.4 1.0 copy-done.18
  29.4 1.6 %local_part.1 = (bf16[4,256,256]{2,1,0:T(8,128)(2,1)S(1)}, bf16[4,256,256]{2,1,0:T(8,128)(2,1)S(1)}, bf16[4,256,256]{2,1,0:T(8,128)(2,1)S(1)}, bf16[4,256,256]{2...) custom-call(f32[3,4,256,128]{3,2,1,0:T(8,128)S(1)} %get-tuple-elemen, ...), custom_call_target="tpu_custom_call" | custom-call | tf_op jit(solution)/shard_map/local_part/pallas_call | solution.py:89
  31.1 1.2 %join.1 = bf16[4,128,256]{2,1,0:T(8,128)(2,1)S(1)} custom-call(s32[2]{0:T(128)S(1)} %pad_add_fusion.place_ref, bf16[4,128,256]{2,1,0:T(8,128)(2,1)} %get-tuple-element.54.own_ref, bf16[4,128,256]{2,1,0:T(8,128)(2,1)S(1)} %collective-permute-done.other_ref.refs_0_.refs_15_), custom_call_target="tpu_custom_call" | custom-call | tf_op jit(solution)/shard_map/join/pallas_call | solution.py:89
  32.3 2.2 %collective-permute-start.3 = (bf16[4,128,256]{2,1,0:T(8,128)(2,1)S(1)}, bf16[4,128,256]{2,1,0:T(8,128)(2,1)S(1)}, u32[]{:S(2)}, u32[]{:S(2)}) collective-permute-start(bf16[4,128,256]{2,1,0:T(8,128)(2,1)S(1)} %join.1), channel_id=1, source_target_pairs={{0,24},{4,28},{8,16},{12,20},{16,8},{20,12},{24,0},{28,4},{1,25},{... | collective-permute-start | bytes 786440 | tf_op jit(solution)/shard_map/ppermute | solution.py:713
  35.8 5.5 %collective-permute-done.3.refs_3_ = bf16[4,128,256]{2,1,0:T(8,128)(2,1)S(1)} collective-permute-done((bf16[4,128,256]{2,1,0:T(8,128)(2,1)S(1)}, bf16[4,128,256]{2,1,0:T(8,128)(2,1)S(1)}, u32[]{:S(2)}, u32[]{:S(2)}) %collective-permute-start.3) | collective-permute-done | bytes 262176 | tf_op jit(solution)/shard_map/ppermute | solution.py:713
  41.2 5.9 %collective-permute-done.2.refs_2_ = bf16[4,128,256]{2,1,0:T(8,128)(2,1)S(1)} collective-permute-done((bf16[4,128,256]{2,1,0:T(8,128)(2,1)S(1)}, bf16[4,128,256]{2,1,0:T(8,128)(2,1)S(1)}, u32[]{:S(2)}, u32[]{:S(2)}) %collective-permute-start.2) | collective-permute-done | bytes 262176 | tf_op jit(solution)/shard_map/ppermute | solution.py:713
  47.2 3.4 %cross.1 = (bf16[256,512]{1,0:T(8,128)(2,1)S(1)}, f32[4,256,128]{2,1,0:T(8,128)S(1)}, f32[4,256,128]{2,1,0:T(8,128)S(1)}, f32[256,128]{1,0:T(8,128)S(1)}, bf16[4...) custom-call(s32[2]{0:T(128)S(1)} %pad_add_fusion.place_ref, ...), custom_call_target="tpu_custom_call" | custom-call | tf_op jit(solution)/shard_map/cross/pallas_call | solution.py:89
  51.7 1.2 %collective-permute-done.9.refs_3_ = bf16[4,128,128]{2,1,0:T(8,128)(2,1)S(1)} collective-permute-done((bf16[4,128,128]{2,1,0:T(8,128)(2,1)S(1)}, bf16[4,128,128]{2,1,0:T(8,128)(2,1)S(1)}, u32[]{:S(2)}, u32[]{:S(2)}) %collective-permute-start.9) | collective-permute-done | bytes 131104 | tf_op jit(solution)/shard_map/ppermute | solution.py:713
  53.0 1.5 %collective-permute-start.12 = (bf16[4,128,128]{2,1,0:T(8,128)(2,1)S(1)}, bf16[4,128,128]{2,1,0:T(8,128)(2,1)S(1)}, u32[]{:S(2)}, u32[]{:S(2)}) collective-permute-start(bf16[4,128,128]{2,1,0:T(8,128)(2,1)S(1)} %get-tuple-element.83), channel_id=1, source_target_pairs={{0,24},{4,28},{8,16},{12,20},{16,8},{20,12},{24,0},{28,4},{1,25},{... | collective-permute-start | bytes 393224 | tf_op jit(solution)/shard_map/ppermute | solution.py:713
  54.5 0.9 collective-permute-start.10
  55.4 1.3 %spread_out.1 = (bf16[256,512]{1,0:T(8,128)(2,1)S(1)}, bf16[256,512]{1,0:T(8,128)(2,1)S(1)}, bf16[256,512]{1,0:T(8,128)(2,1)S(1)}, bf16[256,512]{1,0:T(8,128)(2,1)S(1)}) custom-call(s32[2]{0:T(128)S(1)} %pad_add_fusion.place_ref, bf16[256,512]{1,0:T(8,128)(2,1)S(1)} %get-tuple-element.55.left_ref, bf16[512,2048]{1,0:T(8,128)(2,1)S(1)} %bitcast.13), custom_call_target="tpu_custom_call" | custom-call | tf_op jit(solution)/shard_map/spread_out/pallas_call | solution.py:89
  56.7 1.4 %collective-permute-start.4 = (bf16[256,512]{1,0:T(8,128)(2,1)S(1)}, bf16[256,512]{1,0:T(8,128)(2,1)S(1)}, u32[]{:S(2)}, u32[]{:S(2)}) collective-permute-start(bf16[256,512]{1,0:T(8,128)(2,1)S(1)} %get-tuple-element.57), channel_id=1, source_target_pairs={{0,1},{1,2},{2,3},{3,0},{4,5},{5,6},{6,7},{7,4},{8,9},{9,10},{10,1... | collective-permute-start | bytes 786440 | tf_op jit(solution)/shard_map/ppermute | solution.py:720
  58.1 1.1 %collective-permute-start.5 = (bf16[256,512]{1,0:T(8,128)(2,1)S(1)}, bf16[256,512]{1,0:T(8,128)(2,1)S(1)}, u32[]{:S(2)}, u32[]{:S(2)}) collective-permute-start(bf16[256,512]{1,0:T(8,128)(2,1)S(1)} %get-tuple-element.58), channel_id=1, source_target_pairs={{0,2},{1,3},{2,0},{3,1},{4,6},{5,7},{6,4},{7,5},{8,10},{9,11},{10,... | collective-permute-start | bytes 786440 | tf_op jit(solution)/shard_map/ppermute | solution.py:720
  59.1 1.4 %collective-permute-start.6 = (bf16[256,512]{1,0:T(8,128)(2,1)S(1)}, bf16[256,512]{1,0:T(8,128)(2,1)S(1)}, u32[]{:S(2)}, u32[]{:S(2)}) collective-permute-start(bf16[256,512]{1,0:T(8,128)(2,1)S(1)} %get-tuple-element.59), channel_id=1, source_target_pairs={{0,3},{1,0},{2,1},{3,2},{4,7},{5,4},{6,5},{7,6},{8,11},{9,8},{10,9... | collective-permute-start | bytes 786440 | tf_op jit(solution)/shard_map/ppermute | solution.py:720
  60.9 3.5 %pull_local.1 = (f32[3,4,256,128]{3,2,1,0:T(8,128)S(1)}, f32[4,256,128]{2,1,0:T(8,128)S(1)}, f32[256,128]{1,0:T(8,128)S(1)}, f32[8,256]{1,0:T(8,128)S(1)}) custom-call(f32[3,4,256,128]{3,2,1,0:T(8,128)S(1)} %get-tuple-element.46.qkv_ref.refs_0_, f32[256,128]{1,0:T(8,128)S(1)} %get-tuple-element.45.pack_ref.refs_1_.refs_2_, f32[128,256]{1,0:T(8,128)S(1)} %copy-done.14, ...), custom_call_target="tpu_custom_call" | custom-call | tf_op jit(solution)/shard_map/pull_local/pallas_call | solution.py:89
  64.7 7.3 %finish.1 = (bf16[256,512]{1,0:T(8,128)(2,1)S(1)}, bf16[256,512]{1,0:T(8,128)(2,1)S(1)}, bf16[256,512]{1,0:T(8,128)(2,1)S(1)}, bf16[256,512]{1,0:T(8,128)(2,1)S(1)}) custom-call(s32[2]{0:T(128)S(1)} %pad_add_fusion.place_ref, f32[2,4]{1,0:T(2,128)S(1)} %bitcast.16, f32[3,4,256,128]{3,2,1,0:T(8,128)S(1)} %get-tuple-element.46.qkv_ref.refs_0_, ...), custom_call_target="tpu_custom_call" | custom-call | tf_op jit(solution)/shard_map/finish/pallas_call | solution.py:89
  72.0 1.0 collective-permute-start.13
  73.0 2.2 %collective-permute-start.14 = (bf16[256,512]{1,0:T(8,128)(2,1)S(1)}, bf16[256,512]{1,0:T(8,128)(2,1)S(1)}, u32[]{:S(2)}, u32[]{:S(2)}) collective-permute-start(bf16[256,512]{1,0:T(8,128)(2,1)S(1)} %get-tuple-element.86), channel_id=1, source_target_pairs={{0,2},{1,3},{2,0},{3,1},{4,6},{5,7},{6,4},{7,5},{8,10},{9,11},{10,... | collective-permute-start | bytes 786440 | tf_op jit(solution)/shard_map/ppermute | solution.py:720
  75.5 4.1 %collective-permute-done.5 = bf16[256,512]{1,0:T(8,128)(2,1)S(1)} collective-permute-done((bf16[256,512]{1,0:T(8,128)(2,1)S(1)}, bf16[256,512]{1,0:T(8,128)(2,1)S(1)}, u32[]{:S(2)}, u32[]{:S(2)}) %collective-permute-start.5) | collective-permute-done | bytes 262176 | tf_op jit(solution)/shard_map/ppermute | solution.py:720
  79.6 14.4 %collective-permute-done.6 = bf16[256,512]{1,0:T(8,128)(2,1)S(1)} collective-permute-done((bf16[256,512]{1,0:T(8,128)(2,1)S(1)}, bf16[256,512]{1,0:T(8,128)(2,1)S(1)}, u32[]{:S(2)}, u32[]{:S(2)}) %collective-permute-start.6) | collective-permute-done | bytes 262176 | tf_op jit(solution)/shard_map/ppermute | solution.py:720
  94.8 1.6 %collective-permute-done.13 = bf16[256,512]{1,0:T(8,128)(2,1)S(1)} collective-permute-done((bf16[256,512]{1,0:T(8,128)(2,1)S(1)}, bf16[256,512]{1,0:T(8,128)(2,1)S(1)}, u32[]{:S(2)}, u32[]{:S(2)}) %collective-permute-start.13) | collective-permute-done | bytes 262176 | tf_op jit(solution)/shard_map/ppermute | solution.py:720
  96.4 5.6 %collective-permute-done.14 = bf16[256,512]{1,0:T(8,128)(2,1)S(1)} collective-permute-done((bf16[256,512]{1,0:T(8,128)(2,1)S(1)}, bf16[256,512]{1,0:T(8,128)(2,1)S(1)}, u32[]{:S(2)}, u32[]{:S(2)}) %collective-permute-start.14) | collective-permute-done | bytes 262176 | tf_op jit(solution)/shard_map/ppermute | solution.py:720
  102.0 3.1 %collective-permute-done.15 = bf16[256,512]{1,0:T(8,128)(2,1)S(1)} collective-permute-done((bf16[256,512]{1,0:T(8,128)(2,1)S(1)}, bf16[256,512]{1,0:T(8,128)(2,1)S(1)}, u32[]{:S(2)}, u32[]{:S(2)}) %collective-permute-start.15) | collective-permute-done | bytes 262176 | tf_op jit(solution)/shard_map/ppermute | solution.py:720
  (67 shorter events, 10.3 us)
Async XLA Ops:
  0.6 34.4 %copy-start = (bf16[256,2048]{1,0:T(8,128)(2,1)S(1)}, bf16[256,2048]{1,0:T(8,128)(2,1)}, u32[]{:S(2)}) copy-start(bf16[256,2048]{1,0:T(8,128)(2,1)} %param.13) | copy-start | bytes 3145732
  0.6 2.9 %copy-start.5 = (bf16[2048,3,4,128]{3,2,1,0:T(4,128)(2,1)S(1)}, bf16[2048,3,4,128]{3,2,1,0:T(4,128)(2,1)}, u32[]{:S(2)}) copy-start(bf16[2048,3,4,128]{3,2,1,0:T(4,128)(2,1)} %param.8) | copy-start | bytes 18874372
  3.5 1.2 %copy-start.11 = (bf16[256,2048]{1,0:T(8,128)(2,1)S(1)}, bf16[256,2048]{1,0:T(8,128)(2,1)}, u32[]{:S(2)}) copy-start(bf16[256,2048]{1,0:T(8,128)(2,1)} %tokens_hbm.1) | copy-start | bytes 3145732
  18.0 2.7 %copy-start.4 = (bf16[2048,1536]{1,0:T(8,128)(2,1)}, bf16[2048,1536]{1,0:T(8,128)(2,1)S(1)}, u32[]{:S(2)}) copy-start(bf16[2048,1536]{1,0:T(8,128)(2,1)S(1)} %get-tuple-element.77.refs_14_) | copy-start | bytes 18874372
  25.5 5.6 %collective-permute-start = (bf16[4,128,256]{2,1,0:T(8,128)(2,1)}, bf16[4,128,256]{2,1,0:T(8,128)(2,1)S(1)}, u32[]{:S(2)}, u32[]{:S(2)}) collective-permute-start(bf16[4,128,256]{2,1,0:T(8,128)(2,1)} %get-tuple-element.54.own_ref), channel_id=1, source_target_pairs={{0,4},{4,0},{8,12},{12,8},{16,20},{20,16},{24,28},{28,24},{1,5},{5... | collective-permute-start | bytes 786440 | tf_op jit(solution)/shard_map/ppermute | solution.py:713
  26.2 1.2 %copy-start.2 = (f32[4,256,256]{2,1,0:T(8,128)S(1)}, f32[4,256,256]{2,1,0:T(8,128)}, u32[]{:S(2)}) copy-start(f32[4,256,256]{2,1,0:T(8,128)} %copy-done.1) | copy-start | bytes 3145732
  29.4 5.6 %copy-start.10 = (bf16[4,128,2048]{2,1,0:T(8,128)(2,1)S(1)}, bf16[4,128,2048]{2,1,0:T(8,128)(2,1)}, u32[]{:S(2)}) copy-start(bf16[4,128,2048]{2,1,0:T(8,128)(2,1)} %param.12) | copy-start | bytes 6291460
  31.1 16.0 %copy-start.24 = (f32[128]{0:T(128)S(1)}, f32[128]{0:T(128)}, u32[]{:S(2)}) copy-start(f32[128]{0:T(128)} %param.11) | copy-start | bytes 1540
  32.3 8.9 %collective-permute-start.3 = (bf16[4,128,256]{2,1,0:T(8,128)(2,1)S(1)}, bf16[4,128,256]{2,1,0:T(8,128)(2,1)S(1)}, u32[]{:S(2)}, u32[]{:S(2)}) collective-permute-start(bf16[4,128,256]{2,1,0:T(8,128)(2,1)S(1)} %join.1), channel_id=1, source_target_pairs={{0,24},{4,28},{8,16},{12,20},{16,8},{20,12},{24,0},{28,4},{1,25},{... | collective-permute-start | bytes 786440 | tf_op jit(solution)/shard_map/ppermute | solution.py:713
  34.5 12.6 %collective-permute-start.2 = (bf16[4,128,256]{2,1,0:T(8,128)(2,1)S(1)}, bf16[4,128,256]{2,1,0:T(8,128)(2,1)S(1)}, u32[]{:S(2)}, u32[]{:S(2)}) collective-permute-start(bf16[4,128,256]{2,1,0:T(8,128)(2,1)S(1)} %join.1), channel_id=1, source_target_pairs={{0,16},{4,20},{8,24},{12,28},{16,0},{20,4},{24,8},{28,12},{1,17},{... | collective-permute-start | bytes 786440 | tf_op jit(solution)/shard_map/ppermute | solution.py:713
  34.7 12.4 %collective-permute-start.1 = (bf16[4,128,256]{2,1,0:T(8,128)(2,1)S(1)}, bf16[4,128,256]{2,1,0:T(8,128)(2,1)S(1)}, u32[]{:S(2)}, u32[]{:S(2)}) collective-permute-start(bf16[4,128,256]{2,1,0:T(8,128)(2,1)S(1)} %join.1), channel_id=1, source_target_pairs={{0,8},{4,12},{8,0},{12,4},{16,24},{20,28},{24,16},{28,20},{1,9},{5... | collective-permute-start | bytes 786440 | tf_op jit(solution)/shard_map/ppermute | solution.py:713
  47.1 13.7 %copy-start.14 = (f32[128,256]{1,0:T(8,128)S(1)}, f32[128,256]{1,0:T(8,128)}, u32[]{:S(2)}) copy-start(f32[128,256]{1,0:T(8,128)} %copy-done.12) | copy-start | bytes 393220
  50.6 10.3 %copy-start.3 = (f32[4,256,256]{2,1,0:T(8,128)S(1)}, f32[4,256,256]{2,1,0:T(8,128)}, u32[]{:S(2)}) copy-start(f32[4,256,256]{2,1,0:T(8,128)} %copy-done.1) | copy-start | bytes 3145732
  50.6 10.3 %copy-start.7 = (f32[4,256,256]{2,1,0:T(8,128)S(1)}, f32[4,256,256]{2,1,0:T(8,128)}, u32[]{:S(2)}) copy-start(f32[4,256,256]{2,1,0:T(8,128)} %copy-done.6) | copy-start | bytes 3145732
  50.6 10.3 %copy-start.9 = (f32[4,256,256]{2,1,0:T(8,128)S(1)}, f32[4,256,256]{2,1,0:T(8,128)}, u32[]{:S(2)}) copy-start(f32[4,256,256]{2,1,0:T(8,128)} %copy-done.8) | copy-start | bytes 3145732
  50.6 2.3 %collective-permute-start.8 = (bf16[4,128,256]{2,1,0:T(8,128)(2,1)S(1)}, bf16[4,128,256]{2,1,0:T(8,128)(2,1)S(1)}, u32[]{:S(2)}, u32[]{:S(2)}) collective-permute-start(bf16[4,128,256]{2,1,0:T(8,128)(2,1)S(1)} %get-tuple-element.80.refs_0_), channel_id=1, source_target_pairs={{0,4},{4,0},{8,12},{12,8},{16,20},{20,16},{24,28},{28,24},{1,5},{5... | collective-permute-start | bytes 786440 | tf_op jit(solution)/shard_map/ppermute | solution.py:713
  51.2 7.9 %collective-permute-start.7 = (bf16[4,128,256]{2,1,0:T(8,128)(2,1)S(1)}, bf16[4,128,256]{2,1,0:T(8,128)(2,1)S(1)}, u32[]{:S(2)}, u32[]{:S(2)}) collective-permute-start(bf16[4,128,256]{2,1,0:T(8,128)(2,1)S(1)} %get-tuple-element.79), channel_id=1, source_target_pairs={{0,4},{4,0},{8,12},{12,8},{16,20},{20,16},{24,28},{28,24},{1,5},{5... | collective-permute-start | bytes 786440 | tf_op jit(solution)/shard_map/ppermute | solution.py:713
  51.3 1.6 %collective-permute-start.9 = (bf16[4,128,128]{2,1,0:T(8,128)(2,1)S(1)}, bf16[4,128,128]{2,1,0:T(8,128)(2,1)S(1)}, u32[]{:S(2)}, u32[]{:S(2)}) collective-permute-start(bf16[4,128,128]{2,1,0:T(8,128)(2,1)S(1)} %get-tuple-element.81.refs_1_), channel_id=1, source_target_pairs={{0,4},{4,0},{8,12},{12,8},{16,20},{20,16},{24,28},{28,24},{1,5},{5... | collective-permute-start | bytes 393224 | tf_op jit(solution)/shard_map/ppermute | solution.py:713
  53.0 7.5 %collective-permute-start.12 = (bf16[4,128,128]{2,1,0:T(8,128)(2,1)S(1)}, bf16[4,128,128]{2,1,0:T(8,128)(2,1)S(1)}, u32[]{:S(2)}, u32[]{:S(2)}) collective-permute-start(bf16[4,128,128]{2,1,0:T(8,128)(2,1)S(1)} %get-tuple-element.83), channel_id=1, source_target_pairs={{0,24},{4,28},{8,16},{12,20},{16,8},{20,12},{24,0},{28,4},{1,25},{... | collective-permute-start | bytes 393224 | tf_op jit(solution)/shard_map/ppermute | solution.py:713
  54.5 10.2 %collective-permute-start.10 = (bf16[4,128,256]{2,1,0:T(8,128)(2,1)S(1)}, bf16[4,128,256]{2,1,0:T(8,128)(2,1)S(1)}, u32[]{:S(2)}, u32[]{:S(2)}) collective-permute-start(bf16[4,128,256]{2,1,0:T(8,128)(2,1)S(1)} %get-tuple-element.82), channel_id=1, source_target_pairs={{0,8},{4,12},{8,0},{12,4},{16,24},{20,28},{24,16},{28,20},{1,9},{5... | collective-permute-start | bytes 786440 | tf_op jit(solution)/shard_map/ppermute | solution.py:713
  55.4 9.2 %slice-start = ((s8[6291456]{0:T(1024)(128)(4,1)}), s8[4194304]{0:T(1024)(128)(4,1)S(1)}, s32[]{:S(2)}) async-start(s8[6291456]{0:T(1024)(128)(4,1)} %bitcast.9), calls=%async_computation | async-start | bytes 8388608
  56.7 18.5 %collective-permute-start.4 = (bf16[256,512]{1,0:T(8,128)(2,1)S(1)}, bf16[256,512]{1,0:T(8,128)(2,1)S(1)}, u32[]{:S(2)}, u32[]{:S(2)}) collective-permute-start(bf16[256,512]{1,0:T(8,128)(2,1)S(1)} %get-tuple-element.57), channel_id=1, source_target_pairs={{0,1},{1,2},{2,3},{3,0},{4,5},{5,6},{6,7},{7,4},{8,9},{9,10},{10,1... | collective-permute-start | bytes 786440 | tf_op jit(solution)/shard_map/ppermute | solution.py:720
  58.1 21.5 %collective-permute-start.5 = (bf16[256,512]{1,0:T(8,128)(2,1)S(1)}, bf16[256,512]{1,0:T(8,128)(2,1)S(1)}, u32[]{:S(2)}, u32[]{:S(2)}) collective-permute-start(bf16[256,512]{1,0:T(8,128)(2,1)S(1)} %get-tuple-element.58), channel_id=1, source_target_pairs={{0,2},{1,3},{2,0},{3,1},{4,6},{5,7},{6,4},{7,5},{8,10},{9,11},{10,... | collective-permute-start | bytes 786440 | tf_op jit(solution)/shard_map/ppermute | solution.py:720
  59.1 34.8 %collective-permute-start.6 = (bf16[256,512]{1,0:T(8,128)(2,1)S(1)}, bf16[256,512]{1,0:T(8,128)(2,1)S(1)}, u32[]{:S(2)}, u32[]{:S(2)}) collective-permute-start(bf16[256,512]{1,0:T(8,128)(2,1)S(1)} %get-tuple-element.59), channel_id=1, source_target_pairs={{0,3},{1,0},{2,1},{3,2},{4,7},{5,4},{6,5},{7,6},{8,11},{9,8},{10,9... | collective-permute-start | bytes 786440 | tf_op jit(solution)/shard_map/ppermute | solution.py:720
  60.5 4.1 %collective-permute-start.11 = (bf16[4,128,128]{2,1,0:T(8,128)(2,1)S(1)}, bf16[4,128,128]{2,1,0:T(8,128)(2,1)S(1)}, u32[]{:S(2)}, u32[]{:S(2)}) collective-permute-start(bf16[4,128,128]{2,1,0:T(8,128)(2,1)S(1)} %get-tuple-element.83), channel_id=1, source_target_pairs={{0,16},{4,20},{8,24},{12,28},{16,0},{20,4},{24,8},{28,12},{1,17},{... | collective-permute-start | bytes 393224 | tf_op jit(solution)/shard_map/ppermute | solution.py:713
  60.8 3.8 %slice-start.1 = ((s8[6291456]{0:T(1024)(128)(4,1)}), s8[2097152]{0:T(1024)(128)(4,1)S(1)}, s32[]{:S(2)}) async-start(s8[6291456]{0:T(1024)(128)(4,1)} %bitcast.9), calls=%async_computation.1 | async-start | bytes 4194304
  60.9 3.8 %copy-start.16 = (bf16[128,2048]{1,0:T(8,128)(2,1)S(1)}, bf16[128,2048]{1,0:T(8,128)(2,1)}, u32[]{:S(2)}) copy-start(bf16[128,2048]{1,0:T(8,128)(2,1)} %copy-done.15) | copy-start | bytes 1572868
  60.9 3.8 %copy-start.21 = (f32[256,128]{1,0:T(8,128)S(1)}, f32[256,128]{1,0:T(8,128)}, u32[]{:S(2)}) copy-start(f32[256,128]{1,0:T(8,128)} %copy-done.20) | copy-start | bytes 393220
  60.9 3.8 %copy-start.23 = (f32[4,2]{0,1:T(2,128)S(1)}, f32[4,2]{0,1:T(2,128)}, u32[]{:S(2)}) copy-start(f32[4,2]{0,1:T(2,128)} %param.10) | copy-start | bytes 100
  72.0 24.4 %collective-permute-start.13 = (bf16[256,512]{1,0:T(8,128)(2,1)S(1)}, bf16[256,512]{1,0:T(8,128)(2,1)S(1)}, u32[]{:S(2)}, u32[]{:S(2)}) collective-permute-start(bf16[256,512]{1,0:T(8,128)(2,1)S(1)} %get-tuple-element.85), channel_id=1, source_target_pairs={{0,1},{1,2},{2,3},{3,0},{4,5},{5,6},{6,7},{7,4},{8,9},{9,10},{10,1... | collective-permute-start | bytes 786440 | tf_op jit(solution)/shard_map/ppermute | solution.py:720
  73.0 29.0 %collective-permute-start.14 = (bf16[256,512]{1,0:T(8,128)(2,1)S(1)}, bf16[256,512]{1,0:T(8,128)(2,1)S(1)}, u32[]{:S(2)}, u32[]{:S(2)}) collective-permute-start(bf16[256,512]{1,0:T(8,128)(2,1)S(1)} %get-tuple-element.86), channel_id=1, source_target_pairs={{0,2},{1,3},{2,0},{3,1},{4,6},{5,7},{6,4},{7,5},{8,10},{9,11},{10,... | collective-permute-start | bytes 786440 | tf_op jit(solution)/shard_map/ppermute | solution.py:720
  75.2 29.9 %collective-permute-start.15 = (bf16[256,512]{1,0:T(8,128)(2,1)S(1)}, bf16[256,512]{1,0:T(8,128)(2,1)S(1)}, u32[]{:S(2)}, u32[]{:S(2)}) collective-permute-start(bf16[256,512]{1,0:T(8,128)(2,1)S(1)} %get-tuple-element.87), channel_id=1, source_target_pairs={{0,3},{1,0},{2,1},{3,2},{4,7},{5,4},{6,5},{7,6},{8,11},{9,8},{10,9... | collective-permute-start | bytes 786440 | tf_op jit(solution)/shard_map/ppermute | solution.py:720
  (11 other events, 9.4 us)

commit v3 on v2

--- a/solution.py
+++ b/solution.py
@@ -10,12 +10,12 @@
 BLOCK = 64
 LANES = 128
 EPS = 1e-06
-VMEM_BYTES = 28 * 1024 * 1024
+MIB = 1024 * 1024
 F32 = jnp.float32
 BF16 = jnp.bfloat16
 WHOLE = pl.BlockSpec(memory_space=pltpu.VMEM)
 SCALARS = pl.BlockSpec(memory_space=pltpu.SMEM)
-PARAMS = pltpu.CompilerParams(vmem_limit_bytes=VMEM_BYTES)
+HBM = pl.BlockSpec(memory_space=pltpu.HBM)
 
 
 def contract(left, right, dim_left, dim_right):
@@ -81,22 +81,22 @@
     return pltpu.VMEM(shape, dtype)
 
 
-def pin(values):
-    return [pltpu.with_memory_space_constraint(value, pltpu.VMEM) for value in values]
-
-
-def local_call(body, name, out_shape, scalars, arrays, scratch=(), remote=()):
+def pin(values, space):
+    return [pltpu.with_memory_space_constraint(value, space) for value in values]
+
+
+def local_call(body, name, limit, out_shape, scalars, arrays, scratch=(), remote=()):
     return pl.pallas_call(
         body,
         out_shape=tuple(out_shape),
         in_specs=[SCALARS] * len(scalars)
         + [WHOLE] * len(arrays)
-        + [pl.BlockSpec(memory_space=pl.ANY)] * len(remote),
+        + [HBM] * len(remote),
         out_specs=(WHOLE,) * len(out_shape),
         scratch_shapes=list(scratch),
-        compiler_params=PARAMS,
+        compiler_params=pltpu.CompilerParams(vmem_limit_bytes=limit * MIB),
         name=name,
-    )(*scalars, *pin(arrays), *remote)
+    )(*scalars, *pin(arrays, pltpu.VMEM), *pin(remote, pltpu.HBM))
 
 
 def column(pack, at):
@@ -117,21 +117,22 @@
     rate = jnp.zeros((1, LANES), F32)
     bias = jnp.zeros((1, LANES), F32)
     for head in range(heads):
-        rate = jnp.where(lane_row == decay_col + head, hp_ref[0, head], rate)
-        bias = jnp.where(lane_row == beta_col + head, hp_ref[1, head], bias)
+        rate = jnp.where(lane_row == decay_col + head, hp_ref[0:1, head : head + 1], rate)
+        bias = jnp.where(lane_row == beta_col + head, hp_ref[1:2, head : head + 1], bias)
     return rate, bias
 
 
-def project_body(sizes, hp_ref, tokens_hbm, w_hbm, small_hbm, *refs):
+def project_body(sizes, hp_hbm, tokens_hbm, w_hbm, small_hbm, *refs):
     heads, levels, chunks = sizes
     (wr_ref, small_ref, qkv_ref, gate_ref, pack_ref, pack_t_ref, trans_ref, mixed_t_ref,
-     decay_ref, base_ref, lower_ref, pair_ref) = refs[:12]
-    tokens, wide_in, wide_even, wide_odd, small_in, small_wide, acc, sems = refs[12:]
+     decay_ref, base_ref, lower_ref, rates_ref, pair_ref) = refs[:13]
+    tokens, wide_in, wide_even, wide_odd, small_in, small_wide, acc, hp_ref, sems = refs[13:]
     rows, width = tokens.shape
     depth = width // chunks
     cols = 3 * heads
     fetch_tokens = pltpu.make_async_copy(tokens_hbm, tokens, sems.at[chunks])
     fetch_small = pltpu.make_async_copy(small_hbm, small_in, sems.at[chunks + 1])
+    fetch_rates = pltpu.make_async_copy(hp_hbm, hp_ref, sems.at[chunks + 2])
     fetches = []
     for chunk in range(chunks):
         span = pl.ds(chunk * depth * cols, depth * cols)
@@ -141,6 +142,7 @@
     fetches[0].start()
     fetch_tokens.start()
     fetch_small.start()
+    fetch_rates.start()
     for fetch in fetches[1:]:
         fetch.start()
     for chunk in range(chunks):
@@ -172,7 +174,10 @@
     norm_col = beta_col + heads
     gate_ref[...] = gate
     lane = lane_of(rows)
+    fetch_rates.wait()
     rate, bias = head_rows(hp_ref, heads, decay_col, beta_col)
+    rates_ref[0:1, :] = rate
+    rates_ref[1:2, :] = bias
     switch = jax.nn.sigmoid(gate + bias)
     lam = jnp.maximum(gate, 0.0) + jnp.log1p(jnp.exp(-jnp.abs(gate)))
     row_id, col_id = pair_ids(rows)
@@ -262,6 +267,7 @@
         kept(square, F32),
         kept(square, F32),
         kept(square, F32),
+        kept((2, LANES), F32),
         kept((heads, key, 2 * key), BF16),
     )
     scratch = [
@@ -272,11 +278,12 @@
         pltpu.VMEM(small.shape, BF16),
         pltpu.VMEM((LANES, width), F32),
         pltpu.VMEM((rows, cols * key), F32),
-        pltpu.SemaphoreType.DMA((chunks + 2,)),
+        pltpu.VMEM(head_param.shape, F32),
+        pltpu.SemaphoreType.DMA((chunks + 3,)),
     ]
     return local_call(
-        functools.partial(project_body, (heads, levels, chunks)), "project", out_shape,
-        [head_param], [], scratch, [tokens, flat_w, small],
+        functools.partial(project_body, (heads, levels, chunks)), "project", 22, out_shape,
+        [], [], scratch, [head_param, tokens, flat_w, small],
     )
 
 
@@ -325,7 +332,7 @@
         kept((heads, key, rows), BF16),
     )
     return local_call(
-        functools.partial(local_body, (heads, levels, bits)), "local_part", out_shape,
+        functools.partial(local_body, (heads, levels, bits)), "local_part", 10, out_shape,
         [], [qkv, pack, pack_t, trans, mixed_t, decay],
     )
 
@@ -339,59 +346,64 @@
     return (moved + late).astype(BF16)
 
 
-def join_body(bit, place_ref, own_ref, other_ref, out_ref):
-    upper = ((place_ref[0] >> bit) & 1) == 1
-    for head in range(own_ref.shape[0]):
-        out_ref[head] = join_pair(upper, own_ref[head], other_ref[head])
-
-
-def join(bit, place, own, other):
-    return local_call(
-        functools.partial(join_body, bit), "join", [kept(own.shape, BF16)], [place], [own, other]
-    )[0]
+def join_body(place_ref, own_ref, other_ref, out_ref):
+    half = out_ref.shape[0]
+    upper = (place_ref[0] & 1) == 1
+    for slot in range(half):
+        head = (place_ref[0] & 1) * half + slot
+        out_ref[slot] = join_pair(upper, own_ref[head], other_ref[head])
+
+
+def join_half(place, own, other):
+    half = (own.shape[0] // 2,) + own.shape[1:]
+    return local_call(join_body, "join_half", 6, [kept(half, BF16)], [place], [own, other])[0]
 
 
 def gather_node(head, bit, first, near, uppers):
     if bit == 0:
-        return near[first][head]
+        mine, theirs = near[first]
+        half = mine.shape[0]
+        here = uppers[0] if head >= half else jnp.logical_not(uppers[0])
+        return jnp.where(here, mine[head % half], theirs[head % half])
     own = gather_node(head, bit - 1, first, near, uppers)
     other = gather_node(head, bit - 1, first ^ (1 << (bit - 1)), near, uppers)
     return join_pair(uppers[bit], own, other)
 
 
-def cross_body(sizes, place_ref, gain_ref, pack_ref, local_ref, hat_ref, hat_t_ref, grad_ref, *refs):
-    heads, bits, far, near_count = sizes
+def reach_body(
+    sizes, place_ref, gain_ref, pack_ref, local_ref, hat_ref, grad_ref, weight_ref, *refs
+):
+    heads, bits, far, count, near_count = sizes
     first_ref = refs[0]
-    near = (None,) + refs[1 : near_count + 1]
-    refs = refs[near_count + 1 :]
-    normed_ref, dout_ref, dhat_ref, dfar_ref = refs[:4]
-    nodes = refs[4 : 4 + far - 2]
-    sends = refs[4 + max(far - 2, 0) :]
+    near = [None] + [(refs[1 + at], refs[1 + near_count + at]) for at in range(near_count)]
+    refs = refs[2 * near_count + 1 :]
+    out_refs = refs[:count]
+    dout_ref, found_ref, prefix_ref, dfar_ref = refs[count : count + 4]
+    nodes = refs[count + 4 : -1]
+    normed_ref = refs[-1]
     rows = pack_ref.shape[0]
     key = hat_ref.shape[2]
-    place = place_ref[0]
     pack = pack_ref[...]
     gain = gain_ref[...]
     lane = lane_of(rows)
     all_heads = range(heads)
-    uppers = [((place >> bit) & 1) == 1 for bit in range(far)]
+    uppers = [((place_ref[0] >> bit) & 1) == 1 for bit in range(far)]
     others = []
     for bit in range(far):
         if bit == 0:
             others.append([first_ref[head] for head in all_heads])
-        elif bit == 1:
-            others.append([near[1][head] for head in all_heads])
         else:
             others.append(
                 [gather_node(head, bit - 1, 1 << (bit - 1), near, uppers) for head in all_heads]
             )
             for head in all_heads:
-                nodes[bit - 2][head] = others[bit][head]
+                nodes[bit - 1][head] = others[bit][head]
     eye_key = jnp.where(pair_ids(key)[0] == pair_ids(key)[1], 1.0, 0.0).astype(BF16)
     prefix = [eye_key for head in all_heads]
-    prefixes, found = [], []
+    found = []
     for bit in range(far):
-        prefixes.append(prefix)
+        for head in all_heads:
+            prefix_ref[head, bit] = prefix[head]
         moved = [mm(prefix[head], others[bit][head]) for head in all_heads]
         found.append([jnp.where(uppers[bit], m[:, key:], 0.0).astype(BF16) for m in moved])
         prefix = [
@@ -401,14 +413,13 @@
     found = [jnp.concatenate([found[bit][head] for bit in range(far)], 1) for head in all_heads]
     reached = [mm(hat_ref[head], found[head]) for head in all_heads]
     dfar = jnp.zeros((rows, LANES), F32)
-    spread = []
     for head in all_heads:
+        found_ref[head] = found[head]
         summed = local_ref[head]
-        weights, parts = [], []
+        parts = []
         for bit in range(far):
-            weights.append(column(pack, (bits + 1 + bit) * heads + head))
             parts.append(reached[head][:, bit * key : (bit + 1) * key])
-            summed = summed + weights[bit] * parts[bit]
+            summed = summed + column(pack, (bits + 1 + bit) * heads + head) * parts[bit]
         scale = lax.rsqrt(jnp.mean(summed * summed, -1, keepdims=True) + EPS)
         unit = summed * scale
         normed_ref[:, head * key : (head + 1) * key] = (unit * gain).astype(BF16)
@@ -418,13 +429,54 @@
         for bit in range(far):
             col = (bits + 1 + bit) * heads + head
             dfar = jnp.where(lane == col, row_sum(dout * parts[bit]), dfar)
-        spread.append(
-            jnp.concatenate([(weights[bit] * dout).astype(BF16) for bit in range(far)], 1)
-        )
     dfar_ref[...] = dfar
+    size = out_refs[0].shape[1]
+    for shift in range(count):
+        dest = lax.rem(place_ref[1] + shift, count)
+        cols = pl.ds(pl.multiple_of(dest * size, size), size)
+        out_refs[shift][...] = jnp.dot(
+            normed_ref[...], weight_ref[:, cols], preferred_element_type=F32
+        ).astype(BF16)
+
+
+def reach(place, arrays, first, near, bits, far, count):
+    gain, pack, local_out, hat, grad_normed, weight = arrays
+    heads, rows, key = hat.shape
+    nodes = tuple(kept(first.shape, BF16) for bit in range(1, far))
+    out_shape = (kept((rows, weight.shape[1] // count), BF16),) * count + (
+        kept((heads, rows, key), F32),
+        kept((heads, key, far * key), BF16),
+        kept((heads, far, key, key), BF16),
+        kept((rows, LANES), F32),
+    ) + nodes
+    mine, theirs = near
+    got = local_call(
+        functools.partial(reach_body, (heads, bits, far, count, len(mine))), "reach", 10, out_shape,
+        [place], [*arrays, first, *mine, *theirs], [pltpu.VMEM((rows, heads * key), BF16)],
+    )
+    parts, got = got[:count], got[count:]
+    return parts, got[:4], got[4:]
+
+
+def return_body(sizes, place_ref, pack_ref, hat_t_ref, dout_ref, found_ref, prefix_ref, *refs):
+    heads, bits, far = sizes
+    others = refs[:far]
+    dhat_ref = refs[far]
+    sends = refs[far + 1 :]
+    key = hat_t_ref.shape[1]
+    pack = pack_ref[...]
+    all_heads = range(heads)
+    uppers = [((place_ref[0] >> bit) & 1) == 1 for bit in range(far)]
+    spread = []
+    for head in all_heads:
+        parts = []
+        for bit in range(far):
+            weight = column(pack, (bits + 1 + bit) * heads + head)
+            parts.append((weight * dout_ref[head]).astype(BF16))
+        spread.append(jnp.concatenate(parts, 1))
     dfound = [mm(hat_t_ref[head], spread[head]) for head in all_heads]
     for head in all_heads:
-        dhat_ref[head] = mm_nt(spread[head], found[head])
+        dhat_ref[head] = mm_nt(spread[head], found_ref[head])
     dprefix = [jnp.zeros((key, key), F32) for head in all_heads]
     for bit in reversed(range(far)):
         dfree = [
@@ -435,10 +487,8 @@
             for head in all_heads
         ]
         for head in all_heads:
-            if bit == far - 1:
-                sends[bit][head] = mm_tn(prefixes[bit][head], dfree[head]).astype(BF16)
-            else:
-                sends[bit][head] = mm_tn(prefixes[bit][head], both[head]).astype(BF16)
+            sent = dfree[head] if bit == far - 1 else both[head]
+            sends[bit][head] = mm_tn(prefix_ref[head, bit], sent).astype(BF16)
         if bit > 0:
             moved = [mm_nt(both[head], others[bit][head]) for head in all_heads]
             dprefix = [
@@ -446,40 +496,17 @@
             ]
 
 
-def cross(place, gain, pack, local_out, hat, hat_t, grad_normed, first, near, bits, far):
-    heads, rows, key = hat.shape
-    nodes = tuple(kept(first.shape, BF16) for bit in range(2, far))
+def return_states(place, pack, hat_t, dout, found, prefix, others, bits):
+    heads, rows, key = dout.shape
+    far = len(others)
     sends = tuple(
         kept((heads, key, (1 if bit == far - 1 else 2) * key), BF16) for bit in range(far)
     )
-    out_shape = (
-        kept((rows, heads * key), BF16),
-        kept((heads, rows, key), F32),
-        kept((heads, rows, key), F32),
-        kept((rows, LANES), F32),
-    ) + nodes + sends
     got = local_call(
-        functools.partial(cross_body, (heads, bits, far, len(near))), "cross", out_shape,
-        [place], [gain, pack, local_out, hat, hat_t, grad_normed, first, *near],
-    )
-    return got[:4], got[4 : 4 + len(nodes)], got[4 + len(nodes) :]
-
-
-def spread_body(count, place_ref, left_ref, right_ref, *out_refs):
-    size = out_refs[0].shape[1]
-    for shift in range(count):
-        dest = lax.rem(place_ref[1] + shift, count)
-        cols = pl.ds(pl.multiple_of(dest * size, size), size)
-        out_refs[shift][...] = jnp.dot(
-            left_ref[...], right_ref[:, cols], preferred_element_type=F32
-        ).astype(BF16)
-
-
-def spread_out(place, left, right, count):
-    out = kept((left.shape[0], right.shape[1] // count), BF16)
-    return local_call(
-        functools.partial(spread_body, count), "spread_out", [out] * count, [place], [left, right]
-    )
+        functools.partial(return_body, (heads, bits, far)), "return_states", 8,
+        (kept(dout.shape, F32),) + sends, [place], [pack, hat_t, dout, found, prefix, *others],
+    )
+    return got[0], got[1:]
 
 
 def add_body(*refs):
@@ -491,7 +518,7 @@
 
 def add_all(left, right):
     out_shape = [kept(value.shape, BF16) for value in left]
-    return local_call(add_body, "add_all", out_shape, [], [*left, *right])
+    return local_call(add_body, "add_all", 6, out_shape, [], [*left, *right])
 
 
 def lower_pull(dlower, base, lower, beta, decay, strict, k_in):
@@ -579,16 +606,16 @@
         kept((2 * heads, rows), F32),
     )
     return local_call(
-        functools.partial(pull_body, (heads, levels, bits)), "pull_local", out_shape, [], arrays
-    )
-
-
-def finish_body(sizes, place_ref, hp_ref, *refs):
+        functools.partial(pull_body, (heads, levels, bits)), "pull_local", 12, out_shape, [], arrays
+    )
+
+
+def finish_body(sizes, place_ref, *refs):
     heads, levels, far, count, arrived_counts = sizes
     (qkv_ref, gate_ref, pack_ref, trans_ref, mixed_ref, decay_ref, base_ref, lower_ref,
-     dqkv_ref, dgrown_ref, dcol_ref, drow_ref, dfar_ref, small_ref, wr_ref) = refs[:15]
-    others = refs[15 : 15 + far]
-    refs = refs[15 + far :]
+     dqkv_ref, dgrown_ref, dcol_ref, drow_ref, dfar_ref, rates_ref, small_ref, wr_ref) = refs[:16]
+    others = refs[16 : 16 + far]
+    refs = refs[16 + far :]
     arrived = []
     for found in arrived_counts:
         arrived.append(refs[:found])
@@ -676,7 +703,7 @@
          jnp.zeros((LANES - norm_col, rows), F32)], 0
     )
     dcol = dcol + drow.T
-    rate, bias = head_rows(hp_ref, heads, decay_col, beta_col)
+    rate, bias = rates_ref[0:1, :], rates_ref[1:2, :]
     switch = jax.nn.sigmoid(gate_ref[...] + bias)
     dlog = mm_full((row_id <= col_id).astype(F32), dcol)
     slope = switch * (1.0 - switch)
@@ -694,7 +721,7 @@
         out_refs[shift][...] = part.astype(BF16)
 
 
-def finish(place, head_param, arrays, others, arrived, levels, count):
+def finish(place, arrays, others, arrived, levels, count):
     rows = arrays[0].shape[2]
     width, cols = arrays[-1].shape
     far = len(others)
@@ -702,9 +729,9 @@
     heads = arrays[0].shape[1]
     flat = [value for group in arrived for value in group]
     return local_call(
-        functools.partial(finish_body, (heads, levels, far, count, counts)), "finish",
+        functools.partial(finish_body, (heads, levels, far, count, counts)), "finish", 12,
         [kept((rows, width // count), BF16)] * count,
-        [place, head_param], [*arrays, *others, *flat], [pltpu.VMEM((rows, cols), BF16)],
+        [place], [*arrays, *others, *flat], [pltpu.VMEM((rows, cols), BF16)],
     )
 
 
@@ -737,37 +764,42 @@
     flat_out = out_weight.reshape(heads * key, width)
     gain = norm_gain.reshape(1, key)
 
-    (wr, small_t, qkv, gate, pack, pack_t, trans, mixed_t, decay, base, lower, pair) = project(
+    (wr, small_t, qkv, gate, pack, pack_t, trans, mixed_t, decay, base, lower, rates_row,
+     pair) = project(
         tokens, flat_w, small, rates, heads, levels
     )
     first = swap(pair, "ctx", 1)
-    node = join(0, place, pair, first)
-    near = [swap(node, "ctx", 2 * at) for at in range(1, size // 2)]
+    node = join_half(place, pair, first)
+    mine = [swap(node, "ctx", 2 * at) for at in range(1, size // 2)]
     (attn, attn_t, prod_t, scores, mix, mixed, local_out, hat, hat_t) = local_part(
         qkv, pack, pack_t, trans, mixed_t, decay, levels, bits
     )
     grad_normed = lax.dot_general(
         grad_out, flat_out, (((1,), (1,)), ((), ())), preferred_element_type=F32
     )
-    (normed, dout, dhat, dfar), nodes, sends = cross(
-        place, gain, pack, local_out, hat, hat_t, grad_normed, first, near, bits, far
-    )
-    others = [first, near[0], *nodes]
+    mine, local_out, grad_normed = lax.optimization_barrier((mine, local_out, grad_normed))
+    theirs = [swap(value, "ctx", 1) for value in mine]
+    out_parts, (dout, found, prefix, dfar), nodes = reach(
+        place, [gain, pack, local_out, hat, grad_normed, flat_out], first, (mine, theirs),
+        bits, far, count
+    )
+    layer_out = scatter_sum(out_parts, "head")
+    others = [first, *nodes]
+    dhat, sends = return_states(place, pack, hat_t, dout, found, prefix, others, bits)
     got = [swap(value, "ctx", 1) for value in sends]
     arrived = [[got[0]]]
     sums = add_all(sends[1:], got[1:])
     for bit in range(1, far):
         half = 1 << (bit - 1)
         arrived.append([swap(sums[bit - 1], "ctx", 2 * at) for at in range(half, 2 * half)])
-    layer_out = scatter_sum(spread_out(place, normed, flat_out, count), "head")
     dqkv, dgrown, dcol, drow = pull_local(
         [qkv, pack, pack_t, trans, attn, attn_t, prod_t, scores, mix, decay, base, lower, dout,
          dhat],
         levels, bits,
     )
     arrays = [qkv, gate, pack, trans, mixed, decay, base, lower, dqkv, dgrown, dcol, drow, dfar,
-              small_t, wr]
-    parts = finish(place, rates, arrays, others, arrived, levels, count)
+              rates_row, small_t, wr]
+    parts = finish(place, arrays, others, arrived, levels, count)
     return layer_out, scatter_sum(parts, "head")
 
 

time: 106 us -> 93.6 us (0.88)
  local copies, waits for them, and re-layouts: 17.5 us -> 8.6 us
  waiting for transfers between devices: 41.7 us -> 34.5 us
  starting transfers between devices: 14.5 us -> 16.1 us
  matrix products: 0.75 us -> 2.33 us
    unnamed x54 -> x40, local copies, waits for them, and re-layouts: 17.5 us -> 8.6 us
    ppermute x10 -> x13, waiting for transfers between devices: 12.8 us -> 6.97 us  [swap(): return lax.ppermute(value, axis, [(at, at ^ mask) for at in range(size)])]
    dot_general x1, matrix products: 0.75 us -> 2.33 us  [on_device(): lax.dot_general(grad_out, flat_out, (((1,), (1,)), ((), ())), preferred_e...]
    ppermute x6, waiting for transfers between devices: 28.9 us -> 27.5 us  [scatter_sum(): lax.ppermute(parts[shift], axis, [(at, (at + shift) % count) for at in ra...]
    ppermute x10 -> x13, starting transfers between devices: 7.22 us -> 8.44 us  [swap(): return lax.ppermute(value, axis, [(at, at ^ mask) for at in range(size)])]
  transfers between devices with their start and end apart: 16 -> 19, of which waited for: 9 -> 12; matrix products, arithmetic and copies ran while one was open for 2% -> 3% of each run, Pallas kernels for 13% -> 13%
where the time goes in v3:
time: 93.6 us; the launch traced here: 93.5 us
  waiting for transfers between devices  34.5 us (37%)
  Pallas kernels  29.4 us (31%)
  starting transfers between devices  16.1 us (17%)
  local copies, waits for them, and re-layouts  8.6 us (9%)
  matrix products  2.33 us (2%)
  other arithmetic  1.75 us (2%)
    pallas_call x8, Pallas kernels, local_call(): pl.pallas_call(body, out_shape=tuple(out_shape), in_specs=[SCALARS] * len...  29.4 us
    ppermute x6, waiting for transfers between devices, scatter_sum(): lax.ppermute(parts[shift], axis, [(at, (at + shift) % count) for at in ra...  27.5 us
    unnamed x40, local copies, waits for them, and re-layouts  8.6 us
    ppermute x13, starting transfers between devices, swap(): return lax.ppermute(value, axis, [(at, at ^ mask) for at in range(size)])  8.44 us
    ppermute x6, starting transfers between devices, scatter_sum(): lax.ppermute(parts[shift], axis, [(at, (at + shift) % count) for at in ra...  7.62 us
    ppermute x13, waiting for transfers between devices, swap(): return lax.ppermute(value, axis, [(at, at ^ mask) for at in range(size)])  6.97 us
    dot_general x1, matrix products, on_device(): lax.dot_general(grad_out, flat_out, (((1,), (1,)), ((), ())), preferred_e...  2.33 us
  transfers between devices with their start and end apart: 19, of which 12 were waited for; matrix products, arithmetic and copies ran while one was open for 3% of the time, Pallas kernels for 13%

profile of v3, /device:TPU:9, one launch (start us, length us, event | category | flops | bytes accessed | tf_op | source)
XLA Modules:
  0.0 93.5 jit_solution(2671402596198775497)
XLA Ops:
  0.6 10.6 %project.1 = (bf16[2048,1536]{1,0:T(8,128)(2,1)S(1)}, bf16[128,2048]{1,0:T(8,128)(2,1)S(1)}, f32[3,4,256,128]{3,2,1,0:T(8,128)S(1)}, f32[256,128]{1,0:T(8,128)S(...) custom-call(f32[2,4]{1,0:T(2,128)} %bitcast.16, ...), custom_call_target="tpu_custom_call" | custom-call | tf_op jit(solution)/shard_map/project/pallas_call | solution.py:89
  11.3 1.0 %copy-done.1 = f32[4,256,256]{2,1,0:T(8,128)} copy-done((f32[4,256,256]{2,1,0:T(8,128)}, f32[4,256,256]{2,1,0:T(8,128)S(1)}, u32[]{:S(2)}) %copy-start.1) | copy-done | bytes 1048600
  12.2 2.7 %copy-done.3 = bf16[2048,1536]{1,0:T(8,128)(2,1)} copy-done((bf16[2048,1536]{1,0:T(8,128)(2,1)}, bf16[2048,1536]{1,0:T(8,128)(2,1)S(1)}, u32[]{:S(2)}) %copy-start.3) | copy-done | bytes 6291480
  14.9 1.0 %copy-done.4 = f32[4,256,256]{2,1,0:T(8,128)} copy-done((f32[4,256,256]{2,1,0:T(8,128)}, f32[4,256,256]{2,1,0:T(8,128)S(1)}, u32[]{:S(2)}) %copy-start.4) | copy-done | bytes 1048600
  15.9 1.0 %copy-done.6 = f32[4,256,256]{2,1,0:T(8,128)} copy-done((f32[4,256,256]{2,1,0:T(8,128)}, f32[4,256,256]{2,1,0:T(8,128)S(1)}, u32[]{:S(2)}) %copy-start.6) | copy-done | bytes 1048600
  20.6 1.3 %collective-permute-done.other_ref.refs_0_.refs_16_ = bf16[4,128,256]{2,1,0:T(8,128)(2,1)S(1)} collective-permute-done((bf16[4,128,256]{2,1,0:T(8,128)(2,1)}, bf16[4,128,256]{2,1,0:T(8,128)(2,1)S(1)}, u32[]{:S(2)}, u32[]{:S(2)}) %collective-permute-start) | collective-permute-done | bytes 262176 | tf_op jit(solution)/shard_map/ppermute | solution.py:740
  21.9 1.1 %join_half.1 = bf16[2,128,256]{2,1,0:T(8,128)(2,1)S(1)} custom-call(s32[2]{0:T(128)S(1)} %pad_add_fusion.place_ref, bf16[4,128,256]{2,1,0:T(8,128)(2,1)} %get-tuple-element.54.own_ref, bf16[4,128,256]{2,1,0:T(8,128)(2,1)S(1)} %collective-permute-done.other_ref.refs_0_.refs_16_), custom_call_target="tpu_custom_call" | custom-call | tf_op jit(solution)/shard_map/join_half/pallas_call | solution.py:89
  23.0 2.2 %collective-permute-start.3 = (bf16[2,128,256]{2,1,0:T(8,128)(2,1)S(1)}, bf16[2,128,256]{2,1,0:T(8,128)(2,1)S(1)}, u32[]{:S(2)}, u32[]{:S(2)}) collective-permute-start(bf16[2,128,256]{2,1,0:T(8,128)(2,1)S(1)} %join_half.1), channel_id=1, source_target_pairs={{0,24},{4,28},{8,16},{12,20},{16,8},{20,12},{24,0},{28,4},{1,25},{... | collective-permute-start | bytes 393224 | tf_op jit(solution)/shard_map/ppermute | solution.py:740
  25.7 2.3 %fusion.grad_ref = f32[256,512]{1,0:T(8,128)S(1)} fusion(bf16[256,2048]{1,0:T(8,128)(2,1)S(1)} %copy-done, bf16[512,2048]{1,0:T(8,128)(2,1)} %bitcast.11), kind=kOutput, calls=%fused_computation.3 | convolution fusion | flops 536870912 | bytes 3670016 | tf_op jit(solution)/shard_map/dot_general | solution.py:777
  28.1 1.6 %local_part.1 = (bf16[4,256,256]{2,1,0:T(8,128)(2,1)S(1)}, bf16[4,256,256]{2,1,0:T(8,128)(2,1)S(1)}, bf16[4,256,256]{2,1,0:T(8,128)(2,1)S(1)}, bf16[4,256,256]{2...) custom-call(f32[3,4,256,128]{3,2,1,0:T(8,128)S(1)} %get-tuple-elemen, ...), custom_call_target="tpu_custom_call" | custom-call | tf_op jit(solution)/shard_map/local_part/pallas_call | solution.py:89
  29.8 2.4 %collective-permute-done.2.refs_2_ = bf16[2,128,256]{2,1,0:T(8,128)(2,1)S(1)} collective-permute-done((bf16[2,128,256]{2,1,0:T(8,128)(2,1)S(1)}, bf16[2,128,256]{2,1,0:T(8,128)(2,1)S(1)}, u32[]{:S(2)}, u32[]{:S(2)}) %collective-permute-start.2) | collective-permute-done | bytes 131104 | tf_op jit(solution)/shard_map/ppermute | solution.py:740
  34.3 3.1 %reach.1 = (bf16[256,512]{1,0:T(8,128)(2,1)S(1)}, bf16[256,512]{1,0:T(8,128)(2,1)S(1)}, bf16[256,512]{1,0:T(8,128)(2,1)S(1)}, bf16[256,512]{1,0:T(8,128)(2,1)S(1...) custom-call(s32[2]{0:T(128)S(1)} %pad_add_fusion.place_ref, ...), custom_call_target="tpu_custom_call" | custom-call | tf_op jit(solution)/shard_map/reach/pallas_call | solution.py:89
  37.4 2.1 %return_states.1 = (f32[4,256,128]{2,1,0:T(8,128)S(1)}, bf16[4,128,256]{2,1,0:T(8,128)(2,1)S(1)}, bf16[4,128,256]{2,1,0:T(8,128)(2,1)S(1)}, bf16[4,128,128]{2,1,0:T(8,128)(2,1)S(1)}) custom-call(s32[2]{0:T(128)S(1)} %pad_add_fusion.place_ref, f32[256,128]{1,0:T(8,128)S(1)} %get-tuple-element.53.pack_ref.refs_1_.refs_2_, ...), custom_call_target="tpu_custom_call" | custom-call | tf_op jit(solution)/shard_map/return_states/pallas_call | solution.py:89
  40.4 1.3 %collective-permute-done.12.refs_3_ = bf16[4,128,128]{2,1,0:T(8,128)(2,1)S(1)} collective-permute-done((bf16[4,128,128]{2,1,0:T(8,128)(2,1)S(1)}, bf16[4,128,128]{2,1,0:T(8,128)(2,1)S(1)}, u32[]{:S(2)}, u32[]{:S(2)}) %collective-permute-start.12) | collective-permute-done | bytes 131104 | tf_op jit(solution)/shard_map/ppermute | solution.py:740
  41.8 1.4 %collective-permute-start.15 = (bf16[4,128,128]{2,1,0:T(8,128)(2,1)S(1)}, bf16[4,128,128]{2,1,0:T(8,128)(2,1)S(1)}, u32[]{:S(2)}, u32[]{:S(2)}) collective-permute-start(bf16[4,128,128]{2,1,0:T(8,128)(2,1)S(1)} %get-tuple-element.99), channel_id=1, source_target_pairs={{0,24},{4,28},{8,16},{12,20},{16,8},{20,12},{24,0},{28,4},{1,25},{... | collective-permute-start | bytes 393224 | tf_op jit(solution)/shard_map/ppermute | solution.py:740
  43.2 1.0 %collective-permute-start.13 = (bf16[4,128,256]{2,1,0:T(8,128)(2,1)S(1)}, bf16[4,128,256]{2,1,0:T(8,128)(2,1)S(1)}, u32[]{:S(2)}, u32[]{:S(2)}) collective-permute-start(bf16[4,128,256]{2,1,0:T(8,128)(2,1)S(1)} %get-tuple-element.98), channel_id=1, source_target_pairs={{0,8},{4,12},{8,0},{12,4},{16,24},{20,28},{24,16},{28,20},{1,9},{5... | collective-permute-start | bytes 786440 | tf_op jit(solution)/shard_map/ppermute | solution.py:740
  44.2 1.3 %collective-permute-start.7 = (bf16[256,512]{1,0:T(8,128)(2,1)S(1)}, bf16[256,512]{1,0:T(8,128)(2,1)S(1)}, u32[]{:S(2)}, u32[]{:S(2)}) collective-permute-start(bf16[256,512]{1,0:T(8,128)(2,1)S(1)} %get-tuple-element.68), channel_id=1, source_target_pairs={{0,1},{1,2},{2,3},{3,0},{4,5},{5,6},{6,7},{7,4},{8,9},{9,10},{10,1... | collective-permute-start | bytes 786440 | tf_op jit(solution)/shard_map/ppermute | solution.py:747
  45.5 1.1 %collective-permute-start.8 = (bf16[256,512]{1,0:T(8,128)(2,1)S(1)}, bf16[256,512]{1,0:T(8,128)(2,1)S(1)}, u32[]{:S(2)}, u32[]{:S(2)}) collective-permute-start(bf16[256,512]{1,0:T(8,128)(2,1)S(1)} %get-tuple-element.69), channel_id=1, source_target_pairs={{0,2},{1,3},{2,0},{3,1},{4,6},{5,7},{6,4},{7,5},{8,10},{9,11},{10,... | collective-permute-start | bytes 786440 | tf_op jit(solution)/shard_map/ppermute | solution.py:747
  46.5 1.5 %collective-permute-start.9 = (bf16[256,512]{1,0:T(8,128)(2,1)S(1)}, bf16[256,512]{1,0:T(8,128)(2,1)S(1)}, u32[]{:S(2)}, u32[]{:S(2)}) collective-permute-start(bf16[256,512]{1,0:T(8,128)(2,1)S(1)} %get-tuple-element.70), channel_id=1, source_target_pairs={{0,3},{1,0},{2,1},{3,2},{4,7},{5,4},{6,5},{7,6},{8,11},{9,8},{10,9... | collective-permute-start | bytes 786440 | tf_op jit(solution)/shard_map/ppermute | solution.py:747
  48.7 3.4 %pull_local.1 = (f32[3,4,256,128]{3,2,1,0:T(8,128)S(1)}, f32[4,256,128]{2,1,0:T(8,128)S(1)}, f32[256,128]{1,0:T(8,128)S(1)}, f32[8,256]{1,0:T(8,128)S(1)}) custom-call(f32[3,4,256,128]{3,2,1,0:T(8,128)S(1)} %get-tuple-element.55.qkv_ref.refs_0_, f32[256,128]{1,0:T(8,128)S(1)} %get-tuple-element.53.pack_ref.refs_1_.refs_2_, f32[128,256]{1,0:T(8,128)S(1)} %copy-done.10, ...), custom_call_target="tpu_custom_call" | custom-call | tf_op jit(solution)/shard_map/pull_local/pallas_call | solution.py:89
  52.1 1.0 %collective-permute-done.13.refs_20_ = bf16[4,128,256]{2,1,0:T(8,128)(2,1)S(1)} collective-permute-done((bf16[4,128,256]{2,1,0:T(8,128)(2,1)S(1)}, bf16[4,128,256]{2,1,0:T(8,128)(2,1)S(1)}, u32[]{:S(2)}, u32[]{:S(2)}) %collective-permute-start.13) | collective-permute-done | bytes 262176 | tf_op jit(solution)/shard_map/ppermute | solution.py:740
  53.1 7.3 %finish.1 = (bf16[256,512]{1,0:T(8,128)(2,1)S(1)}, bf16[256,512]{1,0:T(8,128)(2,1)S(1)}, bf16[256,512]{1,0:T(8,128)(2,1)S(1)}, bf16[256,512]{1,0:T(8,128)(2,1)S(1)}) custom-call(s32[2]{0:T(128)S(1)} %pad_add_fusion.place_ref, f32[3,4,256,128]{3,2,1,0:T(8,128)S(1)} %get-tuple-element.55.qkv_ref.refs_0_, f32[256,128]{1,0:T(8,128)S(1)} %copy-done.16, ...), custom_call_target="tpu_custom_call" | custom-call | tf_op jit(solution)/shard_map/finish/pallas_call | solution.py:89
  60.4 1.3 %collective-permute-start.16 = (bf16[256,512]{1,0:T(8,128)(2,1)S(1)}, bf16[256,512]{1,0:T(8,128)(2,1)S(1)}, u32[]{:S(2)}, u32[]{:S(2)}) collective-permute-start(bf16[256,512]{1,0:T(8,128)(2,1)S(1)} %get-tuple-element.101), channel_id=1, source_target_pairs={{0,1},{1,2},{2,3},{3,0},{4,5},{5,6},{6,7},{7,4},{8,9},{9,10},{10,1... | collective-permute-start | bytes 786440 | tf_op jit(solution)/shard_map/ppermute | solution.py:747
  61.7 1.1 %collective-permute-start.17 = (bf16[256,512]{1,0:T(8,128)(2,1)S(1)}, bf16[256,512]{1,0:T(8,128)(2,1)S(1)}, u32[]{:S(2)}, u32[]{:S(2)}) collective-permute-start(bf16[256,512]{1,0:T(8,128)(2,1)S(1)} %get-tuple-element.102), channel_id=1, source_target_pairs={{0,2},{1,3},{2,0},{3,1},{4,6},{5,7},{6,4},{7,5},{8,10},{9,11},{10,... | collective-permute-start | bytes 786440 | tf_op jit(solution)/shard_map/ppermute | solution.py:747
  62.9 1.4 %collective-permute-start.18 = (bf16[256,512]{1,0:T(8,128)(2,1)S(1)}, bf16[256,512]{1,0:T(8,128)(2,1)S(1)}, u32[]{:S(2)}, u32[]{:S(2)}) collective-permute-start(bf16[256,512]{1,0:T(8,128)(2,1)S(1)} %get-tuple-element.103), channel_id=1, source_target_pairs={{0,3},{1,0},{2,1},{3,2},{4,7},{5,4},{6,5},{7,6},{8,11},{9,8},{10,9... | collective-permute-start | bytes 786440 | tf_op jit(solution)/shard_map/ppermute | solution.py:747
  64.3 2.8 %collective-permute-done.8 = bf16[256,512]{1,0:T(8,128)(2,1)S(1)} collective-permute-done((bf16[256,512]{1,0:T(8,128)(2,1)S(1)}, bf16[256,512]{1,0:T(8,128)(2,1)S(1)}, u32[]{:S(2)}, u32[]{:S(2)}) %collective-permute-start.8) | collective-permute-done | bytes 262176 | tf_op jit(solution)/shard_map/ppermute | solution.py:747
  67.0 14.4 %collective-permute-done.9 = bf16[256,512]{1,0:T(8,128)(2,1)S(1)} collective-permute-done((bf16[256,512]{1,0:T(8,128)(2,1)S(1)}, bf16[256,512]{1,0:T(8,128)(2,1)S(1)}, u32[]{:S(2)}, u32[]{:S(2)}) %collective-permute-start.9) | collective-permute-done | bytes 262176 | tf_op jit(solution)/shard_map/ppermute | solution.py:747
  81.4 0.8 add_convert_fusion.1
  82.2 1.6 %collective-permute-done.16 = bf16[256,512]{1,0:T(8,128)(2,1)S(1)} collective-permute-done((bf16[256,512]{1,0:T(8,128)(2,1)S(1)}, bf16[256,512]{1,0:T(8,128)(2,1)S(1)}, u32[]{:S(2)}, u32[]{:S(2)}) %collective-permute-start.16) | collective-permute-done | bytes 262176 | tf_op jit(solution)/shard_map/ppermute | solution.py:747
  83.9 5.6 %collective-permute-done.17 = bf16[256,512]{1,0:T(8,128)(2,1)S(1)} collective-permute-done((bf16[256,512]{1,0:T(8,128)(2,1)S(1)}, bf16[256,512]{1,0:T(8,128)(2,1)S(1)}, u32[]{:S(2)}, u32[]{:S(2)}) %collective-permute-start.17) | collective-permute-done | bytes 262176 | tf_op jit(solution)/shard_map/ppermute | solution.py:747
  89.5 3.1 %collective-permute-done.18 = bf16[256,512]{1,0:T(8,128)(2,1)S(1)} collective-permute-done((bf16[256,512]{1,0:T(8,128)(2,1)S(1)}, bf16[256,512]{1,0:T(8,128)(2,1)S(1)}, u32[]{:S(2)}, u32[]{:S(2)}) %collective-permute-start.18) | collective-permute-done | bytes 262176 | tf_op jit(solution)/shard_map/ppermute | solution.py:747
  92.6 0.8 add_convert_fusion
  (59 shorter events, 8.0 us)
Async XLA Ops:
  0.6 25.1 %copy-start = (bf16[256,2048]{1,0:T(8,128)(2,1)S(1)}, bf16[256,2048]{1,0:T(8,128)(2,1)}, u32[]{:S(2)}) copy-start(bf16[256,2048]{1,0:T(8,128)(2,1)} %param.13) | copy-start | bytes 3145732
  12.2 2.7 %copy-start.3 = (bf16[2048,1536]{1,0:T(8,128)(2,1)}, bf16[2048,1536]{1,0:T(8,128)(2,1)S(1)}, u32[]{:S(2)}) copy-start(bf16[2048,1536]{1,0:T(8,128)(2,1)S(1)} %get-tuple-element.94.refs_15_) | copy-start | bytes 18874372
  19.8 2.0 %collective-permute-start = (bf16[4,128,256]{2,1,0:T(8,128)(2,1)}, bf16[4,128,256]{2,1,0:T(8,128)(2,1)S(1)}, u32[]{:S(2)}, u32[]{:S(2)}) collective-permute-start(bf16[4,128,256]{2,1,0:T(8,128)(2,1)} %get-tuple-element.54.own_ref), channel_id=1, source_target_pairs={{0,4},{4,0},{8,12},{12,8},{16,20},{20,16},{24,28},{28,24},{1,5},{5... | collective-permute-start | bytes 786440 | tf_op jit(solution)/shard_map/ppermute | solution.py:740
  20.6 7.5 %copy-start.2 = (f32[4,256,256]{2,1,0:T(8,128)S(1)}, f32[4,256,256]{2,1,0:T(8,128)}, u32[]{:S(2)}) copy-start(f32[4,256,256]{2,1,0:T(8,128)} %copy-done.1) | copy-start | bytes 3145732
  20.6 7.5 %copy-start.10 = (f32[128,256]{1,0:T(8,128)S(1)}, f32[128,256]{1,0:T(8,128)}, u32[]{:S(2)}) copy-start(f32[128,256]{1,0:T(8,128)} %copy-done.9) | copy-start | bytes 393220
  20.6 7.5 %copy-start.14 = (f32[4,128,256]{2,1,0:T(8,128)S(1)}, f32[4,128,256]{2,1,0:T(8,128)}, u32[]{:S(2)}) copy-start(f32[4,128,256]{2,1,0:T(8,128)} %copy-done.13) | copy-start | bytes 1572868
  23.0 6.8 %collective-permute-start.3 = (bf16[2,128,256]{2,1,0:T(8,128)(2,1)S(1)}, bf16[2,128,256]{2,1,0:T(8,128)(2,1)S(1)}, u32[]{:S(2)}, u32[]{:S(2)}) collective-permute-start(bf16[2,128,256]{2,1,0:T(8,128)(2,1)S(1)} %join_half.1), channel_id=1, source_target_pairs={{0,24},{4,28},{8,16},{12,20},{16,8},{20,12},{24,0},{28,4},{1,25},{... | collective-permute-start | bytes 393224 | tf_op jit(solution)/shard_map/ppermute | solution.py:740
  25.2 7.0 %collective-permute-start.2 = (bf16[2,128,256]{2,1,0:T(8,128)(2,1)S(1)}, bf16[2,128,256]{2,1,0:T(8,128)(2,1)S(1)}, u32[]{:S(2)}, u32[]{:S(2)}) collective-permute-start(bf16[2,128,256]{2,1,0:T(8,128)(2,1)S(1)} %join_half.1), channel_id=1, source_target_pairs={{0,16},{4,20},{8,24},{12,28},{16,0},{20,4},{24,8},{28,12},{1,17},{... | collective-permute-start | bytes 393224 | tf_op jit(solution)/shard_map/ppermute | solution.py:740
  25.5 6.7 %collective-permute-start.1 = (bf16[2,128,256]{2,1,0:T(8,128)(2,1)S(1)}, bf16[2,128,256]{2,1,0:T(8,128)(2,1)S(1)}, u32[]{:S(2)}, u32[]{:S(2)}) collective-permute-start(bf16[2,128,256]{2,1,0:T(8,128)(2,1)S(1)} %join_half.1), channel_id=1, source_target_pairs={{0,8},{4,12},{8,0},{12,4},{16,24},{20,28},{24,16},{28,20},{1,9},{5... | collective-permute-start | bytes 393224 | tf_op jit(solution)/shard_map/ppermute | solution.py:740
  28.1 6.3 %copy-start.8 = (bf16[4,128,2048]{2,1,0:T(8,128)(2,1)S(1)}, bf16[4,128,2048]{2,1,0:T(8,128)(2,1)}, u32[]{:S(2)}) copy-start(bf16[4,128,2048]{2,1,0:T(8,128)(2,1)} %param.12) | copy-start | bytes 6291460
  28.1 6.2 %copy-start.17 = (f32[128]{0:T(128)S(1)}, f32[128]{0:T(128)}, u32[]{:S(2)}) copy-start(f32[128]{0:T(128)} %param.11) | copy-start | bytes 1540
  32.2 1.6 %collective-permute-start.4 = (bf16[2,128,256]{2,1,0:T(8,128)(2,1)S(1)}, bf16[2,128,256]{2,1,0:T(8,128)(2,1)S(1)}, u32[]{:S(2)}, u32[]{:S(2)}) collective-permute-start(bf16[2,128,256]{2,1,0:T(8,128)(2,1)S(1)} %collective-permute-done.1.refs_1_), channel_id=1, source_target_pairs={{0,4},{4,0},{8,12},{12,8},{16,20},{20,16},{24,28},{28,24},{1,5},{5... | collective-permute-start | bytes 393224 | tf_op jit(solution)/shard_map/ppermute | solution.py:740
  32.8 1.3 %collective-permute-start.5 = (bf16[2,128,256]{2,1,0:T(8,128)(2,1)S(1)}, bf16[2,128,256]{2,1,0:T(8,128)(2,1)S(1)}, u32[]{:S(2)}, u32[]{:S(2)}) collective-permute-start(bf16[2,128,256]{2,1,0:T(8,128)(2,1)S(1)} %collective-permute-done.2.refs_2_), channel_id=1, source_target_pairs={{0,4},{4,0},{8,12},{12,8},{16,20},{20,16},{24,28},{28,24},{1,5},{5... | collective-permute-start | bytes 393224 | tf_op jit(solution)/shard_map/ppermute | solution.py:740
  32.8 1.5 %collective-permute-start.6 = (bf16[2,128,256]{2,1,0:T(8,128)(2,1)S(1)}, bf16[2,128,256]{2,1,0:T(8,128)(2,1)S(1)}, u32[]{:S(2)}, u32[]{:S(2)}) collective-permute-start(bf16[2,128,256]{2,1,0:T(8,128)(2,1)S(1)} %collective-permute-done.3.refs_3_), channel_id=1, source_target_pairs={{0,4},{4,0},{8,12},{12,8},{16,20},{20,16},{24,28},{28,24},{1,5},{5... | collective-permute-start | bytes 393224 | tf_op jit(solution)/shard_map/ppermute | solution.py:740
  37.4 11.3 %copy-start.5 = (f32[4,256,256]{2,1,0:T(8,128)S(1)}, f32[4,256,256]{2,1,0:T(8,128)}, u32[]{:S(2)}) copy-start(f32[4,256,256]{2,1,0:T(8,128)} %copy-done.4) | copy-start | bytes 3145732
  37.4 11.3 %copy-start.7 = (f32[4,256,256]{2,1,0:T(8,128)S(1)}, f32[4,256,256]{2,1,0:T(8,128)}, u32[]{:S(2)}) copy-start(f32[4,256,256]{2,1,0:T(8,128)} %copy-done.6) | copy-start | bytes 3145732
  37.4 15.7 %slice-start = ((s8[6291456]{0:T(1024)(128)(4,1)}), s8[4194304]{0:T(1024)(128)(4,1)S(1)}, s32[]{:S(2)}) async-start(s8[6291456]{0:T(1024)(128)(4,1)} %bitcast.9), calls=%async_computation | async-start | bytes 8388608
  39.5 2.2 %collective-permute-start.11 = (bf16[4,128,256]{2,1,0:T(8,128)(2,1)S(1)}, bf16[4,128,256]{2,1,0:T(8,128)(2,1)S(1)}, u32[]{:S(2)}, u32[]{:S(2)}) collective-permute-start(bf16[4,128,256]{2,1,0:T(8,128)(2,1)S(1)} %get-tuple-element.96.refs_0_), channel_id=1, source_target_pairs={{0,4},{4,0},{8,12},{12,8},{16,20},{20,16},{24,28},{28,24},{1,5},{5... | collective-permute-start | bytes 786440 | tf_op jit(solution)/shard_map/ppermute | solution.py:740
  39.9 6.6 %collective-permute-start.10 = (bf16[4,128,256]{2,1,0:T(8,128)(2,1)S(1)}, bf16[4,128,256]{2,1,0:T(8,128)(2,1)S(1)}, u32[]{:S(2)}, u32[]{:S(2)}) collective-permute-start(bf16[4,128,256]{2,1,0:T(8,128)(2,1)S(1)} %get-tuple-element.95), channel_id=1, source_target_pairs={{0,4},{4,0},{8,12},{12,8},{16,20},{20,16},{24,28},{28,24},{1,5},{5... | collective-permute-start | bytes 786440 | tf_op jit(solution)/shard_map/ppermute | solution.py:740
  40.1 1.6 %collective-permute-start.12 = (bf16[4,128,128]{2,1,0:T(8,128)(2,1)S(1)}, bf16[4,128,128]{2,1,0:T(8,128)(2,1)S(1)}, u32[]{:S(2)}, u32[]{:S(2)}) collective-permute-start(bf16[4,128,128]{2,1,0:T(8,128)(2,1)S(1)} %get-tuple-element.97.refs_1_), channel_id=1, source_target_pairs={{0,4},{4,0},{8,12},{12,8},{16,20},{20,16},{24,28},{28,24},{1,5},{5... | collective-permute-start | bytes 393224 | tf_op jit(solution)/shard_map/ppermute | solution.py:740
  41.8 6.2 %collective-permute-start.15 = (bf16[4,128,128]{2,1,0:T(8,128)(2,1)S(1)}, bf16[4,128,128]{2,1,0:T(8,128)(2,1)S(1)}, u32[]{:S(2)}, u32[]{:S(2)}) collective-permute-start(bf16[4,128,128]{2,1,0:T(8,128)(2,1)S(1)} %get-tuple-element.99), channel_id=1, source_target_pairs={{0,24},{4,28},{8,16},{12,20},{16,8},{20,12},{24,0},{28,4},{1,25},{... | collective-permute-start | bytes 393224 | tf_op jit(solution)/shard_map/ppermute | solution.py:740
  43.2 9.9 %collective-permute-start.13 = (bf16[4,128,256]{2,1,0:T(8,128)(2,1)S(1)}, bf16[4,128,256]{2,1,0:T(8,128)(2,1)S(1)}, u32[]{:S(2)}, u32[]{:S(2)}) collective-permute-start(bf16[4,128,256]{2,1,0:T(8,128)(2,1)S(1)} %get-tuple-element.98), channel_id=1, source_target_pairs={{0,8},{4,12},{8,0},{12,4},{16,24},{20,28},{24,16},{28,20},{1,9},{5... | collective-permute-start | bytes 786440 | tf_op jit(solution)/shard_map/ppermute | solution.py:740
  44.2 18.7 %collective-permute-start.7 = (bf16[256,512]{1,0:T(8,128)(2,1)S(1)}, bf16[256,512]{1,0:T(8,128)(2,1)S(1)}, u32[]{:S(2)}, u32[]{:S(2)}) collective-permute-start(bf16[256,512]{1,0:T(8,128)(2,1)S(1)} %get-tuple-element.68), channel_id=1, source_target_pairs={{0,1},{1,2},{2,3},{3,0},{4,5},{5,6},{6,7},{7,4},{8,9},{9,10},{10,1... | collective-permute-start | bytes 786440 | tf_op jit(solution)/shard_map/ppermute | solution.py:747
  45.5 21.6 %collective-permute-start.8 = (bf16[256,512]{1,0:T(8,128)(2,1)S(1)}, bf16[256,512]{1,0:T(8,128)(2,1)S(1)}, u32[]{:S(2)}, u32[]{:S(2)}) collective-permute-start(bf16[256,512]{1,0:T(8,128)(2,1)S(1)} %get-tuple-element.69), channel_id=1, source_target_pairs={{0,2},{1,3},{2,0},{3,1},{4,6},{5,7},{6,4},{7,5},{8,10},{9,11},{10,... | collective-permute-start | bytes 786440 | tf_op jit(solution)/shard_map/ppermute | solution.py:747
  46.5 34.9 %collective-permute-start.9 = (bf16[256,512]{1,0:T(8,128)(2,1)S(1)}, bf16[256,512]{1,0:T(8,128)(2,1)S(1)}, u32[]{:S(2)}, u32[]{:S(2)}) collective-permute-start(bf16[256,512]{1,0:T(8,128)(2,1)S(1)} %get-tuple-element.70), channel_id=1, source_target_pairs={{0,3},{1,0},{2,1},{3,2},{4,7},{5,4},{6,5},{7,6},{8,11},{9,8},{10,9... | collective-permute-start | bytes 786440 | tf_op jit(solution)/shard_map/ppermute | solution.py:747
  48.0 4.2 %collective-permute-start.14 = (bf16[4,128,128]{2,1,0:T(8,128)(2,1)S(1)}, bf16[4,128,128]{2,1,0:T(8,128)(2,1)S(1)}, u32[]{:S(2)}, u32[]{:S(2)}) collective-permute-start(bf16[4,128,128]{2,1,0:T(8,128)(2,1)S(1)} %get-tuple-element.99), channel_id=1, source_target_pairs={{0,16},{4,20},{8,24},{12,28},{16,0},{20,4},{24,8},{28,12},{1,17},{... | collective-permute-start | bytes 393224 | tf_op jit(solution)/shard_map/ppermute | solution.py:740
  48.7 4.4 %slice-start.1 = ((s8[6291456]{0:T(1024)(128)(4,1)}), s8[2097152]{0:T(1024)(128)(4,1)S(1)}, s32[]{:S(2)}) async-start(s8[6291456]{0:T(1024)(128)(4,1)} %bitcast.9), calls=%async_computation.1 | async-start | bytes 4194304
  48.7 4.4 %copy-start.12 = (bf16[128,2048]{1,0:T(8,128)(2,1)S(1)}, bf16[128,2048]{1,0:T(8,128)(2,1)}, u32[]{:S(2)}) copy-start(bf16[128,2048]{1,0:T(8,128)(2,1)} %copy-done.11) | copy-start | bytes 1572868
  48.7 4.4 %copy-start.16 = (f32[256,128]{1,0:T(8,128)S(1)}, f32[256,128]{1,0:T(8,128)}, u32[]{:S(2)}) copy-start(f32[256,128]{1,0:T(8,128)} %copy-done.15) | copy-start | bytes 393220
  60.4 23.5 %collective-permute-start.16 = (bf16[256,512]{1,0:T(8,128)(2,1)S(1)}, bf16[256,512]{1,0:T(8,128)(2,1)S(1)}, u32[]{:S(2)}, u32[]{:S(2)}) collective-permute-start(bf16[256,512]{1,0:T(8,128)(2,1)S(1)} %get-tuple-element.101), channel_id=1, source_target_pairs={{0,1},{1,2},{2,3},{3,0},{4,5},{5,6},{6,7},{7,4},{8,9},{9,10},{10,1... | collective-permute-start | bytes 786440 | tf_op jit(solution)/shard_map/ppermute | solution.py:747
  61.7 27.8 %collective-permute-start.17 = (bf16[256,512]{1,0:T(8,128)(2,1)S(1)}, bf16[256,512]{1,0:T(8,128)(2,1)S(1)}, u32[]{:S(2)}, u32[]{:S(2)}) collective-permute-start(bf16[256,512]{1,0:T(8,128)(2,1)S(1)} %get-tuple-element.102), channel_id=1, source_target_pairs={{0,2},{1,3},{2,0},{3,1},{4,6},{5,7},{6,4},{7,5},{8,10},{9,11},{10,... | collective-permute-start | bytes 786440 | tf_op jit(solution)/shard_map/ppermute | solution.py:747
  62.9 29.8 %collective-permute-start.18 = (bf16[256,512]{1,0:T(8,128)(2,1)S(1)}, bf16[256,512]{1,0:T(8,128)(2,1)S(1)}, u32[]{:S(2)}, u32[]{:S(2)}) collective-permute-start(bf16[256,512]{1,0:T(8,128)(2,1)S(1)} %get-tuple-element.103), channel_id=1, source_target_pairs={{0,3},{1,0},{2,1},{3,2},{4,7},{5,4},{6,5},{7,6},{8,11},{9,8},{10,9... | collective-permute-start | bytes 786440 | tf_op jit(solution)/shard_map/ppermute | solution.py:747
  (7 other events, 5.9 us)

commit v4 on v3

--- a/solution.py
+++ b/solution.py
@@ -122,7 +122,7 @@
     return rate, bias
 
 
-def project_body(sizes, hp_hbm, tokens_hbm, w_hbm, small_hbm, *refs):
+def project_body(sizes, place_ref, hp_hbm, tokens_hbm, w_hbm, small_hbm, *refs):
     heads, levels, chunks = sizes
     (wr_ref, small_ref, qkv_ref, gate_ref, pack_ref, pack_t_ref, trans_ref, mixed_t_ref,
      decay_ref, base_ref, lower_ref, rates_ref, pair_ref) = refs[:13]
@@ -249,7 +249,7 @@
         pair_ref[head, :, LANES:] = pair[:, LANES:].astype(BF16)
 
 
-def project(tokens, flat_w, small, head_param, heads, levels):
+def project(place, tokens, flat_w, small, head_param, heads, levels):
     rows, width = tokens.shape
     chunks = 8
     cols = 3 * heads
@@ -283,14 +283,17 @@
     ]
     return local_call(
         functools.partial(project_body, (heads, levels, chunks)), "project", 22, out_shape,
-        [], [], scratch, [head_param, tokens, flat_w, small],
-    )
-
-
-def local_body(sizes, qkv_ref, pack_ref, pack_t_ref, trans_ref, mixed_t_ref, decay_ref, *outs):
+        [place], [], scratch, [head_param, tokens, flat_w, small],
+    )
+
+
+def local_body(
+    sizes, qkv_ref, pack_ref, pack_t_ref, trans_ref, mixed_t_ref, decay_ref, grad_ref, weight_ref, *outs
+):
     heads, levels, bits = sizes
     (attn_ref, attn_t_ref, prod_t_ref, scores_ref, mix_ref, mixed_ref, local_ref, hat_ref,
-     hat_t_ref) = outs
+     hat_t_ref, grad_normed_ref) = outs
+    grad_normed_ref[...] = mm_nt(grad_ref[...], weight_ref[...])
     rows = pack_ref.shape[0]
     decay_col = levels * heads
     beta_col = decay_col + heads
@@ -317,8 +320,8 @@
         hat_t_ref[head] = hat.T.astype(BF16)
 
 
-def local_part(qkv, pack, pack_t, trans, mixed_t, decay, levels, bits):
-    heads, rows, key = qkv.shape[1:]
+def local_part(arrays, levels, bits):
+    heads, rows, key = arrays[0].shape[1:]
     square = (heads, rows, rows)
     out_shape = (
         kept(square, BF16),
@@ -330,10 +333,11 @@
         kept((heads, rows, key), F32),
         kept((heads, rows, key), BF16),
         kept((heads, key, rows), BF16),
+        kept((rows, heads * key), F32),
     )
     return local_call(
         functools.partial(local_body, (heads, levels, bits)), "local_part", 10, out_shape,
-        [], [qkv, pack, pack_t, trans, mixed_t, decay],
+        [], arrays,
     )
 
 
@@ -373,13 +377,12 @@
 def reach_body(
     sizes, place_ref, gain_ref, pack_ref, local_ref, hat_ref, grad_ref, weight_ref, *refs
 ):
-    heads, bits, far, count, near_count = sizes
+    heads, bits, far, near_count = sizes
     first_ref = refs[0]
     near = [None] + [(refs[1 + at], refs[1 + near_count + at]) for at in range(near_count)]
     refs = refs[2 * near_count + 1 :]
-    out_refs = refs[:count]
-    dout_ref, found_ref, prefix_ref, dfar_ref = refs[count : count + 4]
-    nodes = refs[count + 4 : -1]
+    out_ref, dout_ref, found_ref, prefix_ref, dfar_ref = refs[:5]
+    nodes = refs[5:-1]
     normed_ref = refs[-1]
     rows = pack_ref.shape[0]
     key = hat_ref.shape[2]
@@ -430,20 +433,17 @@
             col = (bits + 1 + bit) * heads + head
             dfar = jnp.where(lane == col, row_sum(dout * parts[bit]), dfar)
     dfar_ref[...] = dfar
-    size = out_refs[0].shape[1]
-    for shift in range(count):
-        dest = lax.rem(place_ref[1] + shift, count)
-        cols = pl.ds(pl.multiple_of(dest * size, size), size)
-        out_refs[shift][...] = jnp.dot(
-            normed_ref[...], weight_ref[:, cols], preferred_element_type=F32
-        ).astype(BF16)
-
-
-def reach(place, arrays, first, near, bits, far, count):
+    out_ref[...] = jnp.dot(
+        normed_ref[...], weight_ref[...], preferred_element_type=F32
+    ).astype(BF16)
+
+
+def reach(place, arrays, first, near, bits, far):
     gain, pack, local_out, hat, grad_normed, weight = arrays
     heads, rows, key = hat.shape
     nodes = tuple(kept(first.shape, BF16) for bit in range(1, far))
-    out_shape = (kept((rows, weight.shape[1] // count), BF16),) * count + (
+    out_shape = (
+        jax.ShapeDtypeStruct((rows, weight.shape[1]), BF16),
         kept((heads, rows, key), F32),
         kept((heads, key, far * key), BF16),
         kept((heads, far, key, key), BF16),
@@ -451,11 +451,10 @@
     ) + nodes
     mine, theirs = near
     got = local_call(
-        functools.partial(reach_body, (heads, bits, far, count, len(mine))), "reach", 10, out_shape,
+        functools.partial(reach_body, (heads, bits, far, len(mine))), "reach", 10, out_shape,
         [place], [*arrays, first, *mine, *theirs], [pltpu.VMEM((rows, heads * key), BF16)],
     )
-    parts, got = got[:count], got[count:]
-    return parts, got[:4], got[4:]
+    return got[:5], got[5:]
 
 
 def return_body(sizes, place_ref, pack_ref, hat_t_ref, dout_ref, found_ref, prefix_ref, *refs):
@@ -620,8 +619,7 @@
     for found in arrived_counts:
         arrived.append(refs[:found])
         refs = refs[found:]
-    out_refs = refs[:count]
-    (dproj,) = refs[count:]
+    out_ref, dproj = refs
     rows = pack_ref.shape[0]
     key = qkv_ref.shape[3]
     decay_col = levels * heads
@@ -713,12 +711,11 @@
         jnp.where(lane < beta_col, -rate * dlog * slope, dcol * slope),
     )
     dgate = jnp.where(lane < norm_col, dgate, 0.0).astype(BF16)
-    size = out_refs[0].shape[1]
-    for shift in range(count):
-        dest = lax.rem(place_ref[1] + shift, count)
-        span = pl.ds(pl.multiple_of(dest * size, size), size)
+    size = out_ref.shape[2]
+    for dest in range(count):
+        span = slice(dest * size, (dest + 1) * size)
         part = mm_nt(dproj[...], wr_ref[span, :]) + mm(dgate, small_ref[:, span])
-        out_refs[shift][...] = part.astype(BF16)
+        out_ref[dest] = part.astype(BF16)
 
 
 def finish(place, arrays, others, arrived, levels, count):
@@ -730,9 +727,9 @@
     flat = [value for group in arrived for value in group]
     return local_call(
         functools.partial(finish_body, (heads, levels, far, count, counts)), "finish", 12,
-        [kept((rows, width // count), BF16)] * count,
+        [kept((count, rows, width // count), BF16)],
         [place], [*arrays, *others, *flat], [pltpu.VMEM((rows, cols), BF16)],
-    )
+    )[0]
 
 
 def swap(value, axis, mask):
@@ -740,13 +737,17 @@
     return lax.ppermute(value, axis, [(at, at ^ mask) for at in range(size)])
 
 
+def sum_body(parts_ref, out_ref):
+    total = parts_ref[0].astype(F32)
+    for at in range(1, parts_ref.shape[0]):
+        total = total + parts_ref[at].astype(F32)
+    out_ref[...] = total.astype(BF16)
+
+
 def scatter_sum(parts, axis):
-    count = lax.axis_size(axis)
-    total = parts[0].astype(F32)
-    for shift in range(1, count):
-        got = lax.ppermute(parts[shift], axis, [(at, (at + shift) % count) for at in range(count)])
-        total = total + got.astype(F32)
-    return total.astype(BF16)
+    parts = lax.all_to_all(parts, axis, 0, 0)
+    out_shape = [jax.ShapeDtypeStruct(parts.shape[1:], BF16)]
+    return local_call(sum_body, "scatter_sum", 6, out_shape, [], [parts])[0]
 
 
 def on_device(tokens, qkv_weight, small_weight, head_param, norm_gain, out_weight, grad_out):
@@ -766,24 +767,21 @@
 
     (wr, small_t, qkv, gate, pack, pack_t, trans, mixed_t, decay, base, lower, rates_row,
      pair) = project(
-        tokens, flat_w, small, rates, heads, levels
+        place, tokens, flat_w, small, rates, heads, levels
     )
     first = swap(pair, "ctx", 1)
     node = join_half(place, pair, first)
     mine = [swap(node, "ctx", 2 * at) for at in range(1, size // 2)]
-    (attn, attn_t, prod_t, scores, mix, mixed, local_out, hat, hat_t) = local_part(
-        qkv, pack, pack_t, trans, mixed_t, decay, levels, bits
-    )
-    grad_normed = lax.dot_general(
-        grad_out, flat_out, (((1,), (1,)), ((), ())), preferred_element_type=F32
+    (attn, attn_t, prod_t, scores, mix, mixed, local_out, hat, hat_t, grad_normed) = local_part(
+        [qkv, pack, pack_t, trans, mixed_t, decay, grad_out, flat_out], levels, bits
     )
     mine, local_out, grad_normed = lax.optimization_barrier((mine, local_out, grad_normed))
     theirs = [swap(value, "ctx", 1) for value in mine]
-    out_parts, (dout, found, prefix, dfar), nodes = reach(
+    (out_part, dout, found, prefix, dfar), nodes = reach(
         place, [gain, pack, local_out, hat, grad_normed, flat_out], first, (mine, theirs),
-        bits, far, count
-    )
-    layer_out = scatter_sum(out_parts, "head")
+        bits, far
+    )
+    layer_out = lax.psum_scatter(out_part, "head", scatter_dimension=1, tiled=True)
     others = [first, *nodes]
     dhat, sends = return_states(place, pack, hat_t, dout, found, prefix, others, bits)
     got = [swap(value, "ctx", 1) for value in sends]

time: 93.6 us -> 114 us (1.22)
  the two profiles are of different devices: /device:TPU:9 before, /device:TPU:0 now
where the time goes in v4:
time: 114 us
  Pallas kernels  32.3 us (28%)
  blocking collectives  30.1 us (26%)
  local copies, waits for them, and re-layouts  22.7 us (20%)
  between operations  14.4 us (13%)
  starting transfers between devices  9.91 us (9%)
  waiting for transfers between devices  4.35 us (4%)
    pallas_call x9, Pallas kernels, local_call(): pl.pallas_call(body, out_shape=tuple(out_shape), in_specs=[SCALARS] * len...  32.3 us
    all_to_all x1, blocking collectives, scatter_sum(): parts = lax.all_to_all(parts, axis, 0, 0)  30.1 us
    unnamed x86, local copies, waits for them, and re-layouts  22.7 us
    ppermute x13, starting transfers between devices, swap(): return lax.ppermute(value, axis, [(at, at ^ mask) for at in range(size)])  9.87 us
    ppermute x13, waiting for transfers between devices, swap(): return lax.ppermute(value, axis, [(at, at ^ mask) for at in range(size)])  4.33 us
  transfers between devices with their start and end apart: 14, of which 7 were waited for; matrix products, arithmetic and copies ran while one was open for 0% of the time, Pallas kernels for 13%

profile of v4, /device:TPU:0, one launch (start us, length us, event | category | flops | bytes accessed | tf_op | source)
XLA Modules:
  0.0 113.8 jit_solution(4681774069603363531)
XLA Ops:
  7.3 10.7 %project.1 = (bf16[2048,1536]{1,0:T(8,128)(2,1)S(1)}, bf16[128,2048]{1,0:T(8,128)(2,1)S(1)}, f32[3,4,256,128]{3,2,1,0:T(8,128)S(1)}, f32[256,128]{1,0:T(8,128)S(...) custom-call(s32[2]{0:T(128)S(1)} %pad_add_fusion.place_ref, ...), custom_call_target="tpu_custom_call" | custom-call | tf_op jit(solution)/shard_map/project/pallas_call | solution.py:89
  18.1 1.0 copy-done.6
  20.4 1.2 %collective-permute-done.other_ref.refs_0_.refs_16_ = bf16[4,128,256]{2,1,0:T(8,128)(2,1)S(1)} collective-permute-done((bf16[4,128,256]{2,1,0:T(8,128)(2,1)S(1)}, bf16[4,128,256]{2,1,0:T(8,128)(2,1)S(1)}, u32[]{:S(2)}, u32[]{:S(2)}) %collective-permute-start) | collective-permute-done | bytes 262176 | tf_op jit(solution)/shard_map/ppermute | solution.py:737
  22.2 3.9 %collective-permute-start.3 = (bf16[2,128,256]{2,1,0:T(8,128)(2,1)S(1)}, bf16[2,128,256]{2,1,0:T(8,128)(2,1)S(1)}, u32[]{:S(2)}, u32[]{:S(2)}) collective-permute-start(bf16[2,128,256]{2,1,0:T(8,128)(2,1)S(1)} %join_half.1), channel_id=1, source_target_pairs={{0,24},{4,28},{8,16},{12,20},{16,8},{20,12},{24,0},{28,4},{1,25},{... | collective-permute-start | bytes 393224 | tf_op jit(solution)/shard_map/ppermute | solution.py:737
  26.8 2.2 %local_part.1 = (bf16[4,256,256]{2,1,0:T(8,128)(2,1)S(1)}, bf16[4,256,256]{2,1,0:T(8,128)(2,1)S(1)}, bf16[4,256,256]{2,1,0:T(8,128)(2,1)S(1)}, bf16[4,256,256]{2...) custom-call(f32[3,4,256,128]{3,2,1,0:T(8,128)S(1)} %get-tuple-elemen, ...), custom_call_target="tpu_custom_call" | custom-call | tf_op jit(solution)/shard_map/local_part/pallas_call | solution.py:89
  29.0 0.8 copy-done.23
  29.9 0.8 copy-done.25
  30.7 0.9 copy-done.27
  33.5 0.8 collective-permute-done.4.refs_4_
  34.9 2.9 %reach.1 = (bf16[256,2048]{1,0:T(8,128)(2,1)S(1)}, f32[4,256,128]{2,1,0:T(8,128)S(1)}, bf16[4,128,384]{2,1,0:T(8,128)(2,1)S(1)}, bf16[4,3,128,128]{3,2,1,0:T(8,1...) custom-call(s32[2]{0:T(128)S(1)} %pad_add_fusion.place_ref, ...), custom_call_target="tpu_custom_call" | custom-call | tf_op jit(solution)/shard_map/reach/pallas_call | solution.py:89
  37.8 2.8 %return_states.1 = (f32[4,256,128]{2,1,0:T(8,128)S(1)}, bf16[4,128,256]{2,1,0:T(8,128)(2,1)S(1)}, bf16[4,128,256]{2,1,0:T(8,128)(2,1)}, bf16[4,128,128]{2,1,0:T(8,128)(2,1)S(1)}) custom-call(s32[2]{0:T(128)S(1)} %pad_add_fusion.place_ref, f32[256,128]{1,0:T(8,128)S(1)} %get-tuple-element.47.pack_ref.refs_1_.refs_2_, ...), custom_call_target="tpu_custom_call" | custom-call | tf_op jit(solution)/shard_map/return_states/pallas_call | solution.py:89
  40.6 0.8 copy-done.9
  44.4 1.1 %collective-permute-done.9.refs_3_ = bf16[4,128,128]{2,1,0:T(8,128)(2,1)S(1)} collective-permute-done((bf16[4,128,128]{2,1,0:T(8,128)(2,1)}, bf16[4,128,128]{2,1,0:T(8,128)(2,1)S(1)}, u32[]{:S(2)}, u32[]{:S(2)}) %collective-permute-start.9) | collective-permute-done | bytes 131104 | tf_op jit(solution)/shard_map/ppermute | solution.py:737
  45.5 0.9 copy-done.40
  46.4 1.1 add_all.1
  47.6 1.6 %collective-permute-start.10 = (bf16[4,128,256]{2,1,0:T(8,128)(2,1)S(1)}, bf16[4,128,256]{2,1,0:T(8,128)(2,1)S(1)}, u32[]{:S(2)}, u32[]{:S(2)}) collective-permute-start(bf16[4,128,256]{2,1,0:T(8,128)(2,1)S(1)} %get-tuple-element.90), channel_id=1, source_target_pairs={{0,8},{4,12},{8,0},{12,4},{16,24},{20,28},{24,16},{28,20},{1,9},{5... | collective-permute-start | bytes 786440 | tf_op jit(solution)/shard_map/ppermute | solution.py:737
  49.1 1.4 %collective-permute-start.12 = (bf16[4,128,128]{2,1,0:T(8,128)(2,1)S(1)}, bf16[4,128,128]{2,1,0:T(8,128)(2,1)S(1)}, u32[]{:S(2)}, u32[]{:S(2)}) collective-permute-start(bf16[4,128,128]{2,1,0:T(8,128)(2,1)S(1)} %get-tuple-element.91), channel_id=1, source_target_pairs={{0,24},{4,28},{8,16},{12,20},{16,8},{20,12},{24,0},{28,4},{1,25},{... | collective-permute-start | bytes 393224 | tf_op jit(solution)/shard_map/ppermute | solution.py:737
  51.1 1.2 %copy-done.4 = f32[4,256,256]{2,1,0:T(8,128)S(1)} copy-done((f32[4,256,256]{2,1,0:T(8,128)S(1)}, f32[4,256,256]{2,1,0:T(8,128)}, u32[]{:S(2)}) %copy-start.4) | copy-done | bytes 1048600
  52.4 1.2 %copy-done.7 = f32[4,256,256]{2,1,0:T(8,128)S(1)} copy-done((f32[4,256,256]{2,1,0:T(8,128)S(1)}, f32[4,256,256]{2,1,0:T(8,128)}, u32[]{:S(2)}) %copy-start.7) | copy-done | bytes 1048600
  53.6 1.0 copy-done.10
  54.6 1.2 %copy-done.17 = f32[4,256,256]{2,1,0:T(8,128)S(1)} copy-done((f32[4,256,256]{2,1,0:T(8,128)S(1)}, f32[4,256,256]{2,1,0:T(8,128)}, u32[]{:S(2)}) %copy-start.17) | copy-done | bytes 1048600
  55.8 0.9 copy-done.20
  56.8 1.0 copy-done.24
  57.8 1.0 copy-done.26
  58.8 1.0 copy-done.28
  59.9 1.0 copy-done.30
  60.9 1.0 copy-done.32
  62.0 3.5 %pull_local.1 = (f32[3,4,256,128]{3,2,1,0:T(8,128)S(1)}, f32[4,256,128]{2,1,0:T(8,128)S(1)}, f32[256,128]{1,0:T(8,128)S(1)}, f32[8,256]{1,0:T(8,128)S(1)}) custom-call(f32[3,4,256,128]{3,2,1,0:T(8,128)S(1)} %get-tuple-element.49.qkv_ref.refs_0_, f32[256,128]{1,0:T(8,128)S(1)} %get-tuple-element.47.pack_ref.refs_1_.refs_2_, f32[128,256]{1,0:T(8,128)S(1)} %copy-done.20, ...), custom_call_target="tpu_custom_call" | custom-call | tf_op jit(solution)/shard_map/pull_local/pallas_call | solution.py:89
  65.6 2.8 %copy-done.2 = bf16[2048,1536]{1,0:T(8,128)(2,1)S(1)} copy-done((bf16[2048,1536]{1,0:T(8,128)(2,1)S(1)}, bf16[2048,1536]{1,0:T(8,128)(2,1)}, u32[]{:S(2)}) %copy-start.2) | copy-done | bytes 6291480
  68.4 7.6 %finish.1 = bf16[4,256,512]{2,1,0:T(8,128)(2,1)S(1)} custom-call(s32[2]{0:T(128)S(1)} %pad_add_fusion.place_ref, f32[3,4,256,128]{3,2,1,0:T(8,128)S(1)} %get-tuple-element.49.qkv_ref.refs_0_, f32[256,128]{1,0:T(8,128)S(1)} %copy-done.36, f32[256,128]{1,0:T(8,128)S(1)} %get-tuple-element.47.pack_ref.refs_1_.refs_2_, ...), custom_call_target="tpu_custom_call" | custom-call | tf_op jit(solution)/shard_map/finish/pallas_call | solution.py:89
  76.0 30.1 %all_to_all.5.parts_ref = bf16[4,256,512]{2,1,0:T(8,128)(2,1)S(1)} all-to-all(bf16[4,256,512]{2,1,0:T(8,128)(2,1)S(1)} %finish.1), channel_id=1, replica_groups=mesh['ctx'=8,'head'=4] {'head'}, dimensions={0} | all-to-all | bytes 2097152 | tf_op jit(solution)/shard_map/all_to_all | solution.py:748
  106.1 0.8 scatter_sum.1
  (94 shorter events, 8.9 us)
Async XLA Ops:
  7.2 99.8 %reduce-scatter.2.cloned.1.call-start = ((), (), s32[]{:S(2)}) async-start(), calls=%async_computation.2 | async-start | bytes 1310720 | tf_op jit(solution)/shard_map/reduce_scatter | solution.py:784
  7.3 19.5 %copy-start = (bf16[4,128,2048]{2,1,0:T(8,128)(2,1)S(1)}, bf16[4,128,2048]{2,1,0:T(8,128)(2,1)}, u32[]{:S(2)}) copy-start(bf16[4,128,2048]{2,1,0:T(8,128)(2,1)} %param.12) | copy-start | bytes 6291460
  7.3 19.5 %copy-start.15 = (bf16[256,2048]{1,0:T(8,128)(2,1)S(1)}, bf16[256,2048]{1,0:T(8,128)(2,1)}, u32[]{:S(2)}) copy-start(bf16[256,2048]{1,0:T(8,128)(2,1)} %grad_ref.1) | copy-start | bytes 3145732
  19.8 9.2 %copy-start.1 = (bf16[2048,1536]{1,0:T(8,128)(2,1)}, bf16[2048,1536]{1,0:T(8,128)(2,1)S(1)}, u32[]{:S(2)}) copy-start(bf16[2048,1536]{1,0:T(8,128)(2,1)S(1)} %get-tuple-element.86.refs_15_) | copy-start | bytes 18874372
  19.8 9.2 %copy-start.3 = (f32[4,256,256]{2,1,0:T(8,128)}, f32[4,256,256]{2,1,0:T(8,128)S(1)}, u32[]{:S(2)}) copy-start(f32[4,256,256]{2,1,0:T(8,128)S(1)} %get-tuple-element.65.refs_10_.refs_6_) | copy-start | bytes 3145732
  19.8 9.2 %copy-start.19 = (f32[128,256]{1,0:T(8,128)}, f32[128,256]{1,0:T(8,128)S(1)}, u32[]{:S(2)}) copy-start(f32[128,256]{1,0:T(8,128)S(1)} %get-tuple-element.50.pack_t_ref.refs_2_) | copy-start | bytes 393220
  19.8 9.2 %copy-start.35 = (f32[256,128]{1,0:T(8,128)}, f32[256,128]{1,0:T(8,128)S(1)}, u32[]{:S(2)}) copy-start(f32[256,128]{1,0:T(8,128)S(1)} %get-tuple-element.63.refs_1_) | copy-start | bytes 393220
  19.8 1.7 %collective-permute-start = (bf16[4,128,256]{2,1,0:T(8,128)(2,1)S(1)}, bf16[4,128,256]{2,1,0:T(8,128)(2,1)S(1)}, u32[]{:S(2)}, u32[]{:S(2)}) collective-permute-start(bf16[4,128,256]{2,1,0:T(8,128)(2,1)S(1)} %get-tuple-element.48.own_ref), channel_id=1, source_target_pairs={{0,4},{4,0},{8,12},{12,8},{16,20},{20,16},{24,28},{28,24},{1,5},{5... | collective-permute-start | bytes 786440 | tf_op jit(solution)/shard_map/ppermute | solution.py:737
  22.2 10.1 %collective-permute-start.3 = (bf16[2,128,256]{2,1,0:T(8,128)(2,1)S(1)}, bf16[2,128,256]{2,1,0:T(8,128)(2,1)S(1)}, u32[]{:S(2)}, u32[]{:S(2)}) collective-permute-start(bf16[2,128,256]{2,1,0:T(8,128)(2,1)S(1)} %join_half.1), channel_id=1, source_target_pairs={{0,24},{4,28},{8,16},{12,20},{16,8},{20,12},{24,0},{28,4},{1,25},{... | collective-permute-start | bytes 393224 | tf_op jit(solution)/shard_map/ppermute | solution.py:737
  26.1 6.6 %collective-permute-start.2 = (bf16[2,128,256]{2,1,0:T(8,128)(2,1)S(1)}, bf16[2,128,256]{2,1,0:T(8,128)(2,1)S(1)}, u32[]{:S(2)}, u32[]{:S(2)}) collective-permute-start(bf16[2,128,256]{2,1,0:T(8,128)(2,1)S(1)} %join_half.1), channel_id=1, source_target_pairs={{0,16},{4,20},{8,24},{12,28},{16,0},{20,4},{24,8},{28,12},{1,17},{... | collective-permute-start | bytes 393224 | tf_op jit(solution)/shard_map/ppermute | solution.py:737
  26.6 6.4 %collective-permute-start.1 = (bf16[2,128,256]{2,1,0:T(8,128)(2,1)S(1)}, bf16[2,128,256]{2,1,0:T(8,128)(2,1)S(1)}, u32[]{:S(2)}, u32[]{:S(2)}) collective-permute-start(bf16[2,128,256]{2,1,0:T(8,128)(2,1)S(1)} %join_half.1), channel_id=1, source_target_pairs={{0,8},{4,12},{8,0},{12,4},{16,24},{20,28},{24,16},{28,20},{1,9},{5... | collective-permute-start | bytes 393224 | tf_op jit(solution)/shard_map/ppermute | solution.py:737
  26.8 8.1 %copy-start.41 = (f32[128]{0:T(128)S(1)}, f32[128]{0:T(128)}, u32[]{:S(2)}) copy-start(f32[128]{0:T(128)} %param.11) | copy-start | bytes 1540
  32.3 5.4 %copy-start.16 = (f32[4,256,256]{2,1,0:T(8,128)}, f32[4,256,256]{2,1,0:T(8,128)S(1)}, u32[]{:S(2)}) copy-start(f32[4,256,256]{2,1,0:T(8,128)S(1)} %get-tuple-element.71.refs_8_) | copy-start | bytes 3145732
  32.3 5.4 %copy-start.33 = (bf16[4,256,128]{2,1,0:T(8,128)(2,1)}, bf16[4,256,128]{2,1,0:T(8,128)(2,1)S(1)}, u32[]{:S(2)}) copy-start(bf16[4,256,128]{2,1,0:T(8,128)(2,1)S(1)} %get-tuple-element.64.refs_4_) | copy-start | bytes 786436
  33.0 1.3 %collective-permute-start.4 = (bf16[2,128,256]{2,1,0:T(8,128)(2,1)S(1)}, bf16[2,128,256]{2,1,0:T(8,128)(2,1)S(1)}, u32[]{:S(2)}, u32[]{:S(2)}) collective-permute-start(bf16[2,128,256]{2,1,0:T(8,128)(2,1)S(1)} %collective-permute-done.1.refs_1_), channel_id=1, source_target_pairs={{0,4},{4,0},{8,12},{12,8},{16,20},{20,16},{24,28},{28,24},{1,5},{5... | collective-permute-start | bytes 393224 | tf_op jit(solution)/shard_map/ppermute | solution.py:737
  33.0 1.5 %collective-permute-start.5 = (bf16[2,128,256]{2,1,0:T(8,128)(2,1)S(1)}, bf16[2,128,256]{2,1,0:T(8,128)(2,1)S(1)}, u32[]{:S(2)}, u32[]{:S(2)}) collective-permute-start(bf16[2,128,256]{2,1,0:T(8,128)(2,1)S(1)} %collective-permute-done.2.refs_2_), channel_id=1, source_target_pairs={{0,4},{4,0},{8,12},{12,8},{16,20},{20,16},{24,28},{28,24},{1,5},{5... | collective-permute-start | bytes 393224 | tf_op jit(solution)/shard_map/ppermute | solution.py:737
  33.5 1.3 %collective-permute-start.6 = (bf16[2,128,256]{2,1,0:T(8,128)(2,1)S(1)}, bf16[2,128,256]{2,1,0:T(8,128)(2,1)S(1)}, u32[]{:S(2)}, u32[]{:S(2)}) collective-permute-start(bf16[2,128,256]{2,1,0:T(8,128)(2,1)S(1)} %collective-permute-done.3.refs_3_), channel_id=1, source_target_pairs={{0,4},{4,0},{8,12},{12,8},{16,20},{20,16},{24,28},{28,24},{1,5},{5... | collective-permute-start | bytes 393224 | tf_op jit(solution)/shard_map/ppermute | solution.py:737
  37.8 5.8 %copy-start.13 = (bf16[4,128,256]{2,1,0:T(8,128)(2,1)}, bf16[4,128,256]{2,1,0:T(8,128)(2,1)S(1)}, u32[]{:S(2)}) copy-start(bf16[4,128,256]{2,1,0:T(8,128)(2,1)S(1)} %get-tuple-element.77.refs_2_.refs_18_) | copy-start | bytes 786436
  37.8 6.0 %copy-start.18 = (bf16[256,2048]{1,0:T(8,128)(2,1)}, bf16[256,2048]{1,0:T(8,128)(2,1)S(1)}, u32[]{:S(2)}) copy-start(bf16[256,2048]{1,0:T(8,128)(2,1)S(1)} %get-tuple-element.62) | copy-start | bytes 3145732
  37.8 6.0 %copy-start.37 = (f32[256,128]{1,0:T(8,128)}, f32[256,128]{1,0:T(8,128)S(1)}, u32[]{:S(2)}) copy-start(f32[256,128]{1,0:T(8,128)S(1)} %get-tuple-element.83.refs_12_) | copy-start | bytes 393220
  43.6 1.9 %collective-permute-start.8 = (bf16[4,128,256]{2,1,0:T(8,128)(2,1)}, bf16[4,128,256]{2,1,0:T(8,128)(2,1)}, u32[]{:S(2)}, u32[]{:S(2)}) collective-permute-start(bf16[4,128,256]{2,1,0:T(8,128)(2,1)} %get-tuple-element.88.refs_0_), channel_id=1, source_target_pairs={{0,4},{4,0},{8,12},{12,8},{16,20},{20,16},{24,28},{28,24},{1,5},{5... | collective-permute-start | bytes 786440 | tf_op jit(solution)/shard_map/ppermute | solution.py:737
  43.8 1.7 %collective-permute-start.9 = (bf16[4,128,128]{2,1,0:T(8,128)(2,1)}, bf16[4,128,128]{2,1,0:T(8,128)(2,1)S(1)}, u32[]{:S(2)}, u32[]{:S(2)}) collective-permute-start(bf16[4,128,128]{2,1,0:T(8,128)(2,1)} %copy-done.39), channel_id=1, source_target_pairs={{0,4},{4,0},{8,12},{12,8},{16,20},{20,16},{24,28},{28,24},{1,5},{5... | collective-permute-start | bytes 393224 | tf_op jit(solution)/shard_map/ppermute | solution.py:737
  44.2 21.3 %collective-permute-start.7 = (bf16[4,128,256]{2,1,0:T(8,128)(2,1)}, bf16[4,128,256]{2,1,0:T(8,128)(2,1)S(1)}, u32[]{:S(2)}, u32[]{:S(2)}) collective-permute-start(bf16[4,128,256]{2,1,0:T(8,128)(2,1)} %copy-done.42), channel_id=1, source_target_pairs={{0,4},{4,0},{8,12},{12,8},{16,20},{20,16},{24,28},{28,24},{1,5},{5... | collective-permute-start | bytes 786440 | tf_op jit(solution)/shard_map/ppermute | solution.py:737
  47.6 18.0 %collective-permute-start.10 = (bf16[4,128,256]{2,1,0:T(8,128)(2,1)S(1)}, bf16[4,128,256]{2,1,0:T(8,128)(2,1)S(1)}, u32[]{:S(2)}, u32[]{:S(2)}) collective-permute-start(bf16[4,128,256]{2,1,0:T(8,128)(2,1)S(1)} %get-tuple-element.90), channel_id=1, source_target_pairs={{0,8},{4,12},{8,0},{12,4},{16,24},{20,28},{24,16},{28,20},{1,9},{5... | collective-permute-start | bytes 786440 | tf_op jit(solution)/shard_map/ppermute | solution.py:737
  49.1 16.4 %collective-permute-start.12 = (bf16[4,128,128]{2,1,0:T(8,128)(2,1)S(1)}, bf16[4,128,128]{2,1,0:T(8,128)(2,1)S(1)}, u32[]{:S(2)}, u32[]{:S(2)}) collective-permute-start(bf16[4,128,128]{2,1,0:T(8,128)(2,1)S(1)} %get-tuple-element.91), channel_id=1, source_target_pairs={{0,24},{4,28},{8,16},{12,20},{16,8},{20,12},{24,0},{28,4},{1,25},{... | collective-permute-start | bytes 393224 | tf_op jit(solution)/shard_map/ppermute | solution.py:737
  50.5 15.0 %collective-permute-start.11 = (bf16[4,128,128]{2,1,0:T(8,128)(2,1)S(1)}, bf16[4,128,128]{2,1,0:T(8,128)(2,1)S(1)}, u32[]{:S(2)}, u32[]{:S(2)}) collective-permute-start(bf16[4,128,128]{2,1,0:T(8,128)(2,1)S(1)} %get-tuple-element.91), channel_id=1, source_target_pairs={{0,16},{4,20},{8,24},{12,28},{16,0},{20,4},{24,8},{28,12},{1,17},{... | collective-permute-start | bytes 393224 | tf_op jit(solution)/shard_map/ppermute | solution.py:737
  62.0 3.6 %copy-start.12 = (bf16[4,128,256]{2,1,0:T(8,128)(2,1)S(1)}, bf16[4,128,256]{2,1,0:T(8,128)(2,1)}, u32[]{:S(2)}) copy-start(bf16[4,128,256]{2,1,0:T(8,128)(2,1)} %copy-done.11) | copy-start | bytes 786436
  62.0 3.6 %copy-start.14 = (bf16[4,128,256]{2,1,0:T(8,128)(2,1)S(1)}, bf16[4,128,256]{2,1,0:T(8,128)(2,1)}, u32[]{:S(2)}) copy-start(bf16[4,128,256]{2,1,0:T(8,128)(2,1)} %copy-done.13) | copy-start | bytes 786436
  62.0 3.6 %copy-start.22 = (bf16[128,2048]{1,0:T(8,128)(2,1)S(1)}, bf16[128,2048]{1,0:T(8,128)(2,1)}, u32[]{:S(2)}) copy-start(bf16[128,2048]{1,0:T(8,128)(2,1)} %copy-done.21) | copy-start | bytes 1572868
  62.0 3.6 %copy-start.34 = (bf16[4,256,128]{2,1,0:T(8,128)(2,1)S(1)}, bf16[4,256,128]{2,1,0:T(8,128)(2,1)}, u32[]{:S(2)}) copy-start(bf16[4,256,128]{2,1,0:T(8,128)(2,1)} %copy-done.33) | copy-start | bytes 786436
  62.0 3.6 %copy-start.36 = (f32[256,128]{1,0:T(8,128)S(1)}, f32[256,128]{1,0:T(8,128)}, u32[]{:S(2)}) copy-start(f32[256,128]{1,0:T(8,128)} %copy-done.35) | copy-start | bytes 393220
  62.0 3.6 %copy-start.38 = (f32[256,128]{1,0:T(8,128)S(1)}, f32[256,128]{1,0:T(8,128)}, u32[]{:S(2)}) copy-start(f32[256,128]{1,0:T(8,128)} %copy-done.37) | copy-start | bytes 393220
  (25 other events, 32.6 us)
Sparse Core Ops, SparseCore 0:
  43.9 28.1 reduce-scatter.1

commit v5 on v3

--- a/solution.py
+++ b/solution.py
@@ -81,18 +81,24 @@
     return pltpu.VMEM(shape, dtype)
 
 
+def stored(shape, dtype):
+    return pltpu.HBM(shape, dtype)
+
+
 def pin(values, space):
     return [pltpu.with_memory_space_constraint(value, space) for value in values]
 
 
-def local_call(body, name, limit, out_shape, scalars, arrays, scratch=(), remote=()):
+def local_call(
+    body, name, limit, out_shape, scalars, arrays, scratch=(), remote=(), out_specs=None
+):
     return pl.pallas_call(
         body,
         out_shape=tuple(out_shape),
         in_specs=[SCALARS] * len(scalars)
         + [WHOLE] * len(arrays)
         + [HBM] * len(remote),
-        out_specs=(WHOLE,) * len(out_shape),
+        out_specs=tuple(out_specs or [WHOLE] * len(out_shape)),
         scratch_shapes=list(scratch),
         compiler_params=pltpu.CompilerParams(vmem_limit_bytes=limit * MIB),
         name=name,
@@ -122,175 +128,236 @@
     return rate, bias
 
 
-def project_body(sizes, hp_hbm, tokens_hbm, w_hbm, small_hbm, *refs):
+def merge_blocks(trans_all, edge_all, levels, first):
+    if first:
+        powers = [edge.astype(BF16) for edge in edge_all]
+        trans_all = [trans - power for trans, power in zip(trans_all, powers)]
+    else:
+        powers = [mm(edge, trans).astype(BF16) for edge, trans in zip(edge_all, trans_all)]
+        yield
+        trans_all = [
+            trans - mm(trans, power).astype(BF16) for trans, power in zip(trans_all, powers)
+        ]
+    for level in range(1, levels):
+        powers = [mm(power, power).astype(BF16) for power in powers]
+        yield
+        trans_all = [
+            trans + mm(trans, power).astype(BF16) for trans, power in zip(trans_all, powers)
+        ]
+    return trans_all
+
+
+def invert(lower_all, eye, apart, rows):
+    trans_all = [eye.astype(BF16) for lower in lower_all]
+    bits = rows.bit_length() - 1
+    start = 0
+    while start < bits:
+        levels = min(2 if bits - start == 2 else 3, bits - start)
+        here = jnp.logical_and((apart >> start) >= 1, (apart >> (start + levels)) == 0)
+        edge_all = [jnp.where(here, lower, 0.0) for lower in lower_all]
+        trans_all = yield from merge_blocks(trans_all, edge_all, levels, start == 0)
+        start += levels
+        yield
+    rest_all = []
+    for trans, lower in zip(trans_all, lower_all):
+        high, low = split(lower)
+        rest_all.append(eye - trans.astype(F32) - mm(high, trans) - mm(low, trans))
+    yield
+    return [
+        (trans.astype(F32) + mm(trans, rest)).astype(BF16)
+        for trans, rest in zip(trans_all, rest_all)
+    ]
+
+
+def project_body(sizes, place_ref, hp_hbm, tokens_hbm, w_hbm, small_hbm, *refs):
     heads, levels, chunks = sizes
-    (wr_ref, small_ref, qkv_ref, gate_ref, pack_ref, pack_t_ref, trans_ref, mixed_t_ref,
+    (wr_hbm, small_ref, qkv_ref, gate_ref, pack_ref, pack_t_ref, trans_ref, mixed_t_ref,
      decay_ref, base_ref, lower_ref, rates_ref, pair_ref) = refs[:13]
-    tokens, wide_in, wide_even, wide_odd, small_in, small_wide, acc, hp_ref, sems = refs[13:]
+    tokens, wide_in, wide, wr, small_in, small_wide, acc, hp_ref, sems = refs[13:]
     rows, width = tokens.shape
     depth = width // chunks
     cols = 3 * heads
     fetch_tokens = pltpu.make_async_copy(tokens_hbm, tokens, sems.at[chunks])
     fetch_small = pltpu.make_async_copy(small_hbm, small_in, sems.at[chunks + 1])
     fetch_rates = pltpu.make_async_copy(hp_hbm, hp_ref, sems.at[chunks + 2])
+    keep_weight = pltpu.make_async_copy(wr, wr_hbm, sems.at[chunks + 3])
     fetches = []
     for chunk in range(chunks):
         span = pl.ds(chunk * depth * cols, depth * cols)
         fetches.append(
             pltpu.make_async_copy(w_hbm.at[span, :], wide_in.at[span, :], sems.at[chunk])
         )
-    fetches[0].start()
-    fetch_tokens.start()
     fetch_small.start()
     fetch_rates.start()
-    for fetch in fetches[1:]:
+    fetch_tokens.start()
+    for fetch in fetches:
         fetch.start()
-    for chunk in range(chunks):
-        fetches[chunk].wait()
-        at = chunk * depth
-        wide = wide_odd if chunk % 2 else wide_even
-        wide[...] = wide_in[at * cols : (at + depth) * cols, :].astype(F32)
-        for col in range(cols):
-            part = wide[pl.ds(col, depth, stride=cols), :]
-            wr_ref[at : at + depth, col * LANES : (col + 1) * LANES] = part.astype(BF16)
-        if chunk == 0:
-            fetch_tokens.wait()
-        own = jnp.dot(
-            tokens[:, at : at + depth], wr_ref[at : at + depth, :], preferred_element_type=F32
-        )
-        if chunk == 0:
-            acc[...] = own
-        else:
-            acc[...] += own
+    decay_col = levels * heads
+    beta_col = decay_col + heads
+    norm_col = beta_col + heads
+    lane = lane_of(rows)
+    row_id, col_id = pair_ids(rows)
+    inclusive = row_id >= col_id
+    strict = row_id > col_id
+    apart = row_id ^ col_id
+    eye = (row_id == col_id).astype(F32)
     fetch_small.wait()
     small_rows = small_in.shape[0] * heads
     for level in range(small_in.shape[0]):
         small_wide[level * heads : (level + 1) * heads, :] = small_in[level].astype(F32)
     small_wide[small_rows:, :] = jnp.zeros((LANES - small_rows, width), F32)
     small_ref[...] = small_wide[...].astype(BF16)
-    gate = mm_nt(tokens[...], small_ref[...])
-    decay_col = levels * heads
-    beta_col = decay_col + heads
-    norm_col = beta_col + heads
-    gate_ref[...] = gate
-    lane = lane_of(rows)
     fetch_rates.wait()
     rate, bias = head_rows(hp_ref, heads, decay_col, beta_col)
     rates_ref[0:1, :] = rate
     rates_ref[1:2, :] = bias
+    fetch_tokens.wait()
+    gate = mm_nt(tokens[...], small_ref[...])
+    gate_ref[...] = gate
     switch = jax.nn.sigmoid(gate + bias)
     lam = jnp.maximum(gate, 0.0) + jnp.log1p(jnp.exp(-jnp.abs(gate)))
-    row_id, col_id = pair_ids(rows)
-    inclusive = row_id >= col_id
-    strict = row_id > col_id
-    apart = row_id ^ col_id
     cum = mm_full(inclusive.astype(F32), -rate * switch)
     pack = jnp.where(lane < decay_col, lam, jnp.where(lane < beta_col, cum, switch))
-    k_all, v_all = [], []
-    for head in range(heads):
-        for part in range(2):
-            col = (part * heads + head) * LANES
-            raw = acc[:, col : col + LANES]
-            scale = lax.rsqrt(row_sum(raw * raw) + EPS)
-            unit = raw * scale
-            qkv_ref[part, head] = unit
-            pack = jnp.where(lane == norm_col + part * heads + head, scale, pack)
-            if part == 1:
-                k_all.append(unit)
-        col = (2 * heads + head) * LANES
-        v_all.append(acc[:, col : col + LANES])
-        qkv_ref[2, head] = v_all[head]
-    pack_ref[...] = pack
     pack_t = pack.T
     pack_t_ref[...] = pack_t
-    eye = (row_id == col_id).astype(F32)
-    lower_all, trans_all = [], []
+
+    def extract(chunk, part):
+        at = chunk * depth
+        for col in range(part * heads, (part + 1) * heads):
+            value = wide[pl.ds(at * cols + col, depth, stride=cols), :]
+            wr[at : at + depth, col * LANES : (col + 1) * LANES] = value.astype(BF16)
+
+    def multiply(part, first, last):
+        span = slice((part * heads) * LANES, (part + 1) * heads * LANES)
+        own = jnp.dot(
+            tokens[:, first * depth : last * depth], wr[first * depth : last * depth, span],
+            preferred_element_type=F32,
+        )
+        if first == 0:
+            acc[:, span] = own
+        else:
+            acc[:, span] += own
+
+    for chunk in range(chunks):
+        fetches[chunk].wait()
+        at = chunk * depth * cols
+        wide[at : at + depth * cols, :] = wide_in[at : at + depth * cols, :].astype(F32)
+        extract(chunk, 1)
+        if chunk % 2 == 1:
+            multiply(1, chunk - 1, chunk + 1)
+
+    def unit_of(part, head):
+        col = (part * heads + head) * LANES
+        raw = acc[:, col : col + LANES]
+        scale = lax.rsqrt(row_sum(raw * raw) + EPS)
+        qkv_ref[part, head] = raw * scale
+        return raw * scale, jnp.where(lane == norm_col + part * heads + head, scale, 0.0)
+
+    scales = jnp.zeros((rows, LANES), F32)
+    k_all, lower_all = [], []
     for head in range(heads):
+        unit, scale = unit_of(1, head)
+        k_all.append(unit)
+        scales = scales + scale
         decay = decay_of(pack, pack_t, decay_col + head, inclusive)
-        decay_ref[head] = decay
-        gram = mm_nt(k_all[head], k_all[head])
-        base = jnp.where(strict, decay * gram, 0.0)
-        base_ref[head] = base
+        decay_ref[head] = decay.astype(BF16)
+        base = jnp.where(strict, decay * mm_nt(unit, unit), 0.0)
+        base_ref[head] = base.astype(BF16)
         lower = column(pack, beta_col + head) * base
-        lower_ref[head] = lower
+        lower_ref[head] = lower.astype(BF16)
         lower_all.append(lower)
-        trans_all.append((eye - jnp.where(apart == 1, lower, 0.0)).astype(BF16))
-    for bit in range(1, rows.bit_length() - 1):
-        here = (apart >> bit) == 1
-        edge = [jnp.where(here, lower, 0.0) for lower in lower_all]
-        half = [mm(trans, part) for trans, part in zip(trans_all, edge)]
-        trans_all = [
-            trans - mm(part, trans).astype(BF16) for trans, part in zip(trans_all, half)
-        ]
-    rest_all = []
-    for trans, lower in zip(trans_all, lower_all):
-        high, low = split(lower)
-        rest_all.append(eye - trans.astype(F32) - mm(high, trans) - mm(low, trans))
-    trans_all = [
-        (trans.astype(F32) + mm(trans, rest)).astype(BF16)
-        for trans, rest in zip(trans_all, rest_all)
-    ]
+
+    def later():
+        for part in (2, 0):
+            for chunk in range(chunks):
+                extract(chunk, part)
+                if chunk % 4 == 3:
+                    multiply(part, chunk - 3, chunk + 1)
+                if chunk % 2 == 1:
+                    yield
+
+    chain, filler = invert(lower_all, eye, apart, rows), later()
+    while True:
+        try:
+            next(chain)
+        except StopIteration as stop:
+            trans_all = stop.value
+            break
+        next(filler, None)
+    for _ in filler:
+        pass
+    keep_weight.start()
     mixed_all = []
     for head in range(heads):
         trans_ref[head] = trans_all[head]
         cum_row = pack_t[decay_col + head : decay_col + head + 1, :]
         tail_t = k_all[head].T * jnp.exp(cum_row[:, rows - 1 :] - cum_row)
-        mixed_all.append(mm(tail_t, trans_all[head]))
+        mixed_all.append(mm(tail_t, trans_all[head]).astype(BF16))
     eye_key = eye[:LANES, :LANES]
     for head in range(heads):
         mixed_t_ref[head] = mixed_all[head]
+        col = (2 * heads + head) * LANES
+        v_in = acc[:, col : col + LANES]
+        qkv_ref[2, head] = v_in
         cum_col = column(pack, decay_col + head)
         beta = column(pack, beta_col + head)
         grown = (beta * jnp.exp(cum_col)) * k_all[head]
-        both = jnp.concatenate([-grown, beta * v_all[head]], 1)
+        both = jnp.concatenate([-grown, beta * v_in], 1)
         pair = mm(mixed_all[head], both)
         last = jnp.exp(cum_col[rows - 1 : rows, :])
         pair_ref[head, :, :LANES] = (last * eye_key + pair[:, :LANES]).astype(BF16)
         pair_ref[head, :, LANES:] = pair[:, LANES:].astype(BF16)
-
-
-def project(tokens, flat_w, small, head_param, heads, levels):
+    for head in range(heads):
+        scales = scales + unit_of(0, head)[1]
+    pack_ref[...] = jnp.where(lane < norm_col, pack, scales)
+    keep_weight.wait()
+
+
+def project(place, tokens, flat_w, small, head_param, heads, levels):
     rows, width = tokens.shape
     chunks = 8
     cols = 3 * heads
     key = flat_w.shape[1]
     square = (heads, rows, rows)
     out_shape = (
-        kept((width, cols * key), BF16),
+        stored((width, cols * key), BF16),
         kept((LANES, width), BF16),
         kept((3, heads, rows, key), F32),
         kept((rows, LANES), F32),
         kept((rows, LANES), F32),
         kept((LANES, rows), F32),
         kept(square, BF16),
-        kept((heads, key, rows), F32),
-        kept(square, F32),
-        kept(square, F32),
-        kept(square, F32),
+        kept((heads, key, rows), BF16),
+        kept(square, BF16),
+        kept(square, BF16),
+        kept(square, BF16),
         kept((2, LANES), F32),
         kept((heads, key, 2 * key), BF16),
     )
     scratch = [
         pltpu.VMEM(tokens.shape, BF16),
         pltpu.VMEM(flat_w.shape, BF16),
-        pltpu.VMEM((width // chunks * cols, key), F32),
-        pltpu.VMEM((width // chunks * cols, key), F32),
+        pltpu.VMEM(flat_w.shape, F32),
+        pltpu.VMEM((width, cols * key), BF16),
         pltpu.VMEM(small.shape, BF16),
         pltpu.VMEM((LANES, width), F32),
         pltpu.VMEM((rows, cols * key), F32),
         pltpu.VMEM(head_param.shape, F32),
-        pltpu.SemaphoreType.DMA((chunks + 3,)),
+        pltpu.SemaphoreType.DMA((chunks + 4,)),
     ]
     return local_call(
-        functools.partial(project_body, (heads, levels, chunks)), "project", 22, out_shape,
-        [], [], scratch, [head_param, tokens, flat_w, small],
-    )
-
-
-def local_body(sizes, qkv_ref, pack_ref, pack_t_ref, trans_ref, mixed_t_ref, decay_ref, *outs):
+        functools.partial(project_body, (heads, levels, chunks)), "project", 36, out_shape,
+        [place], [], scratch, [head_param, tokens, flat_w, small], [HBM] + [WHOLE] * 12,
+    )
+
+
+def local_body(
+    sizes, qkv_ref, pack_ref, pack_t_ref, trans_ref, mixed_t_ref, decay_ref, grad_ref, weight_ref, *outs
+):
     heads, levels, bits = sizes
     (attn_ref, attn_t_ref, prod_t_ref, scores_ref, mix_ref, mixed_ref, local_ref, hat_ref,
-     hat_t_ref) = outs
+     hat_t_ref, grad_normed_ref) = outs
+    grad_normed_ref[...] = mm_nt(grad_ref[...], weight_ref[...])
     rows = pack_ref.shape[0]
     decay_col = levels * heads
     beta_col = decay_col + heads
@@ -299,16 +366,16 @@
     row_id, col_id = pair_ids(rows)
     apart = row_id ^ col_id
     for head in range(heads):
-        scores = mm_nt_fine(qkv_ref[0, head], qkv_ref[1, head]) * decay_ref[head]
+        scores = mm_nt_fine(qkv_ref[0, head], qkv_ref[1, head]) * decay_ref[head].astype(F32)
         scores_ref[head] = scores.astype(BF16)
-        mix_ref[head] = level_mix(pack, head, heads, bits, apart)
-        mixed_ref[head] = mixed_t_ref[head].T.astype(BF16)
+        mix_ref[head] = level_mix(pack, head, heads, bits, apart).astype(BF16)
+        mixed_ref[head] = mixed_t_ref[head].astype(F32).T.astype(BF16)
     for head in range(heads):
         attn = mm(scores_ref[head], trans_ref[head])
         attn_ref[head] = attn.astype(BF16)
         attn_t_ref[head] = attn.T.astype(BF16)
         attn = attn * pack_t[beta_col + head : beta_col + head + 1, :]
-        prod = attn * mix_ref[head]
+        prod = attn * mix_ref[head].astype(F32)
         prod_t_ref[head] = prod.T.astype(BF16)
         growth = jnp.exp(column(pack, decay_col + head))
         local_ref[head] = mm(prod, qkv_ref[2, head])
@@ -317,23 +384,24 @@
         hat_t_ref[head] = hat.T.astype(BF16)
 
 
-def local_part(qkv, pack, pack_t, trans, mixed_t, decay, levels, bits):
-    heads, rows, key = qkv.shape[1:]
+def local_part(arrays, levels, bits):
+    heads, rows, key = arrays[0].shape[1:]
     square = (heads, rows, rows)
     out_shape = (
         kept(square, BF16),
         kept(square, BF16),
         kept(square, BF16),
         kept(square, BF16),
-        kept(square, F32),
+        kept(square, BF16),
         kept((heads, rows, key), BF16),
         kept((heads, rows, key), F32),
         kept((heads, rows, key), BF16),
         kept((heads, key, rows), BF16),
+        kept((rows, heads * key), F32),
     )
     return local_call(
         functools.partial(local_body, (heads, levels, bits)), "local_part", 10, out_shape,
-        [], [qkv, pack, pack_t, trans, mixed_t, decay],
+        [], arrays,
     )
 
 
@@ -377,9 +445,9 @@
     first_ref = refs[0]
     near = [None] + [(refs[1 + at], refs[1 + near_count + at]) for at in range(near_count)]
     refs = refs[2 * near_count + 1 :]
-    out_refs = refs[:count]
-    dout_ref, found_ref, prefix_ref, dfar_ref = refs[count : count + 4]
-    nodes = refs[count + 4 : -1]
+    out_refs = refs[:2]
+    dout_ref, found_ref, prefix_ref, dfar_ref = refs[2:6]
+    nodes = refs[6:-1]
     normed_ref = refs[-1]
     rows = pack_ref.shape[0]
     key = hat_ref.shape[2]
@@ -430,11 +498,11 @@
             col = (bits + 1 + bit) * heads + head
             dfar = jnp.where(lane == col, row_sum(dout * parts[bit]), dfar)
     dfar_ref[...] = dfar
-    size = out_refs[0].shape[1]
-    for shift in range(count):
-        dest = lax.rem(place_ref[1] + shift, count)
+    size = weight_ref.shape[1] // count
+    for mask in range(count):
+        dest = place_ref[1] ^ mask
         cols = pl.ds(pl.multiple_of(dest * size, size), size)
-        out_refs[shift][...] = jnp.dot(
+        out_refs[mask % 2][mask // 2] = jnp.dot(
             normed_ref[...], weight_ref[:, cols], preferred_element_type=F32
         ).astype(BF16)
 
@@ -443,7 +511,8 @@
     gain, pack, local_out, hat, grad_normed, weight = arrays
     heads, rows, key = hat.shape
     nodes = tuple(kept(first.shape, BF16) for bit in range(1, far))
-    out_shape = (kept((rows, weight.shape[1] // count), BF16),) * count + (
+    size = weight.shape[1] // count
+    out_shape = (kept((count // 2, rows, size), BF16),) * 2 + (
         kept((heads, rows, key), F32),
         kept((heads, key, far * key), BF16),
         kept((heads, far, key, key), BF16),
@@ -454,8 +523,7 @@
         functools.partial(reach_body, (heads, bits, far, count, len(mine))), "reach", 10, out_shape,
         [place], [*arrays, first, *mine, *theirs], [pltpu.VMEM((rows, heads * key), BF16)],
     )
-    parts, got = got[:count], got[count:]
-    return parts, got[:4], got[4:]
+    return got[:2], got[2:6], got[6:]
 
 
 def return_body(sizes, place_ref, pack_ref, hat_t_ref, dout_ref, found_ref, prefix_ref, *refs):
@@ -523,10 +591,10 @@
 
 def lower_pull(dlower, base, lower, beta, decay, strict, k_in):
     dlower = jnp.where(strict, dlower, 0.0)
-    dbeta = row_sum(dlower * base)
+    dbeta = row_sum(dlower * base.astype(F32))
     dgram = dlower * (beta * decay)
     dkey = mm(dgram, k_in) + mm_tn(dgram, k_in)
-    return dbeta, beta * dbeta, col_sum(dlower * lower), dkey
+    return dbeta, beta * dbeta, col_sum(dlower * lower.astype(F32)), dkey
 
 
 def pull_body(sizes, *refs):
@@ -564,7 +632,7 @@
             dcol = jnp.where(
                 lane == level * heads + head, row_sum(jnp.where(here, touched, 0.0)), dcol
             )
-        dattn = dprod * mix_ref[head] - mm_nt(dhat_ref[head], growth * qkv_ref[1, head])
+        dattn = dprod * mix_ref[head].astype(F32) - mm_nt(dhat_ref[head], growth * qkv_ref[1, head])
         dbeta_rows.append(col_sum(dattn * attn0))
         dattn_all.append((dattn * beta_row).astype(BF16))
     dscore_all = [mm_nt(dattn_all[head], trans_ref[head]) for head in all_heads]
@@ -579,12 +647,12 @@
         beta = column(pack, beta_col + head)
         growth = jnp.exp(column(pack, decay_col + head))
         dscore = dscore_all[head]
-        dprobs = dscore * decay_ref[head]
+        decay = decay_ref[head].astype(F32)
+        dprobs = dscore * decay
         shift = dscore * scores_ref[head].astype(F32)
         dgrown_ref[head] = -beta * moved_all[head][:, rows:]
         dbeta, dcum_col, dcum_row, dk_lower = lower_pull(
-            -moved_all[head][:, :rows], base_ref[head], lower_ref[head], beta, decay_ref[head],
-            strict, k_in
+            -moved_all[head][:, :rows], base_ref[head], lower_ref[head], beta, decay, strict, k_in
         )
         dhat = dhat_ref[head]
         dqkv_ref[0, head] = growth * dhat + mm(dprobs, k_in)
@@ -613,15 +681,18 @@
 def finish_body(sizes, place_ref, *refs):
     heads, levels, far, count, arrived_counts = sizes
     (qkv_ref, gate_ref, pack_ref, trans_ref, mixed_ref, decay_ref, base_ref, lower_ref,
-     dqkv_ref, dgrown_ref, dcol_ref, drow_ref, dfar_ref, rates_ref, small_ref, wr_ref) = refs[:16]
-    others = refs[16 : 16 + far]
-    refs = refs[16 + far :]
+     dqkv_ref, dgrown_ref, dcol_ref, drow_ref, dfar_ref, rates_ref, small_ref) = refs[:15]
+    others = refs[15 : 15 + far]
+    refs = refs[15 + far :]
     arrived = []
     for found in arrived_counts:
         arrived.append(refs[:found])
         refs = refs[found:]
-    out_refs = refs[:count]
-    (dproj,) = refs[count:]
+    wr_hbm = refs[0]
+    out_refs = refs[1 : 1 + count]
+    dproj, wr_ref, sem = refs[1 + count :]
+    fetch = pltpu.make_async_copy(wr_hbm, wr_ref, sem)
+    fetch.start()
     rows = pack_ref.shape[0]
     key = qkv_ref.shape[3]
     decay_col = levels * heads
@@ -677,7 +748,8 @@
         dbeta_more = row_sum(mixed_ref[head].astype(F32) * dmixed_all[head])
         dtail = dtail_all[head]
         dbeta, dcum_col, dcum_row, dk_lower = lower_pull(
-            dlower_all[head], base_ref[head], lower_ref[head], beta, decay_ref[head], strict, k_in
+            dlower_all[head], base_ref[head], lower_ref[head], beta, decay_ref[head].astype(F32),
+            strict, k_in
         )
         dcum_rows.append(-dcum_row)
         tail_pull = tail * row_sum(k_in * dtail)
@@ -713,6 +785,7 @@
         jnp.where(lane < beta_col, -rate * dlog * slope, dcol * slope),
     )
     dgate = jnp.where(lane < norm_col, dgate, 0.0).astype(BF16)
+    fetch.wait()
     size = out_refs[0].shape[1]
     for shift in range(count):
         dest = lax.rem(place_ref[1] + shift, count)
@@ -721,17 +794,20 @@
         out_refs[shift][...] = part.astype(BF16)
 
 
-def finish(place, arrays, others, arrived, levels, count):
+def finish(place, arrays, others, arrived, wr, levels, count):
     rows = arrays[0].shape[2]
-    width, cols = arrays[-1].shape
+    width, cols = wr.shape
     far = len(others)
     counts = tuple(len(group) for group in arrived)
     heads = arrays[0].shape[1]
     flat = [value for group in arrived for value in group]
+    scratch = [
+        pltpu.VMEM((rows, cols), BF16), pltpu.VMEM(wr.shape, BF16), pltpu.SemaphoreType.DMA
+    ]
     return local_call(
-        functools.partial(finish_body, (heads, levels, far, count, counts)), "finish", 12,
+        functools.partial(finish_body, (heads, levels, far, count, counts)), "finish", 16,
         [kept((rows, width // count), BF16)] * count,
-        [place], [*arrays, *others, *flat], [pltpu.VMEM((rows, cols), BF16)],
+        [place], [*arrays, *others, *flat], scratch, [wr],
     )
 
 
@@ -740,13 +816,44 @@
     return lax.ppermute(value, axis, [(at, at ^ mask) for at in range(size)])
 
 
-def scatter_sum(parts, axis):
+def sum_body(*refs):
+    total = refs[0][...].astype(F32)
+    for ref in refs[1:-1]:
+        total = total + ref[...].astype(F32)
+    refs[-1][...] = total.astype(BF16)
+
+
+def sum_all(values, keep):
+    out = kept if keep else jax.ShapeDtypeStruct
+    return local_call(sum_body, "sum_all", 6, [out(values[0].shape, BF16)], [], values)[0]
+
+
+def shift_sum(parts, axis):
     count = lax.axis_size(axis)
-    total = parts[0].astype(F32)
+    values = [parts[0]]
     for shift in range(1, count):
-        got = lax.ppermute(parts[shift], axis, [(at, (at + shift) % count) for at in range(count)])
-        total = total + got.astype(F32)
-    return total.astype(BF16)
+        pairs = [(at, (at + shift) % count) for at in range(count)]
+        values.append(lax.ppermute(parts[shift], axis, pairs))
+    return sum_all(values, False)
+
+
+def halve_body(own_ref, got_ref, keep_ref, send_ref):
+    for at in range(own_ref.shape[0]):
+        total = own_ref[at].astype(F32) + got_ref[at].astype(F32)
+        target = send_ref if at % 2 else keep_ref
+        target[at // 2] = total.astype(target.dtype)
+
+
+def halving_sum(keep, send, axis):
+    mask = 1
+    while keep.shape[0] > 1:
+        got = swap(send, axis, mask)
+        half = (keep.shape[0] // 2,) + keep.shape[1:]
+        keep, send = local_call(
+            halve_body, "halve", 6, [kept(half, F32), kept(half, BF16)], [], [keep, got]
+        )
+        mask *= 2
+    return sum_all([keep, swap(send, axis, mask)], False)[0]
 
 
 def on_device(tokens, qkv_weight, small_weight, head_param, norm_gain, out_weight, grad_out):
@@ -766,16 +873,13 @@
 
     (wr, small_t, qkv, gate, pack, pack_t, trans, mixed_t, decay, base, lower, rates_row,
      pair) = project(
-        tokens, flat_w, small, rates, heads, levels
+        place, tokens, flat_w, small, rates, heads, levels
     )
     first = swap(pair, "ctx", 1)
     node = join_half(place, pair, first)
     mine = [swap(node, "ctx", 2 * at) for at in range(1, size // 2)]
-    (attn, attn_t, prod_t, scores, mix, mixed, local_out, hat, hat_t) = local_part(
-        qkv, pack, pack_t, trans, mixed_t, decay, levels, bits
-    )
-    grad_normed = lax.dot_general(
-        grad_out, flat_out, (((1,), (1,)), ((), ())), preferred_element_type=F32
+    (attn, attn_t, prod_t, scores, mix, mixed, local_out, hat, hat_t, grad_normed) = local_part(
+        [qkv, pack, pack_t, trans, mixed_t, decay, grad_out, flat_out], levels, bits
     )
     mine, local_out, grad_normed = lax.optimization_barrier((mine, local_out, grad_normed))
     theirs = [swap(value, "ctx", 1) for value in mine]
@@ -783,7 +887,7 @@
         place, [gain, pack, local_out, hat, grad_normed, flat_out], first, (mine, theirs),
         bits, far, count
     )
-    layer_out = scatter_sum(out_parts, "head")
+    layer_out = halving_sum(*out_parts, "head")
     others = [first, *nodes]
     dhat, sends = return_states(place, pack, hat_t, dout, found, prefix, others, bits)
     got = [swap(value, "ctx", 1) for value in sends]
@@ -798,9 +902,9 @@
         levels, bits,
     )
     arrays = [qkv, gate, pack, trans, mixed, decay, base, lower, dqkv, dgrown, dcol, drow, dfar,
-              rates_row, small_t, wr]
-    parts = finish(place, arrays, others, arrived, levels, count)
-    return layer_out, scatter_sum(parts, "head")
+              rates_row, small_t]
+    parts = finish(place, arrays, others, arrived, wr, levels, count)
+    return layer_out, shift_sum(parts, "head")
 
 
 def solution(mesh):

time: 93.6 us -> 82.9 us (0.89)
  the two profiles are of different devices: /device:TPU:9 before, /device:TPU:11 now
where the time goes in v5:
time: 82.9 us; the launch traced here: 82.8 us
  Pallas kernels  35.6 us (43%)
  waiting for transfers between devices  32.3 us (39%)
  starting transfers between devices  14.1 us (17%)
    pallas_call x11, Pallas kernels, local_call(): pl.pallas_call(body, out_shape=tuple(out_shape), in_specs=[SCALARS] * len...  35.6 us
    ppermute x3, waiting for transfers between devices, shift_sum(): values.append(lax.ppermute(parts[shift], axis, pairs))  22.5 us
    ppermute x15, starting transfers between devices, swap(): return lax.ppermute(value, axis, [(at, at ^ mask) for at in range(size)])  11.1 us
    ppermute x15, waiting for transfers between devices, swap(): return lax.ppermute(value, axis, [(at, at ^ mask) for at in range(size)])  9.76 us
    ppermute x3, starting transfers between devices, shift_sum(): values.append(lax.ppermute(parts[shift], axis, pairs))  3.09 us
  transfers between devices with their start and end apart: 18, of which 11 were waited for; matrix products, arithmetic and copies ran while one was open for 0% of the time, Pallas kernels for 23%

profile of v5, /device:TPU:11, one launch (start us, length us, event | category | flops | bytes accessed | tf_op | source)
XLA Modules:
  0.0 82.8 jit_solution(9420119877178036034)
XLA Ops:
  0.7 12.3 %project.1 = (bf16[2048,1536]{1,0:T(8,128)(2,1)}, bf16[128,2048]{1,0:T(8,128)(2,1)S(1)}, f32[3,4,256,128]{3,2,1,0:T(8,128)S(1)}, f32[256,128]{1,0:T(8,128)S(1)},...) custom-call(s32[2]{0:T(128)S(1)} %pad_add_fusion.place_ref, ...), custom_call_target="tpu_custom_call" | custom-call | tf_op jit(solution)/shard_map/project/pallas_call | solution.py:95
  13.0 0.7 collective-permute-start
  13.8 1.2 %collective-permute-done.other_ref.refs_0_.refs_15_ = bf16[4,128,256]{2,1,0:T(8,128)(2,1)S(1)} collective-permute-done((bf16[4,128,256]{2,1,0:T(8,128)(2,1)S(1)}, bf16[4,128,256]{2,1,0:T(8,128)(2,1)S(1)}, u32[]{:S(2)}, u32[]{:S(2)}) %collective-permute-start) | collective-permute-done | bytes 262176 | tf_op jit(solution)/shard_map/ppermute | solution.py:816
  14.9 0.7 join_half.1
  15.6 1.3 %collective-permute-start.3 = (bf16[2,128,256]{2,1,0:T(8,128)(2,1)S(1)}, bf16[2,128,256]{2,1,0:T(8,128)(2,1)S(1)}, u32[]{:S(2)}, u32[]{:S(2)}) collective-permute-start(bf16[2,128,256]{2,1,0:T(8,128)(2,1)S(1)} %join_half.1), channel_id=1, source_target_pairs={{0,24},{4,28},{8,16},{12,20},{16,8},{20,12},{24,0},{28,4},{1,25},{... | collective-permute-start | bytes 393224 | tf_op jit(solution)/shard_map/ppermute | solution.py:816
  17.2 1.2 %collective-permute-start.1 = (bf16[2,128,256]{2,1,0:T(8,128)(2,1)S(1)}, bf16[2,128,256]{2,1,0:T(8,128)(2,1)S(1)}, u32[]{:S(2)}, u32[]{:S(2)}) collective-permute-start(bf16[2,128,256]{2,1,0:T(8,128)(2,1)S(1)} %join_half.1), channel_id=1, source_target_pairs={{0,8},{4,12},{8,0},{12,4},{16,24},{20,28},{24,16},{28,20},{1,9},{5... | collective-permute-start | bytes 393224 | tf_op jit(solution)/shard_map/ppermute | solution.py:816
  18.4 2.3 %local_part.1 = (bf16[4,256,256]{2,1,0:T(8,128)(2,1)S(1)}, bf16[4,256,256]{2,1,0:T(8,128)(2,1)S(1)}, bf16[4,256,256]{2,1,0:T(8,128)(2,1)S(1)}, bf16[4,256,256]{2...) custom-call(f32[3,4,256,128]{3,2,1,0:T(8,128)S(1)} %get-tuple-elemen, ...), custom_call_target="tpu_custom_call" | custom-call | tf_op jit(solution)/shard_map/local_part/pallas_call | solution.py:95
  20.6 0.7 collective-permute-done.3.refs_3_
  21.3 3.5 %collective-permute-done.2.refs_2_ = bf16[2,128,256]{2,1,0:T(8,128)(2,1)S(1)} collective-permute-done((bf16[2,128,256]{2,1,0:T(8,128)(2,1)S(1)}, bf16[2,128,256]{2,1,0:T(8,128)(2,1)S(1)}, u32[]{:S(2)}, u32[]{:S(2)}) %collective-permute-start.2) | collective-permute-done | bytes 131104 | tf_op jit(solution)/shard_map/ppermute | solution.py:816
  24.8 0.6 collective-permute-start.4
  25.4 0.5 collective-permute-start.6
  25.9 0.5 collective-permute-done.4.refs_4_
  26.4 0.4 collective-permute-done.5.refs_5_
  27.0 3.0 %reach.1 = (bf16[2,256,512]{2,1,0:T(8,128)(2,1)S(1)}, bf16[2,256,512]{2,1,0:T(8,128)(2,1)S(1)}, f32[4,256,128]{2,1,0:T(8,128)S(1)}, bf16[4,128,384]{2,1,0:T(8,12...) custom-call(s32[2]{0:T(128)S(1)} %pad_add_fusion.place_ref, ...), custom_call_target="tpu_custom_call" | custom-call | tf_op jit(solution)/shard_map/reach/pallas_call | solution.py:95
  30.2 2.1 %return_states.1 = (f32[4,256,128]{2,1,0:T(8,128)S(1)}, bf16[4,128,256]{2,1,0:T(8,128)(2,1)S(1)}, bf16[4,128,256]{2,1,0:T(8,128)(2,1)S(1)}, bf16[4,128,128]{2,1,0:T(8,128)(2,1)S(1)}) custom-call(s32[2]{0:T(128)S(1)} %pad_add_fusion.place_ref, f32[256,128]{1,0:T(8,128)S(1)} %get-tuple-element.54.pack_ref.refs_1_.refs_2_, ...), custom_call_target="tpu_custom_call" | custom-call | tf_op jit(solution)/shard_map/return_states/pallas_call | solution.py:95
  32.3 0.7 collective-permute-start.10
  33.0 0.4 collective-permute-start.9
  33.5 0.8 %collective-permute-done.11.refs_3_ = bf16[4,128,128]{2,1,0:T(8,128)(2,1)S(1)} collective-permute-done((bf16[4,128,128]{2,1,0:T(8,128)(2,1)S(1)}, bf16[4,128,128]{2,1,0:T(8,128)(2,1)S(1)}, u32[]{:S(2)}, u32[]{:S(2)}) %collective-permute-start.11) | collective-permute-done | bytes 131104 | tf_op jit(solution)/shard_map/ppermute | solution.py:816
  34.7 1.3 %collective-permute-start.14 = (bf16[4,128,128]{2,1,0:T(8,128)(2,1)S(1)}, bf16[4,128,128]{2,1,0:T(8,128)(2,1)S(1)}, u32[]{:S(2)}, u32[]{:S(2)}) collective-permute-start(bf16[4,128,128]{2,1,0:T(8,128)(2,1)S(1)} %get-tuple-element.100), channel_id=1, source_target_pairs={{0,24},{4,28},{8,16},{12,20},{16,8},{20,12},{24,0},{28,4},{1,25},{... | collective-permute-start | bytes 393224 | tf_op jit(solution)/shard_map/ppermute | solution.py:816
  36.0 1.1 %collective-permute-start.13 = (bf16[4,128,128]{2,1,0:T(8,128)(2,1)S(1)}, bf16[4,128,128]{2,1,0:T(8,128)(2,1)S(1)}, u32[]{:S(2)}, u32[]{:S(2)}) collective-permute-start(bf16[4,128,128]{2,1,0:T(8,128)(2,1)S(1)} %get-tuple-element.100), channel_id=1, source_target_pairs={{0,16},{4,20},{8,24},{12,28},{16,0},{20,4},{24,8},{28,12},{1,17},{... | collective-permute-start | bytes 393224 | tf_op jit(solution)/shard_map/ppermute | solution.py:816
  37.1 3.5 %pull_local.1 = (f32[3,4,256,128]{3,2,1,0:T(8,128)S(1)}, f32[4,256,128]{2,1,0:T(8,128)S(1)}, f32[256,128]{1,0:T(8,128)S(1)}, f32[8,256]{1,0:T(8,128)S(1)}) custom-call(f32[3,4,256,128]{3,2,1,0:T(8,128)S(1)} %get-tuple-element.56.qkv_ref.refs_0_, f32[256,128]{1,0:T(8,128)S(1)} %get-tuple-element.54.pack_ref.refs_1_.refs_2_, ...), custom_call_target="tpu_custom_call" | custom-call | tf_op jit(solution)/shard_map/pull_local/pallas_call | solution.py:95
  40.6 2.5 %collective-permute-done.7.got_ref = bf16[2,256,512]{2,1,0:T(8,128)(2,1)S(1)} collective-permute-done((bf16[2,256,512]{2,1,0:T(8,128)(2,1)S(1)}, bf16[2,256,512]{2,1,0:T(8,128)(2,1)S(1)}, u32[]{:S(2)}, u32[]{:S(2)}) %collective-permute-start.7) | collective-permute-done | bytes 524320 | tf_op jit(solution)/shard_map/ppermute | solution.py:816
  43.3 2.4 %collective-permute-start.8 = (bf16[1,256,512]{2,1,0:T(8,128)(2,1)S(1)}, bf16[1,256,512]{2,1,0:T(8,128)(2,1)S(1)}, u32[]{:S(2)}, u32[]{:S(2)}) collective-permute-start(bf16[1,256,512]{2,1,0:T(8,128)(2,1)S(1)} %get-tuple-element.72), channel_id=1, source_target_pairs={{0,2},{1,3},{2,0},{3,1},{4,6},{5,7},{6,4},{7,5},{8,10},{9,11},{10,... | collective-permute-start | bytes 786440 | tf_op jit(solution)/shard_map/ppermute | solution.py:816
  45.7 9.9 %finish.1 = (bf16[256,512]{1,0:T(8,128)(2,1)S(1)}, bf16[256,512]{1,0:T(8,128)(2,1)S(1)}, bf16[256,512]{1,0:T(8,128)(2,1)S(1)}, bf16[256,512]{1,0:T(8,128)(2,1)S(1)}) custom-call(s32[2]{0:T(128)S(1)} %pad_add_fusion.place_ref, f32[3,4,256,128]{3,2,1,0:T(8,128)S(1)} %get-tuple-element.56.qkv_ref.refs_0_, f32[256,128]{1,0:T(8,128)S(1)} %get-tuple-element.73.refs_1_, ...), custom_call_target="tpu_custom_call" | custom-call | tf_op jit(solution)/shard_map/finish/pallas_call | solution.py:95
  55.6 1.7 %collective-permute-start.15 = (bf16[256,512]{1,0:T(8,128)(2,1)S(1)}, bf16[256,512]{1,0:T(8,128)(2,1)S(1)}, u32[]{:S(2)}, u32[]{:S(2)}) collective-permute-start(bf16[256,512]{1,0:T(8,128)(2,1)S(1)} %get-tuple-element.103), channel_id=1, source_target_pairs={{0,1},{1,2},{2,3},{3,0},{4,5},{5,6},{6,7},{7,4},{8,9},{9,10},{10,1... | collective-permute-start | bytes 786440 | tf_op jit(solution)/shard_map/ppermute | solution.py:836
  57.3 1.0 %collective-permute-start.16 = (bf16[256,512]{1,0:T(8,128)(2,1)S(1)}, bf16[256,512]{1,0:T(8,128)(2,1)S(1)}, u32[]{:S(2)}, u32[]{:S(2)}) collective-permute-start(bf16[256,512]{1,0:T(8,128)(2,1)S(1)} %get-tuple-element.104), channel_id=1, source_target_pairs={{0,2},{1,3},{2,0},{3,1},{4,6},{5,7},{6,4},{7,5},{8,10},{9,11},{10,... | collective-permute-start | bytes 786440 | tf_op jit(solution)/shard_map/ppermute | solution.py:836
  58.3 0.4 collective-permute-start.17
  58.7 0.7 sum_all.2
  59.5 2.6 %collective-permute-done.15.refs_1_ = bf16[256,512]{1,0:T(8,128)(2,1)S(1)} collective-permute-done((bf16[256,512]{1,0:T(8,128)(2,1)S(1)}, bf16[256,512]{1,0:T(8,128)(2,1)S(1)}, u32[]{:S(2)}, u32[]{:S(2)}) %collective-permute-start.15) | collective-permute-done | bytes 262176 | tf_op jit(solution)/shard_map/ppermute | solution.py:836
  62.0 16.6 %collective-permute-done.16.refs_2_ = bf16[256,512]{1,0:T(8,128)(2,1)S(1)} collective-permute-done((bf16[256,512]{1,0:T(8,128)(2,1)S(1)}, bf16[256,512]{1,0:T(8,128)(2,1)S(1)}, u32[]{:S(2)}, u32[]{:S(2)}) %collective-permute-start.16) | collective-permute-done | bytes 262176 | tf_op jit(solution)/shard_map/ppermute | solution.py:836
  78.6 3.4 %collective-permute-done.17.refs_3_ = bf16[256,512]{1,0:T(8,128)(2,1)S(1)} collective-permute-done((bf16[256,512]{1,0:T(8,128)(2,1)S(1)}, bf16[256,512]{1,0:T(8,128)(2,1)S(1)}, u32[]{:S(2)}, u32[]{:S(2)}) %collective-permute-start.17) | collective-permute-done | bytes 262176 | tf_op jit(solution)/shard_map/ppermute | solution.py:836
  82.0 0.8 %sum_all.3 = bf16[256,512]{1,0:T(8,128)(2,1)} custom-call(bf16[256,512]{1,0:T(8,128)(2,1)S(1)} %get-tuple-element.102.refs_0_, bf16[256,512]{1,0:T(8,128)(2,1)S(1)} %collective-permute-done.15.refs_1_, bf16[256,512]{1,0:T(8,128)(2,1)S(1)} %collective-permute-done.16.refs_2_, bf16[256,512]{1,0:T(8,128)(2,1)S(1)} %collective-permute-done.17.refs_3_), custom_call_target="tpu_custom_call" | custom-call | tf_op jit(solution)/shard_map/sum_all/pallas_call | solution.py:95
  (22 shorter events, 1.4 us)
Async XLA Ops:
  0.7 17.7 %copy-start = (bf16[4,128,2048]{2,1,0:T(8,128)(2,1)S(1)}, bf16[4,128,2048]{2,1,0:T(8,128)(2,1)}, u32[]{:S(2)}) copy-start(bf16[4,128,2048]{2,1,0:T(8,128)(2,1)} %param.12) | copy-start | bytes 6291460
  0.7 17.7 %copy-start.1 = (bf16[256,2048]{1,0:T(8,128)(2,1)S(1)}, bf16[256,2048]{1,0:T(8,128)(2,1)}, u32[]{:S(2)}) copy-start(bf16[256,2048]{1,0:T(8,128)(2,1)} %grad_ref.1) | copy-start | bytes 3145732
  13.0 1.9 %collective-permute-start = (bf16[4,128,256]{2,1,0:T(8,128)(2,1)S(1)}, bf16[4,128,256]{2,1,0:T(8,128)(2,1)S(1)}, u32[]{:S(2)}, u32[]{:S(2)}) collective-permute-start(bf16[4,128,256]{2,1,0:T(8,128)(2,1)S(1)} %get-tuple-element.55.own_ref), channel_id=1, source_target_pairs={{0,4},{4,0},{8,12},{12,8},{16,20},{20,16},{24,28},{28,24},{1,5},{5... | collective-permute-start | bytes 786440 | tf_op jit(solution)/shard_map/ppermute | solution.py:816
  15.6 5.7 %collective-permute-start.3 = (bf16[2,128,256]{2,1,0:T(8,128)(2,1)S(1)}, bf16[2,128,256]{2,1,0:T(8,128)(2,1)S(1)}, u32[]{:S(2)}, u32[]{:S(2)}) collective-permute-start(bf16[2,128,256]{2,1,0:T(8,128)(2,1)S(1)} %join_half.1), channel_id=1, source_target_pairs={{0,24},{4,28},{8,16},{12,20},{16,8},{20,12},{24,0},{28,4},{1,25},{... | collective-permute-start | bytes 393224 | tf_op jit(solution)/shard_map/ppermute | solution.py:816
  16.9 7.9 %collective-permute-start.2 = (bf16[2,128,256]{2,1,0:T(8,128)(2,1)S(1)}, bf16[2,128,256]{2,1,0:T(8,128)(2,1)S(1)}, u32[]{:S(2)}, u32[]{:S(2)}) collective-permute-start(bf16[2,128,256]{2,1,0:T(8,128)(2,1)S(1)} %join_half.1), channel_id=1, source_target_pairs={{0,16},{4,20},{8,24},{12,28},{16,0},{20,4},{24,8},{28,12},{1,17},{... | collective-permute-start | bytes 393224 | tf_op jit(solution)/shard_map/ppermute | solution.py:816
  17.2 7.7 %collective-permute-start.1 = (bf16[2,128,256]{2,1,0:T(8,128)(2,1)S(1)}, bf16[2,128,256]{2,1,0:T(8,128)(2,1)S(1)}, u32[]{:S(2)}, u32[]{:S(2)}) collective-permute-start(bf16[2,128,256]{2,1,0:T(8,128)(2,1)S(1)} %join_half.1), channel_id=1, source_target_pairs={{0,8},{4,12},{8,0},{12,4},{16,24},{20,28},{24,16},{28,20},{1,9},{5... | collective-permute-start | bytes 393224 | tf_op jit(solution)/shard_map/ppermute | solution.py:816
  18.4 8.6 %copy-start.2 = (f32[128]{0:T(128)S(1)}, f32[128]{0:T(128)}, u32[]{:S(2)}) copy-start(f32[128]{0:T(128)} %param.11) | copy-start | bytes 1540
  24.8 1.6 %collective-permute-start.4 = (bf16[2,128,256]{2,1,0:T(8,128)(2,1)S(1)}, bf16[2,128,256]{2,1,0:T(8,128)(2,1)S(1)}, u32[]{:S(2)}, u32[]{:S(2)}) collective-permute-start(bf16[2,128,256]{2,1,0:T(8,128)(2,1)S(1)} %collective-permute-done.1.refs_1_), channel_id=1, source_target_pairs={{0,4},{4,0},{8,12},{12,8},{16,20},{20,16},{24,28},{28,24},{1,5},{5... | collective-permute-start | bytes 393224 | tf_op jit(solution)/shard_map/ppermute | solution.py:816
  25.4 1.3 %collective-permute-start.5 = (bf16[2,128,256]{2,1,0:T(8,128)(2,1)S(1)}, bf16[2,128,256]{2,1,0:T(8,128)(2,1)S(1)}, u32[]{:S(2)}, u32[]{:S(2)}) collective-permute-start(bf16[2,128,256]{2,1,0:T(8,128)(2,1)S(1)} %collective-permute-done.2.refs_2_), channel_id=1, source_target_pairs={{0,4},{4,0},{8,12},{12,8},{16,20},{20,16},{24,28},{28,24},{1,5},{5... | collective-permute-start | bytes 393224 | tf_op jit(solution)/shard_map/ppermute | solution.py:816
  25.4 1.5 %collective-permute-start.6 = (bf16[2,128,256]{2,1,0:T(8,128)(2,1)S(1)}, bf16[2,128,256]{2,1,0:T(8,128)(2,1)S(1)}, u32[]{:S(2)}, u32[]{:S(2)}) collective-permute-start(bf16[2,128,256]{2,1,0:T(8,128)(2,1)S(1)} %collective-permute-done.3.refs_3_), channel_id=1, source_target_pairs={{0,4},{4,0},{8,12},{12,8},{16,20},{20,16},{24,28},{28,24},{1,5},{5... | collective-permute-start | bytes 393224 | tf_op jit(solution)/shard_map/ppermute | solution.py:816
  29.9 13.3 %collective-permute-start.7 = (bf16[2,256,512]{2,1,0:T(8,128)(2,1)S(1)}, bf16[2,256,512]{2,1,0:T(8,128)(2,1)S(1)}, u32[]{:S(2)}, u32[]{:S(2)}) collective-permute-start(bf16[2,256,512]{2,1,0:T(8,128)(2,1)S(1)} %get-tuple-element.70), channel_id=1, source_target_pairs={{0,1},{1,0},{2,3},{3,2},{4,5},{5,4},{6,7},{7,6},{8,9},{9,8},{10,11... | collective-permute-start | bytes 1572872 | tf_op jit(solution)/shard_map/ppermute | solution.py:816
  32.3 2.0 %collective-permute-start.10 = (bf16[4,128,256]{2,1,0:T(8,128)(2,1)S(1)}, bf16[4,128,256]{2,1,0:T(8,128)(2,1)S(1)}, u32[]{:S(2)}, u32[]{:S(2)}) collective-permute-start(bf16[4,128,256]{2,1,0:T(8,128)(2,1)S(1)} %get-tuple-element.97.refs_0_), channel_id=1, source_target_pairs={{0,4},{4,0},{8,12},{12,8},{16,20},{20,16},{24,28},{28,24},{1,5},{5... | collective-permute-start | bytes 786440 | tf_op jit(solution)/shard_map/ppermute | solution.py:816
  33.0 1.3 %collective-permute-start.11 = (bf16[4,128,128]{2,1,0:T(8,128)(2,1)S(1)}, bf16[4,128,128]{2,1,0:T(8,128)(2,1)S(1)}, u32[]{:S(2)}, u32[]{:S(2)}) collective-permute-start(bf16[4,128,128]{2,1,0:T(8,128)(2,1)S(1)} %get-tuple-element.98.refs_1_), channel_id=1, source_target_pairs={{0,4},{4,0},{8,12},{12,8},{16,20},{20,16},{24,28},{28,24},{1,5},{5... | collective-permute-start | bytes 393224 | tf_op jit(solution)/shard_map/ppermute | solution.py:816
  33.0 12.6 %collective-permute-start.9 = (bf16[4,128,256]{2,1,0:T(8,128)(2,1)S(1)}, bf16[4,128,256]{2,1,0:T(8,128)(2,1)S(1)}, u32[]{:S(2)}, u32[]{:S(2)}) collective-permute-start(bf16[4,128,256]{2,1,0:T(8,128)(2,1)S(1)} %get-tuple-element.96), channel_id=1, source_target_pairs={{0,4},{4,0},{8,12},{12,8},{16,20},{20,16},{24,28},{28,24},{1,5},{5... | collective-permute-start | bytes 786440 | tf_op jit(solution)/shard_map/ppermute | solution.py:816
  34.4 11.3 %collective-permute-start.12 = (bf16[4,128,256]{2,1,0:T(8,128)(2,1)S(1)}, bf16[4,128,256]{2,1,0:T(8,128)(2,1)S(1)}, u32[]{:S(2)}, u32[]{:S(2)}) collective-permute-start(bf16[4,128,256]{2,1,0:T(8,128)(2,1)S(1)} %get-tuple-element.99), channel_id=1, source_target_pairs={{0,8},{4,12},{8,0},{12,4},{16,24},{20,28},{24,16},{28,20},{1,9},{5... | collective-permute-start | bytes 786440 | tf_op jit(solution)/shard_map/ppermute | solution.py:816
  34.7 11.0 %collective-permute-start.14 = (bf16[4,128,128]{2,1,0:T(8,128)(2,1)S(1)}, bf16[4,128,128]{2,1,0:T(8,128)(2,1)S(1)}, u32[]{:S(2)}, u32[]{:S(2)}) collective-permute-start(bf16[4,128,128]{2,1,0:T(8,128)(2,1)S(1)} %get-tuple-element.100), channel_id=1, source_target_pairs={{0,24},{4,28},{8,16},{12,20},{16,8},{20,12},{24,0},{28,4},{1,25},{... | collective-permute-start | bytes 393224 | tf_op jit(solution)/shard_map/ppermute | solution.py:816
  36.0 9.7 %collective-permute-start.13 = (bf16[4,128,128]{2,1,0:T(8,128)(2,1)S(1)}, bf16[4,128,128]{2,1,0:T(8,128)(2,1)S(1)}, u32[]{:S(2)}, u32[]{:S(2)}) collective-permute-start(bf16[4,128,128]{2,1,0:T(8,128)(2,1)S(1)} %get-tuple-element.100), channel_id=1, source_target_pairs={{0,16},{4,20},{8,24},{12,28},{16,0},{20,4},{24,8},{28,12},{1,17},{... | collective-permute-start | bytes 393224 | tf_op jit(solution)/shard_map/ppermute | solution.py:816
  43.3 15.4 %collective-permute-start.8 = (bf16[1,256,512]{2,1,0:T(8,128)(2,1)S(1)}, bf16[1,256,512]{2,1,0:T(8,128)(2,1)S(1)}, u32[]{:S(2)}, u32[]{:S(2)}) collective-permute-start(bf16[1,256,512]{2,1,0:T(8,128)(2,1)S(1)} %get-tuple-element.72), channel_id=1, source_target_pairs={{0,2},{1,3},{2,0},{3,1},{4,6},{5,7},{6,4},{7,5},{8,10},{9,11},{10,... | collective-permute-start | bytes 786440 | tf_op jit(solution)/shard_map/ppermute | solution.py:816
  55.6 6.4 %collective-permute-start.15 = (bf16[256,512]{1,0:T(8,128)(2,1)S(1)}, bf16[256,512]{1,0:T(8,128)(2,1)S(1)}, u32[]{:S(2)}, u32[]{:S(2)}) collective-permute-start(bf16[256,512]{1,0:T(8,128)(2,1)S(1)} %get-tuple-element.103), channel_id=1, source_target_pairs={{0,1},{1,2},{2,3},{3,0},{4,5},{5,6},{6,7},{7,4},{8,9},{9,10},{10,1... | collective-permute-start | bytes 786440 | tf_op jit(solution)/shard_map/ppermute | solution.py:836
  57.3 21.3 %collective-permute-start.16 = (bf16[256,512]{1,0:T(8,128)(2,1)S(1)}, bf16[256,512]{1,0:T(8,128)(2,1)S(1)}, u32[]{:S(2)}, u32[]{:S(2)}) collective-permute-start(bf16[256,512]{1,0:T(8,128)(2,1)S(1)} %get-tuple-element.104), channel_id=1, source_target_pairs={{0,2},{1,3},{2,0},{3,1},{4,6},{5,7},{6,4},{7,5},{8,10},{9,11},{10,... | collective-permute-start | bytes 786440 | tf_op jit(solution)/shard_map/ppermute | solution.py:836
  58.3 23.7 %collective-permute-start.17 = (bf16[256,512]{1,0:T(8,128)(2,1)S(1)}, bf16[256,512]{1,0:T(8,128)(2,1)S(1)}, u32[]{:S(2)}, u32[]{:S(2)}) collective-permute-start(bf16[256,512]{1,0:T(8,128)(2,1)S(1)} %get-tuple-element.105), channel_id=1, source_target_pairs={{0,3},{1,0},{2,1},{3,2},{4,7},{5,4},{6,5},{7,6},{8,11},{9,8},{10,9... | collective-permute-start | bytes 786440 | tf_op jit(solution)/shard_map/ppermute | solution.py:836

commit v6 on v5

--- a/solution.py
+++ b/solution.py
@@ -180,7 +180,11 @@
     fetch_tokens = pltpu.make_async_copy(tokens_hbm, tokens, sems.at[chunks])
     fetch_small = pltpu.make_async_copy(small_hbm, small_in, sems.at[chunks + 1])
     fetch_rates = pltpu.make_async_copy(hp_hbm, hp_ref, sems.at[chunks + 2])
-    keep_weight = pltpu.make_async_copy(wr, wr_hbm, sems.at[chunks + 3])
+    half = width // 2
+    keeps = []
+    for at in range(6):
+        span = (pl.ds(at % 2 * half, half), pl.ds(at // 2 * heads * LANES, heads * LANES))
+        keeps.append(pltpu.make_async_copy(wr.at[span], wr_hbm.at[span], sems.at[chunks + 3 + at]))
     fetches = []
     for chunk in range(chunks):
         span = pl.ds(chunk * depth * cols, depth * cols)
@@ -267,12 +271,16 @@
         lower_ref[head] = lower.astype(BF16)
         lower_all.append(lower)
 
+    keeps[2].start()
+    keeps[3].start()
+
     def later():
         for part in (2, 0):
             for chunk in range(chunks):
                 extract(chunk, part)
                 if chunk % 4 == 3:
                     multiply(part, chunk - 3, chunk + 1)
+                    keeps[2 * part + chunk // 4].start()
                 if chunk % 2 == 1:
                     yield
 
@@ -286,7 +294,6 @@
         next(filler, None)
     for _ in filler:
         pass
-    keep_weight.start()
     mixed_all = []
     for head in range(heads):
         trans_ref[head] = trans_all[head]
@@ -310,7 +317,8 @@
     for head in range(heads):
         scales = scales + unit_of(0, head)[1]
     pack_ref[...] = jnp.where(lane < norm_col, pack, scales)
-    keep_weight.wait()
+    for keep in keeps:
+        keep.wait()
 
 
 def project(place, tokens, flat_w, small, head_param, heads, levels):
@@ -343,7 +351,7 @@
         pltpu.VMEM((LANES, width), F32),
         pltpu.VMEM((rows, cols * key), F32),
         pltpu.VMEM(head_param.shape, F32),
-        pltpu.SemaphoreType.DMA((chunks + 4,)),
+        pltpu.SemaphoreType.DMA((chunks + 9,)),
     ]
     return local_call(
         functools.partial(project_body, (heads, levels, chunks)), "project", 36, out_shape,
@@ -689,10 +697,18 @@
         arrived.append(refs[:found])
         refs = refs[found:]
     wr_hbm = refs[0]
-    out_refs = refs[1 : 1 + count]
-    dproj, wr_ref, sem = refs[1 + count :]
-    fetch = pltpu.make_async_copy(wr_hbm, wr_ref, sem)
-    fetch.start()
+    keep_ref, send_ref = refs[1:3]
+    direct_refs = refs[3 : 3 + count]
+    dproj, wr_ref, sems = refs[3 + count :]
+    size = wr_ref.shape[0] // count
+    order = [*far_first(count), 0]
+    spans, fetches = [], []
+    for at, mask in enumerate(order):
+        dest = place_ref[1] ^ mask
+        spans.append(pl.ds(pl.multiple_of(dest * size, size), size))
+        here, there = wr_hbm.at[spans[at], :], wr_ref.at[spans[at], :]
+        fetches.append(pltpu.make_async_copy(here, there, sems.at[at]))
+        fetches[at].start()
     rows = pack_ref.shape[0]
     key = qkv_ref.shape[3]
     decay_col = levels * heads
@@ -785,13 +801,13 @@
         jnp.where(lane < beta_col, -rate * dlog * slope, dcol * slope),
     )
     dgate = jnp.where(lane < norm_col, dgate, 0.0).astype(BF16)
-    fetch.wait()
-    size = out_refs[0].shape[1]
-    for shift in range(count):
-        dest = lax.rem(place_ref[1] + shift, count)
-        span = pl.ds(pl.multiple_of(dest * size, size), size)
-        part = mm_nt(dproj[...], wr_ref[span, :]) + mm(dgate, small_ref[:, span])
-        out_refs[shift][...] = part.astype(BF16)
+    half = size // 2
+    for at, mask in enumerate(order):
+        fetches[at].wait()
+        part = mm_nt(dproj[...], wr_ref[spans[at], :]) + mm(dgate, small_ref[:, spans[at]])
+        direct_refs[mask][...] = part[:, :half].astype(BF16)
+        target = send_ref if mask % 2 else keep_ref
+        target[mask // 2] = part[:, half:].astype(BF16)
 
 
 def finish(place, arrays, others, arrived, wr, levels, count):
@@ -802,13 +818,16 @@
     heads = arrays[0].shape[1]
     flat = [value for group in arrived for value in group]
     scratch = [
-        pltpu.VMEM((rows, cols), BF16), pltpu.VMEM(wr.shape, BF16), pltpu.SemaphoreType.DMA
+        pltpu.VMEM((rows, cols), BF16), pltpu.VMEM(wr.shape, BF16),
+        pltpu.SemaphoreType.DMA((count,)),
     ]
-    return local_call(
+    half = width // count // 2
+    out_shape = [kept((count // 2, rows, half), BF16)] * 2 + [kept((rows, half), BF16)] * count
+    got = local_call(
         functools.partial(finish_body, (heads, levels, far, count, counts)), "finish", 16,
-        [kept((rows, width // count), BF16)] * count,
-        [place], [*arrays, *others, *flat], scratch, [wr],
-    )
+        out_shape, [place], [*arrays, *others, *flat], scratch, [wr],
+    )
+    return got[0], got[1], got[2:]
 
 
 def swap(value, axis, mask):
@@ -816,25 +835,8 @@
     return lax.ppermute(value, axis, [(at, at ^ mask) for at in range(size)])
 
 
-def sum_body(*refs):
-    total = refs[0][...].astype(F32)
-    for ref in refs[1:-1]:
-        total = total + ref[...].astype(F32)
-    refs[-1][...] = total.astype(BF16)
-
-
-def sum_all(values, keep):
-    out = kept if keep else jax.ShapeDtypeStruct
-    return local_call(sum_body, "sum_all", 6, [out(values[0].shape, BF16)], [], values)[0]
-
-
-def shift_sum(parts, axis):
-    count = lax.axis_size(axis)
-    values = [parts[0]]
-    for shift in range(1, count):
-        pairs = [(at, (at + shift) % count) for at in range(count)]
-        values.append(lax.ppermute(parts[shift], axis, pairs))
-    return sum_all(values, False)
+def far_first(count):
+    return sorted(range(1, count), key=lambda mask: mask < count // 2)
 
 
 def halve_body(own_ref, got_ref, keep_ref, send_ref):
@@ -844,7 +846,7 @@
         target[at // 2] = total.astype(target.dtype)
 
 
-def halving_sum(keep, send, axis):
+def halving(keep, send, axis, tied):
     mask = 1
     while keep.shape[0] > 1:
         got = swap(send, axis, mask)
@@ -852,8 +854,33 @@
         keep, send = local_call(
             halve_body, "halve", 6, [kept(half, F32), kept(half, BF16)], [], [keep, got]
         )
+        send, tied = lax.optimization_barrier((send, tied))
         mask *= 2
-    return sum_all([keep, swap(send, axis, mask)], False)[0]
+    return keep, swap(send, axis, mask), tied
+
+
+def sum_body(count, *refs):
+    keep_ref, got_ref = refs[:2]
+    out_ref = refs[-1]
+    total = keep_ref[0].astype(F32) + got_ref[0].astype(F32)
+    if count == 0:
+        out_ref[...] = total.astype(BF16)
+        return
+    half = out_ref.shape[1] // 2
+    out_ref[:, half:] = total.astype(BF16)
+    total = refs[2][...].astype(F32)
+    for ref in refs[3:-1]:
+        total = total + ref[...].astype(F32)
+    out_ref[:, :half] = total.astype(BF16)
+
+
+def head_sum(keep, last, direct, got):
+    rows, cols = keep.shape[1:]
+    out = jax.ShapeDtypeStruct((rows, cols * (2 if direct else 1)), BF16)
+    return local_call(
+        functools.partial(sum_body, len(direct)), "head_sum", 6, [out], [],
+        [keep, last, *direct[:1], *got],
+    )[0]
 
 
 def on_device(tokens, qkv_weight, small_weight, head_param, norm_gain, out_weight, grad_out):
@@ -887,7 +914,6 @@
         place, [gain, pack, local_out, hat, grad_normed, flat_out], first, (mine, theirs),
         bits, far, count
     )
-    layer_out = halving_sum(*out_parts, "head")
     others = [first, *nodes]
     dhat, sends = return_states(place, pack, hat_t, dout, found, prefix, others, bits)
     got = [swap(value, "ctx", 1) for value in sends]
@@ -901,10 +927,14 @@
          dhat],
         levels, bits,
     )
+    keep_out, last_out, dcol = halving(*out_parts, "head", dcol)
     arrays = [qkv, gate, pack, trans, mixed, decay, base, lower, dqkv, dgrown, dcol, drow, dfar,
               rates_row, small_t]
-    parts = finish(place, arrays, others, arrived, wr, levels, count)
-    return layer_out, shift_sum(parts, "head")
+    keep, send, direct = finish(place, arrays, others, arrived, wr, levels, count)
+    direct, last_out = lax.optimization_barrier((direct, last_out))
+    got = [swap(direct[mask], "head", mask) for mask in far_first(count)]
+    keep, last, _ = halving(keep, send, "head", ())
+    return head_sum(keep_out, last_out, [], []), head_sum(keep, last, direct, got)
 
 
 def solution(mesh):

time: 82.9 us -> 81.3 us (0.981)
  the two profiles are of different devices: /device:TPU:11 before, /device:TPU:0 now
where the time goes in v6:
time: 81.3 us; the launch traced here: 81.2 us
  Pallas kernels  36.3 us (45%)
  waiting for transfers between devices  22.7 us (28%)
  starting transfers between devices  21.4 us (26%)
    pallas_call x12, Pallas kernels, local_call(): pl.pallas_call(body, out_shape=tuple(out_shape), in_specs=[SCALARS] * len...  36.3 us
    ppermute x20, waiting for transfers between devices, swap(): return lax.ppermute(value, axis, [(at, at ^ mask) for at in range(size)])  22.7 us
    ppermute x20, starting transfers between devices, swap(): return lax.ppermute(value, axis, [(at, at ^ mask) for at in range(size)])  21.4 us
  transfers between devices with their start and end apart: 20, of which 14 were waited for; matrix products, arithmetic and copies ran while one was open for 0% of the time, Pallas kernels for 25%

profile of v6, /device:TPU:0, one launch (start us, length us, event | category | flops | bytes accessed | tf_op | source)
XLA Modules:
  0.0 81.2 jit_solution(8338126947035334026)
XLA Ops:
  0.7 11.8 %project.1 = (bf16[2048,1536]{1,0:T(8,128)(2,1)}, bf16[128,2048]{1,0:T(8,128)(2,1)S(1)}, f32[3,4,256,128]{3,2,1,0:T(8,128)S(1)}, f32[256,128]{1,0:T(8,128)S(1)},...) custom-call(s32[2]{0:T(128)S(1)} %pad_add_fusion.place_ref, ...), custom_call_target="tpu_custom_call" | custom-call | tf_op jit(solution)/shard_map/project/pallas_call | solution.py:95
  12.5 0.5 collective-permute-start
  13.0 1.2 %collective-permute-done.other_ref.refs_0_.refs_15_ = bf16[4,128,256]{2,1,0:T(8,128)(2,1)S(1)} collective-permute-done((bf16[4,128,256]{2,1,0:T(8,128)(2,1)S(1)}, bf16[4,128,256]{2,1,0:T(8,128)(2,1)S(1)}, u32[]{:S(2)}, u32[]{:S(2)}) %collective-permute-start) | collective-permute-done | bytes 262176 | tf_op jit(solution)/shard_map/ppermute | solution.py:835
  14.2 0.7 join_half.1
  14.9 3.9 %collective-permute-start.3 = (bf16[2,128,256]{2,1,0:T(8,128)(2,1)S(1)}, bf16[2,128,256]{2,1,0:T(8,128)(2,1)S(1)}, u32[]{:S(2)}, u32[]{:S(2)}) collective-permute-start(bf16[2,128,256]{2,1,0:T(8,128)(2,1)S(1)} %join_half.1), channel_id=1, source_target_pairs={{0,24},{4,28},{8,16},{12,20},{16,8},{20,12},{24,0},{28,4},{1,25},{... | collective-permute-start | bytes 393224 | tf_op jit(solution)/shard_map/ppermute | solution.py:835
  18.8 0.5 collective-permute-start.2
  19.4 2.3 %local_part.1 = (bf16[4,256,256]{2,1,0:T(8,128)(2,1)S(1)}, bf16[4,256,256]{2,1,0:T(8,128)(2,1)S(1)}, bf16[4,256,256]{2,1,0:T(8,128)(2,1)S(1)}, bf16[4,256,256]{2...) custom-call(f32[3,4,256,128]{3,2,1,0:T(8,128)S(1)} %get-tuple-elemen, ...), custom_call_target="tpu_custom_call" | custom-call | tf_op jit(solution)/shard_map/local_part/pallas_call | solution.py:95
  21.7 1.0 %collective-permute-done.3.refs_3_ = bf16[2,128,256]{2,1,0:T(8,128)(2,1)S(1)} collective-permute-done((bf16[2,128,256]{2,1,0:T(8,128)(2,1)S(1)}, bf16[2,128,256]{2,1,0:T(8,128)(2,1)S(1)}, u32[]{:S(2)}, u32[]{:S(2)}) %collective-permute-start.3) | collective-permute-done | bytes 131104 | tf_op jit(solution)/shard_map/ppermute | solution.py:835
  22.7 2.7 %collective-permute-done.2.refs_2_ = bf16[2,128,256]{2,1,0:T(8,128)(2,1)S(1)} collective-permute-done((bf16[2,128,256]{2,1,0:T(8,128)(2,1)S(1)}, bf16[2,128,256]{2,1,0:T(8,128)(2,1)S(1)}, u32[]{:S(2)}, u32[]{:S(2)}) %collective-permute-start.2) | collective-permute-done | bytes 131104 | tf_op jit(solution)/shard_map/ppermute | solution.py:835
  26.2 0.8 %collective-permute-done.4.refs_4_ = bf16[2,128,256]{2,1,0:T(8,128)(2,1)S(1)} collective-permute-done((bf16[2,128,256]{2,1,0:T(8,128)(2,1)S(1)}, bf16[2,128,256]{2,1,0:T(8,128)(2,1)S(1)}, u32[]{:S(2)}, u32[]{:S(2)}) %collective-permute-start.4) | collective-permute-done | bytes 131104 | tf_op jit(solution)/shard_map/ppermute | solution.py:835
  27.5 3.0 %reach.1 = (bf16[2,256,512]{2,1,0:T(8,128)(2,1)S(1)}, bf16[2,256,512]{2,1,0:T(8,128)(2,1)S(1)}, f32[4,256,128]{2,1,0:T(8,128)S(1)}, bf16[4,128,384]{2,1,0:T(8,12...) custom-call(s32[2]{0:T(128)S(1)} %pad_add_fusion.place_ref, ...), custom_call_target="tpu_custom_call" | custom-call | tf_op jit(solution)/shard_map/reach/pallas_call | solution.py:95
  30.6 1.6 %collective-permute-start.7 = (bf16[2,256,512]{2,1,0:T(8,128)(2,1)S(1)}, bf16[2,256,512]{2,1,0:T(8,128)(2,1)S(1)}, u32[]{:S(2)}, u32[]{:S(2)}) collective-permute-start(bf16[2,256,512]{2,1,0:T(8,128)(2,1)S(1)} %get-tuple-element.81), channel_id=1, source_target_pairs={{0,1},{1,0},{2,3},{3,2},{4,5},{5,4},{6,7},{7,6},{8,9},{9,8},{10,11... | collective-permute-start | bytes 1572872 | tf_op jit(solution)/shard_map/ppermute | solution.py:835
  32.2 2.1 %return_states.1 = (f32[4,256,128]{2,1,0:T(8,128)S(1)}, bf16[4,128,256]{2,1,0:T(8,128)(2,1)S(1)}, bf16[4,128,256]{2,1,0:T(8,128)(2,1)S(1)}, bf16[4,128,128]{2,1,0:T(8,128)(2,1)S(1)}) custom-call(s32[2]{0:T(128)S(1)} %pad_add_fusion.place_ref, f32[256,128]{1,0:T(8,128)S(1)} %get-tuple-element.65.pack_ref.refs_1_.refs_2_, ...), custom_call_target="tpu_custom_call" | custom-call | tf_op jit(solution)/shard_map/return_states/pallas_call | solution.py:95
  35.0 1.1 %collective-permute-done.10.refs_3_ = bf16[4,128,128]{2,1,0:T(8,128)(2,1)S(1)} collective-permute-done((bf16[4,128,128]{2,1,0:T(8,128)(2,1)S(1)}, bf16[4,128,128]{2,1,0:T(8,128)(2,1)S(1)}, u32[]{:S(2)}, u32[]{:S(2)}) %collective-permute-start.10) | collective-permute-done | bytes 131104 | tf_op jit(solution)/shard_map/ppermute | solution.py:835
  36.2 1.6 %collective-permute-start.11 = (bf16[4,128,256]{2,1,0:T(8,128)(2,1)S(1)}, bf16[4,128,256]{2,1,0:T(8,128)(2,1)S(1)}, u32[]{:S(2)}, u32[]{:S(2)}) collective-permute-start(bf16[4,128,256]{2,1,0:T(8,128)(2,1)S(1)} %get-tuple-element.111), channel_id=1, source_target_pairs={{0,8},{4,12},{8,0},{12,4},{16,24},{20,28},{24,16},{28,20},{1,9},{5... | collective-permute-start | bytes 786440 | tf_op jit(solution)/shard_map/ppermute | solution.py:835
  37.8 1.4 %collective-permute-start.13 = (bf16[4,128,128]{2,1,0:T(8,128)(2,1)S(1)}, bf16[4,128,128]{2,1,0:T(8,128)(2,1)S(1)}, u32[]{:S(2)}, u32[]{:S(2)}) collective-permute-start(bf16[4,128,128]{2,1,0:T(8,128)(2,1)S(1)} %get-tuple-element.112), channel_id=1, source_target_pairs={{0,24},{4,28},{8,16},{12,20},{16,8},{20,12},{24,0},{28,4},{1,25},{... | collective-permute-start | bytes 393224 | tf_op jit(solution)/shard_map/ppermute | solution.py:835
  39.2 0.6 collective-permute-start.12
  39.7 3.5 %pull_local.1 = (f32[3,4,256,128]{3,2,1,0:T(8,128)S(1)}, f32[4,256,128]{2,1,0:T(8,128)S(1)}, f32[256,128]{1,0:T(8,128)S(1)}, f32[8,256]{1,0:T(8,128)S(1)}) custom-call(f32[3,4,256,128]{3,2,1,0:T(8,128)S(1)} %get-tuple-element.67.qkv_ref.refs_0_, f32[256,128]{1,0:T(8,128)S(1)} %get-tuple-element.65.pack_ref.refs_1_.refs_2_, ...), custom_call_target="tpu_custom_call" | custom-call | tf_op jit(solution)/shard_map/pull_local/pallas_call | solution.py:95
  43.3 1.4 %collective-permute-done.7.got_ref = bf16[2,256,512]{2,1,0:T(8,128)(2,1)S(1)} collective-permute-done((bf16[2,256,512]{2,1,0:T(8,128)(2,1)S(1)}, bf16[2,256,512]{2,1,0:T(8,128)(2,1)S(1)}, u32[]{:S(2)}, u32[]{:S(2)}) %collective-permute-start.7) | collective-permute-done | bytes 524320 | tf_op jit(solution)/shard_map/ppermute | solution.py:835
  44.8 2.7 %collective-permute-start.14 = (bf16[1,256,512]{2,1,0:T(8,128)(2,1)S(1)}, bf16[1,256,512]{2,1,0:T(8,128)(2,1)S(1)}, u32[]{:S(2)}, u32[]{:S(2)}) collective-permute-start(bf16[1,256,512]{2,1,0:T(8,128)(2,1)S(1)} %get-tuple-element.118), channel_id=1, source_target_pairs={{0,2},{1,3},{2,0},{3,1},{4,6},{5,7},{6,4},{7,5},{8,10},{9,11},{10,... | collective-permute-start | bytes 786440 | tf_op jit(solution)/shard_map/ppermute | solution.py:835
  47.4 0.9 %collective-permute-done.13.refs_21_ = bf16[4,128,128]{2,1,0:T(8,128)(2,1)S(1)} collective-permute-done((bf16[4,128,128]{2,1,0:T(8,128)(2,1)S(1)}, bf16[4,128,128]{2,1,0:T(8,128)(2,1)S(1)}, u32[]{:S(2)}, u32[]{:S(2)}) %collective-permute-start.13) | collective-permute-done | bytes 131104 | tf_op jit(solution)/shard_map/ppermute | solution.py:835
  48.3 11.1 %finish.1 = (bf16[2,256,256]{2,1,0:T(8,128)(2,1)S(1)}, bf16[2,256,256]{2,1,0:T(8,128)(2,1)S(1)}, bf16[256,256]{1,0:T(8,128)(2,1)S(1)}, bf16[256,256]{1,0:T(8,128...) custom-call(s32[2]{0:T(128)S(1)} %pad_add_fusion.place_ref, ...), custom_call_target="tpu_custom_call" | custom-call | tf_op jit(solution)/shard_map/finish/pallas_call | solution.py:95
  59.4 0.8 %collective-permute-start.15 = (bf16[2,256,256]{2,1,0:T(8,128)(2,1)S(1)}, bf16[2,256,256]{2,1,0:T(8,128)(2,1)S(1)}, u32[]{:S(2)}, u32[]{:S(2)}) collective-permute-start(bf16[2,256,256]{2,1,0:T(8,128)(2,1)S(1)} %get-tuple-element.121), channel_id=1, source_target_pairs={{0,1},{1,0},{2,3},{3,2},{4,5},{5,4},{6,7},{7,6},{8,9},{9,8},{10,11... | collective-permute-start | bytes 786440 | tf_op jit(solution)/shard_map/ppermute | solution.py:835
  60.2 2.3 %collective-permute-start.17 = (bf16[256,256]{1,0:T(8,128)(2,1)S(1)}, bf16[256,256]{1,0:T(8,128)(2,1)S(1)}, u32[]{:S(2)}, u32[]{:S(2)}) collective-permute-start(bf16[256,256]{1,0:T(8,128)(2,1)S(1)} %get-tuple-element.125), channel_id=1, source_target_pairs={{0,2},{1,3},{2,0},{3,1},{4,6},{5,7},{6,4},{7,5},{8,10},{9,11},{10,... | collective-permute-start | bytes 393224 | tf_op jit(solution)/shard_map/ppermute | solution.py:835
  62.5 1.3 %collective-permute-start.18 = (bf16[256,256]{1,0:T(8,128)(2,1)S(1)}, bf16[256,256]{1,0:T(8,128)(2,1)S(1)}, u32[]{:S(2)}, u32[]{:S(2)}) collective-permute-start(bf16[256,256]{1,0:T(8,128)(2,1)S(1)} %get-tuple-element.126), channel_id=1, source_target_pairs={{0,3},{1,2},{2,1},{3,0},{4,7},{5,6},{6,5},{7,4},{8,11},{9,10},{10,... | collective-permute-start | bytes 393224 | tf_op jit(solution)/shard_map/ppermute | solution.py:835
  64.1 8.0 %collective-permute-done.15.got_ref = bf16[2,256,256]{2,1,0:T(8,128)(2,1)S(1)} collective-permute-done((bf16[2,256,256]{2,1,0:T(8,128)(2,1)S(1)}, bf16[2,256,256]{2,1,0:T(8,128)(2,1)S(1)}, u32[]{:S(2)}, u32[]{:S(2)}) %collective-permute-start.15) | collective-permute-done | bytes 262176 | tf_op jit(solution)/shard_map/ppermute | solution.py:835
  72.1 2.7 %collective-permute-start.16 = (bf16[1,256,256]{2,1,0:T(8,128)(2,1)S(1)}, bf16[1,256,256]{2,1,0:T(8,128)(2,1)S(1)}, u32[]{:S(2)}, u32[]{:S(2)}) collective-permute-start(bf16[1,256,256]{2,1,0:T(8,128)(2,1)S(1)} %get-tuple-element.123), channel_id=1, source_target_pairs={{0,2},{1,3},{2,0},{3,1},{4,6},{5,7},{6,4},{7,5},{8,10},{9,11},{10,... | collective-permute-start | bytes 393224 | tf_op jit(solution)/shard_map/ppermute | solution.py:835
  74.8 0.7 head_sum.2
  75.5 0.8 collective-permute-done.18.refs_4_
  76.3 0.6 collective-permute-done.19.refs_5_
  77.0 3.4 %collective-permute-done.16.refs_1_ = bf16[1,256,256]{2,1,0:T(8,128)(2,1)S(1)} collective-permute-done((bf16[1,256,256]{2,1,0:T(8,128)(2,1)S(1)}, bf16[1,256,256]{2,1,0:T(8,128)(2,1)S(1)}, u32[]{:S(2)}, u32[]{:S(2)}) %collective-permute-start.16) | collective-permute-done | bytes 131104 | tf_op jit(solution)/shard_map/ppermute | solution.py:835
  80.4 0.8 head_sum.3
  (27 shorter events, 2.7 us)
Async XLA Ops:
  0.7 18.7 %copy-start = (bf16[4,128,2048]{2,1,0:T(8,128)(2,1)S(1)}, bf16[4,128,2048]{2,1,0:T(8,128)(2,1)}, u32[]{:S(2)}) copy-start(bf16[4,128,2048]{2,1,0:T(8,128)(2,1)} %param.12) | copy-start | bytes 6291460
  0.7 18.7 %copy-start.1 = (bf16[256,2048]{1,0:T(8,128)(2,1)S(1)}, bf16[256,2048]{1,0:T(8,128)(2,1)}, u32[]{:S(2)}) copy-start(bf16[256,2048]{1,0:T(8,128)(2,1)} %grad_ref.1) | copy-start | bytes 3145732
  12.5 1.7 %collective-permute-start = (bf16[4,128,256]{2,1,0:T(8,128)(2,1)S(1)}, bf16[4,128,256]{2,1,0:T(8,128)(2,1)S(1)}, u32[]{:S(2)}, u32[]{:S(2)}) collective-permute-start(bf16[4,128,256]{2,1,0:T(8,128)(2,1)S(1)} %get-tuple-element.66.own_ref), channel_id=1, source_target_pairs={{0,4},{4,0},{8,12},{12,8},{16,20},{20,16},{24,28},{28,24},{1,5},{5... | collective-permute-start | bytes 786440 | tf_op jit(solution)/shard_map/ppermute | solution.py:835
  14.9 7.8 %collective-permute-start.3 = (bf16[2,128,256]{2,1,0:T(8,128)(2,1)S(1)}, bf16[2,128,256]{2,1,0:T(8,128)(2,1)S(1)}, u32[]{:S(2)}, u32[]{:S(2)}) collective-permute-start(bf16[2,128,256]{2,1,0:T(8,128)(2,1)S(1)} %join_half.1), channel_id=1, source_target_pairs={{0,24},{4,28},{8,16},{12,20},{16,8},{20,12},{24,0},{28,4},{1,25},{... | collective-permute-start | bytes 393224 | tf_op jit(solution)/shard_map/ppermute | solution.py:835
  18.8 6.6 %collective-permute-start.2 = (bf16[2,128,256]{2,1,0:T(8,128)(2,1)S(1)}, bf16[2,128,256]{2,1,0:T(8,128)(2,1)S(1)}, u32[]{:S(2)}, u32[]{:S(2)}) collective-permute-start(bf16[2,128,256]{2,1,0:T(8,128)(2,1)S(1)} %join_half.1), channel_id=1, source_target_pairs={{0,16},{4,20},{8,24},{12,28},{16,0},{20,4},{24,8},{28,12},{1,17},{... | collective-permute-start | bytes 393224 | tf_op jit(solution)/shard_map/ppermute | solution.py:835
  19.3 6.4 %collective-permute-start.1 = (bf16[2,128,256]{2,1,0:T(8,128)(2,1)S(1)}, bf16[2,128,256]{2,1,0:T(8,128)(2,1)S(1)}, u32[]{:S(2)}, u32[]{:S(2)}) collective-permute-start(bf16[2,128,256]{2,1,0:T(8,128)(2,1)S(1)} %join_half.1), channel_id=1, source_target_pairs={{0,8},{4,12},{8,0},{12,4},{16,24},{20,28},{24,16},{28,20},{1,9},{5... | collective-permute-start | bytes 393224 | tf_op jit(solution)/shard_map/ppermute | solution.py:835
  19.4 8.1 %copy-start.2 = (f32[128]{0:T(128)S(1)}, f32[128]{0:T(128)}, u32[]{:S(2)}) copy-start(f32[128]{0:T(128)} %param.11) | copy-start | bytes 1540
  25.6 1.3 %collective-permute-start.4 = (bf16[2,128,256]{2,1,0:T(8,128)(2,1)S(1)}, bf16[2,128,256]{2,1,0:T(8,128)(2,1)S(1)}, u32[]{:S(2)}, u32[]{:S(2)}) collective-permute-start(bf16[2,128,256]{2,1,0:T(8,128)(2,1)S(1)} %collective-permute-done.1.refs_1_), channel_id=1, source_target_pairs={{0,4},{4,0},{8,12},{12,8},{16,20},{20,16},{24,28},{28,24},{1,5},{5... | collective-permute-start | bytes 393224 | tf_op jit(solution)/shard_map/ppermute | solution.py:835
  25.6 1.5 %collective-permute-start.5 = (bf16[2,128,256]{2,1,0:T(8,128)(2,1)S(1)}, bf16[2,128,256]{2,1,0:T(8,128)(2,1)S(1)}, u32[]{:S(2)}, u32[]{:S(2)}) collective-permute-start(bf16[2,128,256]{2,1,0:T(8,128)(2,1)S(1)} %collective-permute-done.2.refs_2_), channel_id=1, source_target_pairs={{0,4},{4,0},{8,12},{12,8},{16,20},{20,16},{24,28},{28,24},{1,5},{5... | collective-permute-start | bytes 393224 | tf_op jit(solution)/shard_map/ppermute | solution.py:835
  26.2 1.3 %collective-permute-start.6 = (bf16[2,128,256]{2,1,0:T(8,128)(2,1)S(1)}, bf16[2,128,256]{2,1,0:T(8,128)(2,1)S(1)}, u32[]{:S(2)}, u32[]{:S(2)}) collective-permute-start(bf16[2,128,256]{2,1,0:T(8,128)(2,1)S(1)} %collective-permute-done.3.refs_3_), channel_id=1, source_target_pairs={{0,4},{4,0},{8,12},{12,8},{16,20},{20,16},{24,28},{28,24},{1,5},{5... | collective-permute-start | bytes 393224 | tf_op jit(solution)/shard_map/ppermute | solution.py:835
  30.6 14.1 %collective-permute-start.7 = (bf16[2,256,512]{2,1,0:T(8,128)(2,1)S(1)}, bf16[2,256,512]{2,1,0:T(8,128)(2,1)S(1)}, u32[]{:S(2)}, u32[]{:S(2)}) collective-permute-start(bf16[2,256,512]{2,1,0:T(8,128)(2,1)S(1)} %get-tuple-element.81), channel_id=1, source_target_pairs={{0,1},{1,0},{2,3},{3,2},{4,5},{5,4},{6,7},{7,6},{8,9},{9,8},{10,11... | collective-permute-start | bytes 1572872 | tf_op jit(solution)/shard_map/ppermute | solution.py:835
  34.3 1.8 %collective-permute-start.9 = (bf16[4,128,256]{2,1,0:T(8,128)(2,1)S(1)}, bf16[4,128,256]{2,1,0:T(8,128)(2,1)S(1)}, u32[]{:S(2)}, u32[]{:S(2)}) collective-permute-start(bf16[4,128,256]{2,1,0:T(8,128)(2,1)S(1)} %get-tuple-element.109.refs_0_), channel_id=1, source_target_pairs={{0,4},{4,0},{8,12},{12,8},{16,20},{20,16},{24,28},{28,24},{1,5},{5... | collective-permute-start | bytes 786440 | tf_op jit(solution)/shard_map/ppermute | solution.py:835
  34.4 1.7 %collective-permute-start.10 = (bf16[4,128,128]{2,1,0:T(8,128)(2,1)S(1)}, bf16[4,128,128]{2,1,0:T(8,128)(2,1)S(1)}, u32[]{:S(2)}, u32[]{:S(2)}) collective-permute-start(bf16[4,128,128]{2,1,0:T(8,128)(2,1)S(1)} %get-tuple-element.110.refs_1_), channel_id=1, source_target_pairs={{0,4},{4,0},{8,12},{12,8},{16,20},{20,16},{24,28},{28,24},{1,5},{5... | collective-permute-start | bytes 393224 | tf_op jit(solution)/shard_map/ppermute | solution.py:835
  34.9 12.5 %collective-permute-start.8 = (bf16[4,128,256]{2,1,0:T(8,128)(2,1)S(1)}, bf16[4,128,256]{2,1,0:T(8,128)(2,1)S(1)}, u32[]{:S(2)}, u32[]{:S(2)}) collective-permute-start(bf16[4,128,256]{2,1,0:T(8,128)(2,1)S(1)} %get-tuple-element.108), channel_id=1, source_target_pairs={{0,4},{4,0},{8,12},{12,8},{16,20},{20,16},{24,28},{28,24},{1,5},{5... | collective-permute-start | bytes 786440 | tf_op jit(solution)/shard_map/ppermute | solution.py:835
  36.2 12.1 %collective-permute-start.11 = (bf16[4,128,256]{2,1,0:T(8,128)(2,1)S(1)}, bf16[4,128,256]{2,1,0:T(8,128)(2,1)S(1)}, u32[]{:S(2)}, u32[]{:S(2)}) collective-permute-start(bf16[4,128,256]{2,1,0:T(8,128)(2,1)S(1)} %get-tuple-element.111), channel_id=1, source_target_pairs={{0,8},{4,12},{8,0},{12,4},{16,24},{20,28},{24,16},{28,20},{1,9},{5... | collective-permute-start | bytes 786440 | tf_op jit(solution)/shard_map/ppermute | solution.py:835
  37.8 10.5 %collective-permute-start.13 = (bf16[4,128,128]{2,1,0:T(8,128)(2,1)S(1)}, bf16[4,128,128]{2,1,0:T(8,128)(2,1)S(1)}, u32[]{:S(2)}, u32[]{:S(2)}) collective-permute-start(bf16[4,128,128]{2,1,0:T(8,128)(2,1)S(1)} %get-tuple-element.112), channel_id=1, source_target_pairs={{0,24},{4,28},{8,16},{12,20},{16,8},{20,12},{24,0},{28,4},{1,25},{... | collective-permute-start | bytes 393224 | tf_op jit(solution)/shard_map/ppermute | solution.py:835
  39.2 9.1 %collective-permute-start.12 = (bf16[4,128,128]{2,1,0:T(8,128)(2,1)S(1)}, bf16[4,128,128]{2,1,0:T(8,128)(2,1)S(1)}, u32[]{:S(2)}, u32[]{:S(2)}) collective-permute-start(bf16[4,128,128]{2,1,0:T(8,128)(2,1)S(1)} %get-tuple-element.112), channel_id=1, source_target_pairs={{0,16},{4,20},{8,24},{12,28},{16,0},{20,4},{24,8},{28,12},{1,17},{... | collective-permute-start | bytes 393224 | tf_op jit(solution)/shard_map/ppermute | solution.py:835
  44.8 15.5 %collective-permute-start.14 = (bf16[1,256,512]{2,1,0:T(8,128)(2,1)S(1)}, bf16[1,256,512]{2,1,0:T(8,128)(2,1)S(1)}, u32[]{:S(2)}, u32[]{:S(2)}) collective-permute-start(bf16[1,256,512]{2,1,0:T(8,128)(2,1)S(1)} %get-tuple-element.118), channel_id=1, source_target_pairs={{0,2},{1,3},{2,0},{3,1},{4,6},{5,7},{6,4},{7,5},{8,10},{9,11},{10,... | collective-permute-start | bytes 786440 | tf_op jit(solution)/shard_map/ppermute | solution.py:835
  59.4 12.7 %collective-permute-start.15 = (bf16[2,256,256]{2,1,0:T(8,128)(2,1)S(1)}, bf16[2,256,256]{2,1,0:T(8,128)(2,1)S(1)}, u32[]{:S(2)}, u32[]{:S(2)}) collective-permute-start(bf16[2,256,256]{2,1,0:T(8,128)(2,1)S(1)} %get-tuple-element.121), channel_id=1, source_target_pairs={{0,1},{1,0},{2,3},{3,2},{4,5},{5,4},{6,7},{7,6},{8,9},{9,8},{10,11... | collective-permute-start | bytes 786440 | tf_op jit(solution)/shard_map/ppermute | solution.py:835
  60.2 15.3 %collective-permute-start.17 = (bf16[256,256]{1,0:T(8,128)(2,1)S(1)}, bf16[256,256]{1,0:T(8,128)(2,1)S(1)}, u32[]{:S(2)}, u32[]{:S(2)}) collective-permute-start(bf16[256,256]{1,0:T(8,128)(2,1)S(1)} %get-tuple-element.125), channel_id=1, source_target_pairs={{0,2},{1,3},{2,0},{3,1},{4,6},{5,7},{6,4},{7,5},{8,10},{9,11},{10,... | collective-permute-start | bytes 393224 | tf_op jit(solution)/shard_map/ppermute | solution.py:835
  62.5 13.8 %collective-permute-start.18 = (bf16[256,256]{1,0:T(8,128)(2,1)S(1)}, bf16[256,256]{1,0:T(8,128)(2,1)S(1)}, u32[]{:S(2)}, u32[]{:S(2)}) collective-permute-start(bf16[256,256]{1,0:T(8,128)(2,1)S(1)} %get-tuple-element.126), channel_id=1, source_target_pairs={{0,3},{1,2},{2,1},{3,0},{4,7},{5,6},{6,5},{7,4},{8,11},{9,10},{10,... | collective-permute-start | bytes 393224 | tf_op jit(solution)/shard_map/ppermute | solution.py:835
  63.8 13.1 %collective-permute-start.19 = (bf16[256,256]{1,0:T(8,128)(2,1)S(1)}, bf16[256,256]{1,0:T(8,128)(2,1)S(1)}, u32[]{:S(2)}, u32[]{:S(2)}) collective-permute-start(bf16[256,256]{1,0:T(8,128)(2,1)S(1)} %get-tuple-element.127), channel_id=1, source_target_pairs={{0,1},{1,0},{2,3},{3,2},{4,5},{5,4},{6,7},{7,6},{8,9},{9,8},{10,11... | collective-permute-start | bytes 393224 | tf_op jit(solution)/shard_map/ppermute | solution.py:835
  72.1 8.3 %collective-permute-start.16 = (bf16[1,256,256]{2,1,0:T(8,128)(2,1)S(1)}, bf16[1,256,256]{2,1,0:T(8,128)(2,1)S(1)}, u32[]{:S(2)}, u32[]{:S(2)}) collective-permute-start(bf16[1,256,256]{2,1,0:T(8,128)(2,1)S(1)} %get-tuple-element.123), channel_id=1, source_target_pairs={{0,2},{1,3},{2,0},{3,1},{4,6},{5,7},{6,4},{7,5},{8,10},{9,11},{10,... | collective-permute-start | bytes 393224 | tf_op jit(solution)/shard_map/ppermute | solution.py:835

commit v7 on v6

--- a/solution.py
+++ b/solution.py
@@ -173,29 +173,32 @@
     heads, levels, chunks = sizes
     (wr_hbm, small_ref, qkv_ref, gate_ref, pack_ref, pack_t_ref, trans_ref, mixed_t_ref,
      decay_ref, base_ref, lower_ref, rates_ref, pair_ref) = refs[:13]
-    tokens, wide_in, wide, wr, small_in, small_wide, acc, hp_ref, sems = refs[13:]
+    tokens, raw_q, raw_k, raw_v, wide_q, wide_k, wide_v, wr = refs[13:21]
+    small_in, small_wide, acc, hp_ref, sems, in_sems, out_sems = refs[21:]
+    raw, wide = (raw_q, raw_k, raw_v), (wide_q, wide_k, wide_v)
     rows, width = tokens.shape
     depth = width // chunks
-    cols = 3 * heads
-    fetch_tokens = pltpu.make_async_copy(tokens_hbm, tokens, sems.at[chunks])
-    fetch_small = pltpu.make_async_copy(small_hbm, small_in, sems.at[chunks + 1])
-    fetch_rates = pltpu.make_async_copy(hp_hbm, hp_ref, sems.at[chunks + 2])
-    half = width // 2
-    keeps = []
-    for at in range(6):
-        span = (pl.ds(at % 2 * half, half), pl.ds(at // 2 * heads * LANES, heads * LANES))
-        keeps.append(pltpu.make_async_copy(wr.at[span], wr_hbm.at[span], sems.at[chunks + 3 + at]))
-    fetches = []
-    for chunk in range(chunks):
-        span = pl.ds(chunk * depth * cols, depth * cols)
-        fetches.append(
-            pltpu.make_async_copy(w_hbm.at[span, :], wide_in.at[span, :], sems.at[chunk])
-        )
+    fetch_tokens = pltpu.make_async_copy(tokens_hbm, tokens, sems.at[0])
+    fetch_small = pltpu.make_async_copy(small_hbm, small_in, sems.at[1])
+    fetch_rates = pltpu.make_async_copy(hp_hbm, hp_ref, sems.at[2])
+    fetches, keeps = {}, {}
+    for part in range(3):
+        for chunk in range(chunks):
+            span = pl.ds(chunk * depth, depth)
+            at = part * chunks + chunk
+            fetches[part, chunk] = pltpu.make_async_copy(
+                w_hbm.at[span, part], raw[part].at[span], in_sems.at[at]
+            )
+            block = (span, pl.ds(part * heads * LANES, heads * LANES))
+            keeps[part, chunk] = pltpu.make_async_copy(
+                wr.at[block], wr_hbm.at[block], out_sems.at[at]
+            )
     fetch_small.start()
     fetch_rates.start()
-    fetch_tokens.start()
-    for fetch in fetches:
-        fetch.start()
+    fetch_tokens.start(priority=1)
+    for part in (1, 2, 0):
+        for chunk in range(chunks):
+            fetches[part, chunk].start(priority=chunk % 2)
     decay_col = levels * heads
     beta_col = decay_col + heads
     norm_col = beta_col + heads
@@ -225,30 +228,27 @@
     pack_t = pack.T
     pack_t_ref[...] = pack_t
 
-    def extract(chunk, part):
-        at = chunk * depth
-        for col in range(part * heads, (part + 1) * heads):
-            value = wide[pl.ds(at * cols + col, depth, stride=cols), :]
-            wr[at : at + depth, col * LANES : (col + 1) * LANES] = value.astype(BF16)
-
-    def multiply(part, first, last):
-        span = slice((part * heads) * LANES, (part + 1) * heads * LANES)
-        own = jnp.dot(
-            tokens[:, first * depth : last * depth], wr[first * depth : last * depth, span],
-            preferred_element_type=F32,
+    def extract(part, chunk):
+        fetches[part, chunk].wait()
+        first, last = chunk * depth, (chunk + 1) * depth
+        flat = raw[part].reshape(width * heads, LANES)
+        wide[part][first * heads : last * heads, :] = (
+            flat[first * heads : last * heads, :].astype(F32)
         )
-        if first == 0:
+        for head in range(heads):
+            value = wide[part][pl.ds(first * heads + head, depth, stride=heads), :]
+            col = (part * heads + head) * LANES
+            wr[first:last, col : col + LANES] = value.astype(BF16)
+        keeps[part, chunk].start(priority=chunk % 2)
+        span = slice(part * heads * LANES, (part + 1) * heads * LANES)
+        own = jnp.dot(tokens[:, first:last], wr[first:last, span], preferred_element_type=F32)
+        if chunk == 0:
             acc[:, span] = own
         else:
             acc[:, span] += own
 
     for chunk in range(chunks):
-        fetches[chunk].wait()
-        at = chunk * depth * cols
-        wide[at : at + depth * cols, :] = wide_in[at : at + depth * cols, :].astype(F32)
-        extract(chunk, 1)
-        if chunk % 2 == 1:
-            multiply(1, chunk - 1, chunk + 1)
+        extract(1, chunk)
 
     def unit_of(part, head):
         col = (part * heads + head) * LANES
@@ -271,18 +271,11 @@
         lower_ref[head] = lower.astype(BF16)
         lower_all.append(lower)
 
-    keeps[2].start()
-    keeps[3].start()
-
     def later():
         for part in (2, 0):
             for chunk in range(chunks):
-                extract(chunk, part)
-                if chunk % 4 == 3:
-                    multiply(part, chunk - 3, chunk + 1)
-                    keeps[2 * part + chunk // 4].start()
-                if chunk % 2 == 1:
-                    yield
+                yield
+                extract(part, chunk)
 
     chain, filler = invert(lower_all, eye, apart, rows), later()
     while True:
@@ -317,15 +310,15 @@
     for head in range(heads):
         scales = scales + unit_of(0, head)[1]
     pack_ref[...] = jnp.where(lane < norm_col, pack, scales)
-    for keep in keeps:
+    for keep in keeps.values():
         keep.wait()
 
 
-def project(place, tokens, flat_w, small, head_param, heads, levels):
+def project(place, tokens, weight, small, head_param, heads, levels):
     rows, width = tokens.shape
-    chunks = 8
+    chunks = 4
     cols = 3 * heads
-    key = flat_w.shape[1]
+    key = weight.shape[3]
     square = (heads, rows, rows)
     out_shape = (
         stored((width, cols * key), BF16),
@@ -344,18 +337,20 @@
     )
     scratch = [
         pltpu.VMEM(tokens.shape, BF16),
-        pltpu.VMEM(flat_w.shape, BF16),
-        pltpu.VMEM(flat_w.shape, F32),
+        *[pltpu.VMEM((width, heads, key), BF16) for part in range(3)],
+        *[pltpu.VMEM((width * heads, key), F32) for part in range(3)],
         pltpu.VMEM((width, cols * key), BF16),
         pltpu.VMEM(small.shape, BF16),
         pltpu.VMEM((LANES, width), F32),
         pltpu.VMEM((rows, cols * key), F32),
         pltpu.VMEM(head_param.shape, F32),
-        pltpu.SemaphoreType.DMA((chunks + 9,)),
+        pltpu.SemaphoreType.DMA((3,)),
+        pltpu.SemaphoreType.DMA((3 * chunks,)),
+        pltpu.SemaphoreType.DMA((3 * chunks,)),
     ]
     return local_call(
         functools.partial(project_body, (heads, levels, chunks)), "project", 36, out_shape,
-        [place], [], scratch, [head_param, tokens, flat_w, small], [HBM] + [WHOLE] * 12,
+        [place], [], scratch, [head_param, tokens, weight, small], [HBM] + [WHOLE] * 12,
     )
 
 
@@ -687,28 +682,16 @@
 
 
 def finish_body(sizes, place_ref, *refs):
-    heads, levels, far, count, arrived_counts = sizes
+    heads, levels, far, arrived_counts = sizes
     (qkv_ref, gate_ref, pack_ref, trans_ref, mixed_ref, decay_ref, base_ref, lower_ref,
-     dqkv_ref, dgrown_ref, dcol_ref, drow_ref, dfar_ref, rates_ref, small_ref) = refs[:15]
-    others = refs[15 : 15 + far]
-    refs = refs[15 + far :]
+     dqkv_ref, dgrown_ref, dcol_ref, drow_ref, dfar_ref, rates_ref) = refs[:14]
+    others = refs[14 : 14 + far]
+    refs = refs[14 + far :]
     arrived = []
     for found in arrived_counts:
         arrived.append(refs[:found])
         refs = refs[found:]
-    wr_hbm = refs[0]
-    keep_ref, send_ref = refs[1:3]
-    direct_refs = refs[3 : 3 + count]
-    dproj, wr_ref, sems = refs[3 + count :]
-    size = wr_ref.shape[0] // count
-    order = [*far_first(count), 0]
-    spans, fetches = [], []
-    for at, mask in enumerate(order):
-        dest = place_ref[1] ^ mask
-        spans.append(pl.ds(pl.multiple_of(dest * size, size), size))
-        here, there = wr_hbm.at[spans[at], :], wr_ref.at[spans[at], :]
-        fetches.append(pltpu.make_async_copy(here, there, sems.at[at]))
-        fetches[at].start()
+    dproj, dgate_ref = refs
     rows = pack_ref.shape[0]
     key = qkv_ref.shape[3]
     decay_col = levels * heads
@@ -800,32 +783,41 @@
         dcol * switch,
         jnp.where(lane < beta_col, -rate * dlog * slope, dcol * slope),
     )
-    dgate = jnp.where(lane < norm_col, dgate, 0.0).astype(BF16)
+    dgate_ref[...] = jnp.where(lane < norm_col, dgate, 0.0).astype(BF16)
+
+
+def finish(place, arrays, others, arrived, levels):
+    heads, rows, key = arrays[0].shape[1:]
+    counts = tuple(len(group) for group in arrived)
+    flat = [value for group in arrived for value in group]
+    return local_call(
+        functools.partial(finish_body, (heads, levels, len(others), counts)), "finish", 10,
+        [kept((rows, 3 * heads * key), BF16), kept((rows, LANES), BF16)],
+        [place], [*arrays, *others, *flat],
+    )
+
+
+def tokens_body(count, place_ref, dproj_ref, dgate_ref, wr_ref, small_ref, *refs):
+    keep_ref, send_ref = refs[:2]
+    direct_refs = refs[2:]
+    size = wr_ref.shape[0] // count
     half = size // 2
-    for at, mask in enumerate(order):
-        fetches[at].wait()
-        part = mm_nt(dproj[...], wr_ref[spans[at], :]) + mm(dgate, small_ref[:, spans[at]])
+    for mask in range(count):
+        dest = place_ref[1] ^ mask
+        span = pl.ds(pl.multiple_of(dest * size, size), size)
+        part = mm_nt(dproj_ref[...], wr_ref[span, :]) + mm(dgate_ref[...], small_ref[:, span])
         direct_refs[mask][...] = part[:, :half].astype(BF16)
         target = send_ref if mask % 2 else keep_ref
         target[mask // 2] = part[:, half:].astype(BF16)
 
 
-def finish(place, arrays, others, arrived, wr, levels, count):
-    rows = arrays[0].shape[2]
-    width, cols = wr.shape
-    far = len(others)
-    counts = tuple(len(group) for group in arrived)
-    heads = arrays[0].shape[1]
-    flat = [value for group in arrived for value in group]
-    scratch = [
-        pltpu.VMEM((rows, cols), BF16), pltpu.VMEM(wr.shape, BF16),
-        pltpu.SemaphoreType.DMA((count,)),
-    ]
-    half = width // count // 2
+def pull_tokens(place, dproj, dgate, wr, small_t, count):
+    rows = dproj.shape[0]
+    half = wr.shape[0] // count // 2
     out_shape = [kept((count // 2, rows, half), BF16)] * 2 + [kept((rows, half), BF16)] * count
     got = local_call(
-        functools.partial(finish_body, (heads, levels, far, count, counts)), "finish", 16,
-        out_shape, [place], [*arrays, *others, *flat], scratch, [wr],
+        functools.partial(tokens_body, count), "pull_tokens", 8, out_shape,
+        [place], [dproj, dgate, wr, small_t],
     )
     return got[0], got[1], got[2:]
 
@@ -892,7 +884,6 @@
     far = size.bit_length() - 1
     count = lax.axis_size("head")
     place = jnp.stack([lax.axis_index("ctx"), lax.axis_index("head")]).astype(jnp.int32)
-    flat_w = qkv_weight.reshape(width * 3 * heads, key)
     small = jnp.transpose(small_weight, (2, 1, 0))
     rates = head_param.T
     flat_out = out_weight.reshape(heads * key, width)
@@ -900,7 +891,7 @@
 
     (wr, small_t, qkv, gate, pack, pack_t, trans, mixed_t, decay, base, lower, rates_row,
      pair) = project(
-        place, tokens, flat_w, small, rates, heads, levels
+        place, tokens, qkv_weight, small, rates, heads, levels
     )
     first = swap(pair, "ctx", 1)
     node = join_half(place, pair, first)
@@ -929,8 +920,9 @@
     )
     keep_out, last_out, dcol = halving(*out_parts, "head", dcol)
     arrays = [qkv, gate, pack, trans, mixed, decay, base, lower, dqkv, dgrown, dcol, drow, dfar,
-              rates_row, small_t]
-    keep, send, direct = finish(place, arrays, others, arrived, wr, levels, count)
+              rates_row]
+    dproj, dgate = finish(place, arrays, others, arrived, levels)
+    keep, send, direct = pull_tokens(place, dproj, dgate, wr, small_t, count)
     direct, last_out = lax.optimization_barrier((direct, last_out))
     got = [swap(direct[mask], "head", mask) for mask in far_first(count)]
     keep, last, _ = halving(keep, send, "head", ())

time: 81.3 us -> 83.2 us (1.023)
  waiting for transfers between devices: 22.7 us -> 26.2 us
  starting transfers between devices: 21.4 us -> 19 us
    ppermute x20, waiting for transfers between devices: 22.7 us -> 26.2 us  [swap(): return lax.ppermute(value, axis, [(at, at ^ mask) for at in range(size)])]
    ppermute x20, starting transfers between devices: 21.4 us -> 19 us  [swap(): return lax.ppermute(value, axis, [(at, at ^ mask) for at in range(size)])]
    pallas_call x12 -> x13, Pallas kernels: 36.3 us -> 37 us  [local_call(): pl.pallas_call(body, out_shape=tuple(out_shape), in_specs=[SCALARS] * len...]
  transfers between devices with their start and end apart: 20 -> 20, of which waited for: 14 -> 14; matrix products, arithmetic and copies ran while one was open for 0% -> 0% of each run, Pallas kernels for 25% -> 21%
where the time goes in v7:
time: 83.2 us; the launch traced here: 83.1 us
  Pallas kernels  37 us (44%)
  waiting for transfers between devices  26.2 us (31%)
  starting transfers between devices  19 us (23%)
    pallas_call x13, Pallas kernels, local_call(): pl.pallas_call(body, out_shape=tuple(out_shape), in_specs=[SCALARS] * len...  37 us
    ppermute x20, waiting for transfers between devices, swap(): return lax.ppermute(value, axis, [(at, at ^ mask) for at in range(size)])  26.2 us
    ppermute x20, starting transfers between devices, swap(): return lax.ppermute(value, axis, [(at, at ^ mask) for at in range(size)])  19 us
  transfers between devices with their start and end apart: 20, of which 14 were waited for; matrix products, arithmetic and copies ran while one was open for 0% of the time, Pallas kernels for 21%

profile of v7, /device:TPU:0, one launch (start us, length us, event | category | flops | bytes accessed | tf_op | source)
XLA Modules:
  0.0 83.1 jit_solution(12002426597234587442)
XLA Ops:
  0.7 15.2 %project.1 = (bf16[2048,1536]{1,0:T(8,128)(2,1)}, bf16[128,2048]{1,0:T(8,128)(2,1)S(1)}, f32[3,4,256,128]{3,2,1,0:T(8,128)S(1)}, f32[256,128]{1,0:T(8,128)S(1)},...) custom-call(s32[2]{0:T(128)S(1)} %pad_add_fusion.place_ref, ...), custom_call_target="tpu_custom_call" | custom-call | tf_op jit(solution)/shard_map/project/pallas_call | solution.py:95
  15.9 0.5 collective-permute-start
  16.4 1.2 %collective-permute-done.other_ref.refs_0_.refs_14_ = bf16[4,128,256]{2,1,0:T(8,128)(2,1)S(1)} collective-permute-done((bf16[4,128,256]{2,1,0:T(8,128)(2,1)S(1)}, bf16[4,128,256]{2,1,0:T(8,128)(2,1)S(1)}, u32[]{:S(2)}, u32[]{:S(2)}) %collective-permute-start) | collective-permute-done | bytes 262176 | tf_op jit(solution)/shard_map/ppermute | solution.py:827
  17.6 0.7 join_half.1
  18.3 3.9 %collective-permute-start.3 = (bf16[2,128,256]{2,1,0:T(8,128)(2,1)S(1)}, bf16[2,128,256]{2,1,0:T(8,128)(2,1)S(1)}, u32[]{:S(2)}, u32[]{:S(2)}) collective-permute-start(bf16[2,128,256]{2,1,0:T(8,128)(2,1)S(1)} %join_half.1), channel_id=1, source_target_pairs={{0,24},{4,28},{8,16},{12,20},{16,8},{20,12},{24,0},{28,4},{1,25},{... | collective-permute-start | bytes 393224 | tf_op jit(solution)/shard_map/ppermute | solution.py:827
  22.8 2.3 %local_part.1 = (bf16[4,256,256]{2,1,0:T(8,128)(2,1)S(1)}, bf16[4,256,256]{2,1,0:T(8,128)(2,1)S(1)}, bf16[4,256,256]{2,1,0:T(8,128)(2,1)S(1)}, bf16[4,256,256]{2...) custom-call(f32[3,4,256,128]{3,2,1,0:T(8,128)S(1)} %get-tuple-elemen, ...), custom_call_target="tpu_custom_call" | custom-call | tf_op jit(solution)/shard_map/local_part/pallas_call | solution.py:95
  25.1 1.0 %collective-permute-done.3.refs_3_ = bf16[2,128,256]{2,1,0:T(8,128)(2,1)S(1)} collective-permute-done((bf16[2,128,256]{2,1,0:T(8,128)(2,1)S(1)}, bf16[2,128,256]{2,1,0:T(8,128)(2,1)S(1)}, u32[]{:S(2)}, u32[]{:S(2)}) %collective-permute-start.3) | collective-permute-done | bytes 131104 | tf_op jit(solution)/shard_map/ppermute | solution.py:827
  26.1 2.7 %collective-permute-done.2.refs_2_ = bf16[2,128,256]{2,1,0:T(8,128)(2,1)S(1)} collective-permute-done((bf16[2,128,256]{2,1,0:T(8,128)(2,1)S(1)}, bf16[2,128,256]{2,1,0:T(8,128)(2,1)S(1)}, u32[]{:S(2)}, u32[]{:S(2)}) %collective-permute-start.2) | collective-permute-done | bytes 131104 | tf_op jit(solution)/shard_map/ppermute | solution.py:827
  29.6 0.8 %collective-permute-done.4.refs_4_ = bf16[2,128,256]{2,1,0:T(8,128)(2,1)S(1)} collective-permute-done((bf16[2,128,256]{2,1,0:T(8,128)(2,1)S(1)}, bf16[2,128,256]{2,1,0:T(8,128)(2,1)S(1)}, u32[]{:S(2)}, u32[]{:S(2)}) %collective-permute-start.4) | collective-permute-done | bytes 131104 | tf_op jit(solution)/shard_map/ppermute | solution.py:827
  30.9 3.0 %reach.1 = (bf16[2,256,512]{2,1,0:T(8,128)(2,1)S(1)}, bf16[2,256,512]{2,1,0:T(8,128)(2,1)S(1)}, f32[4,256,128]{2,1,0:T(8,128)S(1)}, bf16[4,128,384]{2,1,0:T(8,12...) custom-call(s32[2]{0:T(128)S(1)} %pad_add_fusion.place_ref, ...), custom_call_target="tpu_custom_call" | custom-call | tf_op jit(solution)/shard_map/reach/pallas_call | solution.py:95
  33.9 1.6 %collective-permute-start.7 = (bf16[2,256,512]{2,1,0:T(8,128)(2,1)S(1)}, bf16[2,256,512]{2,1,0:T(8,128)(2,1)S(1)}, u32[]{:S(2)}, u32[]{:S(2)}) collective-permute-start(bf16[2,256,512]{2,1,0:T(8,128)(2,1)S(1)} %get-tuple-element.83), channel_id=1, source_target_pairs={{0,1},{1,0},{2,3},{3,2},{4,5},{5,4},{6,7},{7,6},{8,9},{9,8},{10,11... | collective-permute-start | bytes 1572872 | tf_op jit(solution)/shard_map/ppermute | solution.py:827
  35.5 2.1 %return_states.1 = (f32[4,256,128]{2,1,0:T(8,128)S(1)}, bf16[4,128,256]{2,1,0:T(8,128)(2,1)S(1)}, bf16[4,128,256]{2,1,0:T(8,128)(2,1)S(1)}, bf16[4,128,128]{2,1,0:T(8,128)(2,1)S(1)}) custom-call(s32[2]{0:T(128)S(1)} %pad_add_fusion.place_ref, f32[256,128]{1,0:T(8,128)S(1)} %get-tuple-element.67.pack_ref.refs_1_.refs_2_, ...), custom_call_target="tpu_custom_call" | custom-call | tf_op jit(solution)/shard_map/return_states/pallas_call | solution.py:95
  38.3 1.1 %collective-permute-done.10.refs_3_ = bf16[4,128,128]{2,1,0:T(8,128)(2,1)S(1)} collective-permute-done((bf16[4,128,128]{2,1,0:T(8,128)(2,1)S(1)}, bf16[4,128,128]{2,1,0:T(8,128)(2,1)S(1)}, u32[]{:S(2)}, u32[]{:S(2)}) %collective-permute-start.10) | collective-permute-done | bytes 131104 | tf_op jit(solution)/shard_map/ppermute | solution.py:827
  39.5 1.6 %collective-permute-start.11 = (bf16[4,128,256]{2,1,0:T(8,128)(2,1)S(1)}, bf16[4,128,256]{2,1,0:T(8,128)(2,1)S(1)}, u32[]{:S(2)}, u32[]{:S(2)}) collective-permute-start(bf16[4,128,256]{2,1,0:T(8,128)(2,1)S(1)} %get-tuple-element.112), channel_id=1, source_target_pairs={{0,8},{4,12},{8,0},{12,4},{16,24},{20,28},{24,16},{28,20},{1,9},{5... | collective-permute-start | bytes 786440 | tf_op jit(solution)/shard_map/ppermute | solution.py:827
  41.1 1.4 %collective-permute-start.13 = (bf16[4,128,128]{2,1,0:T(8,128)(2,1)S(1)}, bf16[4,128,128]{2,1,0:T(8,128)(2,1)S(1)}, u32[]{:S(2)}, u32[]{:S(2)}) collective-permute-start(bf16[4,128,128]{2,1,0:T(8,128)(2,1)S(1)} %get-tuple-element.113), channel_id=1, source_target_pairs={{0,24},{4,28},{8,16},{12,20},{16,8},{20,12},{24,0},{28,4},{1,25},{... | collective-permute-start | bytes 393224 | tf_op jit(solution)/shard_map/ppermute | solution.py:827
  42.5 0.6 collective-permute-start.12
  43.1 3.5 %pull_local.1 = (f32[3,4,256,128]{3,2,1,0:T(8,128)S(1)}, f32[4,256,128]{2,1,0:T(8,128)S(1)}, f32[256,128]{1,0:T(8,128)S(1)}, f32[8,256]{1,0:T(8,128)S(1)}) custom-call(f32[3,4,256,128]{3,2,1,0:T(8,128)S(1)} %get-tuple-element.69.qkv_ref.refs_0_, f32[256,128]{1,0:T(8,128)S(1)} %get-tuple-element.67.pack_ref.refs_1_.refs_2_, ...), custom_call_target="tpu_custom_call" | custom-call | tf_op jit(solution)/shard_map/pull_local/pallas_call | solution.py:95
  46.6 1.4 %collective-permute-done.7.got_ref = bf16[2,256,512]{2,1,0:T(8,128)(2,1)S(1)} collective-permute-done((bf16[2,256,512]{2,1,0:T(8,128)(2,1)S(1)}, bf16[2,256,512]{2,1,0:T(8,128)(2,1)S(1)}, u32[]{:S(2)}, u32[]{:S(2)}) %collective-permute-start.7) | collective-permute-done | bytes 524320 | tf_op jit(solution)/shard_map/ppermute | solution.py:827
  48.1 2.6 %collective-permute-start.14 = (bf16[1,256,512]{2,1,0:T(8,128)(2,1)S(1)}, bf16[1,256,512]{2,1,0:T(8,128)(2,1)S(1)}, u32[]{:S(2)}, u32[]{:S(2)}) collective-permute-start(bf16[1,256,512]{2,1,0:T(8,128)(2,1)S(1)} %get-tuple-element.122), channel_id=1, source_target_pairs={{0,2},{1,3},{2,0},{3,1},{4,6},{5,7},{6,4},{7,5},{8,10},{9,11},{10,... | collective-permute-start | bytes 786440 | tf_op jit(solution)/shard_map/ppermute | solution.py:827
  50.8 0.9 %collective-permute-done.13.refs_20_ = bf16[4,128,128]{2,1,0:T(8,128)(2,1)S(1)} collective-permute-done((bf16[4,128,128]{2,1,0:T(8,128)(2,1)S(1)}, bf16[4,128,128]{2,1,0:T(8,128)(2,1)S(1)}, u32[]{:S(2)}, u32[]{:S(2)}) %collective-permute-start.13) | collective-permute-done | bytes 131104 | tf_op jit(solution)/shard_map/ppermute | solution.py:827
  51.6 5.8 %finish.1 = (bf16[256,1536]{1,0:T(8,128)(2,1)S(1)}, bf16[256,128]{1,0:T(8,128)(2,1)S(1)}) custom-call(s32[2]{0:T(128)S(1)} %pad_add_fusion.place_ref, f32[3,4,256,128]{3,2,1,0:T(8,128)S(1)} %get-tuple-element.69.qkv_ref.refs_0_, f32[256,128]{1,0:T(8,128)S(1)} %get-tuple-element.85.refs_1_, f32[256,128]{1,0:T(8,128)S(1)} %get-tuple-element.67.pack_ref.refs_1_.refs_2_, ...), custom_call_target="tpu_custom_call" | custom-call | tf_op jit(solution)/shard_map/finish/pallas_call | solution.py:95
  57.5 2.6 %pull_tokens.1 = (bf16[2,256,256]{2,1,0:T(8,128)(2,1)S(1)}, bf16[2,256,256]{2,1,0:T(8,128)(2,1)S(1)}, bf16[256,256]{1,0:T(8,128)(2,1)S(1)}, bf16[256,256]{1,0:T(...) custom-call(s32[2]{0:T(128)S(1)} %pad_add_fusion.place_ref, ...), custom_call_target="tpu_custom_call" | custom-call | tf_op jit(solution)/shard_map/pull_tokens/pallas_call | solution.py:95
  60.1 0.8 collective-permute-start.15
  60.9 1.4 %collective-permute-done.14.refs_1_ = bf16[1,256,512]{2,1,0:T(8,128)(2,1)S(1)} collective-permute-done((bf16[1,256,512]{2,1,0:T(8,128)(2,1)S(1)}, bf16[1,256,512]{2,1,0:T(8,128)(2,1)S(1)}, u32[]{:S(2)}, u32[]{:S(2)}) %collective-permute-start.14) | collective-permute-done | bytes 262176 | tf_op jit(solution)/shard_map/ppermute | solution.py:827
  62.3 0.9 %collective-permute-start.17 = (bf16[256,256]{1,0:T(8,128)(2,1)S(1)}, bf16[256,256]{1,0:T(8,128)(2,1)S(1)}, u32[]{:S(2)}, u32[]{:S(2)}) collective-permute-start(bf16[256,256]{1,0:T(8,128)(2,1)S(1)} %get-tuple-element.129), channel_id=1, source_target_pairs={{0,2},{1,3},{2,0},{3,1},{4,6},{5,7},{6,4},{7,5},{8,10},{9,11},{10,... | collective-permute-start | bytes 393224 | tf_op jit(solution)/shard_map/ppermute | solution.py:827
  63.2 2.7 %collective-permute-start.18 = (bf16[256,256]{1,0:T(8,128)(2,1)S(1)}, bf16[256,256]{1,0:T(8,128)(2,1)S(1)}, u32[]{:S(2)}, u32[]{:S(2)}) collective-permute-start(bf16[256,256]{1,0:T(8,128)(2,1)S(1)} %get-tuple-element.130), channel_id=1, source_target_pairs={{0,3},{1,2},{2,1},{3,0},{4,7},{5,6},{6,5},{7,4},{8,11},{9,10},{10,... | collective-permute-start | bytes 393224 | tf_op jit(solution)/shard_map/ppermute | solution.py:827
  65.9 0.6 collective-permute-start.19
  66.4 6.9 %collective-permute-done.15.got_ref = bf16[2,256,256]{2,1,0:T(8,128)(2,1)S(1)} collective-permute-done((bf16[2,256,256]{2,1,0:T(8,128)(2,1)S(1)}, bf16[2,256,256]{2,1,0:T(8,128)(2,1)S(1)}, u32[]{:S(2)}, u32[]{:S(2)}) %collective-permute-start.15) | collective-permute-done | bytes 262176 | tf_op jit(solution)/shard_map/ppermute | solution.py:827
  73.5 0.7 head_sum.2
  74.3 2.8 %collective-permute-done.18.refs_4_ = bf16[256,256]{1,0:T(8,128)(2,1)S(1)} collective-permute-done((bf16[256,256]{1,0:T(8,128)(2,1)S(1)}, bf16[256,256]{1,0:T(8,128)(2,1)S(1)}, u32[]{:S(2)}, u32[]{:S(2)}) %collective-permute-start.18) | collective-permute-done | bytes 131104 | tf_op jit(solution)/shard_map/ppermute | solution.py:827
  77.1 5.2 %collective-permute-done.16.refs_1_ = bf16[1,256,256]{2,1,0:T(8,128)(2,1)S(1)} collective-permute-done((bf16[1,256,256]{2,1,0:T(8,128)(2,1)S(1)}, bf16[1,256,256]{2,1,0:T(8,128)(2,1)S(1)}, u32[]{:S(2)}, u32[]{:S(2)}) %collective-permute-start.16) | collective-permute-done | bytes 131104 | tf_op jit(solution)/shard_map/ppermute | solution.py:827
  82.3 0.8 head_sum.3
  (33 shorter events, 3.1 us)
Async XLA Ops:
  0.7 22.1 %copy-start = (bf16[4,128,2048]{2,1,0:T(8,128)(2,1)S(1)}, bf16[4,128,2048]{2,1,0:T(8,128)(2,1)}, u32[]{:S(2)}) copy-start(bf16[4,128,2048]{2,1,0:T(8,128)(2,1)} %param.12) | copy-start | bytes 6291460
  0.7 22.1 %copy-start.1 = (bf16[256,2048]{1,0:T(8,128)(2,1)S(1)}, bf16[256,2048]{1,0:T(8,128)(2,1)}, u32[]{:S(2)}) copy-start(bf16[256,2048]{1,0:T(8,128)(2,1)} %grad_ref.1) | copy-start | bytes 3145732
  15.9 1.7 %collective-permute-start = (bf16[4,128,256]{2,1,0:T(8,128)(2,1)S(1)}, bf16[4,128,256]{2,1,0:T(8,128)(2,1)S(1)}, u32[]{:S(2)}, u32[]{:S(2)}) collective-permute-start(bf16[4,128,256]{2,1,0:T(8,128)(2,1)S(1)} %get-tuple-element.68.own_ref), channel_id=1, source_target_pairs={{0,4},{4,0},{8,12},{12,8},{16,20},{20,16},{24,28},{28,24},{1,5},{5... | collective-permute-start | bytes 786440 | tf_op jit(solution)/shard_map/ppermute | solution.py:827
  18.3 7.8 %collective-permute-start.3 = (bf16[2,128,256]{2,1,0:T(8,128)(2,1)S(1)}, bf16[2,128,256]{2,1,0:T(8,128)(2,1)S(1)}, u32[]{:S(2)}, u32[]{:S(2)}) collective-permute-start(bf16[2,128,256]{2,1,0:T(8,128)(2,1)S(1)} %join_half.1), channel_id=1, source_target_pairs={{0,24},{4,28},{8,16},{12,20},{16,8},{20,12},{24,0},{28,4},{1,25},{... | collective-permute-start | bytes 393224 | tf_op jit(solution)/shard_map/ppermute | solution.py:827
  22.2 6.6 %collective-permute-start.2 = (bf16[2,128,256]{2,1,0:T(8,128)(2,1)S(1)}, bf16[2,128,256]{2,1,0:T(8,128)(2,1)S(1)}, u32[]{:S(2)}, u32[]{:S(2)}) collective-permute-start(bf16[2,128,256]{2,1,0:T(8,128)(2,1)S(1)} %join_half.1), channel_id=1, source_target_pairs={{0,16},{4,20},{8,24},{12,28},{16,0},{20,4},{24,8},{28,12},{1,17},{... | collective-permute-start | bytes 393224 | tf_op jit(solution)/shard_map/ppermute | solution.py:827
  22.7 6.4 %collective-permute-start.1 = (bf16[2,128,256]{2,1,0:T(8,128)(2,1)S(1)}, bf16[2,128,256]{2,1,0:T(8,128)(2,1)S(1)}, u32[]{:S(2)}, u32[]{:S(2)}) collective-permute-start(bf16[2,128,256]{2,1,0:T(8,128)(2,1)S(1)} %join_half.1), channel_id=1, source_target_pairs={{0,8},{4,12},{8,0},{12,4},{16,24},{20,28},{24,16},{28,20},{1,9},{5... | collective-permute-start | bytes 393224 | tf_op jit(solution)/shard_map/ppermute | solution.py:827
  22.8 8.1 %copy-start.2 = (f32[128]{0:T(128)S(1)}, f32[128]{0:T(128)}, u32[]{:S(2)}) copy-start(f32[128]{0:T(128)} %param.11) | copy-start | bytes 1540
  29.1 1.3 %collective-permute-start.4 = (bf16[2,128,256]{2,1,0:T(8,128)(2,1)S(1)}, bf16[2,128,256]{2,1,0:T(8,128)(2,1)S(1)}, u32[]{:S(2)}, u32[]{:S(2)}) collective-permute-start(bf16[2,128,256]{2,1,0:T(8,128)(2,1)S(1)} %collective-permute-done.1.refs_1_), channel_id=1, source_target_pairs={{0,4},{4,0},{8,12},{12,8},{16,20},{20,16},{24,28},{28,24},{1,5},{5... | collective-permute-start | bytes 393224 | tf_op jit(solution)/shard_map/ppermute | solution.py:827
  29.1 1.5 %collective-permute-start.5 = (bf16[2,128,256]{2,1,0:T(8,128)(2,1)S(1)}, bf16[2,128,256]{2,1,0:T(8,128)(2,1)S(1)}, u32[]{:S(2)}, u32[]{:S(2)}) collective-permute-start(bf16[2,128,256]{2,1,0:T(8,128)(2,1)S(1)} %collective-permute-done.2.refs_2_), channel_id=1, source_target_pairs={{0,4},{4,0},{8,12},{12,8},{16,20},{20,16},{24,28},{28,24},{1,5},{5... | collective-permute-start | bytes 393224 | tf_op jit(solution)/shard_map/ppermute | solution.py:827
  29.6 1.3 %collective-permute-start.6 = (bf16[2,128,256]{2,1,0:T(8,128)(2,1)S(1)}, bf16[2,128,256]{2,1,0:T(8,128)(2,1)S(1)}, u32[]{:S(2)}, u32[]{:S(2)}) collective-permute-start(bf16[2,128,256]{2,1,0:T(8,128)(2,1)S(1)} %collective-permute-done.3.refs_3_), channel_id=1, source_target_pairs={{0,4},{4,0},{8,12},{12,8},{16,20},{20,16},{24,28},{28,24},{1,5},{5... | collective-permute-start | bytes 393224 | tf_op jit(solution)/shard_map/ppermute | solution.py:827
  33.9 14.1 %collective-permute-start.7 = (bf16[2,256,512]{2,1,0:T(8,128)(2,1)S(1)}, bf16[2,256,512]{2,1,0:T(8,128)(2,1)S(1)}, u32[]{:S(2)}, u32[]{:S(2)}) collective-permute-start(bf16[2,256,512]{2,1,0:T(8,128)(2,1)S(1)} %get-tuple-element.83), channel_id=1, source_target_pairs={{0,1},{1,0},{2,3},{3,2},{4,5},{5,4},{6,7},{7,6},{8,9},{9,8},{10,11... | collective-permute-start | bytes 1572872 | tf_op jit(solution)/shard_map/ppermute | solution.py:827
  37.7 1.8 %collective-permute-start.9 = (bf16[4,128,256]{2,1,0:T(8,128)(2,1)S(1)}, bf16[4,128,256]{2,1,0:T(8,128)(2,1)S(1)}, u32[]{:S(2)}, u32[]{:S(2)}) collective-permute-start(bf16[4,128,256]{2,1,0:T(8,128)(2,1)S(1)} %get-tuple-element.110.refs_0_), channel_id=1, source_target_pairs={{0,4},{4,0},{8,12},{12,8},{16,20},{20,16},{24,28},{28,24},{1,5},{5... | collective-permute-start | bytes 786440 | tf_op jit(solution)/shard_map/ppermute | solution.py:827
  37.7 1.7 %collective-permute-start.10 = (bf16[4,128,128]{2,1,0:T(8,128)(2,1)S(1)}, bf16[4,128,128]{2,1,0:T(8,128)(2,1)S(1)}, u32[]{:S(2)}, u32[]{:S(2)}) collective-permute-start(bf16[4,128,128]{2,1,0:T(8,128)(2,1)S(1)} %get-tuple-element.111.refs_1_), channel_id=1, source_target_pairs={{0,4},{4,0},{8,12},{12,8},{16,20},{20,16},{24,28},{28,24},{1,5},{5... | collective-permute-start | bytes 393224 | tf_op jit(solution)/shard_map/ppermute | solution.py:827
  38.2 12.6 %collective-permute-start.8 = (bf16[4,128,256]{2,1,0:T(8,128)(2,1)S(1)}, bf16[4,128,256]{2,1,0:T(8,128)(2,1)S(1)}, u32[]{:S(2)}, u32[]{:S(2)}) collective-permute-start(bf16[4,128,256]{2,1,0:T(8,128)(2,1)S(1)} %get-tuple-element.109), channel_id=1, source_target_pairs={{0,4},{4,0},{8,12},{12,8},{16,20},{20,16},{24,28},{28,24},{1,5},{5... | collective-permute-start | bytes 786440 | tf_op jit(solution)/shard_map/ppermute | solution.py:827
  39.5 12.1 %collective-permute-start.11 = (bf16[4,128,256]{2,1,0:T(8,128)(2,1)S(1)}, bf16[4,128,256]{2,1,0:T(8,128)(2,1)S(1)}, u32[]{:S(2)}, u32[]{:S(2)}) collective-permute-start(bf16[4,128,256]{2,1,0:T(8,128)(2,1)S(1)} %get-tuple-element.112), channel_id=1, source_target_pairs={{0,8},{4,12},{8,0},{12,4},{16,24},{20,28},{24,16},{28,20},{1,9},{5... | collective-permute-start | bytes 786440 | tf_op jit(solution)/shard_map/ppermute | solution.py:827
  41.1 10.5 %collective-permute-start.13 = (bf16[4,128,128]{2,1,0:T(8,128)(2,1)S(1)}, bf16[4,128,128]{2,1,0:T(8,128)(2,1)S(1)}, u32[]{:S(2)}, u32[]{:S(2)}) collective-permute-start(bf16[4,128,128]{2,1,0:T(8,128)(2,1)S(1)} %get-tuple-element.113), channel_id=1, source_target_pairs={{0,24},{4,28},{8,16},{12,20},{16,8},{20,12},{24,0},{28,4},{1,25},{... | collective-permute-start | bytes 393224 | tf_op jit(solution)/shard_map/ppermute | solution.py:827
  42.5 9.1 %collective-permute-start.12 = (bf16[4,128,128]{2,1,0:T(8,128)(2,1)S(1)}, bf16[4,128,128]{2,1,0:T(8,128)(2,1)S(1)}, u32[]{:S(2)}, u32[]{:S(2)}) collective-permute-start(bf16[4,128,128]{2,1,0:T(8,128)(2,1)S(1)} %get-tuple-element.113), channel_id=1, source_target_pairs={{0,16},{4,20},{8,24},{12,28},{16,0},{20,4},{24,8},{28,12},{1,17},{... | collective-permute-start | bytes 393224 | tf_op jit(solution)/shard_map/ppermute | solution.py:827
  43.1 14.3 %slice-start = ((s8[6291456]{0:T(1024)(128)(4,1)}), s8[2097152]{0:T(1024)(128)(4,1)S(1)}, s32[]{:S(2)}) async-start(s8[6291456]{0:T(1024)(128)(4,1)} %bitcast.8), calls=%async_computation | async-start | bytes 4194304
  48.0 9.4 %slice-start.1 = ((s8[6291456]{0:T(1024)(128)(4,1)}), s8[4194304]{0:T(1024)(128)(4,1)S(1)}, s32[]{:S(2)}) async-start(s8[6291456]{0:T(1024)(128)(4,1)} %bitcast.8), calls=%async_computation.1 | async-start | bytes 8388608
  48.1 14.2 %collective-permute-start.14 = (bf16[1,256,512]{2,1,0:T(8,128)(2,1)S(1)}, bf16[1,256,512]{2,1,0:T(8,128)(2,1)S(1)}, u32[]{:S(2)}, u32[]{:S(2)}) collective-permute-start(bf16[1,256,512]{2,1,0:T(8,128)(2,1)S(1)} %get-tuple-element.122), channel_id=1, source_target_pairs={{0,2},{1,3},{2,0},{3,1},{4,6},{5,7},{6,4},{7,5},{8,10},{9,11},{10,... | collective-permute-start | bytes 786440 | tf_op jit(solution)/shard_map/ppermute | solution.py:827
  60.1 13.3 %collective-permute-start.15 = (bf16[2,256,256]{2,1,0:T(8,128)(2,1)S(1)}, bf16[2,256,256]{2,1,0:T(8,128)(2,1)S(1)}, u32[]{:S(2)}, u32[]{:S(2)}) collective-permute-start(bf16[2,256,256]{2,1,0:T(8,128)(2,1)S(1)} %get-tuple-element.125), channel_id=1, source_target_pairs={{0,1},{1,0},{2,3},{3,2},{4,5},{5,4},{6,7},{7,6},{8,9},{9,8},{10,11... | collective-permute-start | bytes 786440 | tf_op jit(solution)/shard_map/ppermute | solution.py:827
  62.3 12.0 %collective-permute-start.17 = (bf16[256,256]{1,0:T(8,128)(2,1)S(1)}, bf16[256,256]{1,0:T(8,128)(2,1)S(1)}, u32[]{:S(2)}, u32[]{:S(2)}) collective-permute-start(bf16[256,256]{1,0:T(8,128)(2,1)S(1)} %get-tuple-element.129), channel_id=1, source_target_pairs={{0,2},{1,3},{2,0},{3,1},{4,6},{5,7},{6,4},{7,5},{8,10},{9,11},{10,... | collective-permute-start | bytes 393224 | tf_op jit(solution)/shard_map/ppermute | solution.py:827
  63.2 13.9 %collective-permute-start.18 = (bf16[256,256]{1,0:T(8,128)(2,1)S(1)}, bf16[256,256]{1,0:T(8,128)(2,1)S(1)}, u32[]{:S(2)}, u32[]{:S(2)}) collective-permute-start(bf16[256,256]{1,0:T(8,128)(2,1)S(1)} %get-tuple-element.130), channel_id=1, source_target_pairs={{0,3},{1,2},{2,1},{3,0},{4,7},{5,6},{6,5},{7,4},{8,11},{9,10},{10,... | collective-permute-start | bytes 393224 | tf_op jit(solution)/shard_map/ppermute | solution.py:827
  65.9 11.2 %collective-permute-start.19 = (bf16[256,256]{1,0:T(8,128)(2,1)S(1)}, bf16[256,256]{1,0:T(8,128)(2,1)S(1)}, u32[]{:S(2)}, u32[]{:S(2)}) collective-permute-start(bf16[256,256]{1,0:T(8,128)(2,1)S(1)} %get-tuple-element.131), channel_id=1, source_target_pairs={{0,1},{1,0},{2,3},{3,2},{4,5},{5,4},{6,7},{7,6},{8,9},{9,8},{10,11... | collective-permute-start | bytes 393224 | tf_op jit(solution)/shard_map/ppermute | solution.py:827
  73.4 8.8 %collective-permute-start.16 = (bf16[1,256,256]{2,1,0:T(8,128)(2,1)S(1)}, bf16[1,256,256]{2,1,0:T(8,128)(2,1)S(1)}, u32[]{:S(2)}, u32[]{:S(2)}) collective-permute-start(bf16[1,256,256]{2,1,0:T(8,128)(2,1)S(1)} %get-tuple-element.127), channel_id=1, source_target_pairs={{0,2},{1,3},{2,0},{3,1},{4,6},{5,7},{6,4},{7,5},{8,10},{9,11},{10,... | collective-permute-start | bytes 393224 | tf_op jit(solution)/shard_map/ppermute | solution.py:827

commit v8 on v7

--- a/solution.py
+++ b/solution.py
@@ -173,32 +173,50 @@
     heads, levels, chunks = sizes
     (wr_hbm, small_ref, qkv_ref, gate_ref, pack_ref, pack_t_ref, trans_ref, mixed_t_ref,
      decay_ref, base_ref, lower_ref, rates_ref, pair_ref) = refs[:13]
-    tokens, raw_q, raw_k, raw_v, wide_q, wide_k, wide_v, wr = refs[13:21]
-    small_in, small_wide, acc, hp_ref, sems, in_sems, out_sems = refs[21:]
-    raw, wide = (raw_q, raw_k, raw_v), (wide_q, wide_k, wide_v)
+    tokens, wide_in, wr, small_in, small_wide, acc, hp_ref, sems, in_sems, out_sems = refs[13:]
     rows, width = tokens.shape
     depth = width // chunks
+    cols = 3 * heads
     fetch_tokens = pltpu.make_async_copy(tokens_hbm, tokens, sems.at[0])
     fetch_small = pltpu.make_async_copy(small_hbm, small_in, sems.at[1])
     fetch_rates = pltpu.make_async_copy(hp_hbm, hp_ref, sems.at[2])
-    fetches, keeps = {}, {}
-    for part in range(3):
-        for chunk in range(chunks):
-            span = pl.ds(chunk * depth, depth)
-            at = part * chunks + chunk
-            fetches[part, chunk] = pltpu.make_async_copy(
-                w_hbm.at[span, part], raw[part].at[span], in_sems.at[at]
-            )
-            block = (span, pl.ds(part * heads * LANES, heads * LANES))
-            keeps[part, chunk] = pltpu.make_async_copy(
-                wr.at[block], wr_hbm.at[block], out_sems.at[at]
-            )
+    fetches, keeps = [], []
+    for chunk in range(chunks):
+        span = pl.ds(chunk * depth * cols, depth * cols)
+        fetches.append(
+            pltpu.make_async_copy(w_hbm.at[span, :], wide_in.at[span, :], in_sems.at[chunk])
+        )
+        span = pl.ds(chunk * depth, depth)
+        keeps.append(
+            pltpu.make_async_copy(wr.at[span, :], wr_hbm.at[span, :], out_sems.at[chunk])
+        )
     fetch_small.start()
     fetch_rates.start()
-    fetch_tokens.start(priority=1)
-    for part in (1, 2, 0):
-        for chunk in range(chunks):
-            fetches[part, chunk].start(priority=chunk % 2)
+    fetches[0].start()
+    fetch_tokens.start()
+    for fetch in fetches[1:]:
+        fetch.start()
+    group = 16
+    size = group * cols
+    turn_row, turn_col = pair_ids(size)
+    turn = (turn_col == (turn_row % group) * cols + turn_row // group).astype(F32).astype(BF16)
+
+    def relay(chunk):
+        fetches[chunk].wait()
+        first = chunk * depth * cols
+        packs = depth // group
+        side = jnp.concatenate(
+            [wide_in[first + at * size : first + (at + 1) * size, :] for at in range(packs)], 1
+        )
+        turned = jnp.dot(turn, side, preferred_element_type=F32).astype(BF16)
+        for at in range(packs):
+            row = chunk * depth + at * group
+            for col in range(cols):
+                wr[row : row + group, col * LANES : (col + 1) * LANES] = turned[
+                    col * group : (col + 1) * group, at * LANES : (at + 1) * LANES
+                ]
+        keeps[chunk].start()
+
     decay_col = levels * heads
     beta_col = decay_col + heads
     norm_col = beta_col + heads
@@ -228,27 +246,21 @@
     pack_t = pack.T
     pack_t_ref[...] = pack_t
 
-    def extract(part, chunk):
-        fetches[part, chunk].wait()
-        first, last = chunk * depth, (chunk + 1) * depth
-        flat = raw[part].reshape(width * heads, LANES)
-        wide[part][first * heads : last * heads, :] = (
-            flat[first * heads : last * heads, :].astype(F32)
+    def multiply(part, first, last):
+        span = slice((part * heads) * LANES, (part + 1) * heads * LANES)
+        own = jnp.dot(
+            tokens[:, first * depth : last * depth], wr[first * depth : last * depth, span],
+            preferred_element_type=F32,
         )
-        for head in range(heads):
-            value = wide[part][pl.ds(first * heads + head, depth, stride=heads), :]
-            col = (part * heads + head) * LANES
-            wr[first:last, col : col + LANES] = value.astype(BF16)
-        keeps[part, chunk].start(priority=chunk % 2)
-        span = slice(part * heads * LANES, (part + 1) * heads * LANES)
-        own = jnp.dot(tokens[:, first:last], wr[first:last, span], preferred_element_type=F32)
-        if chunk == 0:
+        if first == 0:
             acc[:, span] = own
         else:
             acc[:, span] += own
 
     for chunk in range(chunks):
-        extract(1, chunk)
+        relay(chunk)
+        if chunk % 2 == 1:
+            multiply(1, chunk - 1, chunk + 1)
 
     def unit_of(part, head):
         col = (part * heads + head) * LANES
@@ -273,9 +285,9 @@
 
     def later():
         for part in (2, 0):
-            for chunk in range(chunks):
+            for at in range(0, chunks, chunks // 4):
                 yield
-                extract(part, chunk)
+                multiply(part, at, at + chunks // 4)
 
     chain, filler = invert(lower_all, eye, apart, rows), later()
     while True:
@@ -310,15 +322,15 @@
     for head in range(heads):
         scales = scales + unit_of(0, head)[1]
     pack_ref[...] = jnp.where(lane < norm_col, pack, scales)
-    for keep in keeps.values():
+    for keep in keeps:
         keep.wait()
 
 
-def project(place, tokens, weight, small, head_param, heads, levels):
+def project(place, tokens, flat_w, small, head_param, heads, levels):
     rows, width = tokens.shape
-    chunks = 4
+    chunks = 8
     cols = 3 * heads
-    key = weight.shape[3]
+    key = flat_w.shape[1]
     square = (heads, rows, rows)
     out_shape = (
         stored((width, cols * key), BF16),
@@ -337,20 +349,19 @@
     )
     scratch = [
         pltpu.VMEM(tokens.shape, BF16),
-        *[pltpu.VMEM((width, heads, key), BF16) for part in range(3)],
-        *[pltpu.VMEM((width * heads, key), F32) for part in range(3)],
+        pltpu.VMEM(flat_w.shape, BF16),
         pltpu.VMEM((width, cols * key), BF16),
         pltpu.VMEM(small.shape, BF16),
         pltpu.VMEM((LANES, width), F32),
         pltpu.VMEM((rows, cols * key), F32),
         pltpu.VMEM(head_param.shape, F32),
         pltpu.SemaphoreType.DMA((3,)),
-        pltpu.SemaphoreType.DMA((3 * chunks,)),
-        pltpu.SemaphoreType.DMA((3 * chunks,)),
+        pltpu.SemaphoreType.DMA((chunks,)),
+        pltpu.SemaphoreType.DMA((chunks,)),
     ]
     return local_call(
         functools.partial(project_body, (heads, levels, chunks)), "project", 36, out_shape,
-        [place], [], scratch, [head_param, tokens, weight, small], [HBM] + [WHOLE] * 12,
+        [place], [], scratch, [head_param, tokens, flat_w, small], [HBM] + [WHOLE] * 12,
     )
 
 
@@ -884,6 +895,7 @@
     far = size.bit_length() - 1
     count = lax.axis_size("head")
     place = jnp.stack([lax.axis_index("ctx"), lax.axis_index("head")]).astype(jnp.int32)
+    flat_w = qkv_weight.reshape(width * 3 * heads, key)
     small = jnp.transpose(small_weight, (2, 1, 0))
     rates = head_param.T
     flat_out = out_weight.reshape(heads * key, width)
@@ -891,7 +903,7 @@
 
     (wr, small_t, qkv, gate, pack, pack_t, trans, mixed_t, decay, base, lower, rates_row,
      pair) = project(
-        place, tokens, qkv_weight, small, rates, heads, levels
+        place, tokens, flat_w, small, rates, heads, levels
     )
     first = swap(pair, "ctx", 1)
     node = join_half(place, pair, first)

time: 83.2 us -> 81.5 us (0.980)
  Pallas kernels: 37 us -> 35.2 us
    pallas_call x13, Pallas kernels: 37 us -> 35.2 us  [local_call(): pl.pallas_call(body, out_shape=tuple(out_shape), in_specs=[SCALARS] * len...]
where the time goes in v8:
time: 81.5 us; the launch traced here: 81.3 us
  Pallas kernels  35.2 us (43%)
  waiting for transfers between devices  26.2 us (32%)
  starting transfers between devices  19 us (23%)
    pallas_call x13, Pallas kernels, local_call(): pl.pallas_call(body, out_shape=tuple(out_shape), in_specs=[SCALARS] * len...  35.2 us
    ppermute x20, waiting for transfers between devices, swap(): return lax.ppermute(value, axis, [(at, at ^ mask) for at in range(size)])  26.2 us
    ppermute x20, starting transfers between devices, swap(): return lax.ppermute(value, axis, [(at, at ^ mask) for at in range(size)])  19 us
  transfers between devices with their start and end apart: 20, of which 14 were waited for; matrix products, arithmetic and copies ran while one was open for 0% of the time, Pallas kernels for 21%

profile of v8, /device:TPU:0, one launch (start us, length us, event | category | flops | bytes accessed | tf_op | source)
XLA Modules:
  0.0 81.3 jit_solution(12480336603386406493)
XLA Ops:
  0.7 13.4 %project.1 = (bf16[2048,1536]{1,0:T(8,128)(2,1)}, bf16[128,2048]{1,0:T(8,128)(2,1)S(1)}, f32[3,4,256,128]{3,2,1,0:T(8,128)S(1)}, f32[256,128]{1,0:T(8,128)S(1)},...) custom-call(s32[2]{0:T(128)S(1)} %pad_add_fusion.place_ref, ...), custom_call_target="tpu_custom_call" | custom-call | tf_op jit(solution)/shard_map/project/pallas_call | solution.py:95
  14.1 0.5 collective-permute-start
  14.6 1.2 %collective-permute-done.other_ref.refs_0_.refs_14_ = bf16[4,128,256]{2,1,0:T(8,128)(2,1)S(1)} collective-permute-done((bf16[4,128,256]{2,1,0:T(8,128)(2,1)S(1)}, bf16[4,128,256]{2,1,0:T(8,128)(2,1)S(1)}, u32[]{:S(2)}, u32[]{:S(2)}) %collective-permute-start) | collective-permute-done | bytes 262176 | tf_op jit(solution)/shard_map/ppermute | solution.py:838
  15.8 0.7 join_half.1
  16.5 3.9 %collective-permute-start.3 = (bf16[2,128,256]{2,1,0:T(8,128)(2,1)S(1)}, bf16[2,128,256]{2,1,0:T(8,128)(2,1)S(1)}, u32[]{:S(2)}, u32[]{:S(2)}) collective-permute-start(bf16[2,128,256]{2,1,0:T(8,128)(2,1)S(1)} %join_half.1), channel_id=1, source_target_pairs={{0,24},{4,28},{8,16},{12,20},{16,8},{20,12},{24,0},{28,4},{1,25},{... | collective-permute-start | bytes 393224 | tf_op jit(solution)/shard_map/ppermute | solution.py:838
  21.0 2.3 %local_part.1 = (bf16[4,256,256]{2,1,0:T(8,128)(2,1)S(1)}, bf16[4,256,256]{2,1,0:T(8,128)(2,1)S(1)}, bf16[4,256,256]{2,1,0:T(8,128)(2,1)S(1)}, bf16[4,256,256]{2...) custom-call(f32[3,4,256,128]{3,2,1,0:T(8,128)S(1)} %get-tuple-elemen, ...), custom_call_target="tpu_custom_call" | custom-call | tf_op jit(solution)/shard_map/local_part/pallas_call | solution.py:95
  23.3 1.0 %collective-permute-done.3.refs_3_ = bf16[2,128,256]{2,1,0:T(8,128)(2,1)S(1)} collective-permute-done((bf16[2,128,256]{2,1,0:T(8,128)(2,1)S(1)}, bf16[2,128,256]{2,1,0:T(8,128)(2,1)S(1)}, u32[]{:S(2)}, u32[]{:S(2)}) %collective-permute-start.3) | collective-permute-done | bytes 131104 | tf_op jit(solution)/shard_map/ppermute | solution.py:838
  24.3 2.7 %collective-permute-done.2.refs_2_ = bf16[2,128,256]{2,1,0:T(8,128)(2,1)S(1)} collective-permute-done((bf16[2,128,256]{2,1,0:T(8,128)(2,1)S(1)}, bf16[2,128,256]{2,1,0:T(8,128)(2,1)S(1)}, u32[]{:S(2)}, u32[]{:S(2)}) %collective-permute-start.2) | collective-permute-done | bytes 131104 | tf_op jit(solution)/shard_map/ppermute | solution.py:838
  27.8 0.8 %collective-permute-done.4.refs_4_ = bf16[2,128,256]{2,1,0:T(8,128)(2,1)S(1)} collective-permute-done((bf16[2,128,256]{2,1,0:T(8,128)(2,1)S(1)}, bf16[2,128,256]{2,1,0:T(8,128)(2,1)S(1)}, u32[]{:S(2)}, u32[]{:S(2)}) %collective-permute-start.4) | collective-permute-done | bytes 131104 | tf_op jit(solution)/shard_map/ppermute | solution.py:838
  29.1 3.0 %reach.1 = (bf16[2,256,512]{2,1,0:T(8,128)(2,1)S(1)}, bf16[2,256,512]{2,1,0:T(8,128)(2,1)S(1)}, f32[4,256,128]{2,1,0:T(8,128)S(1)}, bf16[4,128,384]{2,1,0:T(8,12...) custom-call(s32[2]{0:T(128)S(1)} %pad_add_fusion.place_ref, ...), custom_call_target="tpu_custom_call" | custom-call | tf_op jit(solution)/shard_map/reach/pallas_call | solution.py:95
  32.2 1.6 %collective-permute-start.7 = (bf16[2,256,512]{2,1,0:T(8,128)(2,1)S(1)}, bf16[2,256,512]{2,1,0:T(8,128)(2,1)S(1)}, u32[]{:S(2)}, u32[]{:S(2)}) collective-permute-start(bf16[2,256,512]{2,1,0:T(8,128)(2,1)S(1)} %get-tuple-element.83), channel_id=1, source_target_pairs={{0,1},{1,0},{2,3},{3,2},{4,5},{5,4},{6,7},{7,6},{8,9},{9,8},{10,11... | collective-permute-start | bytes 1572872 | tf_op jit(solution)/shard_map/ppermute | solution.py:838
  33.8 2.1 %return_states.1 = (f32[4,256,128]{2,1,0:T(8,128)S(1)}, bf16[4,128,256]{2,1,0:T(8,128)(2,1)S(1)}, bf16[4,128,256]{2,1,0:T(8,128)(2,1)S(1)}, bf16[4,128,128]{2,1,0:T(8,128)(2,1)S(1)}) custom-call(s32[2]{0:T(128)S(1)} %pad_add_fusion.place_ref, f32[256,128]{1,0:T(8,128)S(1)} %get-tuple-element.67.pack_ref.refs_1_.refs_2_, ...), custom_call_target="tpu_custom_call" | custom-call | tf_op jit(solution)/shard_map/return_states/pallas_call | solution.py:95
  36.5 1.1 %collective-permute-done.10.refs_3_ = bf16[4,128,128]{2,1,0:T(8,128)(2,1)S(1)} collective-permute-done((bf16[4,128,128]{2,1,0:T(8,128)(2,1)S(1)}, bf16[4,128,128]{2,1,0:T(8,128)(2,1)S(1)}, u32[]{:S(2)}, u32[]{:S(2)}) %collective-permute-start.10) | collective-permute-done | bytes 131104 | tf_op jit(solution)/shard_map/ppermute | solution.py:838
  37.8 1.6 %collective-permute-start.11 = (bf16[4,128,256]{2,1,0:T(8,128)(2,1)S(1)}, bf16[4,128,256]{2,1,0:T(8,128)(2,1)S(1)}, u32[]{:S(2)}, u32[]{:S(2)}) collective-permute-start(bf16[4,128,256]{2,1,0:T(8,128)(2,1)S(1)} %get-tuple-element.112), channel_id=1, source_target_pairs={{0,8},{4,12},{8,0},{12,4},{16,24},{20,28},{24,16},{28,20},{1,9},{5... | collective-permute-start | bytes 786440 | tf_op jit(solution)/shard_map/ppermute | solution.py:838
  39.3 1.4 %collective-permute-start.13 = (bf16[4,128,128]{2,1,0:T(8,128)(2,1)S(1)}, bf16[4,128,128]{2,1,0:T(8,128)(2,1)S(1)}, u32[]{:S(2)}, u32[]{:S(2)}) collective-permute-start(bf16[4,128,128]{2,1,0:T(8,128)(2,1)S(1)} %get-tuple-element.113), channel_id=1, source_target_pairs={{0,24},{4,28},{8,16},{12,20},{16,8},{20,12},{24,0},{28,4},{1,25},{... | collective-permute-start | bytes 393224 | tf_op jit(solution)/shard_map/ppermute | solution.py:838
  40.7 0.6 collective-permute-start.12
  41.3 3.5 %pull_local.1 = (f32[3,4,256,128]{3,2,1,0:T(8,128)S(1)}, f32[4,256,128]{2,1,0:T(8,128)S(1)}, f32[256,128]{1,0:T(8,128)S(1)}, f32[8,256]{1,0:T(8,128)S(1)}) custom-call(f32[3,4,256,128]{3,2,1,0:T(8,128)S(1)} %get-tuple-element.69.qkv_ref.refs_0_, f32[256,128]{1,0:T(8,128)S(1)} %get-tuple-element.67.pack_ref.refs_1_.refs_2_, ...), custom_call_target="tpu_custom_call" | custom-call | tf_op jit(solution)/shard_map/pull_local/pallas_call | solution.py:95
  44.9 1.4 %collective-permute-done.7.got_ref = bf16[2,256,512]{2,1,0:T(8,128)(2,1)S(1)} collective-permute-done((bf16[2,256,512]{2,1,0:T(8,128)(2,1)S(1)}, bf16[2,256,512]{2,1,0:T(8,128)(2,1)S(1)}, u32[]{:S(2)}, u32[]{:S(2)}) %collective-permute-start.7) | collective-permute-done | bytes 524320 | tf_op jit(solution)/shard_map/ppermute | solution.py:838
  46.4 2.6 %collective-permute-start.14 = (bf16[1,256,512]{2,1,0:T(8,128)(2,1)S(1)}, bf16[1,256,512]{2,1,0:T(8,128)(2,1)S(1)}, u32[]{:S(2)}, u32[]{:S(2)}) collective-permute-start(bf16[1,256,512]{2,1,0:T(8,128)(2,1)S(1)} %get-tuple-element.122), channel_id=1, source_target_pairs={{0,2},{1,3},{2,0},{3,1},{4,6},{5,7},{6,4},{7,5},{8,10},{9,11},{10,... | collective-permute-start | bytes 786440 | tf_op jit(solution)/shard_map/ppermute | solution.py:838
  49.0 0.8 %collective-permute-done.13.refs_20_ = bf16[4,128,128]{2,1,0:T(8,128)(2,1)S(1)} collective-permute-done((bf16[4,128,128]{2,1,0:T(8,128)(2,1)S(1)}, bf16[4,128,128]{2,1,0:T(8,128)(2,1)S(1)}, u32[]{:S(2)}, u32[]{:S(2)}) %collective-permute-start.13) | collective-permute-done | bytes 131104 | tf_op jit(solution)/shard_map/ppermute | solution.py:838
  49.9 5.8 %finish.1 = (bf16[256,1536]{1,0:T(8,128)(2,1)S(1)}, bf16[256,128]{1,0:T(8,128)(2,1)S(1)}) custom-call(s32[2]{0:T(128)S(1)} %pad_add_fusion.place_ref, f32[3,4,256,128]{3,2,1,0:T(8,128)S(1)} %get-tuple-element.69.qkv_ref.refs_0_, f32[256,128]{1,0:T(8,128)S(1)} %get-tuple-element.85.refs_1_, f32[256,128]{1,0:T(8,128)S(1)} %get-tuple-element.67.pack_ref.refs_1_.refs_2_, ...), custom_call_target="tpu_custom_call" | custom-call | tf_op jit(solution)/shard_map/finish/pallas_call | solution.py:95
  55.7 2.6 %pull_tokens.1 = (bf16[2,256,256]{2,1,0:T(8,128)(2,1)S(1)}, bf16[2,256,256]{2,1,0:T(8,128)(2,1)S(1)}, bf16[256,256]{1,0:T(8,128)(2,1)S(1)}, bf16[256,256]{1,0:T(...) custom-call(s32[2]{0:T(128)S(1)} %pad_add_fusion.place_ref, ...), custom_call_target="tpu_custom_call" | custom-call | tf_op jit(solution)/shard_map/pull_tokens/pallas_call | solution.py:95
  58.3 0.8 collective-permute-start.15
  59.1 1.5 %collective-permute-done.14.refs_1_ = bf16[1,256,512]{2,1,0:T(8,128)(2,1)S(1)} collective-permute-done((bf16[1,256,512]{2,1,0:T(8,128)(2,1)S(1)}, bf16[1,256,512]{2,1,0:T(8,128)(2,1)S(1)}, u32[]{:S(2)}, u32[]{:S(2)}) %collective-permute-start.14) | collective-permute-done | bytes 262176 | tf_op jit(solution)/shard_map/ppermute | solution.py:838
  60.6 0.9 %collective-permute-start.17 = (bf16[256,256]{1,0:T(8,128)(2,1)S(1)}, bf16[256,256]{1,0:T(8,128)(2,1)S(1)}, u32[]{:S(2)}, u32[]{:S(2)}) collective-permute-start(bf16[256,256]{1,0:T(8,128)(2,1)S(1)} %get-tuple-element.129), channel_id=1, source_target_pairs={{0,2},{1,3},{2,0},{3,1},{4,6},{5,7},{6,4},{7,5},{8,10},{9,11},{10,... | collective-permute-start | bytes 393224 | tf_op jit(solution)/shard_map/ppermute | solution.py:838
  61.4 2.7 %collective-permute-start.18 = (bf16[256,256]{1,0:T(8,128)(2,1)S(1)}, bf16[256,256]{1,0:T(8,128)(2,1)S(1)}, u32[]{:S(2)}, u32[]{:S(2)}) collective-permute-start(bf16[256,256]{1,0:T(8,128)(2,1)S(1)} %get-tuple-element.130), channel_id=1, source_target_pairs={{0,3},{1,2},{2,1},{3,0},{4,7},{5,6},{6,5},{7,4},{8,11},{9,10},{10,... | collective-permute-start | bytes 393224 | tf_op jit(solution)/shard_map/ppermute | solution.py:838
  64.1 0.6 collective-permute-start.19
  64.7 6.9 %collective-permute-done.15.got_ref = bf16[2,256,256]{2,1,0:T(8,128)(2,1)S(1)} collective-permute-done((bf16[2,256,256]{2,1,0:T(8,128)(2,1)S(1)}, bf16[2,256,256]{2,1,0:T(8,128)(2,1)S(1)}, u32[]{:S(2)}, u32[]{:S(2)}) %collective-permute-start.15) | collective-permute-done | bytes 262176 | tf_op jit(solution)/shard_map/ppermute | solution.py:838
  71.7 0.7 head_sum.2
  72.5 2.8 %collective-permute-done.18.refs_4_ = bf16[256,256]{1,0:T(8,128)(2,1)S(1)} collective-permute-done((bf16[256,256]{1,0:T(8,128)(2,1)S(1)}, bf16[256,256]{1,0:T(8,128)(2,1)S(1)}, u32[]{:S(2)}, u32[]{:S(2)}) %collective-permute-start.18) | collective-permute-done | bytes 131104 | tf_op jit(solution)/shard_map/ppermute | solution.py:838
  75.3 5.2 %collective-permute-done.16.refs_1_ = bf16[1,256,256]{2,1,0:T(8,128)(2,1)S(1)} collective-permute-done((bf16[1,256,256]{2,1,0:T(8,128)(2,1)S(1)}, bf16[1,256,256]{2,1,0:T(8,128)(2,1)S(1)}, u32[]{:S(2)}, u32[]{:S(2)}) %collective-permute-start.16) | collective-permute-done | bytes 131104 | tf_op jit(solution)/shard_map/ppermute | solution.py:838
  80.5 0.8 head_sum.3
  (33 shorter events, 3.0 us)
Async XLA Ops:
  0.7 20.3 %copy-start = (bf16[4,128,2048]{2,1,0:T(8,128)(2,1)S(1)}, bf16[4,128,2048]{2,1,0:T(8,128)(2,1)}, u32[]{:S(2)}) copy-start(bf16[4,128,2048]{2,1,0:T(8,128)(2,1)} %param.12) | copy-start | bytes 6291460
  0.7 20.3 %copy-start.1 = (bf16[256,2048]{1,0:T(8,128)(2,1)S(1)}, bf16[256,2048]{1,0:T(8,128)(2,1)}, u32[]{:S(2)}) copy-start(bf16[256,2048]{1,0:T(8,128)(2,1)} %grad_ref.1) | copy-start | bytes 3145732
  14.1 1.7 %collective-permute-start = (bf16[4,128,256]{2,1,0:T(8,128)(2,1)S(1)}, bf16[4,128,256]{2,1,0:T(8,128)(2,1)S(1)}, u32[]{:S(2)}, u32[]{:S(2)}) collective-permute-start(bf16[4,128,256]{2,1,0:T(8,128)(2,1)S(1)} %get-tuple-element.68.own_ref), channel_id=1, source_target_pairs={{0,4},{4,0},{8,12},{12,8},{16,20},{20,16},{24,28},{28,24},{1,5},{5... | collective-permute-start | bytes 786440 | tf_op jit(solution)/shard_map/ppermute | solution.py:838
  16.5 7.8 %collective-permute-start.3 = (bf16[2,128,256]{2,1,0:T(8,128)(2,1)S(1)}, bf16[2,128,256]{2,1,0:T(8,128)(2,1)S(1)}, u32[]{:S(2)}, u32[]{:S(2)}) collective-permute-start(bf16[2,128,256]{2,1,0:T(8,128)(2,1)S(1)} %join_half.1), channel_id=1, source_target_pairs={{0,24},{4,28},{8,16},{12,20},{16,8},{20,12},{24,0},{28,4},{1,25},{... | collective-permute-start | bytes 393224 | tf_op jit(solution)/shard_map/ppermute | solution.py:838
  20.4 6.6 %collective-permute-start.2 = (bf16[2,128,256]{2,1,0:T(8,128)(2,1)S(1)}, bf16[2,128,256]{2,1,0:T(8,128)(2,1)S(1)}, u32[]{:S(2)}, u32[]{:S(2)}) collective-permute-start(bf16[2,128,256]{2,1,0:T(8,128)(2,1)S(1)} %join_half.1), channel_id=1, source_target_pairs={{0,16},{4,20},{8,24},{12,28},{16,0},{20,4},{24,8},{28,12},{1,17},{... | collective-permute-start | bytes 393224 | tf_op jit(solution)/shard_map/ppermute | solution.py:838
  20.9 6.4 %collective-permute-start.1 = (bf16[2,128,256]{2,1,0:T(8,128)(2,1)S(1)}, bf16[2,128,256]{2,1,0:T(8,128)(2,1)S(1)}, u32[]{:S(2)}, u32[]{:S(2)}) collective-permute-start(bf16[2,128,256]{2,1,0:T(8,128)(2,1)S(1)} %join_half.1), channel_id=1, source_target_pairs={{0,8},{4,12},{8,0},{12,4},{16,24},{20,28},{24,16},{28,20},{1,9},{5... | collective-permute-start | bytes 393224 | tf_op jit(solution)/shard_map/ppermute | solution.py:838
  21.0 8.1 %copy-start.2 = (f32[128]{0:T(128)S(1)}, f32[128]{0:T(128)}, u32[]{:S(2)}) copy-start(f32[128]{0:T(128)} %param.11) | copy-start | bytes 1540
  27.3 1.3 %collective-permute-start.4 = (bf16[2,128,256]{2,1,0:T(8,128)(2,1)S(1)}, bf16[2,128,256]{2,1,0:T(8,128)(2,1)S(1)}, u32[]{:S(2)}, u32[]{:S(2)}) collective-permute-start(bf16[2,128,256]{2,1,0:T(8,128)(2,1)S(1)} %collective-permute-done.1.refs_1_), channel_id=1, source_target_pairs={{0,4},{4,0},{8,12},{12,8},{16,20},{20,16},{24,28},{28,24},{1,5},{5... | collective-permute-start | bytes 393224 | tf_op jit(solution)/shard_map/ppermute | solution.py:838
  27.3 1.5 %collective-permute-start.5 = (bf16[2,128,256]{2,1,0:T(8,128)(2,1)S(1)}, bf16[2,128,256]{2,1,0:T(8,128)(2,1)S(1)}, u32[]{:S(2)}, u32[]{:S(2)}) collective-permute-start(bf16[2,128,256]{2,1,0:T(8,128)(2,1)S(1)} %collective-permute-done.2.refs_2_), channel_id=1, source_target_pairs={{0,4},{4,0},{8,12},{12,8},{16,20},{20,16},{24,28},{28,24},{1,5},{5... | collective-permute-start | bytes 393224 | tf_op jit(solution)/shard_map/ppermute | solution.py:838
  27.8 1.3 %collective-permute-start.6 = (bf16[2,128,256]{2,1,0:T(8,128)(2,1)S(1)}, bf16[2,128,256]{2,1,0:T(8,128)(2,1)S(1)}, u32[]{:S(2)}, u32[]{:S(2)}) collective-permute-start(bf16[2,128,256]{2,1,0:T(8,128)(2,1)S(1)} %collective-permute-done.3.refs_3_), channel_id=1, source_target_pairs={{0,4},{4,0},{8,12},{12,8},{16,20},{20,16},{24,28},{28,24},{1,5},{5... | collective-permute-start | bytes 393224 | tf_op jit(solution)/shard_map/ppermute | solution.py:838
  32.2 14.1 %collective-permute-start.7 = (bf16[2,256,512]{2,1,0:T(8,128)(2,1)S(1)}, bf16[2,256,512]{2,1,0:T(8,128)(2,1)S(1)}, u32[]{:S(2)}, u32[]{:S(2)}) collective-permute-start(bf16[2,256,512]{2,1,0:T(8,128)(2,1)S(1)} %get-tuple-element.83), channel_id=1, source_target_pairs={{0,1},{1,0},{2,3},{3,2},{4,5},{5,4},{6,7},{7,6},{8,9},{9,8},{10,11... | collective-permute-start | bytes 1572872 | tf_op jit(solution)/shard_map/ppermute | solution.py:838
  35.9 1.8 %collective-permute-start.9 = (bf16[4,128,256]{2,1,0:T(8,128)(2,1)S(1)}, bf16[4,128,256]{2,1,0:T(8,128)(2,1)S(1)}, u32[]{:S(2)}, u32[]{:S(2)}) collective-permute-start(bf16[4,128,256]{2,1,0:T(8,128)(2,1)S(1)} %get-tuple-element.110.refs_0_), channel_id=1, source_target_pairs={{0,4},{4,0},{8,12},{12,8},{16,20},{20,16},{24,28},{28,24},{1,5},{5... | collective-permute-start | bytes 786440 | tf_op jit(solution)/shard_map/ppermute | solution.py:838
  36.0 1.7 %collective-permute-start.10 = (bf16[4,128,128]{2,1,0:T(8,128)(2,1)S(1)}, bf16[4,128,128]{2,1,0:T(8,128)(2,1)S(1)}, u32[]{:S(2)}, u32[]{:S(2)}) collective-permute-start(bf16[4,128,128]{2,1,0:T(8,128)(2,1)S(1)} %get-tuple-element.111.refs_1_), channel_id=1, source_target_pairs={{0,4},{4,0},{8,12},{12,8},{16,20},{20,16},{24,28},{28,24},{1,5},{5... | collective-permute-start | bytes 393224 | tf_op jit(solution)/shard_map/ppermute | solution.py:838
  36.5 12.6 %collective-permute-start.8 = (bf16[4,128,256]{2,1,0:T(8,128)(2,1)S(1)}, bf16[4,128,256]{2,1,0:T(8,128)(2,1)S(1)}, u32[]{:S(2)}, u32[]{:S(2)}) collective-permute-start(bf16[4,128,256]{2,1,0:T(8,128)(2,1)S(1)} %get-tuple-element.109), channel_id=1, source_target_pairs={{0,4},{4,0},{8,12},{12,8},{16,20},{20,16},{24,28},{28,24},{1,5},{5... | collective-permute-start | bytes 786440 | tf_op jit(solution)/shard_map/ppermute | solution.py:838
  37.8 12.1 %collective-permute-start.11 = (bf16[4,128,256]{2,1,0:T(8,128)(2,1)S(1)}, bf16[4,128,256]{2,1,0:T(8,128)(2,1)S(1)}, u32[]{:S(2)}, u32[]{:S(2)}) collective-permute-start(bf16[4,128,256]{2,1,0:T(8,128)(2,1)S(1)} %get-tuple-element.112), channel_id=1, source_target_pairs={{0,8},{4,12},{8,0},{12,4},{16,24},{20,28},{24,16},{28,20},{1,9},{5... | collective-permute-start | bytes 786440 | tf_op jit(solution)/shard_map/ppermute | solution.py:838
  39.3 10.5 %collective-permute-start.13 = (bf16[4,128,128]{2,1,0:T(8,128)(2,1)S(1)}, bf16[4,128,128]{2,1,0:T(8,128)(2,1)S(1)}, u32[]{:S(2)}, u32[]{:S(2)}) collective-permute-start(bf16[4,128,128]{2,1,0:T(8,128)(2,1)S(1)} %get-tuple-element.113), channel_id=1, source_target_pairs={{0,24},{4,28},{8,16},{12,20},{16,8},{20,12},{24,0},{28,4},{1,25},{... | collective-permute-start | bytes 393224 | tf_op jit(solution)/shard_map/ppermute | solution.py:838
  40.7 9.1 %collective-permute-start.12 = (bf16[4,128,128]{2,1,0:T(8,128)(2,1)S(1)}, bf16[4,128,128]{2,1,0:T(8,128)(2,1)S(1)}, u32[]{:S(2)}, u32[]{:S(2)}) collective-permute-start(bf16[4,128,128]{2,1,0:T(8,128)(2,1)S(1)} %get-tuple-element.113), channel_id=1, source_target_pairs={{0,16},{4,20},{8,24},{12,28},{16,0},{20,4},{24,8},{28,12},{1,17},{... | collective-permute-start | bytes 393224 | tf_op jit(solution)/shard_map/ppermute | solution.py:838
  41.3 14.3 %slice-start = ((s8[6291456]{0:T(1024)(128)(4,1)}), s8[2097152]{0:T(1024)(128)(4,1)S(1)}, s32[]{:S(2)}) async-start(s8[6291456]{0:T(1024)(128)(4,1)} %bitcast.9), calls=%async_computation | async-start | bytes 4194304
  46.3 9.4 %slice-start.1 = ((s8[6291456]{0:T(1024)(128)(4,1)}), s8[4194304]{0:T(1024)(128)(4,1)S(1)}, s32[]{:S(2)}) async-start(s8[6291456]{0:T(1024)(128)(4,1)} %bitcast.9), calls=%async_computation.1 | async-start | bytes 8388608
  46.4 14.2 %collective-permute-start.14 = (bf16[1,256,512]{2,1,0:T(8,128)(2,1)S(1)}, bf16[1,256,512]{2,1,0:T(8,128)(2,1)S(1)}, u32[]{:S(2)}, u32[]{:S(2)}) collective-permute-start(bf16[1,256,512]{2,1,0:T(8,128)(2,1)S(1)} %get-tuple-element.122), channel_id=1, source_target_pairs={{0,2},{1,3},{2,0},{3,1},{4,6},{5,7},{6,4},{7,5},{8,10},{9,11},{10,... | collective-permute-start | bytes 786440 | tf_op jit(solution)/shard_map/ppermute | solution.py:838
  58.3 13.3 %collective-permute-start.15 = (bf16[2,256,256]{2,1,0:T(8,128)(2,1)S(1)}, bf16[2,256,256]{2,1,0:T(8,128)(2,1)S(1)}, u32[]{:S(2)}, u32[]{:S(2)}) collective-permute-start(bf16[2,256,256]{2,1,0:T(8,128)(2,1)S(1)} %get-tuple-element.125), channel_id=1, source_target_pairs={{0,1},{1,0},{2,3},{3,2},{4,5},{5,4},{6,7},{7,6},{8,9},{9,8},{10,11... | collective-permute-start | bytes 786440 | tf_op jit(solution)/shard_map/ppermute | solution.py:838
  60.6 11.9 %collective-permute-start.17 = (bf16[256,256]{1,0:T(8,128)(2,1)S(1)}, bf16[256,256]{1,0:T(8,128)(2,1)S(1)}, u32[]{:S(2)}, u32[]{:S(2)}) collective-permute-start(bf16[256,256]{1,0:T(8,128)(2,1)S(1)} %get-tuple-element.129), channel_id=1, source_target_pairs={{0,2},{1,3},{2,0},{3,1},{4,6},{5,7},{6,4},{7,5},{8,10},{9,11},{10,... | collective-permute-start | bytes 393224 | tf_op jit(solution)/shard_map/ppermute | solution.py:838
  61.4 13.9 %collective-permute-start.18 = (bf16[256,256]{1,0:T(8,128)(2,1)S(1)}, bf16[256,256]{1,0:T(8,128)(2,1)S(1)}, u32[]{:S(2)}, u32[]{:S(2)}) collective-permute-start(bf16[256,256]{1,0:T(8,128)(2,1)S(1)} %get-tuple-element.130), channel_id=1, source_target_pairs={{0,3},{1,2},{2,1},{3,0},{4,7},{5,6},{6,5},{7,4},{8,11},{9,10},{10,... | collective-permute-start | bytes 393224 | tf_op jit(solution)/shard_map/ppermute | solution.py:838
  64.1 11.2 %collective-permute-start.19 = (bf16[256,256]{1,0:T(8,128)(2,1)S(1)}, bf16[256,256]{1,0:T(8,128)(2,1)S(1)}, u32[]{:S(2)}, u32[]{:S(2)}) collective-permute-start(bf16[256,256]{1,0:T(8,128)(2,1)S(1)} %get-tuple-element.131), channel_id=1, source_target_pairs={{0,1},{1,0},{2,3},{3,2},{4,5},{5,4},{6,7},{7,6},{8,9},{9,8},{10,11... | collective-permute-start | bytes 393224 | tf_op jit(solution)/shard_map/ppermute | solution.py:838
  71.7 8.8 %collective-permute-start.16 = (bf16[1,256,256]{2,1,0:T(8,128)(2,1)S(1)}, bf16[1,256,256]{2,1,0:T(8,128)(2,1)S(1)}, u32[]{:S(2)}, u32[]{:S(2)}) collective-permute-start(bf16[1,256,256]{2,1,0:T(8,128)(2,1)S(1)} %get-tuple-element.127), channel_id=1, source_target_pairs={{0,2},{1,3},{2,0},{3,1},{4,6},{5,7},{6,4},{7,5},{8,10},{9,11},{10,... | collective-permute-start | bytes 393224 | tf_op jit(solution)/shard_map/ppermute | solution.py:838

commit v9 on v8

--- a/solution.py
+++ b/solution.py
@@ -50,8 +50,12 @@
     return mm_nt(left_high, right_high) + (mm_nt(left_low, right_high) + mm_nt(left_high, right_low))
 
 
-def mm_full(left, right):
-    return jnp.dot(left, right, precision=lax.Precision.HIGHEST, preferred_element_type=F32)
+def mm_ones(ones, values):
+    high = values.astype(BF16)
+    rest = values - high.astype(F32)
+    middle = rest.astype(BF16)
+    low = (rest - middle.astype(F32)).astype(BF16)
+    return mm(ones, high) + (mm(ones, middle) + mm(ones, low))
 
 
 def pair_ids(count):
@@ -173,7 +177,8 @@
     heads, levels, chunks = sizes
     (wr_hbm, small_ref, qkv_ref, gate_ref, pack_ref, pack_t_ref, trans_ref, mixed_t_ref,
      decay_ref, base_ref, lower_ref, rates_ref, pair_ref) = refs[:13]
-    tokens, wide_in, wr, small_in, small_wide, acc, hp_ref, sems, in_sems, out_sems = refs[13:]
+    tokens, wide_in, wide_even, wide_odd, wr, small_in, small_wide, acc, hp_ref = refs[13:22]
+    sems, in_sems, out_sems = refs[22:]
     rows, width = tokens.shape
     depth = width // chunks
     cols = 3 * heads
@@ -196,25 +201,15 @@
     fetch_tokens.start()
     for fetch in fetches[1:]:
         fetch.start()
-    group = 16
-    size = group * cols
-    turn_row, turn_col = pair_ids(size)
-    turn = (turn_col == (turn_row % group) * cols + turn_row // group).astype(F32).astype(BF16)
 
     def relay(chunk):
         fetches[chunk].wait()
-        first = chunk * depth * cols
-        packs = depth // group
-        side = jnp.concatenate(
-            [wide_in[first + at * size : first + (at + 1) * size, :] for at in range(packs)], 1
-        )
-        turned = jnp.dot(turn, side, preferred_element_type=F32).astype(BF16)
-        for at in range(packs):
-            row = chunk * depth + at * group
-            for col in range(cols):
-                wr[row : row + group, col * LANES : (col + 1) * LANES] = turned[
-                    col * group : (col + 1) * group, at * LANES : (at + 1) * LANES
-                ]
+        wide = wide_odd if chunk % 2 else wide_even
+        at = chunk * depth
+        wide[...] = wide_in[at * cols : (at + depth) * cols, :].astype(F32)
+        for col in range(cols):
+            value = wide[pl.ds(col, depth, stride=cols), :]
+            wr[at : at + depth, col * LANES : (col + 1) * LANES] = value.astype(BF16)
         keeps[chunk].start()
 
     decay_col = levels * heads
@@ -241,7 +236,7 @@
     gate_ref[...] = gate
     switch = jax.nn.sigmoid(gate + bias)
     lam = jnp.maximum(gate, 0.0) + jnp.log1p(jnp.exp(-jnp.abs(gate)))
-    cum = mm_full(inclusive.astype(F32), -rate * switch)
+    cum = mm_ones(inclusive.astype(F32), -rate * switch)
     pack = jnp.where(lane < decay_col, lam, jnp.where(lane < beta_col, cum, switch))
     pack_t = pack.T
     pack_t_ref[...] = pack_t
@@ -285,9 +280,9 @@
 
     def later():
         for part in (2, 0):
-            for at in range(0, chunks, chunks // 4):
+            for at in range(0, chunks, chunks // 2):
                 yield
-                multiply(part, at, at + chunks // 4)
+                multiply(part, at, at + chunks // 2)
 
     chain, filler = invert(lower_all, eye, apart, rows), later()
     while True:
@@ -350,6 +345,8 @@
     scratch = [
         pltpu.VMEM(tokens.shape, BF16),
         pltpu.VMEM(flat_w.shape, BF16),
+        pltpu.VMEM((width // chunks * cols, key), F32),
+        pltpu.VMEM((width // chunks * cols, key), F32),
         pltpu.VMEM((width, cols * key), BF16),
         pltpu.VMEM(small.shape, BF16),
         pltpu.VMEM((LANES, width), F32),
@@ -787,7 +784,7 @@
     dcol = dcol + drow.T
     rate, bias = rates_ref[0:1, :], rates_ref[1:2, :]
     switch = jax.nn.sigmoid(gate_ref[...] + bias)
-    dlog = mm_full((row_id <= col_id).astype(F32), dcol)
+    dlog = mm_ones((row_id <= col_id).astype(F32), dcol)
     slope = switch * (1.0 - switch)
     dgate = jnp.where(
         lane < decay_col,

time: 81.5 us -> 80.7 us (level)
  Pallas kernels: 35.2 us -> 34.1 us
    pallas_call x13, Pallas kernels: 35.2 us -> 34.1 us  [local_call(): pl.pallas_call(body, out_shape=tuple(out_shape), in_specs=[SCALARS] * len...]
where the time goes in v9:
time: 80.7 us; the launch traced here: 80.6 us
  Pallas kernels  34.1 us (42%)
  waiting for transfers between devices  26.6 us (33%)
  starting transfers between devices  19 us (24%)
    pallas_call x13, Pallas kernels, local_call(): pl.pallas_call(body, out_shape=tuple(out_shape), in_specs=[SCALARS] * len...  34.1 us
    ppermute x20, waiting for transfers between devices, swap(): return lax.ppermute(value, axis, [(at, at ^ mask) for at in range(size)])  26.6 us
    ppermute x20, starting transfers between devices, swap(): return lax.ppermute(value, axis, [(at, at ^ mask) for at in range(size)])  19 us
  transfers between devices with their start and end apart: 20, of which 14 were waited for; matrix products, arithmetic and copies ran while one was open for 0% of the time, Pallas kernels for 21%

profile of v9, /device:TPU:0, one launch (start us, length us, event | category | flops | bytes accessed | tf_op | source)
XLA Modules:
  0.0 80.6 jit_solution(1674694083715622744)
XLA Ops:
  0.7 12.7 %project.1 = (bf16[2048,1536]{1,0:T(8,128)(2,1)}, bf16[128,2048]{1,0:T(8,128)(2,1)S(1)}, f32[3,4,256,128]{3,2,1,0:T(8,128)S(1)}, f32[256,128]{1,0:T(8,128)S(1)},...) custom-call(s32[2]{0:T(128)S(1)} %pad_add_fusion.place_ref, ...), custom_call_target="tpu_custom_call" | custom-call | tf_op jit(solution)/shard_map/project/pallas_call | solution.py:99
  13.4 0.5 collective-permute-start
  13.9 1.2 %collective-permute-done.other_ref.refs_0_.refs_14_ = bf16[4,128,256]{2,1,0:T(8,128)(2,1)S(1)} collective-permute-done((bf16[4,128,256]{2,1,0:T(8,128)(2,1)S(1)}, bf16[4,128,256]{2,1,0:T(8,128)(2,1)S(1)}, u32[]{:S(2)}, u32[]{:S(2)}) %collective-permute-start) | collective-permute-done | bytes 262176 | tf_op jit(solution)/shard_map/ppermute | solution.py:835
  15.1 0.7 join_half.1
  15.8 3.9 %collective-permute-start.3 = (bf16[2,128,256]{2,1,0:T(8,128)(2,1)S(1)}, bf16[2,128,256]{2,1,0:T(8,128)(2,1)S(1)}, u32[]{:S(2)}, u32[]{:S(2)}) collective-permute-start(bf16[2,128,256]{2,1,0:T(8,128)(2,1)S(1)} %join_half.1), channel_id=1, source_target_pairs={{0,24},{4,28},{8,16},{12,20},{16,8},{20,12},{24,0},{28,4},{1,25},{... | collective-permute-start | bytes 393224 | tf_op jit(solution)/shard_map/ppermute | solution.py:835
  19.7 0.5 collective-permute-start.2
  20.4 2.3 %local_part.1 = (bf16[4,256,256]{2,1,0:T(8,128)(2,1)S(1)}, bf16[4,256,256]{2,1,0:T(8,128)(2,1)S(1)}, bf16[4,256,256]{2,1,0:T(8,128)(2,1)S(1)}, bf16[4,256,256]{2...) custom-call(f32[3,4,256,128]{3,2,1,0:T(8,128)S(1)} %get-tuple-elemen, ...), custom_call_target="tpu_custom_call" | custom-call | tf_op jit(solution)/shard_map/local_part/pallas_call | solution.py:99
  22.6 1.0 %collective-permute-done.3.refs_3_ = bf16[2,128,256]{2,1,0:T(8,128)(2,1)S(1)} collective-permute-done((bf16[2,128,256]{2,1,0:T(8,128)(2,1)S(1)}, bf16[2,128,256]{2,1,0:T(8,128)(2,1)S(1)}, u32[]{:S(2)}, u32[]{:S(2)}) %collective-permute-start.3) | collective-permute-done | bytes 131104 | tf_op jit(solution)/shard_map/ppermute | solution.py:835
  23.6 2.7 %collective-permute-done.2.refs_2_ = bf16[2,128,256]{2,1,0:T(8,128)(2,1)S(1)} collective-permute-done((bf16[2,128,256]{2,1,0:T(8,128)(2,1)S(1)}, bf16[2,128,256]{2,1,0:T(8,128)(2,1)S(1)}, u32[]{:S(2)}, u32[]{:S(2)}) %collective-permute-start.2) | collective-permute-done | bytes 131104 | tf_op jit(solution)/shard_map/ppermute | solution.py:835
  27.1 0.8 %collective-permute-done.4.refs_4_ = bf16[2,128,256]{2,1,0:T(8,128)(2,1)S(1)} collective-permute-done((bf16[2,128,256]{2,1,0:T(8,128)(2,1)S(1)}, bf16[2,128,256]{2,1,0:T(8,128)(2,1)S(1)}, u32[]{:S(2)}, u32[]{:S(2)}) %collective-permute-start.4) | collective-permute-done | bytes 131104 | tf_op jit(solution)/shard_map/ppermute | solution.py:835
  28.4 3.0 %reach.1 = (bf16[2,256,512]{2,1,0:T(8,128)(2,1)S(1)}, bf16[2,256,512]{2,1,0:T(8,128)(2,1)S(1)}, f32[4,256,128]{2,1,0:T(8,128)S(1)}, bf16[4,128,384]{2,1,0:T(8,12...) custom-call(s32[2]{0:T(128)S(1)} %pad_add_fusion.place_ref, ...), custom_call_target="tpu_custom_call" | custom-call | tf_op jit(solution)/shard_map/reach/pallas_call | solution.py:99
  31.5 1.6 %collective-permute-start.7 = (bf16[2,256,512]{2,1,0:T(8,128)(2,1)S(1)}, bf16[2,256,512]{2,1,0:T(8,128)(2,1)S(1)}, u32[]{:S(2)}, u32[]{:S(2)}) collective-permute-start(bf16[2,256,512]{2,1,0:T(8,128)(2,1)S(1)} %get-tuple-element.83), channel_id=1, source_target_pairs={{0,1},{1,0},{2,3},{3,2},{4,5},{5,4},{6,7},{7,6},{8,9},{9,8},{10,11... | collective-permute-start | bytes 1572872 | tf_op jit(solution)/shard_map/ppermute | solution.py:835
  33.1 2.1 %return_states.1 = (f32[4,256,128]{2,1,0:T(8,128)S(1)}, bf16[4,128,256]{2,1,0:T(8,128)(2,1)S(1)}, bf16[4,128,256]{2,1,0:T(8,128)(2,1)S(1)}, bf16[4,128,128]{2,1,0:T(8,128)(2,1)S(1)}) custom-call(s32[2]{0:T(128)S(1)} %pad_add_fusion.place_ref, f32[256,128]{1,0:T(8,128)S(1)} %get-tuple-element.67.pack_ref.refs_1_.refs_2_, ...), custom_call_target="tpu_custom_call" | custom-call | tf_op jit(solution)/shard_map/return_states/pallas_call | solution.py:99
  35.8 1.1 %collective-permute-done.10.refs_3_ = bf16[4,128,128]{2,1,0:T(8,128)(2,1)S(1)} collective-permute-done((bf16[4,128,128]{2,1,0:T(8,128)(2,1)S(1)}, bf16[4,128,128]{2,1,0:T(8,128)(2,1)S(1)}, u32[]{:S(2)}, u32[]{:S(2)}) %collective-permute-start.10) | collective-permute-done | bytes 131104 | tf_op jit(solution)/shard_map/ppermute | solution.py:835
  37.1 1.6 %collective-permute-start.11 = (bf16[4,128,256]{2,1,0:T(8,128)(2,1)S(1)}, bf16[4,128,256]{2,1,0:T(8,128)(2,1)S(1)}, u32[]{:S(2)}, u32[]{:S(2)}) collective-permute-start(bf16[4,128,256]{2,1,0:T(8,128)(2,1)S(1)} %get-tuple-element.112), channel_id=1, source_target_pairs={{0,8},{4,12},{8,0},{12,4},{16,24},{20,28},{24,16},{28,20},{1,9},{5... | collective-permute-start | bytes 786440 | tf_op jit(solution)/shard_map/ppermute | solution.py:835
  38.7 1.4 %collective-permute-start.13 = (bf16[4,128,128]{2,1,0:T(8,128)(2,1)S(1)}, bf16[4,128,128]{2,1,0:T(8,128)(2,1)S(1)}, u32[]{:S(2)}, u32[]{:S(2)}) collective-permute-start(bf16[4,128,128]{2,1,0:T(8,128)(2,1)S(1)} %get-tuple-element.113), channel_id=1, source_target_pairs={{0,24},{4,28},{8,16},{12,20},{16,8},{20,12},{24,0},{28,4},{1,25},{... | collective-permute-start | bytes 393224 | tf_op jit(solution)/shard_map/ppermute | solution.py:835
  40.0 0.6 collective-permute-start.12
  40.6 3.5 %pull_local.1 = (f32[3,4,256,128]{3,2,1,0:T(8,128)S(1)}, f32[4,256,128]{2,1,0:T(8,128)S(1)}, f32[256,128]{1,0:T(8,128)S(1)}, f32[8,256]{1,0:T(8,128)S(1)}) custom-call(f32[3,4,256,128]{3,2,1,0:T(8,128)S(1)} %get-tuple-element.69.qkv_ref.refs_0_, f32[256,128]{1,0:T(8,128)S(1)} %get-tuple-element.67.pack_ref.refs_1_.refs_2_, ...), custom_call_target="tpu_custom_call" | custom-call | tf_op jit(solution)/shard_map/pull_local/pallas_call | solution.py:99
  44.2 1.4 %collective-permute-done.7.got_ref = bf16[2,256,512]{2,1,0:T(8,128)(2,1)S(1)} collective-permute-done((bf16[2,256,512]{2,1,0:T(8,128)(2,1)S(1)}, bf16[2,256,512]{2,1,0:T(8,128)(2,1)S(1)}, u32[]{:S(2)}, u32[]{:S(2)}) %collective-permute-start.7) | collective-permute-done | bytes 524320 | tf_op jit(solution)/shard_map/ppermute | solution.py:835
  45.7 2.7 %collective-permute-start.14 = (bf16[1,256,512]{2,1,0:T(8,128)(2,1)S(1)}, bf16[1,256,512]{2,1,0:T(8,128)(2,1)S(1)}, u32[]{:S(2)}, u32[]{:S(2)}) collective-permute-start(bf16[1,256,512]{2,1,0:T(8,128)(2,1)S(1)} %get-tuple-element.122), channel_id=1, source_target_pairs={{0,2},{1,3},{2,0},{3,1},{4,6},{5,7},{6,4},{7,5},{8,10},{9,11},{10,... | collective-permute-start | bytes 786440 | tf_op jit(solution)/shard_map/ppermute | solution.py:835
  48.3 0.8 %collective-permute-done.13.refs_20_ = bf16[4,128,128]{2,1,0:T(8,128)(2,1)S(1)} collective-permute-done((bf16[4,128,128]{2,1,0:T(8,128)(2,1)S(1)}, bf16[4,128,128]{2,1,0:T(8,128)(2,1)S(1)}, u32[]{:S(2)}, u32[]{:S(2)}) %collective-permute-start.13) | collective-permute-done | bytes 131104 | tf_op jit(solution)/shard_map/ppermute | solution.py:835
  49.2 5.4 %finish.1 = (bf16[256,1536]{1,0:T(8,128)(2,1)S(1)}, bf16[256,128]{1,0:T(8,128)(2,1)S(1)}) custom-call(s32[2]{0:T(128)S(1)} %pad_add_fusion.place_ref, f32[3,4,256,128]{3,2,1,0:T(8,128)S(1)} %get-tuple-element.69.qkv_ref.refs_0_, f32[256,128]{1,0:T(8,128)S(1)} %get-tuple-element.85.refs_1_, f32[256,128]{1,0:T(8,128)S(1)} %get-tuple-element.67.pack_ref.refs_1_.refs_2_, ...), custom_call_target="tpu_custom_call" | custom-call | tf_op jit(solution)/shard_map/finish/pallas_call | solution.py:99
  54.6 2.6 %pull_tokens.1 = (bf16[2,256,256]{2,1,0:T(8,128)(2,1)S(1)}, bf16[2,256,256]{2,1,0:T(8,128)(2,1)S(1)}, bf16[256,256]{1,0:T(8,128)(2,1)S(1)}, bf16[256,256]{1,0:T(...) custom-call(s32[2]{0:T(128)S(1)} %pad_add_fusion.place_ref, ...), custom_call_target="tpu_custom_call" | custom-call | tf_op jit(solution)/shard_map/pull_tokens/pallas_call | solution.py:99
  57.2 0.8 collective-permute-start.15
  58.0 1.9 %collective-permute-done.14.refs_1_ = bf16[1,256,512]{2,1,0:T(8,128)(2,1)S(1)} collective-permute-done((bf16[1,256,512]{2,1,0:T(8,128)(2,1)S(1)}, bf16[1,256,512]{2,1,0:T(8,128)(2,1)S(1)}, u32[]{:S(2)}, u32[]{:S(2)}) %collective-permute-start.14) | collective-permute-done | bytes 262176 | tf_op jit(solution)/shard_map/ppermute | solution.py:835
  60.4 3.1 %collective-permute-start.18 = (bf16[256,256]{1,0:T(8,128)(2,1)S(1)}, bf16[256,256]{1,0:T(8,128)(2,1)S(1)}, u32[]{:S(2)}, u32[]{:S(2)}) collective-permute-start(bf16[256,256]{1,0:T(8,128)(2,1)S(1)} %get-tuple-element.130), channel_id=1, source_target_pairs={{0,3},{1,2},{2,1},{3,0},{4,7},{5,6},{6,5},{7,4},{8,11},{9,10},{10,... | collective-permute-start | bytes 393224 | tf_op jit(solution)/shard_map/ppermute | solution.py:835
  63.4 0.6 collective-permute-start.19
  64.0 6.7 %collective-permute-done.15.got_ref = bf16[2,256,256]{2,1,0:T(8,128)(2,1)S(1)} collective-permute-done((bf16[2,256,256]{2,1,0:T(8,128)(2,1)S(1)}, bf16[2,256,256]{2,1,0:T(8,128)(2,1)S(1)}, u32[]{:S(2)}, u32[]{:S(2)}) %collective-permute-start.15) | collective-permute-done | bytes 262176 | tf_op jit(solution)/shard_map/ppermute | solution.py:835
  70.8 0.7 head_sum.2
  71.6 2.7 %collective-permute-done.18.refs_4_ = bf16[256,256]{1,0:T(8,128)(2,1)S(1)} collective-permute-done((bf16[256,256]{1,0:T(8,128)(2,1)S(1)}, bf16[256,256]{1,0:T(8,128)(2,1)S(1)}, u32[]{:S(2)}, u32[]{:S(2)}) %collective-permute-start.18) | collective-permute-done | bytes 131104 | tf_op jit(solution)/shard_map/ppermute | solution.py:835
  74.2 5.6 %collective-permute-done.16.refs_1_ = bf16[1,256,256]{2,1,0:T(8,128)(2,1)S(1)} collective-permute-done((bf16[1,256,256]{2,1,0:T(8,128)(2,1)S(1)}, bf16[1,256,256]{2,1,0:T(8,128)(2,1)S(1)}, u32[]{:S(2)}, u32[]{:S(2)}) %collective-permute-start.16) | collective-permute-done | bytes 131104 | tf_op jit(solution)/shard_map/ppermute | solution.py:835
  79.8 0.8 head_sum.3
  (33 shorter events, 3.0 us)
Async XLA Ops:
  0.7 19.6 %copy-start = (bf16[4,128,2048]{2,1,0:T(8,128)(2,1)S(1)}, bf16[4,128,2048]{2,1,0:T(8,128)(2,1)}, u32[]{:S(2)}) copy-start(bf16[4,128,2048]{2,1,0:T(8,128)(2,1)} %param.12) | copy-start | bytes 6291460
  0.7 19.7 %copy-start.1 = (bf16[256,2048]{1,0:T(8,128)(2,1)S(1)}, bf16[256,2048]{1,0:T(8,128)(2,1)}, u32[]{:S(2)}) copy-start(bf16[256,2048]{1,0:T(8,128)(2,1)} %grad_ref.1) | copy-start | bytes 3145732
  13.4 1.7 %collective-permute-start = (bf16[4,128,256]{2,1,0:T(8,128)(2,1)S(1)}, bf16[4,128,256]{2,1,0:T(8,128)(2,1)S(1)}, u32[]{:S(2)}, u32[]{:S(2)}) collective-permute-start(bf16[4,128,256]{2,1,0:T(8,128)(2,1)S(1)} %get-tuple-element.68.own_ref), channel_id=1, source_target_pairs={{0,4},{4,0},{8,12},{12,8},{16,20},{20,16},{24,28},{28,24},{1,5},{5... | collective-permute-start | bytes 786440 | tf_op jit(solution)/shard_map/ppermute | solution.py:835
  15.8 7.8 %collective-permute-start.3 = (bf16[2,128,256]{2,1,0:T(8,128)(2,1)S(1)}, bf16[2,128,256]{2,1,0:T(8,128)(2,1)S(1)}, u32[]{:S(2)}, u32[]{:S(2)}) collective-permute-start(bf16[2,128,256]{2,1,0:T(8,128)(2,1)S(1)} %join_half.1), channel_id=1, source_target_pairs={{0,24},{4,28},{8,16},{12,20},{16,8},{20,12},{24,0},{28,4},{1,25},{... | collective-permute-start | bytes 393224 | tf_op jit(solution)/shard_map/ppermute | solution.py:835
  19.7 6.6 %collective-permute-start.2 = (bf16[2,128,256]{2,1,0:T(8,128)(2,1)S(1)}, bf16[2,128,256]{2,1,0:T(8,128)(2,1)S(1)}, u32[]{:S(2)}, u32[]{:S(2)}) collective-permute-start(bf16[2,128,256]{2,1,0:T(8,128)(2,1)S(1)} %join_half.1), channel_id=1, source_target_pairs={{0,16},{4,20},{8,24},{12,28},{16,0},{20,4},{24,8},{28,12},{1,17},{... | collective-permute-start | bytes 393224 | tf_op jit(solution)/shard_map/ppermute | solution.py:835
  20.2 6.4 %collective-permute-start.1 = (bf16[2,128,256]{2,1,0:T(8,128)(2,1)S(1)}, bf16[2,128,256]{2,1,0:T(8,128)(2,1)S(1)}, u32[]{:S(2)}, u32[]{:S(2)}) collective-permute-start(bf16[2,128,256]{2,1,0:T(8,128)(2,1)S(1)} %join_half.1), channel_id=1, source_target_pairs={{0,8},{4,12},{8,0},{12,4},{16,24},{20,28},{24,16},{28,20},{1,9},{5... | collective-permute-start | bytes 393224 | tf_op jit(solution)/shard_map/ppermute | solution.py:835
  20.4 8.1 %copy-start.2 = (f32[128]{0:T(128)S(1)}, f32[128]{0:T(128)}, u32[]{:S(2)}) copy-start(f32[128]{0:T(128)} %param.11) | copy-start | bytes 1540
  26.6 1.3 %collective-permute-start.4 = (bf16[2,128,256]{2,1,0:T(8,128)(2,1)S(1)}, bf16[2,128,256]{2,1,0:T(8,128)(2,1)S(1)}, u32[]{:S(2)}, u32[]{:S(2)}) collective-permute-start(bf16[2,128,256]{2,1,0:T(8,128)(2,1)S(1)} %collective-permute-done.1.refs_1_), channel_id=1, source_target_pairs={{0,4},{4,0},{8,12},{12,8},{16,20},{20,16},{24,28},{28,24},{1,5},{5... | collective-permute-start | bytes 393224 | tf_op jit(solution)/shard_map/ppermute | solution.py:835
  26.6 1.5 %collective-permute-start.5 = (bf16[2,128,256]{2,1,0:T(8,128)(2,1)S(1)}, bf16[2,128,256]{2,1,0:T(8,128)(2,1)S(1)}, u32[]{:S(2)}, u32[]{:S(2)}) collective-permute-start(bf16[2,128,256]{2,1,0:T(8,128)(2,1)S(1)} %collective-permute-done.2.refs_2_), channel_id=1, source_target_pairs={{0,4},{4,0},{8,12},{12,8},{16,20},{20,16},{24,28},{28,24},{1,5},{5... | collective-permute-start | bytes 393224 | tf_op jit(solution)/shard_map/ppermute | solution.py:835
  27.1 1.3 %collective-permute-start.6 = (bf16[2,128,256]{2,1,0:T(8,128)(2,1)S(1)}, bf16[2,128,256]{2,1,0:T(8,128)(2,1)S(1)}, u32[]{:S(2)}, u32[]{:S(2)}) collective-permute-start(bf16[2,128,256]{2,1,0:T(8,128)(2,1)S(1)} %collective-permute-done.3.refs_3_), channel_id=1, source_target_pairs={{0,4},{4,0},{8,12},{12,8},{16,20},{20,16},{24,28},{28,24},{1,5},{5... | collective-permute-start | bytes 393224 | tf_op jit(solution)/shard_map/ppermute | solution.py:835
  31.5 14.1 %collective-permute-start.7 = (bf16[2,256,512]{2,1,0:T(8,128)(2,1)S(1)}, bf16[2,256,512]{2,1,0:T(8,128)(2,1)S(1)}, u32[]{:S(2)}, u32[]{:S(2)}) collective-permute-start(bf16[2,256,512]{2,1,0:T(8,128)(2,1)S(1)} %get-tuple-element.83), channel_id=1, source_target_pairs={{0,1},{1,0},{2,3},{3,2},{4,5},{5,4},{6,7},{7,6},{8,9},{9,8},{10,11... | collective-permute-start | bytes 1572872 | tf_op jit(solution)/shard_map/ppermute | solution.py:835
  35.2 1.8 %collective-permute-start.9 = (bf16[4,128,256]{2,1,0:T(8,128)(2,1)S(1)}, bf16[4,128,256]{2,1,0:T(8,128)(2,1)S(1)}, u32[]{:S(2)}, u32[]{:S(2)}) collective-permute-start(bf16[4,128,256]{2,1,0:T(8,128)(2,1)S(1)} %get-tuple-element.110.refs_0_), channel_id=1, source_target_pairs={{0,4},{4,0},{8,12},{12,8},{16,20},{20,16},{24,28},{28,24},{1,5},{5... | collective-permute-start | bytes 786440 | tf_op jit(solution)/shard_map/ppermute | solution.py:835
  35.3 1.7 %collective-permute-start.10 = (bf16[4,128,128]{2,1,0:T(8,128)(2,1)S(1)}, bf16[4,128,128]{2,1,0:T(8,128)(2,1)S(1)}, u32[]{:S(2)}, u32[]{:S(2)}) collective-permute-start(bf16[4,128,128]{2,1,0:T(8,128)(2,1)S(1)} %get-tuple-element.111.refs_1_), channel_id=1, source_target_pairs={{0,4},{4,0},{8,12},{12,8},{16,20},{20,16},{24,28},{28,24},{1,5},{5... | collective-permute-start | bytes 393224 | tf_op jit(solution)/shard_map/ppermute | solution.py:835
  35.8 12.6 %collective-permute-start.8 = (bf16[4,128,256]{2,1,0:T(8,128)(2,1)S(1)}, bf16[4,128,256]{2,1,0:T(8,128)(2,1)S(1)}, u32[]{:S(2)}, u32[]{:S(2)}) collective-permute-start(bf16[4,128,256]{2,1,0:T(8,128)(2,1)S(1)} %get-tuple-element.109), channel_id=1, source_target_pairs={{0,4},{4,0},{8,12},{12,8},{16,20},{20,16},{24,28},{28,24},{1,5},{5... | collective-permute-start | bytes 786440 | tf_op jit(solution)/shard_map/ppermute | solution.py:835
  37.1 12.1 %collective-permute-start.11 = (bf16[4,128,256]{2,1,0:T(8,128)(2,1)S(1)}, bf16[4,128,256]{2,1,0:T(8,128)(2,1)S(1)}, u32[]{:S(2)}, u32[]{:S(2)}) collective-permute-start(bf16[4,128,256]{2,1,0:T(8,128)(2,1)S(1)} %get-tuple-element.112), channel_id=1, source_target_pairs={{0,8},{4,12},{8,0},{12,4},{16,24},{20,28},{24,16},{28,20},{1,9},{5... | collective-permute-start | bytes 786440 | tf_op jit(solution)/shard_map/ppermute | solution.py:835
  38.7 10.5 %collective-permute-start.13 = (bf16[4,128,128]{2,1,0:T(8,128)(2,1)S(1)}, bf16[4,128,128]{2,1,0:T(8,128)(2,1)S(1)}, u32[]{:S(2)}, u32[]{:S(2)}) collective-permute-start(bf16[4,128,128]{2,1,0:T(8,128)(2,1)S(1)} %get-tuple-element.113), channel_id=1, source_target_pairs={{0,24},{4,28},{8,16},{12,20},{16,8},{20,12},{24,0},{28,4},{1,25},{... | collective-permute-start | bytes 393224 | tf_op jit(solution)/shard_map/ppermute | solution.py:835
  40.0 9.1 %collective-permute-start.12 = (bf16[4,128,128]{2,1,0:T(8,128)(2,1)S(1)}, bf16[4,128,128]{2,1,0:T(8,128)(2,1)S(1)}, u32[]{:S(2)}, u32[]{:S(2)}) collective-permute-start(bf16[4,128,128]{2,1,0:T(8,128)(2,1)S(1)} %get-tuple-element.113), channel_id=1, source_target_pairs={{0,16},{4,20},{8,24},{12,28},{16,0},{20,4},{24,8},{28,12},{1,17},{... | collective-permute-start | bytes 393224 | tf_op jit(solution)/shard_map/ppermute | solution.py:835
  40.6 14.0 %slice-start = ((s8[6291456]{0:T(1024)(128)(4,1)}), s8[2097152]{0:T(1024)(128)(4,1)S(1)}, s32[]{:S(2)}) async-start(s8[6291456]{0:T(1024)(128)(4,1)} %bitcast.9), calls=%async_computation | async-start | bytes 4194304
  45.5 9.0 %slice-start.1 = ((s8[6291456]{0:T(1024)(128)(4,1)}), s8[4194304]{0:T(1024)(128)(4,1)S(1)}, s32[]{:S(2)}) async-start(s8[6291456]{0:T(1024)(128)(4,1)} %bitcast.9), calls=%async_computation.1 | async-start | bytes 8388608
  45.7 14.2 %collective-permute-start.14 = (bf16[1,256,512]{2,1,0:T(8,128)(2,1)S(1)}, bf16[1,256,512]{2,1,0:T(8,128)(2,1)S(1)}, u32[]{:S(2)}, u32[]{:S(2)}) collective-permute-start(bf16[1,256,512]{2,1,0:T(8,128)(2,1)S(1)} %get-tuple-element.122), channel_id=1, source_target_pairs={{0,2},{1,3},{2,0},{3,1},{4,6},{5,7},{6,4},{7,5},{8,10},{9,11},{10,... | collective-permute-start | bytes 786440 | tf_op jit(solution)/shard_map/ppermute | solution.py:835
  57.2 13.4 %collective-permute-start.15 = (bf16[2,256,256]{2,1,0:T(8,128)(2,1)S(1)}, bf16[2,256,256]{2,1,0:T(8,128)(2,1)S(1)}, u32[]{:S(2)}, u32[]{:S(2)}) collective-permute-start(bf16[2,256,256]{2,1,0:T(8,128)(2,1)S(1)} %get-tuple-element.125), channel_id=1, source_target_pairs={{0,1},{1,0},{2,3},{3,2},{4,5},{5,4},{6,7},{7,6},{8,9},{9,8},{10,11... | collective-permute-start | bytes 786440 | tf_op jit(solution)/shard_map/ppermute | solution.py:835
  59.9 11.7 %collective-permute-start.17 = (bf16[256,256]{1,0:T(8,128)(2,1)S(1)}, bf16[256,256]{1,0:T(8,128)(2,1)S(1)}, u32[]{:S(2)}, u32[]{:S(2)}) collective-permute-start(bf16[256,256]{1,0:T(8,128)(2,1)S(1)} %get-tuple-element.129), channel_id=1, source_target_pairs={{0,2},{1,3},{2,0},{3,1},{4,6},{5,7},{6,4},{7,5},{8,10},{9,11},{10,... | collective-permute-start | bytes 393224 | tf_op jit(solution)/shard_map/ppermute | solution.py:835
  60.4 13.9 %collective-permute-start.18 = (bf16[256,256]{1,0:T(8,128)(2,1)S(1)}, bf16[256,256]{1,0:T(8,128)(2,1)S(1)}, u32[]{:S(2)}, u32[]{:S(2)}) collective-permute-start(bf16[256,256]{1,0:T(8,128)(2,1)S(1)} %get-tuple-element.130), channel_id=1, source_target_pairs={{0,3},{1,2},{2,1},{3,0},{4,7},{5,6},{6,5},{7,4},{8,11},{9,10},{10,... | collective-permute-start | bytes 393224 | tf_op jit(solution)/shard_map/ppermute | solution.py:835
  63.4 10.8 %collective-permute-start.19 = (bf16[256,256]{1,0:T(8,128)(2,1)S(1)}, bf16[256,256]{1,0:T(8,128)(2,1)S(1)}, u32[]{:S(2)}, u32[]{:S(2)}) collective-permute-start(bf16[256,256]{1,0:T(8,128)(2,1)S(1)} %get-tuple-element.131), channel_id=1, source_target_pairs={{0,1},{1,0},{2,3},{3,2},{4,5},{5,4},{6,7},{7,6},{8,9},{9,8},{10,11... | collective-permute-start | bytes 393224 | tf_op jit(solution)/shard_map/ppermute | solution.py:835
  70.7 9.1 %collective-permute-start.16 = (bf16[1,256,256]{2,1,0:T(8,128)(2,1)S(1)}, bf16[1,256,256]{2,1,0:T(8,128)(2,1)S(1)}, u32[]{:S(2)}, u32[]{:S(2)}) collective-permute-start(bf16[1,256,256]{2,1,0:T(8,128)(2,1)S(1)} %get-tuple-element.127), channel_id=1, source_target_pairs={{0,2},{1,3},{2,0},{3,1},{4,6},{5,7},{6,4},{7,5},{8,10},{9,11},{10,... | collective-permute-start | bytes 393224 | tf_op jit(solution)/shard_map/ppermute | solution.py:835

commit v10 on v9

--- a/solution.py
+++ b/solution.py
@@ -94,7 +94,7 @@
 
 
 def local_call(
-    body, name, limit, out_shape, scalars, arrays, scratch=(), remote=(), out_specs=None
+    body, name, limit, out_shape, scalars, arrays, scratch=(), remote=(), out_specs=None, alias=None
 ):
     return pl.pallas_call(
         body,
@@ -104,6 +104,7 @@
         + [HBM] * len(remote),
         out_specs=tuple(out_specs or [WHOLE] * len(out_shape)),
         scratch_shapes=list(scratch),
+        input_output_aliases=alias or {},
         compiler_params=pltpu.CompilerParams(vmem_limit_bytes=limit * MIB),
         name=name,
     )(*scalars, *pin(arrays, pltpu.VMEM), *pin(remote, pltpu.HBM))
@@ -175,10 +176,11 @@
 
 def project_body(sizes, place_ref, hp_hbm, tokens_hbm, w_hbm, small_hbm, *refs):
     heads, levels, chunks = sizes
-    (wr_hbm, small_ref, qkv_ref, gate_ref, pack_ref, pack_t_ref, trans_ref, mixed_t_ref,
-     decay_ref, base_ref, lower_ref, rates_ref, pair_ref) = refs[:13]
-    tokens, wide_in, wide_even, wide_odd, wr, small_in, small_wide, acc, hp_ref = refs[13:22]
-    sems, in_sems, out_sems = refs[22:]
+    (wr_hbm, query_ref, value_ref, small_ref, qkv_ref, gate_ref, pack_ref, pack_t_ref, trans_ref, mixed_t_ref,
+     decay_ref, base_ref, lower_ref, rates_ref, pair_ref) = refs[:15]
+    tokens, wide_in, wide, key_ref, small_in, small_wide, acc, hp_ref = refs[15:23]
+    sems, in_sems, out_sems = refs[23:]
+    laid = (query_ref, key_ref, value_ref)
     rows, width = tokens.shape
     depth = width // chunks
     cols = 3 * heads
@@ -192,9 +194,8 @@
             pltpu.make_async_copy(w_hbm.at[span, :], wide_in.at[span, :], in_sems.at[chunk])
         )
         span = pl.ds(chunk * depth, depth)
-        keeps.append(
-            pltpu.make_async_copy(wr.at[span, :], wr_hbm.at[span, :], out_sems.at[chunk])
-        )
+        block = wr_hbm.at[span, pl.ds(heads * LANES, heads * LANES)]
+        keeps.append(pltpu.make_async_copy(key_ref.at[span, :], block, out_sems.at[chunk]))
     fetch_small.start()
     fetch_rates.start()
     fetches[0].start()
@@ -202,14 +203,18 @@
     for fetch in fetches[1:]:
         fetch.start()
 
+    def extract(part, chunk):
+        at = chunk * depth
+        for head in range(heads):
+            first = at * cols + part * heads + head
+            value = wide[pl.ds(first, depth, stride=cols), :]
+            laid[part][at : at + depth, head * LANES : (head + 1) * LANES] = value.astype(BF16)
+
     def relay(chunk):
         fetches[chunk].wait()
-        wide = wide_odd if chunk % 2 else wide_even
-        at = chunk * depth
-        wide[...] = wide_in[at * cols : (at + depth) * cols, :].astype(F32)
-        for col in range(cols):
-            value = wide[pl.ds(col, depth, stride=cols), :]
-            wr[at : at + depth, col * LANES : (col + 1) * LANES] = value.astype(BF16)
+        span = slice(chunk * depth * cols, (chunk + 1) * depth * cols)
+        wide[span, :] = wide_in[span, :].astype(F32)
+        extract(1, chunk)
         keeps[chunk].start()
 
     decay_col = levels * heads
@@ -244,7 +249,8 @@
     def multiply(part, first, last):
         span = slice((part * heads) * LANES, (part + 1) * heads * LANES)
         own = jnp.dot(
-            tokens[:, first * depth : last * depth], wr[first * depth : last * depth, span],
+            tokens[:, first * depth : last * depth],
+            laid[part][first * depth : last * depth, :],
             preferred_element_type=F32,
         )
         if first == 0:
@@ -280,9 +286,12 @@
 
     def later():
         for part in (2, 0):
-            for at in range(0, chunks, chunks // 2):
-                yield
-                multiply(part, at, at + chunks // 2)
+            for chunk in range(chunks):
+                extract(part, chunk)
+                if chunk % 4 == 3:
+                    multiply(part, chunk - 3, chunk + 1)
+                if chunk % 2 == 1:
+                    yield
 
     chain, filler = invert(lower_all, eye, apart, rows), later()
     while True:
@@ -329,6 +338,8 @@
     square = (heads, rows, rows)
     out_shape = (
         stored((width, cols * key), BF16),
+        kept((width, heads * key), BF16),
+        kept((width, heads * key), BF16),
         kept((LANES, width), BF16),
         kept((3, heads, rows, key), F32),
         kept((rows, LANES), F32),
@@ -345,9 +356,8 @@
     scratch = [
         pltpu.VMEM(tokens.shape, BF16),
         pltpu.VMEM(flat_w.shape, BF16),
-        pltpu.VMEM((width // chunks * cols, key), F32),
-        pltpu.VMEM((width // chunks * cols, key), F32),
-        pltpu.VMEM((width, cols * key), BF16),
+        pltpu.VMEM(flat_w.shape, F32),
+        pltpu.VMEM((width, heads * key), BF16),
         pltpu.VMEM(small.shape, BF16),
         pltpu.VMEM((LANES, width), F32),
         pltpu.VMEM((rows, cols * key), F32),
@@ -358,16 +368,26 @@
     ]
     return local_call(
         functools.partial(project_body, (heads, levels, chunks)), "project", 36, out_shape,
-        [place], [], scratch, [head_param, tokens, flat_w, small], [HBM] + [WHOLE] * 12,
+        [place], [], scratch, [head_param, tokens, flat_w, small], [HBM] + [WHOLE] * 14,
     )
 
 
 def local_body(
-    sizes, qkv_ref, pack_ref, pack_t_ref, trans_ref, mixed_t_ref, decay_ref, grad_ref, weight_ref, *outs
+    sizes, qkv_ref, pack_ref, pack_t_ref, trans_ref, mixed_t_ref, decay_ref, grad_ref, weight_ref,
+    query_ref, value_ref, wr_in, *outs
 ):
     heads, levels, bits = sizes
     (attn_ref, attn_t_ref, prod_t_ref, scores_ref, mix_ref, mixed_ref, local_ref, hat_ref,
-     hat_t_ref, grad_normed_ref) = outs
+     hat_t_ref, grad_normed_ref, wr_hbm, sems) = outs
+    del wr_in
+    half, size = query_ref.shape[0] // 2, query_ref.shape[1]
+    keeps = []
+    for at in range(4):
+        span = pl.ds(at % 2 * half, half)
+        here, col = ((query_ref, 0), (value_ref, 2 * size))[at // 2]
+        there = wr_hbm.at[span, pl.ds(col, size)]
+        keeps.append(pltpu.make_async_copy(here.at[span, :], there, sems.at[at]))
+        keeps[at].start()
     grad_normed_ref[...] = mm_nt(grad_ref[...], weight_ref[...])
     rows = pack_ref.shape[0]
     decay_col = levels * heads
@@ -393,9 +413,11 @@
         hat = growth * qkv_ref[0, head] - mm(attn, growth * qkv_ref[1, head])
         hat_ref[head] = hat.astype(BF16)
         hat_t_ref[head] = hat.T.astype(BF16)
-
-
-def local_part(arrays, levels, bits):
+    for keep in keeps:
+        keep.wait()
+
+
+def local_part(arrays, wr, levels, bits):
     heads, rows, key = arrays[0].shape[1:]
     square = (heads, rows, rows)
     out_shape = (
@@ -409,10 +431,12 @@
         kept((heads, rows, key), BF16),
         kept((heads, key, rows), BF16),
         kept((rows, heads * key), F32),
+        stored(wr.shape, BF16),
     )
     return local_call(
         functools.partial(local_body, (heads, levels, bits)), "local_part", 10, out_shape,
-        [], arrays,
+        [], arrays, [pltpu.SemaphoreType.DMA((4,))], [wr], [WHOLE] * 10 + [HBM],
+        {len(arrays): 10},
     )
 
 
@@ -898,15 +922,16 @@
     flat_out = out_weight.reshape(heads * key, width)
     gain = norm_gain.reshape(1, key)
 
-    (wr, small_t, qkv, gate, pack, pack_t, trans, mixed_t, decay, base, lower, rates_row,
+    (wr, query_w, value_w, small_t, qkv, gate, pack, pack_t, trans, mixed_t, decay, base, lower, rates_row,
      pair) = project(
         place, tokens, flat_w, small, rates, heads, levels
     )
     first = swap(pair, "ctx", 1)
     node = join_half(place, pair, first)
     mine = [swap(node, "ctx", 2 * at) for at in range(1, size // 2)]
-    (attn, attn_t, prod_t, scores, mix, mixed, local_out, hat, hat_t, grad_normed) = local_part(
-        [qkv, pack, pack_t, trans, mixed_t, decay, grad_out, flat_out], levels, bits
+    (attn, attn_t, prod_t, scores, mix, mixed, local_out, hat, hat_t, grad_normed, wr) = local_part(
+        [qkv, pack, pack_t, trans, mixed_t, decay, grad_out, flat_out, query_w, value_w],
+        wr, levels, bits,
     )
     mine, local_out, grad_normed = lax.optimization_barrier((mine, local_out, grad_normed))
     theirs = [swap(value, "ctx", 1) for value in mine]

time: 80.7 us -> 81.4 us (level)
  Pallas kernels: 34.1 us -> 36.7 us
  waiting for transfers between devices: 26.6 us -> 24.6 us
    pallas_call x13, Pallas kernels: 34.1 us -> 36.7 us  [local_call(): pl.pallas_call(body, out_shape=tuple(out_shape), in_specs=[SCALARS] * len...]
    ppermute x20, waiting for transfers between devices: 26.6 us -> 24.6 us  [swap(): return lax.ppermute(value, axis, [(at, at ^ mask) for at in range(size)])]
  transfers between devices with their start and end apart: 20 -> 20, of which waited for: 14 -> 13; matrix products, arithmetic and copies ran while one was open for 0% -> 0% of each run, Pallas kernels for 21% -> 23%
where the time goes in v10:
time: 81.4 us; the launch traced here: 81.2 us
  Pallas kernels  36.7 us (45%)
  waiting for transfers between devices  24.6 us (30%)
  starting transfers between devices  19 us (23%)
    pallas_call x13, Pallas kernels, local_call(): pl.pallas_call(body, out_shape=tuple(out_shape), in_specs=[SCALARS] * len...  36.7 us
    ppermute x20, waiting for transfers between devices, swap(): return lax.ppermute(value, axis, [(at, at ^ mask) for at in range(size)])  24.6 us
    ppermute x20, starting transfers between devices, swap(): return lax.ppermute(value, axis, [(at, at ^ mask) for at in range(size)])  19 us
  transfers between devices with their start and end apart: 20, of which 13 were waited for; matrix products, arithmetic and copies ran while one was open for 0% of the time, Pallas kernels for 23%

profile of v10, /device:TPU:0, one launch (start us, length us, event | category | flops | bytes accessed | tf_op | source)
XLA Modules:
  0.0 81.2 jit_solution(11916125727432097992)
XLA Ops:
  0.7 13.3 %project.1 = (bf16[2048,1536]{1,0:T(8,128)(2,1)}, bf16[2048,512]{1,0:T(8,128)(2,1)S(1)}, bf16[2048,512]{1,0:T(8,128)(2,1)S(1)}, bf16[128,2048]{1,0:T(8,128)(2,1)...) custom-call(s32[2]{0:T(128)S(1)} %pad_add_fusion.place_ref, ...), custom_call_target="tpu_custom_call" | custom-call | tf_op jit(solution)/shard_map/project/pallas_call | solution.py:99
  14.0 0.5 collective-permute-start
  14.5 1.2 %collective-permute-done.other_ref.refs_0_.refs_14_ = bf16[4,128,256]{2,1,0:T(8,128)(2,1)S(1)} collective-permute-done((bf16[4,128,256]{2,1,0:T(8,128)(2,1)S(1)}, bf16[4,128,256]{2,1,0:T(8,128)(2,1)S(1)}, u32[]{:S(2)}, u32[]{:S(2)}) %collective-permute-start) | collective-permute-done | bytes 262176 | tf_op jit(solution)/shard_map/ppermute | solution.py:859
  15.7 0.7 join_half.1
  16.4 3.9 %collective-permute-start.3 = (bf16[2,128,256]{2,1,0:T(8,128)(2,1)S(1)}, bf16[2,128,256]{2,1,0:T(8,128)(2,1)S(1)}, u32[]{:S(2)}, u32[]{:S(2)}) collective-permute-start(bf16[2,128,256]{2,1,0:T(8,128)(2,1)S(1)} %join_half.1), channel_id=1, source_target_pairs={{0,24},{4,28},{8,16},{12,20},{16,8},{20,12},{24,0},{28,4},{1,25},{... | collective-permute-start | bytes 393224 | tf_op jit(solution)/shard_map/ppermute | solution.py:859
  20.3 0.5 collective-permute-start.2
  21.0 4.2 %local_part.1 = (bf16[4,256,256]{2,1,0:T(8,128)(2,1)S(1)}, bf16[4,256,256]{2,1,0:T(8,128)(2,1)S(1)}, bf16[4,256,256]{2,1,0:T(8,128)(2,1)S(1)}, bf16[4,256,256]{2...) custom-call(f32[3,4,256,128]{3,2,1,0:T(8,128)S(1)} %get-tuple-elemen, ...), custom_call_target="tpu_custom_call", output_to_operand_aliasing={{10}: (10, {})} | custom-call | tf_op jit(solution)/shard_map/local_part/pallas_call | solution.py:99
  25.2 1.7 %collective-permute-done.2.refs_2_ = bf16[2,128,256]{2,1,0:T(8,128)(2,1)S(1)} collective-permute-done((bf16[2,128,256]{2,1,0:T(8,128)(2,1)S(1)}, bf16[2,128,256]{2,1,0:T(8,128)(2,1)S(1)}, u32[]{:S(2)}, u32[]{:S(2)}) %collective-permute-start.2) | collective-permute-done | bytes 131104 | tf_op jit(solution)/shard_map/ppermute | solution.py:859
  27.2 0.5 collective-permute-start.5
  27.7 0.8 %collective-permute-done.4.refs_4_ = bf16[2,128,256]{2,1,0:T(8,128)(2,1)S(1)} collective-permute-done((bf16[2,128,256]{2,1,0:T(8,128)(2,1)S(1)}, bf16[2,128,256]{2,1,0:T(8,128)(2,1)S(1)}, u32[]{:S(2)}, u32[]{:S(2)}) %collective-permute-start.4) | collective-permute-done | bytes 131104 | tf_op jit(solution)/shard_map/ppermute | solution.py:859
  29.0 3.0 %reach.1 = (bf16[2,256,512]{2,1,0:T(8,128)(2,1)S(1)}, bf16[2,256,512]{2,1,0:T(8,128)(2,1)S(1)}, f32[4,256,128]{2,1,0:T(8,128)S(1)}, bf16[4,128,384]{2,1,0:T(8,12...) custom-call(s32[2]{0:T(128)S(1)} %pad_add_fusion.place_ref, ...), custom_call_target="tpu_custom_call" | custom-call | tf_op jit(solution)/shard_map/reach/pallas_call | solution.py:99
  32.1 1.6 %collective-permute-start.7 = (bf16[2,256,512]{2,1,0:T(8,128)(2,1)S(1)}, bf16[2,256,512]{2,1,0:T(8,128)(2,1)S(1)}, u32[]{:S(2)}, u32[]{:S(2)}) collective-permute-start(bf16[2,256,512]{2,1,0:T(8,128)(2,1)S(1)} %get-tuple-element.89), channel_id=1, source_target_pairs={{0,1},{1,0},{2,3},{3,2},{4,5},{5,4},{6,7},{7,6},{8,9},{9,8},{10,11... | collective-permute-start | bytes 1572872 | tf_op jit(solution)/shard_map/ppermute | solution.py:859
  33.7 2.1 %return_states.1 = (f32[4,256,128]{2,1,0:T(8,128)S(1)}, bf16[4,128,256]{2,1,0:T(8,128)(2,1)S(1)}, bf16[4,128,256]{2,1,0:T(8,128)(2,1)S(1)}, bf16[4,128,128]{2,1,0:T(8,128)(2,1)S(1)}) custom-call(s32[2]{0:T(128)S(1)} %pad_add_fusion.place_ref, f32[256,128]{1,0:T(8,128)S(1)} %get-tuple-element.70.pack_ref.refs_1_.refs_2_, ...), custom_call_target="tpu_custom_call" | custom-call | tf_op jit(solution)/shard_map/return_states/pallas_call | solution.py:99
  36.5 1.1 %collective-permute-done.10.refs_3_ = bf16[4,128,128]{2,1,0:T(8,128)(2,1)S(1)} collective-permute-done((bf16[4,128,128]{2,1,0:T(8,128)(2,1)S(1)}, bf16[4,128,128]{2,1,0:T(8,128)(2,1)S(1)}, u32[]{:S(2)}, u32[]{:S(2)}) %collective-permute-start.10) | collective-permute-done | bytes 131104 | tf_op jit(solution)/shard_map/ppermute | solution.py:859
  37.7 1.6 %collective-permute-start.11 = (bf16[4,128,256]{2,1,0:T(8,128)(2,1)S(1)}, bf16[4,128,256]{2,1,0:T(8,128)(2,1)S(1)}, u32[]{:S(2)}, u32[]{:S(2)}) collective-permute-start(bf16[4,128,256]{2,1,0:T(8,128)(2,1)S(1)} %get-tuple-element.118), channel_id=1, source_target_pairs={{0,8},{4,12},{8,0},{12,4},{16,24},{20,28},{24,16},{28,20},{1,9},{5... | collective-permute-start | bytes 786440 | tf_op jit(solution)/shard_map/ppermute | solution.py:859
  39.3 1.4 %collective-permute-start.13 = (bf16[4,128,128]{2,1,0:T(8,128)(2,1)S(1)}, bf16[4,128,128]{2,1,0:T(8,128)(2,1)S(1)}, u32[]{:S(2)}, u32[]{:S(2)}) collective-permute-start(bf16[4,128,128]{2,1,0:T(8,128)(2,1)S(1)} %get-tuple-element.119), channel_id=1, source_target_pairs={{0,24},{4,28},{8,16},{12,20},{16,8},{20,12},{24,0},{28,4},{1,25},{... | collective-permute-start | bytes 393224 | tf_op jit(solution)/shard_map/ppermute | solution.py:859
  40.7 0.6 collective-permute-start.12
  41.3 3.5 %pull_local.1 = (f32[3,4,256,128]{3,2,1,0:T(8,128)S(1)}, f32[4,256,128]{2,1,0:T(8,128)S(1)}, f32[256,128]{1,0:T(8,128)S(1)}, f32[8,256]{1,0:T(8,128)S(1)}) custom-call(f32[3,4,256,128]{3,2,1,0:T(8,128)S(1)} %get-tuple-element.72.qkv_ref.refs_0_, f32[256,128]{1,0:T(8,128)S(1)} %get-tuple-element.70.pack_ref.refs_1_.refs_2_, ...), custom_call_target="tpu_custom_call" | custom-call | tf_op jit(solution)/shard_map/pull_local/pallas_call | solution.py:99
  44.8 1.4 %collective-permute-done.7.got_ref = bf16[2,256,512]{2,1,0:T(8,128)(2,1)S(1)} collective-permute-done((bf16[2,256,512]{2,1,0:T(8,128)(2,1)S(1)}, bf16[2,256,512]{2,1,0:T(8,128)(2,1)S(1)}, u32[]{:S(2)}, u32[]{:S(2)}) %collective-permute-start.7) | collective-permute-done | bytes 524320 | tf_op jit(solution)/shard_map/ppermute | solution.py:859
  46.3 2.7 %collective-permute-start.14 = (bf16[1,256,512]{2,1,0:T(8,128)(2,1)S(1)}, bf16[1,256,512]{2,1,0:T(8,128)(2,1)S(1)}, u32[]{:S(2)}, u32[]{:S(2)}) collective-permute-start(bf16[1,256,512]{2,1,0:T(8,128)(2,1)S(1)} %get-tuple-element.128), channel_id=1, source_target_pairs={{0,2},{1,3},{2,0},{3,1},{4,6},{5,7},{6,4},{7,5},{8,10},{9,11},{10,... | collective-permute-start | bytes 786440 | tf_op jit(solution)/shard_map/ppermute | solution.py:859
  49.0 0.9 %collective-permute-done.13.refs_20_ = bf16[4,128,128]{2,1,0:T(8,128)(2,1)S(1)} collective-permute-done((bf16[4,128,128]{2,1,0:T(8,128)(2,1)S(1)}, bf16[4,128,128]{2,1,0:T(8,128)(2,1)S(1)}, u32[]{:S(2)}, u32[]{:S(2)}) %collective-permute-start.13) | collective-permute-done | bytes 131104 | tf_op jit(solution)/shard_map/ppermute | solution.py:859
  49.8 5.4 %finish.1 = (bf16[256,1536]{1,0:T(8,128)(2,1)S(1)}, bf16[256,128]{1,0:T(8,128)(2,1)S(1)}) custom-call(s32[2]{0:T(128)S(1)} %pad_add_fusion.place_ref, f32[3,4,256,128]{3,2,1,0:T(8,128)S(1)} %get-tuple-element.72.qkv_ref.refs_0_, f32[256,128]{1,0:T(8,128)S(1)} %get-tuple-element.91.refs_1_, f32[256,128]{1,0:T(8,128)S(1)} %get-tuple-element.70.pack_ref.refs_1_.refs_2_, ...), custom_call_target="tpu_custom_call" | custom-call | tf_op jit(solution)/shard_map/finish/pallas_call | solution.py:99
  55.2 2.6 %pull_tokens.1 = (bf16[2,256,256]{2,1,0:T(8,128)(2,1)S(1)}, bf16[2,256,256]{2,1,0:T(8,128)(2,1)S(1)}, bf16[256,256]{1,0:T(8,128)(2,1)S(1)}, bf16[256,256]{1,0:T(...) custom-call(s32[2]{0:T(128)S(1)} %pad_add_fusion.place_ref, ...), custom_call_target="tpu_custom_call" | custom-call | tf_op jit(solution)/shard_map/pull_tokens/pallas_call | solution.py:99
  57.9 0.8 %collective-permute-start.15 = (bf16[2,256,256]{2,1,0:T(8,128)(2,1)S(1)}, bf16[2,256,256]{2,1,0:T(8,128)(2,1)S(1)}, u32[]{:S(2)}, u32[]{:S(2)}) collective-permute-start(bf16[2,256,256]{2,1,0:T(8,128)(2,1)S(1)} %get-tuple-element.131), channel_id=1, source_target_pairs={{0,1},{1,0},{2,3},{3,2},{4,5},{5,4},{6,7},{7,6},{8,9},{9,8},{10,11... | collective-permute-start | bytes 786440 | tf_op jit(solution)/shard_map/ppermute | solution.py:859
  58.7 1.9 %collective-permute-done.14.refs_1_ = bf16[1,256,512]{2,1,0:T(8,128)(2,1)S(1)} collective-permute-done((bf16[1,256,512]{2,1,0:T(8,128)(2,1)S(1)}, bf16[1,256,512]{2,1,0:T(8,128)(2,1)S(1)}, u32[]{:S(2)}, u32[]{:S(2)}) %collective-permute-start.14) | collective-permute-done | bytes 262176 | tf_op jit(solution)/shard_map/ppermute | solution.py:859
  61.0 3.1 %collective-permute-start.18 = (bf16[256,256]{1,0:T(8,128)(2,1)S(1)}, bf16[256,256]{1,0:T(8,128)(2,1)S(1)}, u32[]{:S(2)}, u32[]{:S(2)}) collective-permute-start(bf16[256,256]{1,0:T(8,128)(2,1)S(1)} %get-tuple-element.136), channel_id=1, source_target_pairs={{0,3},{1,2},{2,1},{3,0},{4,7},{5,6},{6,5},{7,4},{8,11},{9,10},{10,... | collective-permute-start | bytes 393224 | tf_op jit(solution)/shard_map/ppermute | solution.py:859
  64.1 0.6 collective-permute-start.19
  64.6 6.6 %collective-permute-done.15.got_ref = bf16[2,256,256]{2,1,0:T(8,128)(2,1)S(1)} collective-permute-done((bf16[2,256,256]{2,1,0:T(8,128)(2,1)S(1)}, bf16[2,256,256]{2,1,0:T(8,128)(2,1)S(1)}, u32[]{:S(2)}, u32[]{:S(2)}) %collective-permute-start.15) | collective-permute-done | bytes 262176 | tf_op jit(solution)/shard_map/ppermute | solution.py:859
  71.4 0.8 head_sum.2
  72.2 2.7 %collective-permute-done.18.refs_4_ = bf16[256,256]{1,0:T(8,128)(2,1)S(1)} collective-permute-done((bf16[256,256]{1,0:T(8,128)(2,1)S(1)}, bf16[256,256]{1,0:T(8,128)(2,1)S(1)}, u32[]{:S(2)}, u32[]{:S(2)}) %collective-permute-start.18) | collective-permute-done | bytes 131104 | tf_op jit(solution)/shard_map/ppermute | solution.py:859
  74.9 5.6 %collective-permute-done.16.refs_1_ = bf16[1,256,256]{2,1,0:T(8,128)(2,1)S(1)} collective-permute-done((bf16[1,256,256]{2,1,0:T(8,128)(2,1)S(1)}, bf16[1,256,256]{2,1,0:T(8,128)(2,1)S(1)}, u32[]{:S(2)}, u32[]{:S(2)}) %collective-permute-start.16) | collective-permute-done | bytes 131104 | tf_op jit(solution)/shard_map/ppermute | solution.py:859
  80.4 0.8 head_sum.3
  (33 shorter events, 2.5 us)
Async XLA Ops:
  0.7 20.2 %copy-start = (bf16[4,128,2048]{2,1,0:T(8,128)(2,1)S(1)}, bf16[4,128,2048]{2,1,0:T(8,128)(2,1)}, u32[]{:S(2)}) copy-start(bf16[4,128,2048]{2,1,0:T(8,128)(2,1)} %param.12) | copy-start | bytes 6291460
  0.7 20.2 %copy-start.1 = (bf16[256,2048]{1,0:T(8,128)(2,1)S(1)}, bf16[256,2048]{1,0:T(8,128)(2,1)}, u32[]{:S(2)}) copy-start(bf16[256,2048]{1,0:T(8,128)(2,1)} %grad_ref.1) | copy-start | bytes 3145732
  14.0 1.7 %collective-permute-start = (bf16[4,128,256]{2,1,0:T(8,128)(2,1)S(1)}, bf16[4,128,256]{2,1,0:T(8,128)(2,1)S(1)}, u32[]{:S(2)}, u32[]{:S(2)}) collective-permute-start(bf16[4,128,256]{2,1,0:T(8,128)(2,1)S(1)} %get-tuple-element.71.own_ref), channel_id=1, source_target_pairs={{0,4},{4,0},{8,12},{12,8},{16,20},{20,16},{24,28},{28,24},{1,5},{5... | collective-permute-start | bytes 786440 | tf_op jit(solution)/shard_map/ppermute | solution.py:859
  16.4 8.8 %collective-permute-start.3 = (bf16[2,128,256]{2,1,0:T(8,128)(2,1)S(1)}, bf16[2,128,256]{2,1,0:T(8,128)(2,1)S(1)}, u32[]{:S(2)}, u32[]{:S(2)}) collective-permute-start(bf16[2,128,256]{2,1,0:T(8,128)(2,1)S(1)} %join_half.1), channel_id=1, source_target_pairs={{0,24},{4,28},{8,16},{12,20},{16,8},{20,12},{24,0},{28,4},{1,25},{... | collective-permute-start | bytes 393224 | tf_op jit(solution)/shard_map/ppermute | solution.py:859
  20.3 6.6 %collective-permute-start.2 = (bf16[2,128,256]{2,1,0:T(8,128)(2,1)S(1)}, bf16[2,128,256]{2,1,0:T(8,128)(2,1)S(1)}, u32[]{:S(2)}, u32[]{:S(2)}) collective-permute-start(bf16[2,128,256]{2,1,0:T(8,128)(2,1)S(1)} %join_half.1), channel_id=1, source_target_pairs={{0,16},{4,20},{8,24},{12,28},{16,0},{20,4},{24,8},{28,12},{1,17},{... | collective-permute-start | bytes 393224 | tf_op jit(solution)/shard_map/ppermute | solution.py:859
  20.8 6.4 %collective-permute-start.1 = (bf16[2,128,256]{2,1,0:T(8,128)(2,1)S(1)}, bf16[2,128,256]{2,1,0:T(8,128)(2,1)S(1)}, u32[]{:S(2)}, u32[]{:S(2)}) collective-permute-start(bf16[2,128,256]{2,1,0:T(8,128)(2,1)S(1)} %join_half.1), channel_id=1, source_target_pairs={{0,8},{4,12},{8,0},{12,4},{16,24},{20,28},{24,16},{28,20},{1,9},{5... | collective-permute-start | bytes 393224 | tf_op jit(solution)/shard_map/ppermute | solution.py:859
  21.0 8.1 %copy-start.2 = (f32[128]{0:T(128)S(1)}, f32[128]{0:T(128)}, u32[]{:S(2)}) copy-start(f32[128]{0:T(128)} %param.11) | copy-start | bytes 1540
  27.2 1.3 %collective-permute-start.4 = (bf16[2,128,256]{2,1,0:T(8,128)(2,1)S(1)}, bf16[2,128,256]{2,1,0:T(8,128)(2,1)S(1)}, u32[]{:S(2)}, u32[]{:S(2)}) collective-permute-start(bf16[2,128,256]{2,1,0:T(8,128)(2,1)S(1)} %collective-permute-done.1.refs_1_), channel_id=1, source_target_pairs={{0,4},{4,0},{8,12},{12,8},{16,20},{20,16},{24,28},{28,24},{1,5},{5... | collective-permute-start | bytes 393224 | tf_op jit(solution)/shard_map/ppermute | solution.py:859
  27.2 1.5 %collective-permute-start.5 = (bf16[2,128,256]{2,1,0:T(8,128)(2,1)S(1)}, bf16[2,128,256]{2,1,0:T(8,128)(2,1)S(1)}, u32[]{:S(2)}, u32[]{:S(2)}) collective-permute-start(bf16[2,128,256]{2,1,0:T(8,128)(2,1)S(1)} %collective-permute-done.2.refs_2_), channel_id=1, source_target_pairs={{0,4},{4,0},{8,12},{12,8},{16,20},{20,16},{24,28},{28,24},{1,5},{5... | collective-permute-start | bytes 393224 | tf_op jit(solution)/shard_map/ppermute | solution.py:859
  27.7 1.3 %collective-permute-start.6 = (bf16[2,128,256]{2,1,0:T(8,128)(2,1)S(1)}, bf16[2,128,256]{2,1,0:T(8,128)(2,1)S(1)}, u32[]{:S(2)}, u32[]{:S(2)}) collective-permute-start(bf16[2,128,256]{2,1,0:T(8,128)(2,1)S(1)} %collective-permute-done.3.refs_3_), channel_id=1, source_target_pairs={{0,4},{4,0},{8,12},{12,8},{16,20},{20,16},{24,28},{28,24},{1,5},{5... | collective-permute-start | bytes 393224 | tf_op jit(solution)/shard_map/ppermute | solution.py:859
  32.1 14.1 %collective-permute-start.7 = (bf16[2,256,512]{2,1,0:T(8,128)(2,1)S(1)}, bf16[2,256,512]{2,1,0:T(8,128)(2,1)S(1)}, u32[]{:S(2)}, u32[]{:S(2)}) collective-permute-start(bf16[2,256,512]{2,1,0:T(8,128)(2,1)S(1)} %get-tuple-element.89), channel_id=1, source_target_pairs={{0,1},{1,0},{2,3},{3,2},{4,5},{5,4},{6,7},{7,6},{8,9},{9,8},{10,11... | collective-permute-start | bytes 1572872 | tf_op jit(solution)/shard_map/ppermute | solution.py:859
  35.8 1.8 %collective-permute-start.9 = (bf16[4,128,256]{2,1,0:T(8,128)(2,1)S(1)}, bf16[4,128,256]{2,1,0:T(8,128)(2,1)S(1)}, u32[]{:S(2)}, u32[]{:S(2)}) collective-permute-start(bf16[4,128,256]{2,1,0:T(8,128)(2,1)S(1)} %get-tuple-element.116.refs_0_), channel_id=1, source_target_pairs={{0,4},{4,0},{8,12},{12,8},{16,20},{20,16},{24,28},{28,24},{1,5},{5... | collective-permute-start | bytes 786440 | tf_op jit(solution)/shard_map/ppermute | solution.py:859
  35.9 1.7 %collective-permute-start.10 = (bf16[4,128,128]{2,1,0:T(8,128)(2,1)S(1)}, bf16[4,128,128]{2,1,0:T(8,128)(2,1)S(1)}, u32[]{:S(2)}, u32[]{:S(2)}) collective-permute-start(bf16[4,128,128]{2,1,0:T(8,128)(2,1)S(1)} %get-tuple-element.117.refs_1_), channel_id=1, source_target_pairs={{0,4},{4,0},{8,12},{12,8},{16,20},{20,16},{24,28},{28,24},{1,5},{5... | collective-permute-start | bytes 393224 | tf_op jit(solution)/shard_map/ppermute | solution.py:859
  36.4 12.6 %collective-permute-start.8 = (bf16[4,128,256]{2,1,0:T(8,128)(2,1)S(1)}, bf16[4,128,256]{2,1,0:T(8,128)(2,1)S(1)}, u32[]{:S(2)}, u32[]{:S(2)}) collective-permute-start(bf16[4,128,256]{2,1,0:T(8,128)(2,1)S(1)} %get-tuple-element.115), channel_id=1, source_target_pairs={{0,4},{4,0},{8,12},{12,8},{16,20},{20,16},{24,28},{28,24},{1,5},{5... | collective-permute-start | bytes 786440 | tf_op jit(solution)/shard_map/ppermute | solution.py:859
  37.7 12.1 %collective-permute-start.11 = (bf16[4,128,256]{2,1,0:T(8,128)(2,1)S(1)}, bf16[4,128,256]{2,1,0:T(8,128)(2,1)S(1)}, u32[]{:S(2)}, u32[]{:S(2)}) collective-permute-start(bf16[4,128,256]{2,1,0:T(8,128)(2,1)S(1)} %get-tuple-element.118), channel_id=1, source_target_pairs={{0,8},{4,12},{8,0},{12,4},{16,24},{20,28},{24,16},{28,20},{1,9},{5... | collective-permute-start | bytes 786440 | tf_op jit(solution)/shard_map/ppermute | solution.py:859
  39.3 10.5 %collective-permute-start.13 = (bf16[4,128,128]{2,1,0:T(8,128)(2,1)S(1)}, bf16[4,128,128]{2,1,0:T(8,128)(2,1)S(1)}, u32[]{:S(2)}, u32[]{:S(2)}) collective-permute-start(bf16[4,128,128]{2,1,0:T(8,128)(2,1)S(1)} %get-tuple-element.119), channel_id=1, source_target_pairs={{0,24},{4,28},{8,16},{12,20},{16,8},{20,12},{24,0},{28,4},{1,25},{... | collective-permute-start | bytes 393224 | tf_op jit(solution)/shard_map/ppermute | solution.py:859
  40.7 9.1 %collective-permute-start.12 = (bf16[4,128,128]{2,1,0:T(8,128)(2,1)S(1)}, bf16[4,128,128]{2,1,0:T(8,128)(2,1)S(1)}, u32[]{:S(2)}, u32[]{:S(2)}) collective-permute-start(bf16[4,128,128]{2,1,0:T(8,128)(2,1)S(1)} %get-tuple-element.119), channel_id=1, source_target_pairs={{0,16},{4,20},{8,24},{12,28},{16,0},{20,4},{24,8},{28,12},{1,17},{... | collective-permute-start | bytes 393224 | tf_op jit(solution)/shard_map/ppermute | solution.py:859
  41.3 13.9 %slice-start = ((s8[6291456]{0:T(1024)(128)(4,1)}), s8[2097152]{0:T(1024)(128)(4,1)S(1)}, s32[]{:S(2)}) async-start(s8[6291456]{0:T(1024)(128)(4,1)} %bitcast.7), calls=%async_computation | async-start | bytes 4194304
  46.2 9.0 %slice-start.1 = ((s8[6291456]{0:T(1024)(128)(4,1)}), s8[4194304]{0:T(1024)(128)(4,1)S(1)}, s32[]{:S(2)}) async-start(s8[6291456]{0:T(1024)(128)(4,1)} %bitcast.7), calls=%async_computation.1 | async-start | bytes 8388608
  46.3 14.2 %collective-permute-start.14 = (bf16[1,256,512]{2,1,0:T(8,128)(2,1)S(1)}, bf16[1,256,512]{2,1,0:T(8,128)(2,1)S(1)}, u32[]{:S(2)}, u32[]{:S(2)}) collective-permute-start(bf16[1,256,512]{2,1,0:T(8,128)(2,1)S(1)} %get-tuple-element.128), channel_id=1, source_target_pairs={{0,2},{1,3},{2,0},{3,1},{4,6},{5,7},{6,4},{7,5},{8,10},{9,11},{10,... | collective-permute-start | bytes 786440 | tf_op jit(solution)/shard_map/ppermute | solution.py:859
  57.9 13.4 %collective-permute-start.15 = (bf16[2,256,256]{2,1,0:T(8,128)(2,1)S(1)}, bf16[2,256,256]{2,1,0:T(8,128)(2,1)S(1)}, u32[]{:S(2)}, u32[]{:S(2)}) collective-permute-start(bf16[2,256,256]{2,1,0:T(8,128)(2,1)S(1)} %get-tuple-element.131), channel_id=1, source_target_pairs={{0,1},{1,0},{2,3},{3,2},{4,5},{5,4},{6,7},{7,6},{8,9},{9,8},{10,11... | collective-permute-start | bytes 786440 | tf_op jit(solution)/shard_map/ppermute | solution.py:859
  60.5 11.6 %collective-permute-start.17 = (bf16[256,256]{1,0:T(8,128)(2,1)S(1)}, bf16[256,256]{1,0:T(8,128)(2,1)S(1)}, u32[]{:S(2)}, u32[]{:S(2)}) collective-permute-start(bf16[256,256]{1,0:T(8,128)(2,1)S(1)} %get-tuple-element.135), channel_id=1, source_target_pairs={{0,2},{1,3},{2,0},{3,1},{4,6},{5,7},{6,4},{7,5},{8,10},{9,11},{10,... | collective-permute-start | bytes 393224 | tf_op jit(solution)/shard_map/ppermute | solution.py:859
  61.0 13.9 %collective-permute-start.18 = (bf16[256,256]{1,0:T(8,128)(2,1)S(1)}, bf16[256,256]{1,0:T(8,128)(2,1)S(1)}, u32[]{:S(2)}, u32[]{:S(2)}) collective-permute-start(bf16[256,256]{1,0:T(8,128)(2,1)S(1)} %get-tuple-element.136), channel_id=1, source_target_pairs={{0,3},{1,2},{2,1},{3,0},{4,7},{5,6},{6,5},{7,4},{8,11},{9,10},{10,... | collective-permute-start | bytes 393224 | tf_op jit(solution)/shard_map/ppermute | solution.py:859
  64.1 10.8 %collective-permute-start.19 = (bf16[256,256]{1,0:T(8,128)(2,1)S(1)}, bf16[256,256]{1,0:T(8,128)(2,1)S(1)}, u32[]{:S(2)}, u32[]{:S(2)}) collective-permute-start(bf16[256,256]{1,0:T(8,128)(2,1)S(1)} %get-tuple-element.137), channel_id=1, source_target_pairs={{0,1},{1,0},{2,3},{3,2},{4,5},{5,4},{6,7},{7,6},{8,9},{9,8},{10,11... | collective-permute-start | bytes 393224 | tf_op jit(solution)/shard_map/ppermute | solution.py:859
  71.3 9.1 %collective-permute-start.16 = (bf16[1,256,256]{2,1,0:T(8,128)(2,1)S(1)}, bf16[1,256,256]{2,1,0:T(8,128)(2,1)S(1)}, u32[]{:S(2)}, u32[]{:S(2)}) collective-permute-start(bf16[1,256,256]{2,1,0:T(8,128)(2,1)S(1)} %get-tuple-element.133), channel_id=1, source_target_pairs={{0,2},{1,3},{2,0},{3,1},{4,6},{5,7},{6,4},{7,5},{8,10},{9,11},{10,... | collective-permute-start | bytes 393224 | tf_op jit(solution)/shard_map/ppermute | solution.py:859

commit v11 on v10

--- a/solution.py
+++ b/solution.py
@@ -139,13 +139,11 @@
         trans_all = [trans - power for trans, power in zip(trans_all, powers)]
     else:
         powers = [mm(edge, trans).astype(BF16) for edge, trans in zip(edge_all, trans_all)]
-        yield
         trans_all = [
             trans - mm(trans, power).astype(BF16) for trans, power in zip(trans_all, powers)
         ]
     for level in range(1, levels):
         powers = [mm(power, power).astype(BF16) for power in powers]
-        yield
         trans_all = [
             trans + mm(trans, power).astype(BF16) for trans, power in zip(trans_all, powers)
         ]
@@ -160,14 +158,12 @@
         levels = min(2 if bits - start == 2 else 3, bits - start)
         here = jnp.logical_and((apart >> start) >= 1, (apart >> (start + levels)) == 0)
         edge_all = [jnp.where(here, lower, 0.0) for lower in lower_all]
-        trans_all = yield from merge_blocks(trans_all, edge_all, levels, start == 0)
+        trans_all = merge_blocks(trans_all, edge_all, levels, start == 0)
         start += levels
-        yield
     rest_all = []
     for trans, lower in zip(trans_all, lower_all):
         high, low = split(lower)
         rest_all.append(eye - trans.astype(F32) - mm(high, trans) - mm(low, trans))
-    yield
     return [
         (trans.astype(F32) + mm(trans, rest)).astype(BF16)
         for trans, rest in zip(trans_all, rest_all)
@@ -178,8 +174,8 @@
     heads, levels, chunks = sizes
     (wr_hbm, query_ref, value_ref, small_ref, qkv_ref, gate_ref, pack_ref, pack_t_ref, trans_ref, mixed_t_ref,
      decay_ref, base_ref, lower_ref, rates_ref, pair_ref) = refs[:15]
-    tokens, wide_in, wide, key_ref, small_in, small_wide, acc, hp_ref = refs[15:23]
-    sems, in_sems, out_sems = refs[23:]
+    tokens, wide_in, wide_even, wide_odd, key_ref, small_in, small_wide, acc, hp_ref = refs[15:24]
+    sems, in_sems, out_sems = refs[24:]
     laid = (query_ref, key_ref, value_ref)
     rows, width = tokens.shape
     depth = width // chunks
@@ -196,26 +192,45 @@
         span = pl.ds(chunk * depth, depth)
         block = wr_hbm.at[span, pl.ds(heads * LANES, heads * LANES)]
         keeps.append(pltpu.make_async_copy(key_ref.at[span, :], block, out_sems.at[chunk]))
+    fetches[0].start()
+    fetch_tokens.start()
+    fetches[1].start()
     fetch_small.start()
     fetch_rates.start()
-    fetches[0].start()
-    fetch_tokens.start()
-    for fetch in fetches[1:]:
+    for fetch in fetches[2:]:
         fetch.start()
-
-    def extract(part, chunk):
-        at = chunk * depth
-        for head in range(heads):
-            first = at * cols + part * heads + head
-            value = wide[pl.ds(first, depth, stride=cols), :]
-            laid[part][at : at + depth, head * LANES : (head + 1) * LANES] = value.astype(BF16)
 
     def relay(chunk):
         fetches[chunk].wait()
-        span = slice(chunk * depth * cols, (chunk + 1) * depth * cols)
-        wide[span, :] = wide_in[span, :].astype(F32)
-        extract(1, chunk)
+        wide = wide_odd if chunk % 2 else wide_even
+        at = chunk * depth
+        wide[...] = wide_in[at * cols : (at + depth) * cols, :].astype(F32)
+        for col in range(cols):
+            value = wide[pl.ds(col, depth, stride=cols), :].astype(BF16)
+            lanes = slice(col % heads * LANES, (col % heads + 1) * LANES)
+            laid[col // heads][at : at + depth, lanes] = value
         keeps[chunk].start()
+
+    def multiply(first, last):
+        for part in (1, 2, 0):
+            span = slice((part * heads) * LANES, (part + 1) * heads * LANES)
+            own = jnp.dot(
+                tokens[:, first * depth : last * depth],
+                laid[part][first * depth : last * depth, :],
+                preferred_element_type=F32,
+            )
+            if first == 0:
+                acc[:, span] = own
+            else:
+                acc[:, span] += own
+
+    def lay(first, last):
+        for chunk in range(first, last, 2):
+            relay(chunk)
+            relay(chunk + 1)
+            if chunk == 0:
+                fetch_tokens.wait()
+            multiply(chunk, chunk + 2)
 
     decay_col = levels * heads
     beta_col = decay_col + heads
@@ -226,6 +241,7 @@
     strict = row_id > col_id
     apart = row_id ^ col_id
     eye = (row_id == col_id).astype(F32)
+    lay(0, chunks // 2)
     fetch_small.wait()
     small_rows = small_in.shape[0] * heads
     for level in range(small_in.shape[0]):
@@ -236,7 +252,6 @@
     rate, bias = head_rows(hp_ref, heads, decay_col, beta_col)
     rates_ref[0:1, :] = rate
     rates_ref[1:2, :] = bias
-    fetch_tokens.wait()
     gate = mm_nt(tokens[...], small_ref[...])
     gate_ref[...] = gate
     switch = jax.nn.sigmoid(gate + bias)
@@ -246,22 +261,7 @@
     pack_t = pack.T
     pack_t_ref[...] = pack_t
 
-    def multiply(part, first, last):
-        span = slice((part * heads) * LANES, (part + 1) * heads * LANES)
-        own = jnp.dot(
-            tokens[:, first * depth : last * depth],
-            laid[part][first * depth : last * depth, :],
-            preferred_element_type=F32,
-        )
-        if first == 0:
-            acc[:, span] = own
-        else:
-            acc[:, span] += own
-
-    for chunk in range(chunks):
-        relay(chunk)
-        if chunk % 2 == 1:
-            multiply(1, chunk - 1, chunk + 1)
+    lay(chunks // 2, chunks)
 
     def unit_of(part, head):
         col = (part * heads + head) * LANES
@@ -284,25 +284,7 @@
         lower_ref[head] = lower.astype(BF16)
         lower_all.append(lower)
 
-    def later():
-        for part in (2, 0):
-            for chunk in range(chunks):
-                extract(part, chunk)
-                if chunk % 4 == 3:
-                    multiply(part, chunk - 3, chunk + 1)
-                if chunk % 2 == 1:
-                    yield
-
-    chain, filler = invert(lower_all, eye, apart, rows), later()
-    while True:
-        try:
-            next(chain)
-        except StopIteration as stop:
-            trans_all = stop.value
-            break
-        next(filler, None)
-    for _ in filler:
-        pass
+    trans_all = invert(lower_all, eye, apart, rows)
     mixed_all = []
     for head in range(heads):
         trans_ref[head] = trans_all[head]
@@ -356,7 +338,8 @@
     scratch = [
         pltpu.VMEM(tokens.shape, BF16),
         pltpu.VMEM(flat_w.shape, BF16),
-        pltpu.VMEM(flat_w.shape, F32),
+        pltpu.VMEM((width // chunks * cols, key), F32),
+        pltpu.VMEM((width // chunks * cols, key), F32),
         pltpu.VMEM((width, heads * key), BF16),
         pltpu.VMEM(small.shape, BF16),
         pltpu.VMEM((LANES, width), F32),

time: 81.4 us -> 80.4 us (0.988)
  Pallas kernels: 36.7 us -> 35.8 us
    pallas_call x13, Pallas kernels: 36.7 us -> 35.8 us  [local_call(): pl.pallas_call(body, out_shape=tuple(out_shape), in_specs=[SCALARS] * len...]
where the time goes in v11:
time: 80.4 us; the launch traced here: 80.3 us
  Pallas kernels  35.8 us (45%)
  waiting for transfers between devices  24.7 us (31%)
  starting transfers between devices  19 us (24%)
    pallas_call x13, Pallas kernels, local_call(): pl.pallas_call(body, out_shape=tuple(out_shape), in_specs=[SCALARS] * len...  35.8 us
    ppermute x20, waiting for transfers between devices, swap(): return lax.ppermute(value, axis, [(at, at ^ mask) for at in range(size)])  24.7 us
    ppermute x20, starting transfers between devices, swap(): return lax.ppermute(value, axis, [(at, at ^ mask) for at in range(size)])  19 us
  transfers between devices with their start and end apart: 20, of which 13 were waited for; matrix products, arithmetic and copies ran while one was open for 0% of the time, Pallas kernels for 23%

profile of v11, /device:TPU:0, one launch (start us, length us, event | category | flops | bytes accessed | tf_op | source)
XLA Modules:
  0.0 80.3 jit_solution(1422461605637762414)
XLA Ops:
  0.7 12.3 %project.1 = (bf16[2048,1536]{1,0:T(8,128)(2,1)}, bf16[2048,512]{1,0:T(8,128)(2,1)S(1)}, bf16[2048,512]{1,0:T(8,128)(2,1)S(1)}, bf16[128,2048]{1,0:T(8,128)(2,1)...) custom-call(s32[2]{0:T(128)S(1)} %pad_add_fusion.place_ref, ...), custom_call_target="tpu_custom_call" | custom-call | tf_op jit(solution)/shard_map/project/pallas_call | solution.py:99
  13.1 0.5 collective-permute-start
  13.6 1.2 %collective-permute-done.other_ref.refs_0_.refs_14_ = bf16[4,128,256]{2,1,0:T(8,128)(2,1)S(1)} collective-permute-done((bf16[4,128,256]{2,1,0:T(8,128)(2,1)S(1)}, bf16[4,128,256]{2,1,0:T(8,128)(2,1)S(1)}, u32[]{:S(2)}, u32[]{:S(2)}) %collective-permute-start) | collective-permute-done | bytes 262176 | tf_op jit(solution)/shard_map/ppermute | solution.py:842
  14.8 0.7 join_half.1
  15.5 3.9 %collective-permute-start.3 = (bf16[2,128,256]{2,1,0:T(8,128)(2,1)S(1)}, bf16[2,128,256]{2,1,0:T(8,128)(2,1)S(1)}, u32[]{:S(2)}, u32[]{:S(2)}) collective-permute-start(bf16[2,128,256]{2,1,0:T(8,128)(2,1)S(1)} %join_half.1), channel_id=1, source_target_pairs={{0,24},{4,28},{8,16},{12,20},{16,8},{20,12},{24,0},{28,4},{1,25},{... | collective-permute-start | bytes 393224 | tf_op jit(solution)/shard_map/ppermute | solution.py:842
  19.4 0.5 collective-permute-start.2
  20.0 4.2 %local_part.1 = (bf16[4,256,256]{2,1,0:T(8,128)(2,1)S(1)}, bf16[4,256,256]{2,1,0:T(8,128)(2,1)S(1)}, bf16[4,256,256]{2,1,0:T(8,128)(2,1)S(1)}, bf16[4,256,256]{2...) custom-call(f32[3,4,256,128]{3,2,1,0:T(8,128)S(1)} %get-tuple-elemen, ...), custom_call_target="tpu_custom_call", output_to_operand_aliasing={{10}: (10, {})} | custom-call | tf_op jit(solution)/shard_map/local_part/pallas_call | solution.py:99
  24.2 1.7 %collective-permute-done.2.refs_2_ = bf16[2,128,256]{2,1,0:T(8,128)(2,1)S(1)} collective-permute-done((bf16[2,128,256]{2,1,0:T(8,128)(2,1)S(1)}, bf16[2,128,256]{2,1,0:T(8,128)(2,1)S(1)}, u32[]{:S(2)}, u32[]{:S(2)}) %collective-permute-start.2) | collective-permute-done | bytes 131104 | tf_op jit(solution)/shard_map/ppermute | solution.py:842
  26.2 0.5 collective-permute-start.5
  26.8 0.8 %collective-permute-done.4.refs_4_ = bf16[2,128,256]{2,1,0:T(8,128)(2,1)S(1)} collective-permute-done((bf16[2,128,256]{2,1,0:T(8,128)(2,1)S(1)}, bf16[2,128,256]{2,1,0:T(8,128)(2,1)S(1)}, u32[]{:S(2)}, u32[]{:S(2)}) %collective-permute-start.4) | collective-permute-done | bytes 131104 | tf_op jit(solution)/shard_map/ppermute | solution.py:842
  28.1 3.0 %reach.1 = (bf16[2,256,512]{2,1,0:T(8,128)(2,1)S(1)}, bf16[2,256,512]{2,1,0:T(8,128)(2,1)S(1)}, f32[4,256,128]{2,1,0:T(8,128)S(1)}, bf16[4,128,384]{2,1,0:T(8,12...) custom-call(s32[2]{0:T(128)S(1)} %pad_add_fusion.place_ref, ...), custom_call_target="tpu_custom_call" | custom-call | tf_op jit(solution)/shard_map/reach/pallas_call | solution.py:99
  31.1 1.6 %collective-permute-start.7 = (bf16[2,256,512]{2,1,0:T(8,128)(2,1)S(1)}, bf16[2,256,512]{2,1,0:T(8,128)(2,1)S(1)}, u32[]{:S(2)}, u32[]{:S(2)}) collective-permute-start(bf16[2,256,512]{2,1,0:T(8,128)(2,1)S(1)} %get-tuple-element.89), channel_id=1, source_target_pairs={{0,1},{1,0},{2,3},{3,2},{4,5},{5,4},{6,7},{7,6},{8,9},{9,8},{10,11... | collective-permute-start | bytes 1572872 | tf_op jit(solution)/shard_map/ppermute | solution.py:842
  32.8 2.1 %return_states.1 = (f32[4,256,128]{2,1,0:T(8,128)S(1)}, bf16[4,128,256]{2,1,0:T(8,128)(2,1)S(1)}, bf16[4,128,256]{2,1,0:T(8,128)(2,1)S(1)}, bf16[4,128,128]{2,1,0:T(8,128)(2,1)S(1)}) custom-call(s32[2]{0:T(128)S(1)} %pad_add_fusion.place_ref, f32[256,128]{1,0:T(8,128)S(1)} %get-tuple-element.70.pack_ref.refs_1_.refs_2_, ...), custom_call_target="tpu_custom_call" | custom-call | tf_op jit(solution)/shard_map/return_states/pallas_call | solution.py:99
  35.6 1.1 %collective-permute-done.10.refs_3_ = bf16[4,128,128]{2,1,0:T(8,128)(2,1)S(1)} collective-permute-done((bf16[4,128,128]{2,1,0:T(8,128)(2,1)S(1)}, bf16[4,128,128]{2,1,0:T(8,128)(2,1)S(1)}, u32[]{:S(2)}, u32[]{:S(2)}) %collective-permute-start.10) | collective-permute-done | bytes 131104 | tf_op jit(solution)/shard_map/ppermute | solution.py:842
  36.8 1.6 %collective-permute-start.11 = (bf16[4,128,256]{2,1,0:T(8,128)(2,1)S(1)}, bf16[4,128,256]{2,1,0:T(8,128)(2,1)S(1)}, u32[]{:S(2)}, u32[]{:S(2)}) collective-permute-start(bf16[4,128,256]{2,1,0:T(8,128)(2,1)S(1)} %get-tuple-element.118), channel_id=1, source_target_pairs={{0,8},{4,12},{8,0},{12,4},{16,24},{20,28},{24,16},{28,20},{1,9},{5... | collective-permute-start | bytes 786440 | tf_op jit(solution)/shard_map/ppermute | solution.py:842
  38.4 1.4 %collective-permute-start.13 = (bf16[4,128,128]{2,1,0:T(8,128)(2,1)S(1)}, bf16[4,128,128]{2,1,0:T(8,128)(2,1)S(1)}, u32[]{:S(2)}, u32[]{:S(2)}) collective-permute-start(bf16[4,128,128]{2,1,0:T(8,128)(2,1)S(1)} %get-tuple-element.119), channel_id=1, source_target_pairs={{0,24},{4,28},{8,16},{12,20},{16,8},{20,12},{24,0},{28,4},{1,25},{... | collective-permute-start | bytes 393224 | tf_op jit(solution)/shard_map/ppermute | solution.py:842
  39.8 0.6 collective-permute-start.12
  40.3 3.5 %pull_local.1 = (f32[3,4,256,128]{3,2,1,0:T(8,128)S(1)}, f32[4,256,128]{2,1,0:T(8,128)S(1)}, f32[256,128]{1,0:T(8,128)S(1)}, f32[8,256]{1,0:T(8,128)S(1)}) custom-call(f32[3,4,256,128]{3,2,1,0:T(8,128)S(1)} %get-tuple-element.72.qkv_ref.refs_0_, f32[256,128]{1,0:T(8,128)S(1)} %get-tuple-element.70.pack_ref.refs_1_.refs_2_, ...), custom_call_target="tpu_custom_call" | custom-call | tf_op jit(solution)/shard_map/pull_local/pallas_call | solution.py:99
  43.9 1.3 %collective-permute-done.7.got_ref = bf16[2,256,512]{2,1,0:T(8,128)(2,1)S(1)} collective-permute-done((bf16[2,256,512]{2,1,0:T(8,128)(2,1)S(1)}, bf16[2,256,512]{2,1,0:T(8,128)(2,1)S(1)}, u32[]{:S(2)}, u32[]{:S(2)}) %collective-permute-start.7) | collective-permute-done | bytes 524320 | tf_op jit(solution)/shard_map/ppermute | solution.py:842
  45.4 2.7 %collective-permute-start.14 = (bf16[1,256,512]{2,1,0:T(8,128)(2,1)S(1)}, bf16[1,256,512]{2,1,0:T(8,128)(2,1)S(1)}, u32[]{:S(2)}, u32[]{:S(2)}) collective-permute-start(bf16[1,256,512]{2,1,0:T(8,128)(2,1)S(1)} %get-tuple-element.128), channel_id=1, source_target_pairs={{0,2},{1,3},{2,0},{3,1},{4,6},{5,7},{6,4},{7,5},{8,10},{9,11},{10,... | collective-permute-start | bytes 786440 | tf_op jit(solution)/shard_map/ppermute | solution.py:842
  48.0 0.9 %collective-permute-done.13.refs_20_ = bf16[4,128,128]{2,1,0:T(8,128)(2,1)S(1)} collective-permute-done((bf16[4,128,128]{2,1,0:T(8,128)(2,1)S(1)}, bf16[4,128,128]{2,1,0:T(8,128)(2,1)S(1)}, u32[]{:S(2)}, u32[]{:S(2)}) %collective-permute-start.13) | collective-permute-done | bytes 131104 | tf_op jit(solution)/shard_map/ppermute | solution.py:842
  48.9 5.4 %finish.1 = (bf16[256,1536]{1,0:T(8,128)(2,1)S(1)}, bf16[256,128]{1,0:T(8,128)(2,1)S(1)}) custom-call(s32[2]{0:T(128)S(1)} %pad_add_fusion.place_ref, f32[3,4,256,128]{3,2,1,0:T(8,128)S(1)} %get-tuple-element.72.qkv_ref.refs_0_, f32[256,128]{1,0:T(8,128)S(1)} %get-tuple-element.91.refs_1_, f32[256,128]{1,0:T(8,128)S(1)} %get-tuple-element.70.pack_ref.refs_1_.refs_2_, ...), custom_call_target="tpu_custom_call" | custom-call | tf_op jit(solution)/shard_map/finish/pallas_call | solution.py:99
  54.3 2.6 %pull_tokens.1 = (bf16[2,256,256]{2,1,0:T(8,128)(2,1)S(1)}, bf16[2,256,256]{2,1,0:T(8,128)(2,1)S(1)}, bf16[256,256]{1,0:T(8,128)(2,1)S(1)}, bf16[256,256]{1,0:T(...) custom-call(s32[2]{0:T(128)S(1)} %pad_add_fusion.place_ref, ...), custom_call_target="tpu_custom_call" | custom-call | tf_op jit(solution)/shard_map/pull_tokens/pallas_call | solution.py:99
  56.9 0.8 collective-permute-start.15
  57.7 1.9 %collective-permute-done.14.refs_1_ = bf16[1,256,512]{2,1,0:T(8,128)(2,1)S(1)} collective-permute-done((bf16[1,256,512]{2,1,0:T(8,128)(2,1)S(1)}, bf16[1,256,512]{2,1,0:T(8,128)(2,1)S(1)}, u32[]{:S(2)}, u32[]{:S(2)}) %collective-permute-start.14) | collective-permute-done | bytes 262176 | tf_op jit(solution)/shard_map/ppermute | solution.py:842
  60.0 3.1 %collective-permute-start.18 = (bf16[256,256]{1,0:T(8,128)(2,1)S(1)}, bf16[256,256]{1,0:T(8,128)(2,1)S(1)}, u32[]{:S(2)}, u32[]{:S(2)}) collective-permute-start(bf16[256,256]{1,0:T(8,128)(2,1)S(1)} %get-tuple-element.136), channel_id=1, source_target_pairs={{0,3},{1,2},{2,1},{3,0},{4,7},{5,6},{6,5},{7,4},{8,11},{9,10},{10,... | collective-permute-start | bytes 393224 | tf_op jit(solution)/shard_map/ppermute | solution.py:842
  63.1 0.6 collective-permute-start.19
  63.7 6.7 %collective-permute-done.15.got_ref = bf16[2,256,256]{2,1,0:T(8,128)(2,1)S(1)} collective-permute-done((bf16[2,256,256]{2,1,0:T(8,128)(2,1)S(1)}, bf16[2,256,256]{2,1,0:T(8,128)(2,1)S(1)}, u32[]{:S(2)}, u32[]{:S(2)}) %collective-permute-start.15) | collective-permute-done | bytes 262176 | tf_op jit(solution)/shard_map/ppermute | solution.py:842
  70.5 0.8 head_sum.2
  71.3 2.6 %collective-permute-done.18.refs_4_ = bf16[256,256]{1,0:T(8,128)(2,1)S(1)} collective-permute-done((bf16[256,256]{1,0:T(8,128)(2,1)S(1)}, bf16[256,256]{1,0:T(8,128)(2,1)S(1)}, u32[]{:S(2)}, u32[]{:S(2)}) %collective-permute-start.18) | collective-permute-done | bytes 131104 | tf_op jit(solution)/shard_map/ppermute | solution.py:842
  73.9 5.6 %collective-permute-done.16.refs_1_ = bf16[1,256,256]{2,1,0:T(8,128)(2,1)S(1)} collective-permute-done((bf16[1,256,256]{2,1,0:T(8,128)(2,1)S(1)}, bf16[1,256,256]{2,1,0:T(8,128)(2,1)S(1)}, u32[]{:S(2)}, u32[]{:S(2)}) %collective-permute-start.16) | collective-permute-done | bytes 131104 | tf_op jit(solution)/shard_map/ppermute | solution.py:842
  79.5 0.8 head_sum.3
  (33 shorter events, 2.5 us)
Async XLA Ops:
  0.7 19.3 %copy-start = (bf16[4,128,2048]{2,1,0:T(8,128)(2,1)S(1)}, bf16[4,128,2048]{2,1,0:T(8,128)(2,1)}, u32[]{:S(2)}) copy-start(bf16[4,128,2048]{2,1,0:T(8,128)(2,1)} %param.12) | copy-start | bytes 6291460
  0.7 19.3 %copy-start.1 = (bf16[256,2048]{1,0:T(8,128)(2,1)S(1)}, bf16[256,2048]{1,0:T(8,128)(2,1)}, u32[]{:S(2)}) copy-start(bf16[256,2048]{1,0:T(8,128)(2,1)} %grad_ref.1) | copy-start | bytes 3145732
  13.1 1.7 %collective-permute-start = (bf16[4,128,256]{2,1,0:T(8,128)(2,1)S(1)}, bf16[4,128,256]{2,1,0:T(8,128)(2,1)S(1)}, u32[]{:S(2)}, u32[]{:S(2)}) collective-permute-start(bf16[4,128,256]{2,1,0:T(8,128)(2,1)S(1)} %get-tuple-element.71.own_ref), channel_id=1, source_target_pairs={{0,4},{4,0},{8,12},{12,8},{16,20},{20,16},{24,28},{28,24},{1,5},{5... | collective-permute-start | bytes 786440 | tf_op jit(solution)/shard_map/ppermute | solution.py:842
  15.5 8.7 %collective-permute-start.3 = (bf16[2,128,256]{2,1,0:T(8,128)(2,1)S(1)}, bf16[2,128,256]{2,1,0:T(8,128)(2,1)S(1)}, u32[]{:S(2)}, u32[]{:S(2)}) collective-permute-start(bf16[2,128,256]{2,1,0:T(8,128)(2,1)S(1)} %join_half.1), channel_id=1, source_target_pairs={{0,24},{4,28},{8,16},{12,20},{16,8},{20,12},{24,0},{28,4},{1,25},{... | collective-permute-start | bytes 393224 | tf_op jit(solution)/shard_map/ppermute | solution.py:842
  19.4 6.6 %collective-permute-start.2 = (bf16[2,128,256]{2,1,0:T(8,128)(2,1)S(1)}, bf16[2,128,256]{2,1,0:T(8,128)(2,1)S(1)}, u32[]{:S(2)}, u32[]{:S(2)}) collective-permute-start(bf16[2,128,256]{2,1,0:T(8,128)(2,1)S(1)} %join_half.1), channel_id=1, source_target_pairs={{0,16},{4,20},{8,24},{12,28},{16,0},{20,4},{24,8},{28,12},{1,17},{... | collective-permute-start | bytes 393224 | tf_op jit(solution)/shard_map/ppermute | solution.py:842
  19.9 6.4 %collective-permute-start.1 = (bf16[2,128,256]{2,1,0:T(8,128)(2,1)S(1)}, bf16[2,128,256]{2,1,0:T(8,128)(2,1)S(1)}, u32[]{:S(2)}, u32[]{:S(2)}) collective-permute-start(bf16[2,128,256]{2,1,0:T(8,128)(2,1)S(1)} %join_half.1), channel_id=1, source_target_pairs={{0,8},{4,12},{8,0},{12,4},{16,24},{20,28},{24,16},{28,20},{1,9},{5... | collective-permute-start | bytes 393224 | tf_op jit(solution)/shard_map/ppermute | solution.py:842
  20.0 8.1 %copy-start.2 = (f32[128]{0:T(128)S(1)}, f32[128]{0:T(128)}, u32[]{:S(2)}) copy-start(f32[128]{0:T(128)} %param.11) | copy-start | bytes 1540
  26.2 1.3 %collective-permute-start.4 = (bf16[2,128,256]{2,1,0:T(8,128)(2,1)S(1)}, bf16[2,128,256]{2,1,0:T(8,128)(2,1)S(1)}, u32[]{:S(2)}, u32[]{:S(2)}) collective-permute-start(bf16[2,128,256]{2,1,0:T(8,128)(2,1)S(1)} %collective-permute-done.1.refs_1_), channel_id=1, source_target_pairs={{0,4},{4,0},{8,12},{12,8},{16,20},{20,16},{24,28},{28,24},{1,5},{5... | collective-permute-start | bytes 393224 | tf_op jit(solution)/shard_map/ppermute | solution.py:842
  26.2 1.5 %collective-permute-start.5 = (bf16[2,128,256]{2,1,0:T(8,128)(2,1)S(1)}, bf16[2,128,256]{2,1,0:T(8,128)(2,1)S(1)}, u32[]{:S(2)}, u32[]{:S(2)}) collective-permute-start(bf16[2,128,256]{2,1,0:T(8,128)(2,1)S(1)} %collective-permute-done.2.refs_2_), channel_id=1, source_target_pairs={{0,4},{4,0},{8,12},{12,8},{16,20},{20,16},{24,28},{28,24},{1,5},{5... | collective-permute-start | bytes 393224 | tf_op jit(solution)/shard_map/ppermute | solution.py:842
  26.8 1.3 %collective-permute-start.6 = (bf16[2,128,256]{2,1,0:T(8,128)(2,1)S(1)}, bf16[2,128,256]{2,1,0:T(8,128)(2,1)S(1)}, u32[]{:S(2)}, u32[]{:S(2)}) collective-permute-start(bf16[2,128,256]{2,1,0:T(8,128)(2,1)S(1)} %collective-permute-done.3.refs_3_), channel_id=1, source_target_pairs={{0,4},{4,0},{8,12},{12,8},{16,20},{20,16},{24,28},{28,24},{1,5},{5... | collective-permute-start | bytes 393224 | tf_op jit(solution)/shard_map/ppermute | solution.py:842
  31.1 14.1 %collective-permute-start.7 = (bf16[2,256,512]{2,1,0:T(8,128)(2,1)S(1)}, bf16[2,256,512]{2,1,0:T(8,128)(2,1)S(1)}, u32[]{:S(2)}, u32[]{:S(2)}) collective-permute-start(bf16[2,256,512]{2,1,0:T(8,128)(2,1)S(1)} %get-tuple-element.89), channel_id=1, source_target_pairs={{0,1},{1,0},{2,3},{3,2},{4,5},{5,4},{6,7},{7,6},{8,9},{9,8},{10,11... | collective-permute-start | bytes 1572872 | tf_op jit(solution)/shard_map/ppermute | solution.py:842
  34.9 1.8 %collective-permute-start.9 = (bf16[4,128,256]{2,1,0:T(8,128)(2,1)S(1)}, bf16[4,128,256]{2,1,0:T(8,128)(2,1)S(1)}, u32[]{:S(2)}, u32[]{:S(2)}) collective-permute-start(bf16[4,128,256]{2,1,0:T(8,128)(2,1)S(1)} %get-tuple-element.116.refs_0_), channel_id=1, source_target_pairs={{0,4},{4,0},{8,12},{12,8},{16,20},{20,16},{24,28},{28,24},{1,5},{5... | collective-permute-start | bytes 786440 | tf_op jit(solution)/shard_map/ppermute | solution.py:842
  35.0 1.7 %collective-permute-start.10 = (bf16[4,128,128]{2,1,0:T(8,128)(2,1)S(1)}, bf16[4,128,128]{2,1,0:T(8,128)(2,1)S(1)}, u32[]{:S(2)}, u32[]{:S(2)}) collective-permute-start(bf16[4,128,128]{2,1,0:T(8,128)(2,1)S(1)} %get-tuple-element.117.refs_1_), channel_id=1, source_target_pairs={{0,4},{4,0},{8,12},{12,8},{16,20},{20,16},{24,28},{28,24},{1,5},{5... | collective-permute-start | bytes 393224 | tf_op jit(solution)/shard_map/ppermute | solution.py:842
  35.5 12.5 %collective-permute-start.8 = (bf16[4,128,256]{2,1,0:T(8,128)(2,1)S(1)}, bf16[4,128,256]{2,1,0:T(8,128)(2,1)S(1)}, u32[]{:S(2)}, u32[]{:S(2)}) collective-permute-start(bf16[4,128,256]{2,1,0:T(8,128)(2,1)S(1)} %get-tuple-element.115), channel_id=1, source_target_pairs={{0,4},{4,0},{8,12},{12,8},{16,20},{20,16},{24,28},{28,24},{1,5},{5... | collective-permute-start | bytes 786440 | tf_op jit(solution)/shard_map/ppermute | solution.py:842
  36.8 12.1 %collective-permute-start.11 = (bf16[4,128,256]{2,1,0:T(8,128)(2,1)S(1)}, bf16[4,128,256]{2,1,0:T(8,128)(2,1)S(1)}, u32[]{:S(2)}, u32[]{:S(2)}) collective-permute-start(bf16[4,128,256]{2,1,0:T(8,128)(2,1)S(1)} %get-tuple-element.118), channel_id=1, source_target_pairs={{0,8},{4,12},{8,0},{12,4},{16,24},{20,28},{24,16},{28,20},{1,9},{5... | collective-permute-start | bytes 786440 | tf_op jit(solution)/shard_map/ppermute | solution.py:842
  38.4 10.5 %collective-permute-start.13 = (bf16[4,128,128]{2,1,0:T(8,128)(2,1)S(1)}, bf16[4,128,128]{2,1,0:T(8,128)(2,1)S(1)}, u32[]{:S(2)}, u32[]{:S(2)}) collective-permute-start(bf16[4,128,128]{2,1,0:T(8,128)(2,1)S(1)} %get-tuple-element.119), channel_id=1, source_target_pairs={{0,24},{4,28},{8,16},{12,20},{16,8},{20,12},{24,0},{28,4},{1,25},{... | collective-permute-start | bytes 393224 | tf_op jit(solution)/shard_map/ppermute | solution.py:842
  39.8 9.1 %collective-permute-start.12 = (bf16[4,128,128]{2,1,0:T(8,128)(2,1)S(1)}, bf16[4,128,128]{2,1,0:T(8,128)(2,1)S(1)}, u32[]{:S(2)}, u32[]{:S(2)}) collective-permute-start(bf16[4,128,128]{2,1,0:T(8,128)(2,1)S(1)} %get-tuple-element.119), channel_id=1, source_target_pairs={{0,16},{4,20},{8,24},{12,28},{16,0},{20,4},{24,8},{28,12},{1,17},{... | collective-permute-start | bytes 393224 | tf_op jit(solution)/shard_map/ppermute | solution.py:842
  40.3 13.9 %slice-start = ((s8[6291456]{0:T(1024)(128)(4,1)}), s8[2097152]{0:T(1024)(128)(4,1)S(1)}, s32[]{:S(2)}) async-start(s8[6291456]{0:T(1024)(128)(4,1)} %bitcast.7), calls=%async_computation | async-start | bytes 4194304
  45.2 9.0 %slice-start.1 = ((s8[6291456]{0:T(1024)(128)(4,1)}), s8[4194304]{0:T(1024)(128)(4,1)S(1)}, s32[]{:S(2)}) async-start(s8[6291456]{0:T(1024)(128)(4,1)} %bitcast.7), calls=%async_computation.1 | async-start | bytes 8388608
  45.4 14.2 %collective-permute-start.14 = (bf16[1,256,512]{2,1,0:T(8,128)(2,1)S(1)}, bf16[1,256,512]{2,1,0:T(8,128)(2,1)S(1)}, u32[]{:S(2)}, u32[]{:S(2)}) collective-permute-start(bf16[1,256,512]{2,1,0:T(8,128)(2,1)S(1)} %get-tuple-element.128), channel_id=1, source_target_pairs={{0,2},{1,3},{2,0},{3,1},{4,6},{5,7},{6,4},{7,5},{8,10},{9,11},{10,... | collective-permute-start | bytes 786440 | tf_op jit(solution)/shard_map/ppermute | solution.py:842
  56.9 13.5 %collective-permute-start.15 = (bf16[2,256,256]{2,1,0:T(8,128)(2,1)S(1)}, bf16[2,256,256]{2,1,0:T(8,128)(2,1)S(1)}, u32[]{:S(2)}, u32[]{:S(2)}) collective-permute-start(bf16[2,256,256]{2,1,0:T(8,128)(2,1)S(1)} %get-tuple-element.131), channel_id=1, source_target_pairs={{0,1},{1,0},{2,3},{3,2},{4,5},{5,4},{6,7},{7,6},{8,9},{9,8},{10,11... | collective-permute-start | bytes 786440 | tf_op jit(solution)/shard_map/ppermute | solution.py:842
  59.6 11.7 %collective-permute-start.17 = (bf16[256,256]{1,0:T(8,128)(2,1)S(1)}, bf16[256,256]{1,0:T(8,128)(2,1)S(1)}, u32[]{:S(2)}, u32[]{:S(2)}) collective-permute-start(bf16[256,256]{1,0:T(8,128)(2,1)S(1)} %get-tuple-element.135), channel_id=1, source_target_pairs={{0,2},{1,3},{2,0},{3,1},{4,6},{5,7},{6,4},{7,5},{8,10},{9,11},{10,... | collective-permute-start | bytes 393224 | tf_op jit(solution)/shard_map/ppermute | solution.py:842
  60.0 13.9 %collective-permute-start.18 = (bf16[256,256]{1,0:T(8,128)(2,1)S(1)}, bf16[256,256]{1,0:T(8,128)(2,1)S(1)}, u32[]{:S(2)}, u32[]{:S(2)}) collective-permute-start(bf16[256,256]{1,0:T(8,128)(2,1)S(1)} %get-tuple-element.136), channel_id=1, source_target_pairs={{0,3},{1,2},{2,1},{3,0},{4,7},{5,6},{6,5},{7,4},{8,11},{9,10},{10,... | collective-permute-start | bytes 393224 | tf_op jit(solution)/shard_map/ppermute | solution.py:842
  63.1 10.8 %collective-permute-start.19 = (bf16[256,256]{1,0:T(8,128)(2,1)S(1)}, bf16[256,256]{1,0:T(8,128)(2,1)S(1)}, u32[]{:S(2)}, u32[]{:S(2)}) collective-permute-start(bf16[256,256]{1,0:T(8,128)(2,1)S(1)} %get-tuple-element.137), channel_id=1, source_target_pairs={{0,1},{1,0},{2,3},{3,2},{4,5},{5,4},{6,7},{7,6},{8,9},{9,8},{10,11... | collective-permute-start | bytes 393224 | tf_op jit(solution)/shard_map/ppermute | solution.py:842
  70.4 9.1 %collective-permute-start.16 = (bf16[1,256,256]{2,1,0:T(8,128)(2,1)S(1)}, bf16[1,256,256]{2,1,0:T(8,128)(2,1)S(1)}, u32[]{:S(2)}, u32[]{:S(2)}) collective-permute-start(bf16[1,256,256]{2,1,0:T(8,128)(2,1)S(1)} %get-tuple-element.133), channel_id=1, source_target_pairs={{0,2},{1,3},{2,0},{3,1},{4,6},{5,7},{6,4},{7,5},{8,10},{9,11},{10,... | collective-permute-start | bytes 393224 | tf_op jit(solution)/shard_map/ppermute | solution.py:842

commit v12 on v11

--- a/solution.py
+++ b/solution.py
@@ -48,6 +48,10 @@
     left_high, left_low = split(left)
     right_high, right_low = split(right)
     return mm_nt(left_high, right_high) + (mm_nt(left_low, right_high) + mm_nt(left_high, right_low))
+
+
+def mm_full(left, right):
+    return jnp.dot(left, right, precision=lax.Precision.HIGHEST, preferred_element_type=F32)
 
 
 def mm_ones(ones, values):
@@ -133,33 +137,15 @@
     return rate, bias
 
 
-def merge_blocks(trans_all, edge_all, levels, first):
-    if first:
-        powers = [edge.astype(BF16) for edge in edge_all]
-        trans_all = [trans - power for trans, power in zip(trans_all, powers)]
-    else:
-        powers = [mm(edge, trans).astype(BF16) for edge, trans in zip(edge_all, trans_all)]
+def invert(lower_all, eye, apart, rows):
+    trans_all = [(eye - jnp.where(apart == 1, lower, 0.0)).astype(BF16) for lower in lower_all]
+    for bit in range(1, rows.bit_length() - 1):
+        here = (apart >> bit) == 1
+        edge = [jnp.where(here, lower, 0.0) for lower in lower_all]
+        half = [mm(trans, part) for trans, part in zip(trans_all, edge)]
         trans_all = [
-            trans - mm(trans, power).astype(BF16) for trans, power in zip(trans_all, powers)
+            trans - mm(part, trans).astype(BF16) for trans, part in zip(trans_all, half)
         ]
-    for level in range(1, levels):
-        powers = [mm(power, power).astype(BF16) for power in powers]
-        trans_all = [
-            trans + mm(trans, power).astype(BF16) for trans, power in zip(trans_all, powers)
-        ]
-    return trans_all
-
-
-def invert(lower_all, eye, apart, rows):
-    trans_all = [eye.astype(BF16) for lower in lower_all]
-    bits = rows.bit_length() - 1
-    start = 0
-    while start < bits:
-        levels = min(2 if bits - start == 2 else 3, bits - start)
-        here = jnp.logical_and((apart >> start) >= 1, (apart >> (start + levels)) == 0)
-        edge_all = [jnp.where(here, lower, 0.0) for lower in lower_all]
-        trans_all = merge_blocks(trans_all, edge_all, levels, start == 0)
-        start += levels
     rest_all = []
     for trans, lower in zip(trans_all, lower_all):
         high, low = split(lower)
@@ -194,10 +180,9 @@
         keeps.append(pltpu.make_async_copy(key_ref.at[span, :], block, out_sems.at[chunk]))
     fetches[0].start()
     fetch_tokens.start()
-    fetches[1].start()
     fetch_small.start()
     fetch_rates.start()
-    for fetch in fetches[2:]:
+    for fetch in fetches[1:]:
         fetch.start()
 
     def relay(chunk):
@@ -209,7 +194,6 @@
             value = wide[pl.ds(col, depth, stride=cols), :].astype(BF16)
             lanes = slice(col % heads * LANES, (col % heads + 1) * LANES)
             laid[col // heads][at : at + depth, lanes] = value
-        keeps[chunk].start()
 
     def multiply(first, last):
         for part in (1, 2, 0):
@@ -225,12 +209,11 @@
                 acc[:, span] += own
 
     def lay(first, last):
-        for chunk in range(first, last, 2):
+        for chunk in range(first, last):
             relay(chunk)
-            relay(chunk + 1)
             if chunk == 0:
                 fetch_tokens.wait()
-            multiply(chunk, chunk + 2)
+            multiply(chunk, chunk + 1)
 
     decay_col = levels * heads
     beta_col = decay_col + heads
@@ -241,7 +224,9 @@
     strict = row_id > col_id
     apart = row_id ^ col_id
     eye = (row_id == col_id).astype(F32)
-    lay(0, chunks // 2)
+    lay(0, chunks)
+    for keep in keeps:
+        keep.start()
     fetch_small.wait()
     small_rows = small_in.shape[0] * heads
     for level in range(small_in.shape[0]):
@@ -256,12 +241,10 @@
     gate_ref[...] = gate
     switch = jax.nn.sigmoid(gate + bias)
     lam = jnp.maximum(gate, 0.0) + jnp.log1p(jnp.exp(-jnp.abs(gate)))
-    cum = mm_ones(inclusive.astype(F32), -rate * switch)
+    cum = mm_full(inclusive.astype(F32), -rate * switch)
     pack = jnp.where(lane < decay_col, lam, jnp.where(lane < beta_col, cum, switch))
     pack_t = pack.T
     pack_t_ref[...] = pack_t
-
-    lay(chunks // 2, chunks)
 
     def unit_of(part, head):
         col = (part * heads + head) * LANES
@@ -941,8 +924,9 @@
     dproj, dgate = finish(place, arrays, others, arrived, levels)
     keep, send, direct = pull_tokens(place, dproj, dgate, wr, small_t, count)
     direct, last_out = lax.optimization_barrier((direct, last_out))
+    keep, last, late = halving(keep, send, "head", direct[1])
+    direct = [direct[0], late, *direct[2:]]
     got = [swap(direct[mask], "head", mask) for mask in far_first(count)]
-    keep, last, _ = halving(keep, send, "head", ())
     return head_sum(keep_out, last_out, [], []), head_sum(keep, last, direct, got)
 
 

time: 80.4 us -> 79.6 us (0.990)
  waiting for transfers between devices: 24.7 us -> 21.5 us
  starting transfers between devices: 19 us -> 22 us
    ppermute x20, waiting for transfers between devices: 24.7 us -> 21.5 us  [swap(): return lax.ppermute(value, axis, [(at, at ^ mask) for at in range(size)])]
    ppermute x20, starting transfers between devices: 19 us -> 22 us  [swap(): return lax.ppermute(value, axis, [(at, at ^ mask) for at in range(size)])]
  transfers between devices with their start and end apart: 20 -> 20, of which waited for: 13 -> 12; matrix products, arithmetic and copies ran while one was open for 0% -> 0% of each run, Pallas kernels for 23% -> 24%
where the time goes in v12:
time: 79.6 us; the launch traced here: 79.4 us
  Pallas kernels  35 us (44%)
  starting transfers between devices  22 us (28%)
  waiting for transfers between devices  21.5 us (27%)
    pallas_call x13, Pallas kernels, local_call(): pl.pallas_call(body, out_shape=tuple(out_shape), in_specs=[SCALARS] * len...  35 us
    ppermute x20, starting transfers between devices, swap(): return lax.ppermute(value, axis, [(at, at ^ mask) for at in range(size)])  22 us
    ppermute x20, waiting for transfers between devices, swap(): return lax.ppermute(value, axis, [(at, at ^ mask) for at in range(size)])  21.5 us
  transfers between devices with their start and end apart: 20, of which 12 were waited for; matrix products, arithmetic and copies ran while one was open for 0% of the time, Pallas kernels for 24%

profile of v12, /device:TPU:0, one launch (start us, length us, event | category | flops | bytes accessed | tf_op | source)
XLA Modules:
  0.0 79.4 jit_solution(17251268442457840900)
XLA Ops:
  0.7 11.7 %project.1 = (bf16[2048,1536]{1,0:T(8,128)(2,1)}, bf16[2048,512]{1,0:T(8,128)(2,1)S(1)}, bf16[2048,512]{1,0:T(8,128)(2,1)S(1)}, bf16[128,2048]{1,0:T(8,128)(2,1)...) custom-call(s32[2]{0:T(128)S(1)} %pad_add_fusion.place_ref, ...), custom_call_target="tpu_custom_call" | custom-call | tf_op jit(solution)/shard_map/project/pallas_call | solution.py:103
  12.4 0.5 collective-permute-start
  12.9 1.2 %collective-permute-done.other_ref.refs_0_.refs_14_ = bf16[4,128,256]{2,1,0:T(8,128)(2,1)S(1)} collective-permute-done((bf16[4,128,256]{2,1,0:T(8,128)(2,1)S(1)}, bf16[4,128,256]{2,1,0:T(8,128)(2,1)S(1)}, u32[]{:S(2)}, u32[]{:S(2)}) %collective-permute-start) | collective-permute-done | bytes 262176 | tf_op jit(solution)/shard_map/ppermute | solution.py:825
  14.1 0.7 join_half.1
  14.8 3.9 %collective-permute-start.3 = (bf16[2,128,256]{2,1,0:T(8,128)(2,1)S(1)}, bf16[2,128,256]{2,1,0:T(8,128)(2,1)S(1)}, u32[]{:S(2)}, u32[]{:S(2)}) collective-permute-start(bf16[2,128,256]{2,1,0:T(8,128)(2,1)S(1)} %join_half.1), channel_id=1, source_target_pairs={{0,24},{4,28},{8,16},{12,20},{16,8},{20,12},{24,0},{28,4},{1,25},{... | collective-permute-start | bytes 393224 | tf_op jit(solution)/shard_map/ppermute | solution.py:825
  19.3 4.2 %local_part.1 = (bf16[4,256,256]{2,1,0:T(8,128)(2,1)S(1)}, bf16[4,256,256]{2,1,0:T(8,128)(2,1)S(1)}, bf16[4,256,256]{2,1,0:T(8,128)(2,1)S(1)}, bf16[4,256,256]{2...) custom-call(f32[3,4,256,128]{3,2,1,0:T(8,128)S(1)} %get-tuple-elemen, ...), custom_call_target="tpu_custom_call", output_to_operand_aliasing={{10}: (10, {})} | custom-call | tf_op jit(solution)/shard_map/local_part/pallas_call | solution.py:103
  23.5 1.7 %collective-permute-done.2.refs_2_ = bf16[2,128,256]{2,1,0:T(8,128)(2,1)S(1)} collective-permute-done((bf16[2,128,256]{2,1,0:T(8,128)(2,1)S(1)}, bf16[2,128,256]{2,1,0:T(8,128)(2,1)S(1)}, u32[]{:S(2)}, u32[]{:S(2)}) %collective-permute-start.2) | collective-permute-done | bytes 131104 | tf_op jit(solution)/shard_map/ppermute | solution.py:825
  25.6 0.5 collective-permute-start.5
  26.1 0.8 %collective-permute-done.4.refs_4_ = bf16[2,128,256]{2,1,0:T(8,128)(2,1)S(1)} collective-permute-done((bf16[2,128,256]{2,1,0:T(8,128)(2,1)S(1)}, bf16[2,128,256]{2,1,0:T(8,128)(2,1)S(1)}, u32[]{:S(2)}, u32[]{:S(2)}) %collective-permute-start.4) | collective-permute-done | bytes 131104 | tf_op jit(solution)/shard_map/ppermute | solution.py:825
  27.4 2.8 %reach.1 = (bf16[2,256,512]{2,1,0:T(8,128)(2,1)S(1)}, bf16[2,256,512]{2,1,0:T(8,128)(2,1)S(1)}, f32[4,256,128]{2,1,0:T(8,128)S(1)}, bf16[4,128,384]{2,1,0:T(8,12...) custom-call(s32[2]{0:T(128)S(1)} %pad_add_fusion.place_ref, ...), custom_call_target="tpu_custom_call" | custom-call | tf_op jit(solution)/shard_map/reach/pallas_call | solution.py:103
  30.3 1.6 %collective-permute-start.7 = (bf16[2,256,512]{2,1,0:T(8,128)(2,1)S(1)}, bf16[2,256,512]{2,1,0:T(8,128)(2,1)S(1)}, u32[]{:S(2)}, u32[]{:S(2)}) collective-permute-start(bf16[2,256,512]{2,1,0:T(8,128)(2,1)S(1)} %get-tuple-element.91), channel_id=1, source_target_pairs={{0,1},{1,0},{2,3},{3,2},{4,5},{5,4},{6,7},{7,6},{8,9},{9,8},{10,11... | collective-permute-start | bytes 1572872 | tf_op jit(solution)/shard_map/ppermute | solution.py:825
  31.9 2.3 %return_states.1 = (f32[4,256,128]{2,1,0:T(8,128)S(1)}, bf16[4,128,256]{2,1,0:T(8,128)(2,1)S(1)}, bf16[4,128,256]{2,1,0:T(8,128)(2,1)S(1)}, bf16[4,128,128]{2,1,0:T(8,128)(2,1)S(1)}) custom-call(s32[2]{0:T(128)S(1)} %pad_add_fusion.place_ref, f32[256,128]{1,0:T(8,128)S(1)} %get-tuple-element.72.pack_ref.refs_1_.refs_2_, ...), custom_call_target="tpu_custom_call" | custom-call | tf_op jit(solution)/shard_map/return_states/pallas_call | solution.py:103
  34.8 1.1 %collective-permute-done.10.refs_3_ = bf16[4,128,128]{2,1,0:T(8,128)(2,1)S(1)} collective-permute-done((bf16[4,128,128]{2,1,0:T(8,128)(2,1)S(1)}, bf16[4,128,128]{2,1,0:T(8,128)(2,1)S(1)}, u32[]{:S(2)}, u32[]{:S(2)}) %collective-permute-start.10) | collective-permute-done | bytes 131104 | tf_op jit(solution)/shard_map/ppermute | solution.py:825
  36.1 1.6 %collective-permute-start.11 = (bf16[4,128,256]{2,1,0:T(8,128)(2,1)S(1)}, bf16[4,128,256]{2,1,0:T(8,128)(2,1)S(1)}, u32[]{:S(2)}, u32[]{:S(2)}) collective-permute-start(bf16[4,128,256]{2,1,0:T(8,128)(2,1)S(1)} %get-tuple-element.120), channel_id=1, source_target_pairs={{0,8},{4,12},{8,0},{12,4},{16,24},{20,28},{24,16},{28,20},{1,9},{5... | collective-permute-start | bytes 786440 | tf_op jit(solution)/shard_map/ppermute | solution.py:825
  37.6 1.4 %collective-permute-start.13 = (bf16[4,128,128]{2,1,0:T(8,128)(2,1)S(1)}, bf16[4,128,128]{2,1,0:T(8,128)(2,1)S(1)}, u32[]{:S(2)}, u32[]{:S(2)}) collective-permute-start(bf16[4,128,128]{2,1,0:T(8,128)(2,1)S(1)} %get-tuple-element.121), channel_id=1, source_target_pairs={{0,24},{4,28},{8,16},{12,20},{16,8},{20,12},{24,0},{28,4},{1,25},{... | collective-permute-start | bytes 393224 | tf_op jit(solution)/shard_map/ppermute | solution.py:825
  39.0 0.6 collective-permute-start.12
  39.6 3.5 %pull_local.1 = (f32[3,4,256,128]{3,2,1,0:T(8,128)S(1)}, f32[4,256,128]{2,1,0:T(8,128)S(1)}, f32[256,128]{1,0:T(8,128)S(1)}, f32[8,256]{1,0:T(8,128)S(1)}) custom-call(f32[3,4,256,128]{3,2,1,0:T(8,128)S(1)} %get-tuple-element.74.qkv_ref.refs_0_, f32[256,128]{1,0:T(8,128)S(1)} %get-tuple-element.72.pack_ref.refs_1_.refs_2_, ...), custom_call_target="tpu_custom_call" | custom-call | tf_op jit(solution)/shard_map/pull_local/pallas_call | solution.py:103
  43.2 1.2 %collective-permute-done.7.got_ref = bf16[2,256,512]{2,1,0:T(8,128)(2,1)S(1)} collective-permute-done((bf16[2,256,512]{2,1,0:T(8,128)(2,1)S(1)}, bf16[2,256,512]{2,1,0:T(8,128)(2,1)S(1)}, u32[]{:S(2)}, u32[]{:S(2)}) %collective-permute-start.7) | collective-permute-done | bytes 524320 | tf_op jit(solution)/shard_map/ppermute | solution.py:825
  44.5 2.7 %collective-permute-start.14 = (bf16[1,256,512]{2,1,0:T(8,128)(2,1)S(1)}, bf16[1,256,512]{2,1,0:T(8,128)(2,1)S(1)}, u32[]{:S(2)}, u32[]{:S(2)}) collective-permute-start(bf16[1,256,512]{2,1,0:T(8,128)(2,1)S(1)} %get-tuple-element.130), channel_id=1, source_target_pairs={{0,2},{1,3},{2,0},{3,1},{4,6},{5,7},{6,4},{7,5},{8,10},{9,11},{10,... | collective-permute-start | bytes 786440 | tf_op jit(solution)/shard_map/ppermute | solution.py:825
  47.1 1.0 %collective-permute-done.13.refs_20_ = bf16[4,128,128]{2,1,0:T(8,128)(2,1)S(1)} collective-permute-done((bf16[4,128,128]{2,1,0:T(8,128)(2,1)S(1)}, bf16[4,128,128]{2,1,0:T(8,128)(2,1)S(1)}, u32[]{:S(2)}, u32[]{:S(2)}) %collective-permute-start.13) | collective-permute-done | bytes 131104 | tf_op jit(solution)/shard_map/ppermute | solution.py:825
  48.2 5.4 %finish.1 = (bf16[256,1536]{1,0:T(8,128)(2,1)S(1)}, bf16[256,128]{1,0:T(8,128)(2,1)S(1)}) custom-call(s32[2]{0:T(128)S(1)} %pad_add_fusion.place_ref, f32[3,4,256,128]{3,2,1,0:T(8,128)S(1)} %get-tuple-element.74.qkv_ref.refs_0_, f32[256,128]{1,0:T(8,128)S(1)} %get-tuple-element.93.refs_1_, f32[256,128]{1,0:T(8,128)S(1)} %get-tuple-element.72.pack_ref.refs_1_.refs_2_, ...), custom_call_target="tpu_custom_call" | custom-call | tf_op jit(solution)/shard_map/finish/pallas_call | solution.py:103
  53.6 2.6 %pull_tokens.1 = (bf16[2,256,256]{2,1,0:T(8,128)(2,1)S(1)}, bf16[2,256,256]{2,1,0:T(8,128)(2,1)S(1)}, bf16[256,256]{1,0:T(8,128)(2,1)S(1)}, bf16[256,256]{1,0:T(...) custom-call(s32[2]{0:T(128)S(1)} %pad_add_fusion.place_ref, ...), custom_call_target="tpu_custom_call" | custom-call | tf_op jit(solution)/shard_map/pull_tokens/pallas_call | solution.py:103
  56.2 0.6 collective-permute-start.15
  56.8 1.9 %collective-permute-done.14.refs_1_ = bf16[1,256,512]{2,1,0:T(8,128)(2,1)S(1)} collective-permute-done((bf16[1,256,512]{2,1,0:T(8,128)(2,1)S(1)}, bf16[1,256,512]{2,1,0:T(8,128)(2,1)S(1)}, u32[]{:S(2)}, u32[]{:S(2)}) %collective-permute-start.14) | collective-permute-done | bytes 262176 | tf_op jit(solution)/shard_map/ppermute | solution.py:825
  58.7 0.7 collective-permute-start.17
  59.3 2.9 %collective-permute-start.18 = (bf16[256,256]{1,0:T(8,128)(2,1)S(1)}, bf16[256,256]{1,0:T(8,128)(2,1)S(1)}, u32[]{:S(2)}, u32[]{:S(2)}) collective-permute-start(bf16[256,256]{1,0:T(8,128)(2,1)S(1)} %get-tuple-element.140), channel_id=1, source_target_pairs={{0,3},{1,2},{2,1},{3,0},{4,7},{5,6},{6,5},{7,4},{8,11},{9,10},{10,... | collective-permute-start | bytes 393224 | tf_op jit(solution)/shard_map/ppermute | solution.py:825
  62.2 5.0 %collective-permute-done.15.got_ref = bf16[2,256,256]{2,1,0:T(8,128)(2,1)S(1)} collective-permute-done((bf16[2,256,256]{2,1,0:T(8,128)(2,1)S(1)}, bf16[2,256,256]{2,1,0:T(8,128)(2,1)S(1)}, u32[]{:S(2)}, u32[]{:S(2)}) %collective-permute-start.15) | collective-permute-done | bytes 262176 | tf_op jit(solution)/shard_map/ppermute | solution.py:825
  67.2 1.4 %collective-permute-start.16 = (bf16[1,256,256]{2,1,0:T(8,128)(2,1)S(1)}, bf16[1,256,256]{2,1,0:T(8,128)(2,1)S(1)}, u32[]{:S(2)}, u32[]{:S(2)}) collective-permute-start(bf16[1,256,256]{2,1,0:T(8,128)(2,1)S(1)} %get-tuple-element.137), channel_id=1, source_target_pairs={{0,2},{1,3},{2,0},{3,1},{4,6},{5,7},{6,4},{7,5},{8,10},{9,11},{10,... | collective-permute-start | bytes 393224 | tf_op jit(solution)/shard_map/ppermute | solution.py:825
  68.6 2.4 %collective-permute-start.19 = (bf16[256,256]{1,0:T(8,128)(2,1)S(1)}, bf16[256,256]{1,0:T(8,128)(2,1)S(1)}, u32[]{:S(2)}, u32[]{:S(2)}) collective-permute-start(bf16[256,256]{1,0:T(8,128)(2,1)S(1)} %get-tuple-element.141), channel_id=1, source_target_pairs={{0,1},{1,0},{2,3},{3,2},{4,5},{5,4},{6,7},{7,6},{8,9},{9,8},{10,11... | collective-permute-start | bytes 393224 | tf_op jit(solution)/shard_map/ppermute | solution.py:825
  71.0 0.8 head_sum.2
  71.8 6.8 %collective-permute-done.16.refs_1_ = bf16[1,256,256]{2,1,0:T(8,128)(2,1)S(1)} collective-permute-done((bf16[1,256,256]{2,1,0:T(8,128)(2,1)S(1)}, bf16[1,256,256]{2,1,0:T(8,128)(2,1)S(1)}, u32[]{:S(2)}, u32[]{:S(2)}) %collective-permute-start.16) | collective-permute-done | bytes 131104 | tf_op jit(solution)/shard_map/ppermute | solution.py:825
  78.6 0.8 %head_sum.3 = bf16[256,512]{1,0:T(8,128)(2,1)} custom-call(f32[1,256,256]{2,1,0:T(8,128)S(1)} %get-tuple-element.134.refs_0_, bf16[1,256,256]{2,1,0:T(8,128)(2,1)S(1)} %collective-permute-done.16.refs_1_, bf16[256,256]{1,0:T(8,128)(2,1)S(1)} %get-tuple-element.138.refs_2_, bf16[256,256]{1,0:T(8,128)(2,1)S(1)} %collective-permute-done.17.refs_3_, ...), custom_call_target="tpu_custom_call" | custom-call | tf_op jit(solution)/shard_map/head_sum/pallas_call | solution.py:103
  (33 shorter events, 2.5 us)
Async XLA Ops:
  0.7 18.6 %copy-start = (bf16[4,128,2048]{2,1,0:T(8,128)(2,1)S(1)}, bf16[4,128,2048]{2,1,0:T(8,128)(2,1)}, u32[]{:S(2)}) copy-start(bf16[4,128,2048]{2,1,0:T(8,128)(2,1)} %param.12) | copy-start | bytes 6291460
  0.7 18.6 %copy-start.1 = (bf16[256,2048]{1,0:T(8,128)(2,1)S(1)}, bf16[256,2048]{1,0:T(8,128)(2,1)}, u32[]{:S(2)}) copy-start(bf16[256,2048]{1,0:T(8,128)(2,1)} %grad_ref.1) | copy-start | bytes 3145732
  12.4 1.7 %collective-permute-start = (bf16[4,128,256]{2,1,0:T(8,128)(2,1)S(1)}, bf16[4,128,256]{2,1,0:T(8,128)(2,1)S(1)}, u32[]{:S(2)}, u32[]{:S(2)}) collective-permute-start(bf16[4,128,256]{2,1,0:T(8,128)(2,1)S(1)} %get-tuple-element.73.own_ref), channel_id=1, source_target_pairs={{0,4},{4,0},{8,12},{12,8},{16,20},{20,16},{24,28},{28,24},{1,5},{5... | collective-permute-start | bytes 786440 | tf_op jit(solution)/shard_map/ppermute | solution.py:825
  14.8 8.7 %collective-permute-start.3 = (bf16[2,128,256]{2,1,0:T(8,128)(2,1)S(1)}, bf16[2,128,256]{2,1,0:T(8,128)(2,1)S(1)}, u32[]{:S(2)}, u32[]{:S(2)}) collective-permute-start(bf16[2,128,256]{2,1,0:T(8,128)(2,1)S(1)} %join_half.1), channel_id=1, source_target_pairs={{0,24},{4,28},{8,16},{12,20},{16,8},{20,12},{24,0},{28,4},{1,25},{... | collective-permute-start | bytes 393224 | tf_op jit(solution)/shard_map/ppermute | solution.py:825
  18.7 6.6 %collective-permute-start.2 = (bf16[2,128,256]{2,1,0:T(8,128)(2,1)S(1)}, bf16[2,128,256]{2,1,0:T(8,128)(2,1)S(1)}, u32[]{:S(2)}, u32[]{:S(2)}) collective-permute-start(bf16[2,128,256]{2,1,0:T(8,128)(2,1)S(1)} %join_half.1), channel_id=1, source_target_pairs={{0,16},{4,20},{8,24},{12,28},{16,0},{20,4},{24,8},{28,12},{1,17},{... | collective-permute-start | bytes 393224 | tf_op jit(solution)/shard_map/ppermute | solution.py:825
  19.2 6.4 %collective-permute-start.1 = (bf16[2,128,256]{2,1,0:T(8,128)(2,1)S(1)}, bf16[2,128,256]{2,1,0:T(8,128)(2,1)S(1)}, u32[]{:S(2)}, u32[]{:S(2)}) collective-permute-start(bf16[2,128,256]{2,1,0:T(8,128)(2,1)S(1)} %join_half.1), channel_id=1, source_target_pairs={{0,8},{4,12},{8,0},{12,4},{16,24},{20,28},{24,16},{28,20},{1,9},{5... | collective-permute-start | bytes 393224 | tf_op jit(solution)/shard_map/ppermute | solution.py:825
  19.3 8.1 %copy-start.2 = (f32[128]{0:T(128)S(1)}, f32[128]{0:T(128)}, u32[]{:S(2)}) copy-start(f32[128]{0:T(128)} %param.11) | copy-start | bytes 1540
  25.6 1.3 %collective-permute-start.4 = (bf16[2,128,256]{2,1,0:T(8,128)(2,1)S(1)}, bf16[2,128,256]{2,1,0:T(8,128)(2,1)S(1)}, u32[]{:S(2)}, u32[]{:S(2)}) collective-permute-start(bf16[2,128,256]{2,1,0:T(8,128)(2,1)S(1)} %collective-permute-done.1.refs_1_), channel_id=1, source_target_pairs={{0,4},{4,0},{8,12},{12,8},{16,20},{20,16},{24,28},{28,24},{1,5},{5... | collective-permute-start | bytes 393224 | tf_op jit(solution)/shard_map/ppermute | solution.py:825
  25.6 1.5 %collective-permute-start.5 = (bf16[2,128,256]{2,1,0:T(8,128)(2,1)S(1)}, bf16[2,128,256]{2,1,0:T(8,128)(2,1)S(1)}, u32[]{:S(2)}, u32[]{:S(2)}) collective-permute-start(bf16[2,128,256]{2,1,0:T(8,128)(2,1)S(1)} %collective-permute-done.2.refs_2_), channel_id=1, source_target_pairs={{0,4},{4,0},{8,12},{12,8},{16,20},{20,16},{24,28},{28,24},{1,5},{5... | collective-permute-start | bytes 393224 | tf_op jit(solution)/shard_map/ppermute | solution.py:825
  26.1 1.3 %collective-permute-start.6 = (bf16[2,128,256]{2,1,0:T(8,128)(2,1)S(1)}, bf16[2,128,256]{2,1,0:T(8,128)(2,1)S(1)}, u32[]{:S(2)}, u32[]{:S(2)}) collective-permute-start(bf16[2,128,256]{2,1,0:T(8,128)(2,1)S(1)} %collective-permute-done.3.refs_3_), channel_id=1, source_target_pairs={{0,4},{4,0},{8,12},{12,8},{16,20},{20,16},{24,28},{28,24},{1,5},{5... | collective-permute-start | bytes 393224 | tf_op jit(solution)/shard_map/ppermute | solution.py:825
  30.3 14.1 %collective-permute-start.7 = (bf16[2,256,512]{2,1,0:T(8,128)(2,1)S(1)}, bf16[2,256,512]{2,1,0:T(8,128)(2,1)S(1)}, u32[]{:S(2)}, u32[]{:S(2)}) collective-permute-start(bf16[2,256,512]{2,1,0:T(8,128)(2,1)S(1)} %get-tuple-element.91), channel_id=1, source_target_pairs={{0,1},{1,0},{2,3},{3,2},{4,5},{5,4},{6,7},{7,6},{8,9},{9,8},{10,11... | collective-permute-start | bytes 1572872 | tf_op jit(solution)/shard_map/ppermute | solution.py:825
  34.2 1.8 %collective-permute-start.9 = (bf16[4,128,256]{2,1,0:T(8,128)(2,1)S(1)}, bf16[4,128,256]{2,1,0:T(8,128)(2,1)S(1)}, u32[]{:S(2)}, u32[]{:S(2)}) collective-permute-start(bf16[4,128,256]{2,1,0:T(8,128)(2,1)S(1)} %get-tuple-element.118.refs_0_), channel_id=1, source_target_pairs={{0,4},{4,0},{8,12},{12,8},{16,20},{20,16},{24,28},{28,24},{1,5},{5... | collective-permute-start | bytes 786440 | tf_op jit(solution)/shard_map/ppermute | solution.py:825
  34.2 1.7 %collective-permute-start.10 = (bf16[4,128,128]{2,1,0:T(8,128)(2,1)S(1)}, bf16[4,128,128]{2,1,0:T(8,128)(2,1)S(1)}, u32[]{:S(2)}, u32[]{:S(2)}) collective-permute-start(bf16[4,128,128]{2,1,0:T(8,128)(2,1)S(1)} %get-tuple-element.119.refs_1_), channel_id=1, source_target_pairs={{0,4},{4,0},{8,12},{12,8},{16,20},{20,16},{24,28},{28,24},{1,5},{5... | collective-permute-start | bytes 393224 | tf_op jit(solution)/shard_map/ppermute | solution.py:825
  34.7 12.4 %collective-permute-start.8 = (bf16[4,128,256]{2,1,0:T(8,128)(2,1)S(1)}, bf16[4,128,256]{2,1,0:T(8,128)(2,1)S(1)}, u32[]{:S(2)}, u32[]{:S(2)}) collective-permute-start(bf16[4,128,256]{2,1,0:T(8,128)(2,1)S(1)} %get-tuple-element.117), channel_id=1, source_target_pairs={{0,4},{4,0},{8,12},{12,8},{16,20},{20,16},{24,28},{28,24},{1,5},{5... | collective-permute-start | bytes 786440 | tf_op jit(solution)/shard_map/ppermute | solution.py:825
  36.1 12.1 %collective-permute-start.11 = (bf16[4,128,256]{2,1,0:T(8,128)(2,1)S(1)}, bf16[4,128,256]{2,1,0:T(8,128)(2,1)S(1)}, u32[]{:S(2)}, u32[]{:S(2)}) collective-permute-start(bf16[4,128,256]{2,1,0:T(8,128)(2,1)S(1)} %get-tuple-element.120), channel_id=1, source_target_pairs={{0,8},{4,12},{8,0},{12,4},{16,24},{20,28},{24,16},{28,20},{1,9},{5... | collective-permute-start | bytes 786440 | tf_op jit(solution)/shard_map/ppermute | solution.py:825
  37.6 10.5 %collective-permute-start.13 = (bf16[4,128,128]{2,1,0:T(8,128)(2,1)S(1)}, bf16[4,128,128]{2,1,0:T(8,128)(2,1)S(1)}, u32[]{:S(2)}, u32[]{:S(2)}) collective-permute-start(bf16[4,128,128]{2,1,0:T(8,128)(2,1)S(1)} %get-tuple-element.121), channel_id=1, source_target_pairs={{0,24},{4,28},{8,16},{12,20},{16,8},{20,12},{24,0},{28,4},{1,25},{... | collective-permute-start | bytes 393224 | tf_op jit(solution)/shard_map/ppermute | solution.py:825
  39.0 9.1 %collective-permute-start.12 = (bf16[4,128,128]{2,1,0:T(8,128)(2,1)S(1)}, bf16[4,128,128]{2,1,0:T(8,128)(2,1)S(1)}, u32[]{:S(2)}, u32[]{:S(2)}) collective-permute-start(bf16[4,128,128]{2,1,0:T(8,128)(2,1)S(1)} %get-tuple-element.121), channel_id=1, source_target_pairs={{0,16},{4,20},{8,24},{12,28},{16,0},{20,4},{24,8},{28,12},{1,17},{... | collective-permute-start | bytes 393224 | tf_op jit(solution)/shard_map/ppermute | solution.py:825
  39.6 13.9 %slice-start = ((s8[6291456]{0:T(1024)(128)(4,1)}), s8[2097152]{0:T(1024)(128)(4,1)S(1)}, s32[]{:S(2)}) async-start(s8[6291456]{0:T(1024)(128)(4,1)} %bitcast.7), calls=%async_computation | async-start | bytes 4194304
  44.3 9.2 %slice-start.1 = ((s8[6291456]{0:T(1024)(128)(4,1)}), s8[4194304]{0:T(1024)(128)(4,1)S(1)}, s32[]{:S(2)}) async-start(s8[6291456]{0:T(1024)(128)(4,1)} %bitcast.7), calls=%async_computation.1 | async-start | bytes 8388608
  44.5 14.2 %collective-permute-start.14 = (bf16[1,256,512]{2,1,0:T(8,128)(2,1)S(1)}, bf16[1,256,512]{2,1,0:T(8,128)(2,1)S(1)}, u32[]{:S(2)}, u32[]{:S(2)}) collective-permute-start(bf16[1,256,512]{2,1,0:T(8,128)(2,1)S(1)} %get-tuple-element.130), channel_id=1, source_target_pairs={{0,2},{1,3},{2,0},{3,1},{4,6},{5,7},{6,4},{7,5},{8,10},{9,11},{10,... | collective-permute-start | bytes 786440 | tf_op jit(solution)/shard_map/ppermute | solution.py:825
  56.2 11.0 %collective-permute-start.15 = (bf16[2,256,256]{2,1,0:T(8,128)(2,1)S(1)}, bf16[2,256,256]{2,1,0:T(8,128)(2,1)S(1)}, u32[]{:S(2)}, u32[]{:S(2)}) collective-permute-start(bf16[2,256,256]{2,1,0:T(8,128)(2,1)S(1)} %get-tuple-element.133), channel_id=1, source_target_pairs={{0,1},{1,0},{2,3},{3,2},{4,5},{5,4},{6,7},{7,6},{8,9},{9,8},{10,11... | collective-permute-start | bytes 786440 | tf_op jit(solution)/shard_map/ppermute | solution.py:825
  58.7 13.1 %collective-permute-start.17 = (bf16[256,256]{1,0:T(8,128)(2,1)S(1)}, bf16[256,256]{1,0:T(8,128)(2,1)S(1)}, u32[]{:S(2)}, u32[]{:S(2)}) collective-permute-start(bf16[256,256]{1,0:T(8,128)(2,1)S(1)} %get-tuple-element.139), channel_id=1, source_target_pairs={{0,2},{1,3},{2,0},{3,1},{4,6},{5,7},{6,4},{7,5},{8,10},{9,11},{10,... | collective-permute-start | bytes 393224 | tf_op jit(solution)/shard_map/ppermute | solution.py:825
  59.3 12.5 %collective-permute-start.18 = (bf16[256,256]{1,0:T(8,128)(2,1)S(1)}, bf16[256,256]{1,0:T(8,128)(2,1)S(1)}, u32[]{:S(2)}, u32[]{:S(2)}) collective-permute-start(bf16[256,256]{1,0:T(8,128)(2,1)S(1)} %get-tuple-element.140), channel_id=1, source_target_pairs={{0,3},{1,2},{2,1},{3,0},{4,7},{5,6},{6,5},{7,4},{8,11},{9,10},{10,... | collective-permute-start | bytes 393224 | tf_op jit(solution)/shard_map/ppermute | solution.py:825
  67.2 11.4 %collective-permute-start.16 = (bf16[1,256,256]{2,1,0:T(8,128)(2,1)S(1)}, bf16[1,256,256]{2,1,0:T(8,128)(2,1)S(1)}, u32[]{:S(2)}, u32[]{:S(2)}) collective-permute-start(bf16[1,256,256]{2,1,0:T(8,128)(2,1)S(1)} %get-tuple-element.137), channel_id=1, source_target_pairs={{0,2},{1,3},{2,0},{3,1},{4,6},{5,7},{6,4},{7,5},{8,10},{9,11},{10,... | collective-permute-start | bytes 393224 | tf_op jit(solution)/shard_map/ppermute | solution.py:825
  68.6 10.0 %collective-permute-start.19 = (bf16[256,256]{1,0:T(8,128)(2,1)S(1)}, bf16[256,256]{1,0:T(8,128)(2,1)S(1)}, u32[]{:S(2)}, u32[]{:S(2)}) collective-permute-start(bf16[256,256]{1,0:T(8,128)(2,1)S(1)} %get-tuple-element.141), channel_id=1, source_target_pairs={{0,1},{1,0},{2,3},{3,2},{4,5},{5,4},{6,7},{7,6},{8,9},{9,8},{10,11... | collective-permute-start | bytes 393224 | tf_op jit(solution)/shard_map/ppermute | solution.py:825

commit v13 on v12

--- a/solution.py
+++ b/solution.py
@@ -196,7 +196,7 @@
             laid[col // heads][at : at + depth, lanes] = value
 
     def multiply(first, last):
-        for part in (1, 2, 0):
+        for part in (1, 2):
             span = slice((part * heads) * LANES, (part + 1) * heads * LANES)
             own = jnp.dot(
                 tokens[:, first * depth : last * depth],
@@ -288,8 +288,6 @@
         last = jnp.exp(cum_col[rows - 1 : rows, :])
         pair_ref[head, :, :LANES] = (last * eye_key + pair[:, :LANES]).astype(BF16)
         pair_ref[head, :, LANES:] = pair[:, LANES:].astype(BF16)
-    for head in range(heads):
-        scales = scales + unit_of(0, head)[1]
     pack_ref[...] = jnp.where(lane < norm_col, pack, scales)
     for keep in keeps:
         keep.wait()
@@ -340,11 +338,11 @@
 
 def local_body(
     sizes, qkv_ref, pack_ref, pack_t_ref, trans_ref, mixed_t_ref, decay_ref, grad_ref, weight_ref,
-    query_ref, value_ref, wr_in, *outs
+    query_ref, value_ref, tokens_ref, wr_in, *outs
 ):
     heads, levels, bits = sizes
     (attn_ref, attn_t_ref, prod_t_ref, scores_ref, mix_ref, mixed_ref, local_ref, hat_ref,
-     hat_t_ref, grad_normed_ref, wr_hbm, sems) = outs
+     hat_t_ref, grad_normed_ref, qkv_out, pack_out, wr_hbm, sems) = outs
     del wr_in
     half, size = query_ref.shape[0] // 2, query_ref.shape[1]
     keeps = []
@@ -354,16 +352,27 @@
         there = wr_hbm.at[span, pl.ds(col, size)]
         keeps.append(pltpu.make_async_copy(here.at[span, :], there, sems.at[at]))
         keeps[at].start()
-    grad_normed_ref[...] = mm_nt(grad_ref[...], weight_ref[...])
     rows = pack_ref.shape[0]
     decay_col = levels * heads
     beta_col = decay_col + heads
+    norm_col = beta_col + heads
+    lane = lane_of(rows)
+    raw_all = jnp.dot(tokens_ref[...], query_ref[...], preferred_element_type=F32)
     pack = pack_ref[...]
+    q_all = []
+    for head in range(heads):
+        raw = raw_all[:, head * LANES : (head + 1) * LANES]
+        scale = lax.rsqrt(row_sum(raw * raw) + EPS)
+        q_all.append(raw * scale)
+        qkv_out[0, head] = q_all[head]
+        pack = jnp.where(lane == norm_col + head, scale, pack)
+    pack_out[...] = pack
+    grad_normed_ref[...] = mm_nt(grad_ref[...], weight_ref[...])
     pack_t = pack_t_ref[...]
     row_id, col_id = pair_ids(rows)
     apart = row_id ^ col_id
     for head in range(heads):
-        scores = mm_nt_fine(qkv_ref[0, head], qkv_ref[1, head]) * decay_ref[head].astype(F32)
+        scores = mm_nt_fine(q_all[head], qkv_ref[1, head]) * decay_ref[head].astype(F32)
         scores_ref[head] = scores.astype(BF16)
         mix_ref[head] = level_mix(pack, head, heads, bits, apart).astype(BF16)
         mixed_ref[head] = mixed_t_ref[head].astype(F32).T.astype(BF16)
@@ -376,7 +385,7 @@
         prod_t_ref[head] = prod.T.astype(BF16)
         growth = jnp.exp(column(pack, decay_col + head))
         local_ref[head] = mm(prod, qkv_ref[2, head])
-        hat = growth * qkv_ref[0, head] - mm(attn, growth * qkv_ref[1, head])
+        hat = growth * q_all[head] - mm(attn, growth * qkv_ref[1, head])
         hat_ref[head] = hat.astype(BF16)
         hat_t_ref[head] = hat.T.astype(BF16)
     for keep in keeps:
@@ -397,12 +406,14 @@
         kept((heads, rows, key), BF16),
         kept((heads, key, rows), BF16),
         kept((rows, heads * key), F32),
+        kept(arrays[0].shape, F32),
+        kept(arrays[1].shape, F32),
         stored(wr.shape, BF16),
     )
     return local_call(
         functools.partial(local_body, (heads, levels, bits)), "local_part", 10, out_shape,
-        [], arrays, [pltpu.SemaphoreType.DMA((4,))], [wr], [WHOLE] * 10 + [HBM],
-        {len(arrays): 10},
+        [], arrays, [pltpu.SemaphoreType.DMA((4,))], [wr], [WHOLE] * 12 + [HBM],
+        {0: 10, 1: 11, len(arrays): 12},
     )
 
 
@@ -440,14 +451,14 @@
 
 
 def reach_body(
-    sizes, place_ref, gain_ref, pack_ref, local_ref, hat_ref, grad_ref, weight_ref, *refs
+    sizes, place_ref, gain_ref, pack_ref, local_ref, hat_ref, weight_ref, *refs
 ):
     heads, bits, far, count, near_count = sizes
     first_ref = refs[0]
     near = [None] + [(refs[1 + at], refs[1 + near_count + at]) for at in range(near_count)]
     refs = refs[2 * near_count + 1 :]
     out_refs = refs[:2]
-    dout_ref, found_ref, prefix_ref, dfar_ref = refs[2:6]
+    summed_ref, scale_ref, found_ref, prefix_ref = refs[2:6]
     nodes = refs[6:-1]
     normed_ref = refs[-1]
     rows = pack_ref.shape[0]
@@ -481,24 +492,19 @@
         ]
     found = [jnp.concatenate([found[bit][head] for bit in range(far)], 1) for head in all_heads]
     reached = [mm(hat_ref[head], found[head]) for head in all_heads]
-    dfar = jnp.zeros((rows, LANES), F32)
+    scales = jnp.zeros((rows, LANES), F32)
     for head in all_heads:
         found_ref[head] = found[head]
         summed = local_ref[head]
-        parts = []
         for bit in range(far):
-            parts.append(reached[head][:, bit * key : (bit + 1) * key])
-            summed = summed + column(pack, (bits + 1 + bit) * heads + head) * parts[bit]
+            part = reached[head][:, bit * key : (bit + 1) * key]
+            summed = summed + column(pack, (bits + 1 + bit) * heads + head) * part
         scale = lax.rsqrt(jnp.mean(summed * summed, -1, keepdims=True) + EPS)
         unit = summed * scale
         normed_ref[:, head * key : (head + 1) * key] = (unit * gain).astype(BF16)
-        pulled = grad_ref[:, head * key : (head + 1) * key] * gain
-        dout = scale * (pulled - unit * jnp.mean(pulled * unit, -1, keepdims=True))
-        dout_ref[head] = dout
-        for bit in range(far):
-            col = (bits + 1 + bit) * heads + head
-            dfar = jnp.where(lane == col, row_sum(dout * parts[bit]), dfar)
-    dfar_ref[...] = dfar
+        summed_ref[head] = unit
+        scales = jnp.where(lane == head, scale, scales)
+    scale_ref[...] = scales
     size = weight_ref.shape[1] // count
     for mask in range(count):
         dest = place_ref[1] ^ mask
@@ -509,15 +515,15 @@
 
 
 def reach(place, arrays, first, near, bits, far, count):
-    gain, pack, local_out, hat, grad_normed, weight = arrays
+    gain, pack, local_out, hat, weight = arrays
     heads, rows, key = hat.shape
     nodes = tuple(kept(first.shape, BF16) for bit in range(1, far))
     size = weight.shape[1] // count
     out_shape = (kept((count // 2, rows, size), BF16),) * 2 + (
         kept((heads, rows, key), F32),
+        kept((rows, LANES), F32),
         kept((heads, key, far * key), BF16),
         kept((heads, far, key, key), BF16),
-        kept((rows, LANES), F32),
     ) + nodes
     mine, theirs = near
     got = local_call(
@@ -527,22 +533,38 @@
     return got[:2], got[2:6], got[6:]
 
 
-def return_body(sizes, place_ref, pack_ref, hat_t_ref, dout_ref, found_ref, prefix_ref, *refs):
+def return_body(
+    sizes, place_ref, gain_ref, pack_ref, hat_ref, hat_t_ref, grad_ref, unit_ref, scale_ref,
+    found_ref, prefix_ref, *refs
+):
     heads, bits, far = sizes
     others = refs[:far]
-    dhat_ref = refs[far]
-    sends = refs[far + 1 :]
+    dhat_ref, dout_ref, dfar_ref = refs[far : far + 3]
+    sends = refs[far + 3 :]
+    rows = pack_ref.shape[0]
+    lane = lane_of(rows)
+    gain, scales = gain_ref[...], scale_ref[...]
     key = hat_t_ref.shape[1]
     pack = pack_ref[...]
     all_heads = range(heads)
     uppers = [((place_ref[0] >> bit) & 1) == 1 for bit in range(far)]
+    reached = [mm(hat_ref[head], found_ref[head]) for head in all_heads]
+    dfar = jnp.zeros((rows, LANES), F32)
     spread = []
     for head in all_heads:
+        unit = unit_ref[head]
+        pulled = grad_ref[:, head * key : (head + 1) * key] * gain
+        mean = jnp.mean(pulled * unit, -1, keepdims=True)
+        dout = column(scales, head) * (pulled - unit * mean)
+        dout_ref[head] = dout
         parts = []
         for bit in range(far):
-            weight = column(pack, (bits + 1 + bit) * heads + head)
-            parts.append((weight * dout_ref[head]).astype(BF16))
+            col = (bits + 1 + bit) * heads + head
+            parts.append((column(pack, col) * dout).astype(BF16))
+            here = reached[head][:, bit * key : (bit + 1) * key]
+            dfar = jnp.where(lane == col, row_sum(dout * here), dfar)
         spread.append(jnp.concatenate(parts, 1))
+    dfar_ref[...] = dfar
     dfound = [mm(hat_t_ref[head], spread[head]) for head in all_heads]
     for head in all_heads:
         dhat_ref[head] = mm_nt(spread[head], found_ref[head])
@@ -565,17 +587,18 @@
             ]
 
 
-def return_states(place, pack, hat_t, dout, found, prefix, others, bits):
-    heads, rows, key = dout.shape
+def return_states(place, arrays, others, bits):
+    heads, rows, key = arrays[2].shape
     far = len(others)
     sends = tuple(
         kept((heads, key, (1 if bit == far - 1 else 2) * key), BF16) for bit in range(far)
     )
+    wide = kept((heads, rows, key), F32)
     got = local_call(
         functools.partial(return_body, (heads, bits, far)), "return_states", 8,
-        (kept(dout.shape, F32),) + sends, [place], [pack, hat_t, dout, found, prefix, *others],
-    )
-    return got[0], got[1:]
+        (wide, wide, kept((rows, LANES), F32)) + sends, [place], [*arrays, *others],
+    )
+    return got[:3], got[3:]
 
 
 def add_body(*refs):
@@ -895,18 +918,20 @@
     first = swap(pair, "ctx", 1)
     node = join_half(place, pair, first)
     mine = [swap(node, "ctx", 2 * at) for at in range(1, size // 2)]
-    (attn, attn_t, prod_t, scores, mix, mixed, local_out, hat, hat_t, grad_normed, wr) = local_part(
-        [qkv, pack, pack_t, trans, mixed_t, decay, grad_out, flat_out, query_w, value_w],
+    (attn, attn_t, prod_t, scores, mix, mixed, local_out, hat, hat_t, grad_normed, qkv, pack,
+     wr) = local_part(
+        [qkv, pack, pack_t, trans, mixed_t, decay, grad_out, flat_out, query_w, value_w, tokens],
         wr, levels, bits,
     )
     mine, local_out, grad_normed = lax.optimization_barrier((mine, local_out, grad_normed))
     theirs = [swap(value, "ctx", 1) for value in mine]
-    out_parts, (dout, found, prefix, dfar), nodes = reach(
-        place, [gain, pack, local_out, hat, grad_normed, flat_out], first, (mine, theirs),
-        bits, far, count
+    out_parts, (unit, scale, found, prefix), nodes = reach(
+        place, [gain, pack, local_out, hat, flat_out], first, (mine, theirs), bits, far, count
     )
     others = [first, *nodes]
-    dhat, sends = return_states(place, pack, hat_t, dout, found, prefix, others, bits)
+    (dhat, dout, dfar), sends = return_states(
+        place, [gain, pack, hat, hat_t, grad_normed, unit, scale, found, prefix], others, bits
+    )
     got = [swap(value, "ctx", 1) for value in sends]
     arrived = [[got[0]]]
     sums = add_all(sends[1:], got[1:])

time: 79.6 us -> 79.3 us (level)
  Pallas kernels: 35 us -> 36.5 us
  waiting for transfers between devices: 21.5 us -> 20.2 us
    pallas_call x13, Pallas kernels: 35 us -> 36.5 us  [local_call(): pl.pallas_call(body, out_shape=tuple(out_shape), in_specs=[SCALARS] * len...]
    ppermute x20, waiting for transfers between devices: 21.5 us -> 20.2 us  [swap(): return lax.ppermute(value, axis, [(at, at ^ mask) for at in range(size)])]
  transfers between devices with their start and end apart: 20 -> 20, of which waited for: 12 -> 13; matrix products, arithmetic and copies ran while one was open for 0% -> 0% of each run, Pallas kernels for 24% -> 26%
where the time goes in v13:
time: 79.3 us; the launch traced here: 79.2 us
  Pallas kernels  36.5 us (46%)
  starting transfers between devices  21.6 us (27%)
  waiting for transfers between devices  20.2 us (25%)
    pallas_call x13, Pallas kernels, local_call(): pl.pallas_call(body, out_shape=tuple(out_shape), in_specs=[SCALARS] * len...  36.5 us
    ppermute x20, starting transfers between devices, swap(): return lax.ppermute(value, axis, [(at, at ^ mask) for at in range(size)])  21.6 us
    ppermute x20, waiting for transfers between devices, swap(): return lax.ppermute(value, axis, [(at, at ^ mask) for at in range(size)])  20.2 us
  transfers between devices with their start and end apart: 20, of which 13 were waited for; matrix products, arithmetic and copies ran while one was open for 0% of the time, Pallas kernels for 26%

profile of v13, /device:TPU:0, one launch (start us, length us, event | category | flops | bytes accessed | tf_op | source)
XLA Modules:
  0.0 79.2 jit_solution(12578349219925885256)
XLA Ops:
  0.7 11.6 %project.1 = (bf16[2048,1536]{1,0:T(8,128)(2,1)}, bf16[2048,512]{1,0:T(8,128)(2,1)S(1)}, bf16[2048,512]{1,0:T(8,128)(2,1)S(1)}, bf16[128,2048]{1,0:T(8,128)(2,1)...) custom-call(s32[2]{0:T(128)S(1)} %pad_add_fusion.place_ref, ...), custom_call_target="tpu_custom_call" | custom-call | tf_op jit(solution)/shard_map/project/pallas_call | solution.py:103
  12.3 0.5 collective-permute-start
  12.8 1.2 %collective-permute-done.other_ref.refs_0_.refs_14_ = bf16[4,128,256]{2,1,0:T(8,128)(2,1)S(1)} collective-permute-done((bf16[4,128,256]{2,1,0:T(8,128)(2,1)S(1)}, bf16[4,128,256]{2,1,0:T(8,128)(2,1)S(1)}, u32[]{:S(2)}, u32[]{:S(2)}) %collective-permute-start) | collective-permute-done | bytes 262176 | tf_op jit(solution)/shard_map/ppermute | solution.py:848
  14.0 0.7 join_half.1
  14.7 3.9 %collective-permute-start.3 = (bf16[2,128,256]{2,1,0:T(8,128)(2,1)S(1)}, bf16[2,128,256]{2,1,0:T(8,128)(2,1)S(1)}, u32[]{:S(2)}, u32[]{:S(2)}) collective-permute-start(bf16[2,128,256]{2,1,0:T(8,128)(2,1)S(1)} %join_half.1), channel_id=1, source_target_pairs={{0,24},{4,28},{8,16},{12,20},{16,8},{20,12},{24,0},{28,4},{1,25},{... | collective-permute-start | bytes 393224 | tf_op jit(solution)/shard_map/ppermute | solution.py:848
  19.3 4.8 %local_part.1 = (bf16[4,256,256]{2,1,0:T(8,128)(2,1)S(1)}, bf16[4,256,256]{2,1,0:T(8,128)(2,1)S(1)}, bf16[4,256,256]{2,1,0:T(8,128)(2,1)S(1)}, bf16[4,256,256]{2...) custom-call(f32[3,4,256,128]{3,2,1,0:T(8,128)S(1)} %get-tuple-elemen, ...), custom_call_target="tpu_custom_call", output_to_operand_aliasing={{10}: (0, {}), {11}: (1, {}), {12}: (11, {})} | custom-call | tf_op jit(solution)/shard_map/local_part/pallas_call | solution.py:103
  24.0 1.2 %collective-permute-done.2.refs_2_ = bf16[2,128,256]{2,1,0:T(8,128)(2,1)S(1)} collective-permute-done((bf16[2,128,256]{2,1,0:T(8,128)(2,1)S(1)}, bf16[2,128,256]{2,1,0:T(8,128)(2,1)S(1)}, u32[]{:S(2)}, u32[]{:S(2)}) %collective-permute-start.2) | collective-permute-done | bytes 131104 | tf_op jit(solution)/shard_map/ppermute | solution.py:848
  25.5 0.5 collective-permute-start.5
  26.0 0.8 %collective-permute-done.4.refs_4_ = bf16[2,128,256]{2,1,0:T(8,128)(2,1)S(1)} collective-permute-done((bf16[2,128,256]{2,1,0:T(8,128)(2,1)S(1)}, bf16[2,128,256]{2,1,0:T(8,128)(2,1)S(1)}, u32[]{:S(2)}, u32[]{:S(2)}) %collective-permute-start.4) | collective-permute-done | bytes 131104 | tf_op jit(solution)/shard_map/ppermute | solution.py:848
  27.3 2.7 %reach.1 = (bf16[2,256,512]{2,1,0:T(8,128)(2,1)S(1)}, bf16[2,256,512]{2,1,0:T(8,128)(2,1)S(1)}, f32[4,256,128]{2,1,0:T(8,128)S(1)}, f32[256,128]{1,0:T(8,128)S(1...) custom-call(s32[2]{0:T(128)S(1)} %pad_add_fusion.place_ref, ...), custom_call_target="tpu_custom_call" | custom-call | tf_op jit(solution)/shard_map/reach/pallas_call | solution.py:103
  30.1 1.6 %collective-permute-start.7 = (bf16[2,256,512]{2,1,0:T(8,128)(2,1)S(1)}, bf16[2,256,512]{2,1,0:T(8,128)(2,1)S(1)}, u32[]{:S(2)}, u32[]{:S(2)}) collective-permute-start(bf16[2,256,512]{2,1,0:T(8,128)(2,1)S(1)} %get-tuple-element.95), channel_id=1, source_target_pairs={{0,1},{1,0},{2,3},{3,2},{4,5},{5,4},{6,7},{7,6},{8,9},{9,8},{10,11... | collective-permute-start | bytes 1572872 | tf_op jit(solution)/shard_map/ppermute | solution.py:848
  31.7 3.4 %return_states.1 = (f32[4,256,128]{2,1,0:T(8,128)S(1)}, f32[4,256,128]{2,1,0:T(8,128)S(1)}, f32[256,128]{1,0:T(8,128)S(1)}, bf16[4,128,256]{2,1,0:T(8,128)(2,1)S...) custom-call(s32[2]{0:T(128)S(1)} %pad_add_fusion.place_ref, f32[1,128]{1,0:T(1,128)S(1)} %bitcast.12, ...), custom_call_target="tpu_custom_call" | custom-call | tf_op jit(solution)/shard_map/return_states/pallas_call | solution.py:103
  35.8 1.1 %collective-permute-done.10.refs_3_ = bf16[4,128,128]{2,1,0:T(8,128)(2,1)S(1)} collective-permute-done((bf16[4,128,128]{2,1,0:T(8,128)(2,1)S(1)}, bf16[4,128,128]{2,1,0:T(8,128)(2,1)S(1)}, u32[]{:S(2)}, u32[]{:S(2)}) %collective-permute-start.10) | collective-permute-done | bytes 131104 | tf_op jit(solution)/shard_map/ppermute | solution.py:848
  37.0 1.6 %collective-permute-start.11 = (bf16[4,128,256]{2,1,0:T(8,128)(2,1)S(1)}, bf16[4,128,256]{2,1,0:T(8,128)(2,1)S(1)}, u32[]{:S(2)}, u32[]{:S(2)}) collective-permute-start(bf16[4,128,256]{2,1,0:T(8,128)(2,1)S(1)} %get-tuple-element.128), channel_id=1, source_target_pairs={{0,8},{4,12},{8,0},{12,4},{16,24},{20,28},{24,16},{28,20},{1,9},{5... | collective-permute-start | bytes 786440 | tf_op jit(solution)/shard_map/ppermute | solution.py:848
  38.6 1.4 %collective-permute-start.13 = (bf16[4,128,128]{2,1,0:T(8,128)(2,1)S(1)}, bf16[4,128,128]{2,1,0:T(8,128)(2,1)S(1)}, u32[]{:S(2)}, u32[]{:S(2)}) collective-permute-start(bf16[4,128,128]{2,1,0:T(8,128)(2,1)S(1)} %get-tuple-element.129), channel_id=1, source_target_pairs={{0,24},{4,28},{8,16},{12,20},{16,8},{20,12},{24,0},{28,4},{1,25},{... | collective-permute-start | bytes 393224 | tf_op jit(solution)/shard_map/ppermute | solution.py:848
  40.0 0.6 collective-permute-start.12
  40.5 3.5 %pull_local.1 = (f32[3,4,256,128]{3,2,1,0:T(8,128)S(1)}, f32[4,256,128]{2,1,0:T(8,128)S(1)}, f32[256,128]{1,0:T(8,128)S(1)}, f32[8,256]{1,0:T(8,128)S(1)}) custom-call(f32[3,4,256,128]{3,2,1,0:T(8,128)S(1)} %get-tuple-element.97.refs_0_, f32[256,128]{1,0:T(8,128)S(1)} %get-tuple-element.85.pack_ref.refs_1_.refs_2_, ...), custom_call_target="tpu_custom_call" | custom-call | tf_op jit(solution)/shard_map/pull_local/pallas_call | solution.py:103
  44.3 2.7 %collective-permute-start.14 = (bf16[1,256,512]{2,1,0:T(8,128)(2,1)S(1)}, bf16[1,256,512]{2,1,0:T(8,128)(2,1)S(1)}, u32[]{:S(2)}, u32[]{:S(2)}) collective-permute-start(bf16[1,256,512]{2,1,0:T(8,128)(2,1)S(1)} %get-tuple-element.138), channel_id=1, source_target_pairs={{0,2},{1,3},{2,0},{3,1},{4,6},{5,7},{6,4},{7,5},{8,10},{9,11},{10,... | collective-permute-start | bytes 786440 | tf_op jit(solution)/shard_map/ppermute | solution.py:848
  46.9 2.2 %collective-permute-done.13.refs_20_ = bf16[4,128,128]{2,1,0:T(8,128)(2,1)S(1)} collective-permute-done((bf16[4,128,128]{2,1,0:T(8,128)(2,1)S(1)}, bf16[4,128,128]{2,1,0:T(8,128)(2,1)S(1)}, u32[]{:S(2)}, u32[]{:S(2)}) %collective-permute-start.13) | collective-permute-done | bytes 131104 | tf_op jit(solution)/shard_map/ppermute | solution.py:848
  49.1 5.4 %finish.1 = (bf16[256,1536]{1,0:T(8,128)(2,1)S(1)}, bf16[256,128]{1,0:T(8,128)(2,1)S(1)}) custom-call(s32[2]{0:T(128)S(1)} %pad_add_fusion.place_ref, f32[3,4,256,128]{3,2,1,0:T(8,128)S(1)} %get-tuple-element.97.refs_0_, f32[256,128]{1,0:T(8,128)S(1)} %get-tuple-element.98.refs_1_, f32[256,128]{1,0:T(8,128)S(1)} %get-tuple-element.85.pack_ref.refs_1_.refs_2_, ...), custom_call_target="tpu_custom_call" | custom-call | tf_op jit(solution)/shard_map/finish/pallas_call | solution.py:103
  54.5 2.6 %pull_tokens.1 = (bf16[2,256,256]{2,1,0:T(8,128)(2,1)S(1)}, bf16[2,256,256]{2,1,0:T(8,128)(2,1)S(1)}, bf16[256,256]{1,0:T(8,128)(2,1)S(1)}, bf16[256,256]{1,0:T(...) custom-call(s32[2]{0:T(128)S(1)} %pad_add_fusion.place_ref, ...), custom_call_target="tpu_custom_call" | custom-call | tf_op jit(solution)/shard_map/pull_tokens/pallas_call | solution.py:103
  57.1 0.5 collective-permute-start.15
  57.6 0.8 collective-permute-done.14.refs_1_
  58.4 1.8 %collective-permute-start.17 = (bf16[256,256]{1,0:T(8,128)(2,1)S(1)}, bf16[256,256]{1,0:T(8,128)(2,1)S(1)}, u32[]{:S(2)}, u32[]{:S(2)}) collective-permute-start(bf16[256,256]{1,0:T(8,128)(2,1)S(1)} %get-tuple-element.147), channel_id=1, source_target_pairs={{0,2},{1,3},{2,0},{3,1},{4,6},{5,7},{6,4},{7,5},{8,10},{9,11},{10,... | collective-permute-start | bytes 393224 | tf_op jit(solution)/shard_map/ppermute | solution.py:848
  60.2 1.7 %collective-permute-start.18 = (bf16[256,256]{1,0:T(8,128)(2,1)S(1)}, bf16[256,256]{1,0:T(8,128)(2,1)S(1)}, u32[]{:S(2)}, u32[]{:S(2)}) collective-permute-start(bf16[256,256]{1,0:T(8,128)(2,1)S(1)} %get-tuple-element.148), channel_id=1, source_target_pairs={{0,3},{1,2},{2,1},{3,0},{4,7},{5,6},{6,5},{7,4},{8,11},{9,10},{10,... | collective-permute-start | bytes 393224 | tf_op jit(solution)/shard_map/ppermute | solution.py:848
  61.9 5.6 %collective-permute-done.15.got_ref = bf16[2,256,256]{2,1,0:T(8,128)(2,1)S(1)} collective-permute-done((bf16[2,256,256]{2,1,0:T(8,128)(2,1)S(1)}, bf16[2,256,256]{2,1,0:T(8,128)(2,1)S(1)}, u32[]{:S(2)}, u32[]{:S(2)}) %collective-permute-start.15) | collective-permute-done | bytes 262176 | tf_op jit(solution)/shard_map/ppermute | solution.py:848
  67.6 1.6 %collective-permute-start.16 = (bf16[1,256,256]{2,1,0:T(8,128)(2,1)S(1)}, bf16[1,256,256]{2,1,0:T(8,128)(2,1)S(1)}, u32[]{:S(2)}, u32[]{:S(2)}) collective-permute-start(bf16[1,256,256]{2,1,0:T(8,128)(2,1)S(1)} %get-tuple-element.145), channel_id=1, source_target_pairs={{0,2},{1,3},{2,0},{3,1},{4,6},{5,7},{6,4},{7,5},{8,10},{9,11},{10,... | collective-permute-start | bytes 393224 | tf_op jit(solution)/shard_map/ppermute | solution.py:848
  69.1 1.9 %collective-permute-start.19 = (bf16[256,256]{1,0:T(8,128)(2,1)S(1)}, bf16[256,256]{1,0:T(8,128)(2,1)S(1)}, u32[]{:S(2)}, u32[]{:S(2)}) collective-permute-start(bf16[256,256]{1,0:T(8,128)(2,1)S(1)} %get-tuple-element.149), channel_id=1, source_target_pairs={{0,1},{1,0},{2,3},{3,2},{4,5},{5,4},{6,7},{7,6},{8,9},{9,8},{10,11... | collective-permute-start | bytes 393224 | tf_op jit(solution)/shard_map/ppermute | solution.py:848
  71.1 0.8 head_sum.2
  71.8 2.3 %collective-permute-done.18.refs_4_ = bf16[256,256]{1,0:T(8,128)(2,1)S(1)} collective-permute-done((bf16[256,256]{1,0:T(8,128)(2,1)S(1)}, bf16[256,256]{1,0:T(8,128)(2,1)S(1)}, u32[]{:S(2)}, u32[]{:S(2)}) %collective-permute-start.18) | collective-permute-done | bytes 131104 | tf_op jit(solution)/shard_map/ppermute | solution.py:848
  74.1 4.3 %collective-permute-done.16.refs_1_ = bf16[1,256,256]{2,1,0:T(8,128)(2,1)S(1)} collective-permute-done((bf16[1,256,256]{2,1,0:T(8,128)(2,1)S(1)}, bf16[1,256,256]{2,1,0:T(8,128)(2,1)S(1)}, u32[]{:S(2)}, u32[]{:S(2)}) %collective-permute-start.16) | collective-permute-done | bytes 131104 | tf_op jit(solution)/shard_map/ppermute | solution.py:848
  78.4 0.8 %head_sum.3 = bf16[256,512]{1,0:T(8,128)(2,1)} custom-call(f32[1,256,256]{2,1,0:T(8,128)S(1)} %get-tuple-element.142.refs_0_, bf16[1,256,256]{2,1,0:T(8,128)(2,1)S(1)} %collective-permute-done.16.refs_1_, bf16[256,256]{1,0:T(8,128)(2,1)S(1)} %get-tuple-element.146.refs_2_, bf16[256,256]{1,0:T(8,128)(2,1)S(1)} %collective-permute-done.17.refs_3_, ...), custom_call_target="tpu_custom_call" | custom-call | tf_op jit(solution)/shard_map/head_sum/pallas_call | solution.py:103
  (35 shorter events, 2.5 us)
Async XLA Ops:
  0.7 18.5 %copy-start = (bf16[4,128,2048]{2,1,0:T(8,128)(2,1)S(1)}, bf16[4,128,2048]{2,1,0:T(8,128)(2,1)}, u32[]{:S(2)}) copy-start(bf16[4,128,2048]{2,1,0:T(8,128)(2,1)} %param.12) | copy-start | bytes 6291460
  0.7 18.5 %copy-start.1 = (bf16[256,2048]{1,0:T(8,128)(2,1)S(1)}, bf16[256,2048]{1,0:T(8,128)(2,1)}, u32[]{:S(2)}) copy-start(bf16[256,2048]{1,0:T(8,128)(2,1)} %tokens_ref.1) | copy-start | bytes 3145732
  0.7 18.5 %copy-start.2 = (bf16[256,2048]{1,0:T(8,128)(2,1)S(1)}, bf16[256,2048]{1,0:T(8,128)(2,1)}, u32[]{:S(2)}) copy-start(bf16[256,2048]{1,0:T(8,128)(2,1)} %grad_ref.1) | copy-start | bytes 3145732
  12.3 1.7 %collective-permute-start = (bf16[4,128,256]{2,1,0:T(8,128)(2,1)S(1)}, bf16[4,128,256]{2,1,0:T(8,128)(2,1)S(1)}, u32[]{:S(2)}, u32[]{:S(2)}) collective-permute-start(bf16[4,128,256]{2,1,0:T(8,128)(2,1)S(1)} %get-tuple-element.86.own_ref), channel_id=1, source_target_pairs={{0,4},{4,0},{8,12},{12,8},{16,20},{20,16},{24,28},{28,24},{1,5},{5... | collective-permute-start | bytes 786440 | tf_op jit(solution)/shard_map/ppermute | solution.py:848
  14.7 9.3 %collective-permute-start.3 = (bf16[2,128,256]{2,1,0:T(8,128)(2,1)S(1)}, bf16[2,128,256]{2,1,0:T(8,128)(2,1)S(1)}, u32[]{:S(2)}, u32[]{:S(2)}) collective-permute-start(bf16[2,128,256]{2,1,0:T(8,128)(2,1)S(1)} %join_half.1), channel_id=1, source_target_pairs={{0,24},{4,28},{8,16},{12,20},{16,8},{20,12},{24,0},{28,4},{1,25},{... | collective-permute-start | bytes 393224 | tf_op jit(solution)/shard_map/ppermute | solution.py:848
  18.6 6.6 %collective-permute-start.2 = (bf16[2,128,256]{2,1,0:T(8,128)(2,1)S(1)}, bf16[2,128,256]{2,1,0:T(8,128)(2,1)S(1)}, u32[]{:S(2)}, u32[]{:S(2)}) collective-permute-start(bf16[2,128,256]{2,1,0:T(8,128)(2,1)S(1)} %join_half.1), channel_id=1, source_target_pairs={{0,16},{4,20},{8,24},{12,28},{16,0},{20,4},{24,8},{28,12},{1,17},{... | collective-permute-start | bytes 393224 | tf_op jit(solution)/shard_map/ppermute | solution.py:848
  19.1 6.4 %collective-permute-start.1 = (bf16[2,128,256]{2,1,0:T(8,128)(2,1)S(1)}, bf16[2,128,256]{2,1,0:T(8,128)(2,1)S(1)}, u32[]{:S(2)}, u32[]{:S(2)}) collective-permute-start(bf16[2,128,256]{2,1,0:T(8,128)(2,1)S(1)} %join_half.1), channel_id=1, source_target_pairs={{0,8},{4,12},{8,0},{12,4},{16,24},{20,28},{24,16},{28,20},{1,9},{5... | collective-permute-start | bytes 393224 | tf_op jit(solution)/shard_map/ppermute | solution.py:848
  19.2 8.1 %copy-start.3 = (f32[128]{0:T(128)S(1)}, f32[128]{0:T(128)}, u32[]{:S(2)}) copy-start(f32[128]{0:T(128)} %param.11) | copy-start | bytes 1540
  25.5 1.3 %collective-permute-start.4 = (bf16[2,128,256]{2,1,0:T(8,128)(2,1)S(1)}, bf16[2,128,256]{2,1,0:T(8,128)(2,1)S(1)}, u32[]{:S(2)}, u32[]{:S(2)}) collective-permute-start(bf16[2,128,256]{2,1,0:T(8,128)(2,1)S(1)} %collective-permute-done.1.refs_1_), channel_id=1, source_target_pairs={{0,4},{4,0},{8,12},{12,8},{16,20},{20,16},{24,28},{28,24},{1,5},{5... | collective-permute-start | bytes 393224 | tf_op jit(solution)/shard_map/ppermute | solution.py:848
  25.5 1.5 %collective-permute-start.5 = (bf16[2,128,256]{2,1,0:T(8,128)(2,1)S(1)}, bf16[2,128,256]{2,1,0:T(8,128)(2,1)S(1)}, u32[]{:S(2)}, u32[]{:S(2)}) collective-permute-start(bf16[2,128,256]{2,1,0:T(8,128)(2,1)S(1)} %collective-permute-done.2.refs_2_), channel_id=1, source_target_pairs={{0,4},{4,0},{8,12},{12,8},{16,20},{20,16},{24,28},{28,24},{1,5},{5... | collective-permute-start | bytes 393224 | tf_op jit(solution)/shard_map/ppermute | solution.py:848
  26.0 1.3 %collective-permute-start.6 = (bf16[2,128,256]{2,1,0:T(8,128)(2,1)S(1)}, bf16[2,128,256]{2,1,0:T(8,128)(2,1)S(1)}, u32[]{:S(2)}, u32[]{:S(2)}) collective-permute-start(bf16[2,128,256]{2,1,0:T(8,128)(2,1)S(1)} %collective-permute-done.3.refs_3_), channel_id=1, source_target_pairs={{0,4},{4,0},{8,12},{12,8},{16,20},{20,16},{24,28},{28,24},{1,5},{5... | collective-permute-start | bytes 393224 | tf_op jit(solution)/shard_map/ppermute | solution.py:848
  30.1 14.1 %collective-permute-start.7 = (bf16[2,256,512]{2,1,0:T(8,128)(2,1)S(1)}, bf16[2,256,512]{2,1,0:T(8,128)(2,1)S(1)}, u32[]{:S(2)}, u32[]{:S(2)}) collective-permute-start(bf16[2,256,512]{2,1,0:T(8,128)(2,1)S(1)} %get-tuple-element.95), channel_id=1, source_target_pairs={{0,1},{1,0},{2,3},{3,2},{4,5},{5,4},{6,7},{7,6},{8,9},{9,8},{10,11... | collective-permute-start | bytes 1572872 | tf_op jit(solution)/shard_map/ppermute | solution.py:848
  35.1 1.8 %collective-permute-start.9 = (bf16[4,128,256]{2,1,0:T(8,128)(2,1)S(1)}, bf16[4,128,256]{2,1,0:T(8,128)(2,1)S(1)}, u32[]{:S(2)}, u32[]{:S(2)}) collective-permute-start(bf16[4,128,256]{2,1,0:T(8,128)(2,1)S(1)} %get-tuple-element.126.refs_0_), channel_id=1, source_target_pairs={{0,4},{4,0},{8,12},{12,8},{16,20},{20,16},{24,28},{28,24},{1,5},{5... | collective-permute-start | bytes 786440 | tf_op jit(solution)/shard_map/ppermute | solution.py:848
  35.2 1.7 %collective-permute-start.10 = (bf16[4,128,128]{2,1,0:T(8,128)(2,1)S(1)}, bf16[4,128,128]{2,1,0:T(8,128)(2,1)S(1)}, u32[]{:S(2)}, u32[]{:S(2)}) collective-permute-start(bf16[4,128,128]{2,1,0:T(8,128)(2,1)S(1)} %get-tuple-element.127.refs_1_), channel_id=1, source_target_pairs={{0,4},{4,0},{8,12},{12,8},{16,20},{20,16},{24,28},{28,24},{1,5},{5... | collective-permute-start | bytes 393224 | tf_op jit(solution)/shard_map/ppermute | solution.py:848
  35.7 11.2 %collective-permute-start.8 = (bf16[4,128,256]{2,1,0:T(8,128)(2,1)S(1)}, bf16[4,128,256]{2,1,0:T(8,128)(2,1)S(1)}, u32[]{:S(2)}, u32[]{:S(2)}) collective-permute-start(bf16[4,128,256]{2,1,0:T(8,128)(2,1)S(1)} %get-tuple-element.125), channel_id=1, source_target_pairs={{0,4},{4,0},{8,12},{12,8},{16,20},{20,16},{24,28},{28,24},{1,5},{5... | collective-permute-start | bytes 786440 | tf_op jit(solution)/shard_map/ppermute | solution.py:848
  37.0 12.1 %collective-permute-start.11 = (bf16[4,128,256]{2,1,0:T(8,128)(2,1)S(1)}, bf16[4,128,256]{2,1,0:T(8,128)(2,1)S(1)}, u32[]{:S(2)}, u32[]{:S(2)}) collective-permute-start(bf16[4,128,256]{2,1,0:T(8,128)(2,1)S(1)} %get-tuple-element.128), channel_id=1, source_target_pairs={{0,8},{4,12},{8,0},{12,4},{16,24},{20,28},{24,16},{28,20},{1,9},{5... | collective-permute-start | bytes 786440 | tf_op jit(solution)/shard_map/ppermute | solution.py:848
  38.6 10.5 %collective-permute-start.13 = (bf16[4,128,128]{2,1,0:T(8,128)(2,1)S(1)}, bf16[4,128,128]{2,1,0:T(8,128)(2,1)S(1)}, u32[]{:S(2)}, u32[]{:S(2)}) collective-permute-start(bf16[4,128,128]{2,1,0:T(8,128)(2,1)S(1)} %get-tuple-element.129), channel_id=1, source_target_pairs={{0,24},{4,28},{8,16},{12,20},{16,8},{20,12},{24,0},{28,4},{1,25},{... | collective-permute-start | bytes 393224 | tf_op jit(solution)/shard_map/ppermute | solution.py:848
  40.0 9.1 %collective-permute-start.12 = (bf16[4,128,128]{2,1,0:T(8,128)(2,1)S(1)}, bf16[4,128,128]{2,1,0:T(8,128)(2,1)S(1)}, u32[]{:S(2)}, u32[]{:S(2)}) collective-permute-start(bf16[4,128,128]{2,1,0:T(8,128)(2,1)S(1)} %get-tuple-element.129), channel_id=1, source_target_pairs={{0,16},{4,20},{8,24},{12,28},{16,0},{20,4},{24,8},{28,12},{1,17},{... | collective-permute-start | bytes 393224 | tf_op jit(solution)/shard_map/ppermute | solution.py:848
  40.5 14.0 %slice-start = ((s8[6291456]{0:T(1024)(128)(4,1)}), s8[2097152]{0:T(1024)(128)(4,1)S(1)}, s32[]{:S(2)}) async-start(s8[6291456]{0:T(1024)(128)(4,1)} %bitcast.7), calls=%async_computation | async-start | bytes 4194304
  44.1 10.4 %slice-start.1 = ((s8[6291456]{0:T(1024)(128)(4,1)}), s8[4194304]{0:T(1024)(128)(4,1)S(1)}, s32[]{:S(2)}) async-start(s8[6291456]{0:T(1024)(128)(4,1)} %bitcast.7), calls=%async_computation.1 | async-start | bytes 8388608
  44.3 14.2 %collective-permute-start.14 = (bf16[1,256,512]{2,1,0:T(8,128)(2,1)S(1)}, bf16[1,256,512]{2,1,0:T(8,128)(2,1)S(1)}, u32[]{:S(2)}, u32[]{:S(2)}) collective-permute-start(bf16[1,256,512]{2,1,0:T(8,128)(2,1)S(1)} %get-tuple-element.138), channel_id=1, source_target_pairs={{0,2},{1,3},{2,0},{3,1},{4,6},{5,7},{6,4},{7,5},{8,10},{9,11},{10,... | collective-permute-start | bytes 786440 | tf_op jit(solution)/shard_map/ppermute | solution.py:848
  57.1 10.4 %collective-permute-start.15 = (bf16[2,256,256]{2,1,0:T(8,128)(2,1)S(1)}, bf16[2,256,256]{2,1,0:T(8,128)(2,1)S(1)}, u32[]{:S(2)}, u32[]{:S(2)}) collective-permute-start(bf16[2,256,256]{2,1,0:T(8,128)(2,1)S(1)} %get-tuple-element.141), channel_id=1, source_target_pairs={{0,1},{1,0},{2,3},{3,2},{4,5},{5,4},{6,7},{7,6},{8,9},{9,8},{10,11... | collective-permute-start | bytes 786440 | tf_op jit(solution)/shard_map/ppermute | solution.py:848
  58.4 13.4 %collective-permute-start.17 = (bf16[256,256]{1,0:T(8,128)(2,1)S(1)}, bf16[256,256]{1,0:T(8,128)(2,1)S(1)}, u32[]{:S(2)}, u32[]{:S(2)}) collective-permute-start(bf16[256,256]{1,0:T(8,128)(2,1)S(1)} %get-tuple-element.147), channel_id=1, source_target_pairs={{0,2},{1,3},{2,0},{3,1},{4,6},{5,7},{6,4},{7,5},{8,10},{9,11},{10,... | collective-permute-start | bytes 393224 | tf_op jit(solution)/shard_map/ppermute | solution.py:848
  60.2 13.9 %collective-permute-start.18 = (bf16[256,256]{1,0:T(8,128)(2,1)S(1)}, bf16[256,256]{1,0:T(8,128)(2,1)S(1)}, u32[]{:S(2)}, u32[]{:S(2)}) collective-permute-start(bf16[256,256]{1,0:T(8,128)(2,1)S(1)} %get-tuple-element.148), channel_id=1, source_target_pairs={{0,3},{1,2},{2,1},{3,0},{4,7},{5,6},{6,5},{7,4},{8,11},{9,10},{10,... | collective-permute-start | bytes 393224 | tf_op jit(solution)/shard_map/ppermute | solution.py:848
  67.6 10.8 %collective-permute-start.16 = (bf16[1,256,256]{2,1,0:T(8,128)(2,1)S(1)}, bf16[1,256,256]{2,1,0:T(8,128)(2,1)S(1)}, u32[]{:S(2)}, u32[]{:S(2)}) collective-permute-start(bf16[1,256,256]{2,1,0:T(8,128)(2,1)S(1)} %get-tuple-element.145), channel_id=1, source_target_pairs={{0,2},{1,3},{2,0},{3,1},{4,6},{5,7},{6,4},{7,5},{8,10},{9,11},{10,... | collective-permute-start | bytes 393224 | tf_op jit(solution)/shard_map/ppermute | solution.py:848
  69.1 9.2 %collective-permute-start.19 = (bf16[256,256]{1,0:T(8,128)(2,1)S(1)}, bf16[256,256]{1,0:T(8,128)(2,1)S(1)}, u32[]{:S(2)}, u32[]{:S(2)}) collective-permute-start(bf16[256,256]{1,0:T(8,128)(2,1)S(1)} %get-tuple-element.149), channel_id=1, source_target_pairs={{0,1},{1,0},{2,3},{3,2},{4,5},{5,4},{6,7},{7,6},{8,9},{9,8},{10,11... | collective-permute-start | bytes 393224 | tf_op jit(solution)/shard_map/ppermute | solution.py:848

commit v14 on v13

--- a/solution.py
+++ b/solution.py
@@ -179,11 +179,12 @@
         block = wr_hbm.at[span, pl.ds(heads * LANES, heads * LANES)]
         keeps.append(pltpu.make_async_copy(key_ref.at[span, :], block, out_sems.at[chunk]))
     fetches[0].start()
+    fetches[1].start(priority=1)
     fetch_tokens.start()
-    fetch_small.start()
-    fetch_rates.start()
-    for fetch in fetches[1:]:
-        fetch.start()
+    fetch_small.start(priority=1)
+    fetch_rates.start(priority=1)
+    for chunk in range(2, chunks):
+        fetches[chunk].start(priority=chunk % 2)
 
     def relay(chunk):
         fetches[chunk].wait()
@@ -209,11 +210,12 @@
                 acc[:, span] += own
 
     def lay(first, last):
-        for chunk in range(first, last):
+        for chunk in range(first, last, 2):
             relay(chunk)
+            relay(chunk + 1)
             if chunk == 0:
                 fetch_tokens.wait()
-            multiply(chunk, chunk + 1)
+            multiply(chunk, chunk + 2)
 
     decay_col = levels * heads
     beta_col = decay_col + heads
@@ -225,8 +227,8 @@
     apart = row_id ^ col_id
     eye = (row_id == col_id).astype(F32)
     lay(0, chunks)
-    for keep in keeps:
-        keep.start()
+    for chunk, keep in enumerate(keeps):
+        keep.start(priority=chunk % 2)
     fetch_small.wait()
     small_rows = small_in.shape[0] * heads
     for level in range(small_in.shape[0]):
@@ -295,7 +297,7 @@
 
 def project(place, tokens, flat_w, small, head_param, heads, levels):
     rows, width = tokens.shape
-    chunks = 8
+    chunks = 16
     cols = 3 * heads
     key = flat_w.shape[1]
     square = (heads, rows, rows)

time: 79.3 us -> 79 us (level)
  no operation moved by 1% of the time
where the time goes in v14:
time: 79 us; the launch traced here: 78.9 us
  Pallas kernels  36.2 us (46%)
  starting transfers between devices  21.7 us (27%)
  waiting for transfers between devices  20.1 us (25%)
    pallas_call x13, Pallas kernels, local_call(): pl.pallas_call(body, out_shape=tuple(out_shape), in_specs=[SCALARS] * len...  36.2 us
    ppermute x20, starting transfers between devices, swap(): return lax.ppermute(value, axis, [(at, at ^ mask) for at in range(size)])  21.7 us
    ppermute x20, waiting for transfers between devices, swap(): return lax.ppermute(value, axis, [(at, at ^ mask) for at in range(size)])  20.1 us
  transfers between devices with their start and end apart: 20, of which 13 were waited for; matrix products, arithmetic and copies ran while one was open for 0% of the time, Pallas kernels for 26%

profile of v14, /device:TPU:0, one launch (start us, length us, event | category | flops | bytes accessed | tf_op | source)
XLA Modules:
  0.0 78.9 jit_solution(8442792418168663827)
XLA Ops:
  0.7 11.3 %project.1 = (bf16[2048,1536]{1,0:T(8,128)(2,1)}, bf16[2048,512]{1,0:T(8,128)(2,1)S(1)}, bf16[2048,512]{1,0:T(8,128)(2,1)S(1)}, bf16[128,2048]{1,0:T(8,128)(2,1)...) custom-call(s32[2]{0:T(128)S(1)} %pad_add_fusion.place_ref, ...), custom_call_target="tpu_custom_call" | custom-call | tf_op jit(solution)/shard_map/project/pallas_call | solution.py:103
  12.0 0.5 collective-permute-start
  12.6 1.2 %collective-permute-done.other_ref.refs_0_.refs_14_ = bf16[4,128,256]{2,1,0:T(8,128)(2,1)S(1)} collective-permute-done((bf16[4,128,256]{2,1,0:T(8,128)(2,1)S(1)}, bf16[4,128,256]{2,1,0:T(8,128)(2,1)S(1)}, u32[]{:S(2)}, u32[]{:S(2)}) %collective-permute-start) | collective-permute-done | bytes 262176 | tf_op jit(solution)/shard_map/ppermute | solution.py:850
  13.7 0.7 join_half.1
  14.4 3.9 %collective-permute-start.3 = (bf16[2,128,256]{2,1,0:T(8,128)(2,1)S(1)}, bf16[2,128,256]{2,1,0:T(8,128)(2,1)S(1)}, u32[]{:S(2)}, u32[]{:S(2)}) collective-permute-start(bf16[2,128,256]{2,1,0:T(8,128)(2,1)S(1)} %join_half.1), channel_id=1, source_target_pairs={{0,24},{4,28},{8,16},{12,20},{16,8},{20,12},{24,0},{28,4},{1,25},{... | collective-permute-start | bytes 393224 | tf_op jit(solution)/shard_map/ppermute | solution.py:850
  18.3 0.5 collective-permute-start.2
  19.0 4.8 %local_part.1 = (bf16[4,256,256]{2,1,0:T(8,128)(2,1)S(1)}, bf16[4,256,256]{2,1,0:T(8,128)(2,1)S(1)}, bf16[4,256,256]{2,1,0:T(8,128)(2,1)S(1)}, bf16[4,256,256]{2...) custom-call(f32[3,4,256,128]{3,2,1,0:T(8,128)S(1)} %get-tuple-elemen, ...), custom_call_target="tpu_custom_call", output_to_operand_aliasing={{10}: (0, {}), {11}: (1, {}), {12}: (11, {})} | custom-call | tf_op jit(solution)/shard_map/local_part/pallas_call | solution.py:103
  23.8 1.2 %collective-permute-done.2.refs_2_ = bf16[2,128,256]{2,1,0:T(8,128)(2,1)S(1)} collective-permute-done((bf16[2,128,256]{2,1,0:T(8,128)(2,1)S(1)}, bf16[2,128,256]{2,1,0:T(8,128)(2,1)S(1)}, u32[]{:S(2)}, u32[]{:S(2)}) %collective-permute-start.2) | collective-permute-done | bytes 131104 | tf_op jit(solution)/shard_map/ppermute | solution.py:850
  25.7 0.8 %collective-permute-done.4.refs_4_ = bf16[2,128,256]{2,1,0:T(8,128)(2,1)S(1)} collective-permute-done((bf16[2,128,256]{2,1,0:T(8,128)(2,1)S(1)}, bf16[2,128,256]{2,1,0:T(8,128)(2,1)S(1)}, u32[]{:S(2)}, u32[]{:S(2)}) %collective-permute-start.4) | collective-permute-done | bytes 131104 | tf_op jit(solution)/shard_map/ppermute | solution.py:850
  27.1 2.7 %reach.1 = (bf16[2,256,512]{2,1,0:T(8,128)(2,1)S(1)}, bf16[2,256,512]{2,1,0:T(8,128)(2,1)S(1)}, f32[4,256,128]{2,1,0:T(8,128)S(1)}, f32[256,128]{1,0:T(8,128)S(1...) custom-call(s32[2]{0:T(128)S(1)} %pad_add_fusion.place_ref, ...), custom_call_target="tpu_custom_call" | custom-call | tf_op jit(solution)/shard_map/reach/pallas_call | solution.py:103
  29.8 1.6 %collective-permute-start.7 = (bf16[2,256,512]{2,1,0:T(8,128)(2,1)S(1)}, bf16[2,256,512]{2,1,0:T(8,128)(2,1)S(1)}, u32[]{:S(2)}, u32[]{:S(2)}) collective-permute-start(bf16[2,256,512]{2,1,0:T(8,128)(2,1)S(1)} %get-tuple-element.95), channel_id=1, source_target_pairs={{0,1},{1,0},{2,3},{3,2},{4,5},{5,4},{6,7},{7,6},{8,9},{9,8},{10,11... | collective-permute-start | bytes 1572872 | tf_op jit(solution)/shard_map/ppermute | solution.py:850
  31.4 3.4 %return_states.1 = (f32[4,256,128]{2,1,0:T(8,128)S(1)}, f32[4,256,128]{2,1,0:T(8,128)S(1)}, f32[256,128]{1,0:T(8,128)S(1)}, bf16[4,128,256]{2,1,0:T(8,128)(2,1)S...) custom-call(s32[2]{0:T(128)S(1)} %pad_add_fusion.place_ref, f32[1,128]{1,0:T(1,128)S(1)} %bitcast.12, ...), custom_call_target="tpu_custom_call" | custom-call | tf_op jit(solution)/shard_map/return_states/pallas_call | solution.py:103
  35.5 1.1 %collective-permute-done.10.refs_3_ = bf16[4,128,128]{2,1,0:T(8,128)(2,1)S(1)} collective-permute-done((bf16[4,128,128]{2,1,0:T(8,128)(2,1)S(1)}, bf16[4,128,128]{2,1,0:T(8,128)(2,1)S(1)}, u32[]{:S(2)}, u32[]{:S(2)}) %collective-permute-start.10) | collective-permute-done | bytes 131104 | tf_op jit(solution)/shard_map/ppermute | solution.py:850
  36.7 1.6 %collective-permute-start.11 = (bf16[4,128,256]{2,1,0:T(8,128)(2,1)S(1)}, bf16[4,128,256]{2,1,0:T(8,128)(2,1)S(1)}, u32[]{:S(2)}, u32[]{:S(2)}) collective-permute-start(bf16[4,128,256]{2,1,0:T(8,128)(2,1)S(1)} %get-tuple-element.128), channel_id=1, source_target_pairs={{0,8},{4,12},{8,0},{12,4},{16,24},{20,28},{24,16},{28,20},{1,9},{5... | collective-permute-start | bytes 786440 | tf_op jit(solution)/shard_map/ppermute | solution.py:850
  38.3 1.4 %collective-permute-start.13 = (bf16[4,128,128]{2,1,0:T(8,128)(2,1)S(1)}, bf16[4,128,128]{2,1,0:T(8,128)(2,1)S(1)}, u32[]{:S(2)}, u32[]{:S(2)}) collective-permute-start(bf16[4,128,128]{2,1,0:T(8,128)(2,1)S(1)} %get-tuple-element.129), channel_id=1, source_target_pairs={{0,24},{4,28},{8,16},{12,20},{16,8},{20,12},{24,0},{28,4},{1,25},{... | collective-permute-start | bytes 393224 | tf_op jit(solution)/shard_map/ppermute | solution.py:850
  39.7 0.6 collective-permute-start.12
  40.3 3.5 %pull_local.1 = (f32[3,4,256,128]{3,2,1,0:T(8,128)S(1)}, f32[4,256,128]{2,1,0:T(8,128)S(1)}, f32[256,128]{1,0:T(8,128)S(1)}, f32[8,256]{1,0:T(8,128)S(1)}) custom-call(f32[3,4,256,128]{3,2,1,0:T(8,128)S(1)} %get-tuple-element.97.refs_0_, f32[256,128]{1,0:T(8,128)S(1)} %get-tuple-element.85.pack_ref.refs_1_.refs_2_, ...), custom_call_target="tpu_custom_call" | custom-call | tf_op jit(solution)/shard_map/pull_local/pallas_call | solution.py:103
  44.0 2.7 %collective-permute-start.14 = (bf16[1,256,512]{2,1,0:T(8,128)(2,1)S(1)}, bf16[1,256,512]{2,1,0:T(8,128)(2,1)S(1)}, u32[]{:S(2)}, u32[]{:S(2)}) collective-permute-start(bf16[1,256,512]{2,1,0:T(8,128)(2,1)S(1)} %get-tuple-element.138), channel_id=1, source_target_pairs={{0,2},{1,3},{2,0},{3,1},{4,6},{5,7},{6,4},{7,5},{8,10},{9,11},{10,... | collective-permute-start | bytes 786440 | tf_op jit(solution)/shard_map/ppermute | solution.py:850
  46.7 2.1 %collective-permute-done.13.refs_20_ = bf16[4,128,128]{2,1,0:T(8,128)(2,1)S(1)} collective-permute-done((bf16[4,128,128]{2,1,0:T(8,128)(2,1)S(1)}, bf16[4,128,128]{2,1,0:T(8,128)(2,1)S(1)}, u32[]{:S(2)}, u32[]{:S(2)}) %collective-permute-start.13) | collective-permute-done | bytes 131104 | tf_op jit(solution)/shard_map/ppermute | solution.py:850
  48.8 5.4 %finish.1 = (bf16[256,1536]{1,0:T(8,128)(2,1)S(1)}, bf16[256,128]{1,0:T(8,128)(2,1)S(1)}) custom-call(s32[2]{0:T(128)S(1)} %pad_add_fusion.place_ref, f32[3,4,256,128]{3,2,1,0:T(8,128)S(1)} %get-tuple-element.97.refs_0_, f32[256,128]{1,0:T(8,128)S(1)} %get-tuple-element.98.refs_1_, f32[256,128]{1,0:T(8,128)S(1)} %get-tuple-element.85.pack_ref.refs_1_.refs_2_, ...), custom_call_target="tpu_custom_call" | custom-call | tf_op jit(solution)/shard_map/finish/pallas_call | solution.py:103
  54.2 2.6 %pull_tokens.1 = (bf16[2,256,256]{2,1,0:T(8,128)(2,1)S(1)}, bf16[2,256,256]{2,1,0:T(8,128)(2,1)S(1)}, bf16[256,256]{1,0:T(8,128)(2,1)S(1)}, bf16[256,256]{1,0:T(...) custom-call(s32[2]{0:T(128)S(1)} %pad_add_fusion.place_ref, ...), custom_call_target="tpu_custom_call" | custom-call | tf_op jit(solution)/shard_map/pull_tokens/pallas_call | solution.py:103
  56.8 0.5 collective-permute-start.15
  57.4 0.8 collective-permute-done.14.refs_1_
  58.1 1.8 %collective-permute-start.17 = (bf16[256,256]{1,0:T(8,128)(2,1)S(1)}, bf16[256,256]{1,0:T(8,128)(2,1)S(1)}, u32[]{:S(2)}, u32[]{:S(2)}) collective-permute-start(bf16[256,256]{1,0:T(8,128)(2,1)S(1)} %get-tuple-element.147), channel_id=1, source_target_pairs={{0,2},{1,3},{2,0},{3,1},{4,6},{5,7},{6,4},{7,5},{8,10},{9,11},{10,... | collective-permute-start | bytes 393224 | tf_op jit(solution)/shard_map/ppermute | solution.py:850
  60.0 1.7 %collective-permute-start.18 = (bf16[256,256]{1,0:T(8,128)(2,1)S(1)}, bf16[256,256]{1,0:T(8,128)(2,1)S(1)}, u32[]{:S(2)}, u32[]{:S(2)}) collective-permute-start(bf16[256,256]{1,0:T(8,128)(2,1)S(1)} %get-tuple-element.148), channel_id=1, source_target_pairs={{0,3},{1,2},{2,1},{3,0},{4,7},{5,6},{6,5},{7,4},{8,11},{9,10},{10,... | collective-permute-start | bytes 393224 | tf_op jit(solution)/shard_map/ppermute | solution.py:850
  61.7 5.5 %collective-permute-done.15.got_ref = bf16[2,256,256]{2,1,0:T(8,128)(2,1)S(1)} collective-permute-done((bf16[2,256,256]{2,1,0:T(8,128)(2,1)S(1)}, bf16[2,256,256]{2,1,0:T(8,128)(2,1)S(1)}, u32[]{:S(2)}, u32[]{:S(2)}) %collective-permute-start.15) | collective-permute-done | bytes 262176 | tf_op jit(solution)/shard_map/ppermute | solution.py:850
  67.3 1.6 %collective-permute-start.16 = (bf16[1,256,256]{2,1,0:T(8,128)(2,1)S(1)}, bf16[1,256,256]{2,1,0:T(8,128)(2,1)S(1)}, u32[]{:S(2)}, u32[]{:S(2)}) collective-permute-start(bf16[1,256,256]{2,1,0:T(8,128)(2,1)S(1)} %get-tuple-element.145), channel_id=1, source_target_pairs={{0,2},{1,3},{2,0},{3,1},{4,6},{5,7},{6,4},{7,5},{8,10},{9,11},{10,... | collective-permute-start | bytes 393224 | tf_op jit(solution)/shard_map/ppermute | solution.py:850
  68.9 1.9 %collective-permute-start.19 = (bf16[256,256]{1,0:T(8,128)(2,1)S(1)}, bf16[256,256]{1,0:T(8,128)(2,1)S(1)}, u32[]{:S(2)}, u32[]{:S(2)}) collective-permute-start(bf16[256,256]{1,0:T(8,128)(2,1)S(1)} %get-tuple-element.149), channel_id=1, source_target_pairs={{0,1},{1,0},{2,3},{3,2},{4,5},{5,4},{6,7},{7,6},{8,9},{9,8},{10,11... | collective-permute-start | bytes 393224 | tf_op jit(solution)/shard_map/ppermute | solution.py:850
  70.8 0.8 head_sum.2
  71.6 2.3 %collective-permute-done.18.refs_4_ = bf16[256,256]{1,0:T(8,128)(2,1)S(1)} collective-permute-done((bf16[256,256]{1,0:T(8,128)(2,1)S(1)}, bf16[256,256]{1,0:T(8,128)(2,1)S(1)}, u32[]{:S(2)}, u32[]{:S(2)}) %collective-permute-start.18) | collective-permute-done | bytes 131104 | tf_op jit(solution)/shard_map/ppermute | solution.py:850
  73.8 4.2 %collective-permute-done.16.refs_1_ = bf16[1,256,256]{2,1,0:T(8,128)(2,1)S(1)} collective-permute-done((bf16[1,256,256]{2,1,0:T(8,128)(2,1)S(1)}, bf16[1,256,256]{2,1,0:T(8,128)(2,1)S(1)}, u32[]{:S(2)}, u32[]{:S(2)}) %collective-permute-start.16) | collective-permute-done | bytes 131104 | tf_op jit(solution)/shard_map/ppermute | solution.py:850
  78.1 0.8 %head_sum.3 = bf16[256,512]{1,0:T(8,128)(2,1)} custom-call(f32[1,256,256]{2,1,0:T(8,128)S(1)} %get-tuple-element.142.refs_0_, bf16[1,256,256]{2,1,0:T(8,128)(2,1)S(1)} %collective-permute-done.16.refs_1_, bf16[256,256]{1,0:T(8,128)(2,1)S(1)} %get-tuple-element.146.refs_2_, bf16[256,256]{1,0:T(8,128)(2,1)S(1)} %collective-permute-done.17.refs_3_, ...), custom_call_target="tpu_custom_call" | custom-call | tf_op jit(solution)/shard_map/head_sum/pallas_call | solution.py:103
  (35 shorter events, 2.5 us)
Async XLA Ops:
  0.7 18.3 %copy-start = (bf16[4,128,2048]{2,1,0:T(8,128)(2,1)S(1)}, bf16[4,128,2048]{2,1,0:T(8,128)(2,1)}, u32[]{:S(2)}) copy-start(bf16[4,128,2048]{2,1,0:T(8,128)(2,1)} %param.12) | copy-start | bytes 6291460
  0.7 18.3 %copy-start.1 = (bf16[256,2048]{1,0:T(8,128)(2,1)S(1)}, bf16[256,2048]{1,0:T(8,128)(2,1)}, u32[]{:S(2)}) copy-start(bf16[256,2048]{1,0:T(8,128)(2,1)} %tokens_ref.1) | copy-start | bytes 3145732
  0.7 18.3 %copy-start.2 = (bf16[256,2048]{1,0:T(8,128)(2,1)S(1)}, bf16[256,2048]{1,0:T(8,128)(2,1)}, u32[]{:S(2)}) copy-start(bf16[256,2048]{1,0:T(8,128)(2,1)} %grad_ref.1) | copy-start | bytes 3145732
  12.0 1.7 %collective-permute-start = (bf16[4,128,256]{2,1,0:T(8,128)(2,1)S(1)}, bf16[4,128,256]{2,1,0:T(8,128)(2,1)S(1)}, u32[]{:S(2)}, u32[]{:S(2)}) collective-permute-start(bf16[4,128,256]{2,1,0:T(8,128)(2,1)S(1)} %get-tuple-element.86.own_ref), channel_id=1, source_target_pairs={{0,4},{4,0},{8,12},{12,8},{16,20},{20,16},{24,28},{28,24},{1,5},{5... | collective-permute-start | bytes 786440 | tf_op jit(solution)/shard_map/ppermute | solution.py:850
  14.4 9.3 %collective-permute-start.3 = (bf16[2,128,256]{2,1,0:T(8,128)(2,1)S(1)}, bf16[2,128,256]{2,1,0:T(8,128)(2,1)S(1)}, u32[]{:S(2)}, u32[]{:S(2)}) collective-permute-start(bf16[2,128,256]{2,1,0:T(8,128)(2,1)S(1)} %join_half.1), channel_id=1, source_target_pairs={{0,24},{4,28},{8,16},{12,20},{16,8},{20,12},{24,0},{28,4},{1,25},{... | collective-permute-start | bytes 393224 | tf_op jit(solution)/shard_map/ppermute | solution.py:850
  18.3 6.6 %collective-permute-start.2 = (bf16[2,128,256]{2,1,0:T(8,128)(2,1)S(1)}, bf16[2,128,256]{2,1,0:T(8,128)(2,1)S(1)}, u32[]{:S(2)}, u32[]{:S(2)}) collective-permute-start(bf16[2,128,256]{2,1,0:T(8,128)(2,1)S(1)} %join_half.1), channel_id=1, source_target_pairs={{0,16},{4,20},{8,24},{12,28},{16,0},{20,4},{24,8},{28,12},{1,17},{... | collective-permute-start | bytes 393224 | tf_op jit(solution)/shard_map/ppermute | solution.py:850
  18.8 6.4 %collective-permute-start.1 = (bf16[2,128,256]{2,1,0:T(8,128)(2,1)S(1)}, bf16[2,128,256]{2,1,0:T(8,128)(2,1)S(1)}, u32[]{:S(2)}, u32[]{:S(2)}) collective-permute-start(bf16[2,128,256]{2,1,0:T(8,128)(2,1)S(1)} %join_half.1), channel_id=1, source_target_pairs={{0,8},{4,12},{8,0},{12,4},{16,24},{20,28},{24,16},{28,20},{1,9},{5... | collective-permute-start | bytes 393224 | tf_op jit(solution)/shard_map/ppermute | solution.py:850
  19.0 8.1 %copy-start.3 = (f32[128]{0:T(128)S(1)}, f32[128]{0:T(128)}, u32[]{:S(2)}) copy-start(f32[128]{0:T(128)} %param.11) | copy-start | bytes 1540
  25.2 1.3 %collective-permute-start.4 = (bf16[2,128,256]{2,1,0:T(8,128)(2,1)S(1)}, bf16[2,128,256]{2,1,0:T(8,128)(2,1)S(1)}, u32[]{:S(2)}, u32[]{:S(2)}) collective-permute-start(bf16[2,128,256]{2,1,0:T(8,128)(2,1)S(1)} %collective-permute-done.1.refs_1_), channel_id=1, source_target_pairs={{0,4},{4,0},{8,12},{12,8},{16,20},{20,16},{24,28},{28,24},{1,5},{5... | collective-permute-start | bytes 393224 | tf_op jit(solution)/shard_map/ppermute | solution.py:850
  25.2 1.5 %collective-permute-start.5 = (bf16[2,128,256]{2,1,0:T(8,128)(2,1)S(1)}, bf16[2,128,256]{2,1,0:T(8,128)(2,1)S(1)}, u32[]{:S(2)}, u32[]{:S(2)}) collective-permute-start(bf16[2,128,256]{2,1,0:T(8,128)(2,1)S(1)} %collective-permute-done.2.refs_2_), channel_id=1, source_target_pairs={{0,4},{4,0},{8,12},{12,8},{16,20},{20,16},{24,28},{28,24},{1,5},{5... | collective-permute-start | bytes 393224 | tf_op jit(solution)/shard_map/ppermute | solution.py:850
  25.7 1.3 %collective-permute-start.6 = (bf16[2,128,256]{2,1,0:T(8,128)(2,1)S(1)}, bf16[2,128,256]{2,1,0:T(8,128)(2,1)S(1)}, u32[]{:S(2)}, u32[]{:S(2)}) collective-permute-start(bf16[2,128,256]{2,1,0:T(8,128)(2,1)S(1)} %collective-permute-done.3.refs_3_), channel_id=1, source_target_pairs={{0,4},{4,0},{8,12},{12,8},{16,20},{20,16},{24,28},{28,24},{1,5},{5... | collective-permute-start | bytes 393224 | tf_op jit(solution)/shard_map/ppermute | solution.py:850
  29.8 14.1 %collective-permute-start.7 = (bf16[2,256,512]{2,1,0:T(8,128)(2,1)S(1)}, bf16[2,256,512]{2,1,0:T(8,128)(2,1)S(1)}, u32[]{:S(2)}, u32[]{:S(2)}) collective-permute-start(bf16[2,256,512]{2,1,0:T(8,128)(2,1)S(1)} %get-tuple-element.95), channel_id=1, source_target_pairs={{0,1},{1,0},{2,3},{3,2},{4,5},{5,4},{6,7},{7,6},{8,9},{9,8},{10,11... | collective-permute-start | bytes 1572872 | tf_op jit(solution)/shard_map/ppermute | solution.py:850
  34.8 1.8 %collective-permute-start.9 = (bf16[4,128,256]{2,1,0:T(8,128)(2,1)S(1)}, bf16[4,128,256]{2,1,0:T(8,128)(2,1)S(1)}, u32[]{:S(2)}, u32[]{:S(2)}) collective-permute-start(bf16[4,128,256]{2,1,0:T(8,128)(2,1)S(1)} %get-tuple-element.126.refs_0_), channel_id=1, source_target_pairs={{0,4},{4,0},{8,12},{12,8},{16,20},{20,16},{24,28},{28,24},{1,5},{5... | collective-permute-start | bytes 786440 | tf_op jit(solution)/shard_map/ppermute | solution.py:850
  34.9 1.7 %collective-permute-start.10 = (bf16[4,128,128]{2,1,0:T(8,128)(2,1)S(1)}, bf16[4,128,128]{2,1,0:T(8,128)(2,1)S(1)}, u32[]{:S(2)}, u32[]{:S(2)}) collective-permute-start(bf16[4,128,128]{2,1,0:T(8,128)(2,1)S(1)} %get-tuple-element.127.refs_1_), channel_id=1, source_target_pairs={{0,4},{4,0},{8,12},{12,8},{16,20},{20,16},{24,28},{28,24},{1,5},{5... | collective-permute-start | bytes 393224 | tf_op jit(solution)/shard_map/ppermute | solution.py:850
  35.4 11.3 %collective-permute-start.8 = (bf16[4,128,256]{2,1,0:T(8,128)(2,1)S(1)}, bf16[4,128,256]{2,1,0:T(8,128)(2,1)S(1)}, u32[]{:S(2)}, u32[]{:S(2)}) collective-permute-start(bf16[4,128,256]{2,1,0:T(8,128)(2,1)S(1)} %get-tuple-element.125), channel_id=1, source_target_pairs={{0,4},{4,0},{8,12},{12,8},{16,20},{20,16},{24,28},{28,24},{1,5},{5... | collective-permute-start | bytes 786440 | tf_op jit(solution)/shard_map/ppermute | solution.py:850
  36.7 12.1 %collective-permute-start.11 = (bf16[4,128,256]{2,1,0:T(8,128)(2,1)S(1)}, bf16[4,128,256]{2,1,0:T(8,128)(2,1)S(1)}, u32[]{:S(2)}, u32[]{:S(2)}) collective-permute-start(bf16[4,128,256]{2,1,0:T(8,128)(2,1)S(1)} %get-tuple-element.128), channel_id=1, source_target_pairs={{0,8},{4,12},{8,0},{12,4},{16,24},{20,28},{24,16},{28,20},{1,9},{5... | collective-permute-start | bytes 786440 | tf_op jit(solution)/shard_map/ppermute | solution.py:850
  38.3 10.5 %collective-permute-start.13 = (bf16[4,128,128]{2,1,0:T(8,128)(2,1)S(1)}, bf16[4,128,128]{2,1,0:T(8,128)(2,1)S(1)}, u32[]{:S(2)}, u32[]{:S(2)}) collective-permute-start(bf16[4,128,128]{2,1,0:T(8,128)(2,1)S(1)} %get-tuple-element.129), channel_id=1, source_target_pairs={{0,24},{4,28},{8,16},{12,20},{16,8},{20,12},{24,0},{28,4},{1,25},{... | collective-permute-start | bytes 393224 | tf_op jit(solution)/shard_map/ppermute | solution.py:850
  39.7 9.1 %collective-permute-start.12 = (bf16[4,128,128]{2,1,0:T(8,128)(2,1)S(1)}, bf16[4,128,128]{2,1,0:T(8,128)(2,1)S(1)}, u32[]{:S(2)}, u32[]{:S(2)}) collective-permute-start(bf16[4,128,128]{2,1,0:T(8,128)(2,1)S(1)} %get-tuple-element.129), channel_id=1, source_target_pairs={{0,16},{4,20},{8,24},{12,28},{16,0},{20,4},{24,8},{28,12},{1,17},{... | collective-permute-start | bytes 393224 | tf_op jit(solution)/shard_map/ppermute | solution.py:850
  40.3 14.0 %slice-start = ((s8[6291456]{0:T(1024)(128)(4,1)}), s8[2097152]{0:T(1024)(128)(4,1)S(1)}, s32[]{:S(2)}) async-start(s8[6291456]{0:T(1024)(128)(4,1)} %bitcast.7), calls=%async_computation | async-start | bytes 4194304
  43.9 10.4 %slice-start.1 = ((s8[6291456]{0:T(1024)(128)(4,1)}), s8[4194304]{0:T(1024)(128)(4,1)S(1)}, s32[]{:S(2)}) async-start(s8[6291456]{0:T(1024)(128)(4,1)} %bitcast.7), calls=%async_computation.1 | async-start | bytes 8388608
  44.0 14.2 %collective-permute-start.14 = (bf16[1,256,512]{2,1,0:T(8,128)(2,1)S(1)}, bf16[1,256,512]{2,1,0:T(8,128)(2,1)S(1)}, u32[]{:S(2)}, u32[]{:S(2)}) collective-permute-start(bf16[1,256,512]{2,1,0:T(8,128)(2,1)S(1)} %get-tuple-element.138), channel_id=1, source_target_pairs={{0,2},{1,3},{2,0},{3,1},{4,6},{5,7},{6,4},{7,5},{8,10},{9,11},{10,... | collective-permute-start | bytes 786440 | tf_op jit(solution)/shard_map/ppermute | solution.py:850
  56.8 10.4 %collective-permute-start.15 = (bf16[2,256,256]{2,1,0:T(8,128)(2,1)S(1)}, bf16[2,256,256]{2,1,0:T(8,128)(2,1)S(1)}, u32[]{:S(2)}, u32[]{:S(2)}) collective-permute-start(bf16[2,256,256]{2,1,0:T(8,128)(2,1)S(1)} %get-tuple-element.141), channel_id=1, source_target_pairs={{0,1},{1,0},{2,3},{3,2},{4,5},{5,4},{6,7},{7,6},{8,9},{9,8},{10,11... | collective-permute-start | bytes 786440 | tf_op jit(solution)/shard_map/ppermute | solution.py:850
  58.1 13.4 %collective-permute-start.17 = (bf16[256,256]{1,0:T(8,128)(2,1)S(1)}, bf16[256,256]{1,0:T(8,128)(2,1)S(1)}, u32[]{:S(2)}, u32[]{:S(2)}) collective-permute-start(bf16[256,256]{1,0:T(8,128)(2,1)S(1)} %get-tuple-element.147), channel_id=1, source_target_pairs={{0,2},{1,3},{2,0},{3,1},{4,6},{5,7},{6,4},{7,5},{8,10},{9,11},{10,... | collective-permute-start | bytes 393224 | tf_op jit(solution)/shard_map/ppermute | solution.py:850
  60.0 13.9 %collective-permute-start.18 = (bf16[256,256]{1,0:T(8,128)(2,1)S(1)}, bf16[256,256]{1,0:T(8,128)(2,1)S(1)}, u32[]{:S(2)}, u32[]{:S(2)}) collective-permute-start(bf16[256,256]{1,0:T(8,128)(2,1)S(1)} %get-tuple-element.148), channel_id=1, source_target_pairs={{0,3},{1,2},{2,1},{3,0},{4,7},{5,6},{6,5},{7,4},{8,11},{9,10},{10,... | collective-permute-start | bytes 393224 | tf_op jit(solution)/shard_map/ppermute | solution.py:850
  67.3 10.8 %collective-permute-start.16 = (bf16[1,256,256]{2,1,0:T(8,128)(2,1)S(1)}, bf16[1,256,256]{2,1,0:T(8,128)(2,1)S(1)}, u32[]{:S(2)}, u32[]{:S(2)}) collective-permute-start(bf16[1,256,256]{2,1,0:T(8,128)(2,1)S(1)} %get-tuple-element.145), channel_id=1, source_target_pairs={{0,2},{1,3},{2,0},{3,1},{4,6},{5,7},{6,4},{7,5},{8,10},{9,11},{10,... | collective-permute-start | bytes 393224 | tf_op jit(solution)/shard_map/ppermute | solution.py:850
  68.9 9.2 %collective-permute-start.19 = (bf16[256,256]{1,0:T(8,128)(2,1)S(1)}, bf16[256,256]{1,0:T(8,128)(2,1)S(1)}, u32[]{:S(2)}, u32[]{:S(2)}) collective-permute-start(bf16[256,256]{1,0:T(8,128)(2,1)S(1)} %get-tuple-element.149), channel_id=1, source_target_pairs={{0,1},{1,0},{2,3},{3,2},{4,5},{5,4},{6,7},{7,6},{8,9},{9,8},{10,11... | collective-permute-start | bytes 393224 | tf_op jit(solution)/shard_map/ppermute | solution.py:850

commit v15 on v14

--- a/solution.py
+++ b/solution.py
@@ -536,22 +536,18 @@
 
 
 def return_body(
-    sizes, place_ref, gain_ref, pack_ref, hat_ref, hat_t_ref, grad_ref, unit_ref, scale_ref,
+    sizes, place_ref, gain_ref, pack_ref, hat_t_ref, grad_ref, unit_ref, scale_ref,
     found_ref, prefix_ref, *refs
 ):
     heads, bits, far = sizes
     others = refs[:far]
-    dhat_ref, dout_ref, dfar_ref = refs[far : far + 3]
-    sends = refs[far + 3 :]
-    rows = pack_ref.shape[0]
-    lane = lane_of(rows)
+    dhat_ref, dout_ref = refs[far : far + 2]
+    sends = refs[far + 2 :]
     gain, scales = gain_ref[...], scale_ref[...]
     key = hat_t_ref.shape[1]
     pack = pack_ref[...]
     all_heads = range(heads)
     uppers = [((place_ref[0] >> bit) & 1) == 1 for bit in range(far)]
-    reached = [mm(hat_ref[head], found_ref[head]) for head in all_heads]
-    dfar = jnp.zeros((rows, LANES), F32)
     spread = []
     for head in all_heads:
         unit = unit_ref[head]
@@ -563,10 +559,7 @@
         for bit in range(far):
             col = (bits + 1 + bit) * heads + head
             parts.append((column(pack, col) * dout).astype(BF16))
-            here = reached[head][:, bit * key : (bit + 1) * key]
-            dfar = jnp.where(lane == col, row_sum(dout * here), dfar)
         spread.append(jnp.concatenate(parts, 1))
-    dfar_ref[...] = dfar
     dfound = [mm(hat_t_ref[head], spread[head]) for head in all_heads]
     for head in all_heads:
         dhat_ref[head] = mm_nt(spread[head], found_ref[head])
@@ -590,7 +583,7 @@
 
 
 def return_states(place, arrays, others, bits):
-    heads, rows, key = arrays[2].shape
+    heads, key, rows = arrays[2].shape
     far = len(others)
     sends = tuple(
         kept((heads, key, (1 if bit == far - 1 else 2) * key), BF16) for bit in range(far)
@@ -598,9 +591,9 @@
     wide = kept((heads, rows, key), F32)
     got = local_call(
         functools.partial(return_body, (heads, bits, far)), "return_states", 8,
-        (wide, wide, kept((rows, LANES), F32)) + sends, [place], [*arrays, *others],
-    )
-    return got[:3], got[3:]
+        (wide, wide) + sends, [place], [*arrays, *others],
+    )
+    return got[:2], got[2:]
 
 
 def add_body(*refs):
@@ -626,8 +619,8 @@
 def pull_body(sizes, *refs):
     heads, levels, bits = sizes
     (qkv_ref, pack_ref, pack_t_ref, trans_ref, attn_ref, attn_t_ref, prod_t_ref, scores_ref,
-     mix_ref, decay_ref, base_ref, lower_ref, dout_ref, dhat_ref) = refs[:14]
-    dqkv_ref, dgrown_ref, dcol_ref, drow_ref = refs[14:]
+     mix_ref, decay_ref, base_ref, lower_ref, dout_ref, dhat_ref, hat_ref, found_ref) = refs[:16]
+    dqkv_ref, dgrown_ref, dcol_ref, drow_ref, dfar_ref = refs[16:]
     rows = pack_ref.shape[0]
     decay_col = levels * heads
     beta_col = decay_col + heads
@@ -641,6 +634,14 @@
     all_heads = range(heads)
     dcol = jnp.zeros((rows, LANES), F32)
     dbeta_rows, dcum_rows, dattn_all = [], [], []
+    key = hat_ref.shape[2]
+    dfar = jnp.zeros((rows, LANES), F32)
+    for head in all_heads:
+        reached = mm(hat_ref[head], found_ref[head])
+        for bit in range(reached.shape[1] // key):
+            here = row_sum(dout_ref[head] * reached[:, bit * key : (bit + 1) * key])
+            dfar = jnp.where(lane == (bits + 1 + bit) * heads + head, here, dfar)
+    dfar_ref[...] = dfar
     for head in all_heads:
         high, low = split(dout_ref[head])
         v_in = qkv_ref[2, head].astype(BF16)
@@ -698,6 +699,7 @@
         kept((heads, rows, key), F32),
         kept((rows, LANES), F32),
         kept((2 * heads, rows), F32),
+        kept((rows, LANES), F32),
     )
     return local_call(
         functools.partial(pull_body, (heads, levels, bits)), "pull_local", 12, out_shape, [], arrays
@@ -931,8 +933,8 @@
         place, [gain, pack, local_out, hat, flat_out], first, (mine, theirs), bits, far, count
     )
     others = [first, *nodes]
-    (dhat, dout, dfar), sends = return_states(
-        place, [gain, pack, hat, hat_t, grad_normed, unit, scale, found, prefix], others, bits
+    (dhat, dout), sends = return_states(
+        place, [gain, pack, hat_t, grad_normed, unit, scale, found, prefix], others, bits
     )
     got = [swap(value, "ctx", 1) for value in sends]
     arrived = [[got[0]]]
@@ -940,9 +942,9 @@
     for bit in range(1, far):
         half = 1 << (bit - 1)
         arrived.append([swap(sums[bit - 1], "ctx", 2 * at) for at in range(half, 2 * half)])
-    dqkv, dgrown, dcol, drow = pull_local(
+    dqkv, dgrown, dcol, drow, dfar = pull_local(
         [qkv, pack, pack_t, trans, attn, attn_t, prod_t, scores, mix, decay, base, lower, dout,
-         dhat],
+         dhat, hat, found],
         levels, bits,
     )
     keep_out, last_out, dcol = halving(*out_parts, "head", dcol)

time: 79 us -> 79.1 us (level)
  transfers between devices with their start and end apart: 20 -> 20, of which waited for: 13 -> 12; matrix products, arithmetic and copies ran while one was open for 0% -> 0% of each run, Pallas kernels for 26% -> 26%
where the time goes in v15:
time: 79.1 us; the launch traced here: 79 us
  Pallas kernels  36.5 us (46%)
  starting transfers between devices  22.2 us (28%)
  waiting for transfers between devices  19.4 us (25%)
    pallas_call x13, Pallas kernels, local_call(): pl.pallas_call(body, out_shape=tuple(out_shape), in_specs=[SCALARS] * len...  36.5 us
    ppermute x20, starting transfers between devices, swap(): return lax.ppermute(value, axis, [(at, at ^ mask) for at in range(size)])  22.2 us
    ppermute x20, waiting for transfers between devices, swap(): return lax.ppermute(value, axis, [(at, at ^ mask) for at in range(size)])  19.4 us
  transfers between devices with their start and end apart: 20, of which 12 were waited for; matrix products, arithmetic and copies ran while one was open for 0% of the time, Pallas kernels for 26%

profile of v15, /device:TPU:0, one launch (start us, length us, event | category | flops | bytes accessed | tf_op | source)
XLA Modules:
  0.0 79.0 jit_solution(8013323229056773695)
XLA Ops:
  0.7 11.3 %project.1 = (bf16[2048,1536]{1,0:T(8,128)(2,1)}, bf16[2048,512]{1,0:T(8,128)(2,1)S(1)}, bf16[2048,512]{1,0:T(8,128)(2,1)S(1)}, bf16[128,2048]{1,0:T(8,128)(2,1)...) custom-call(s32[2]{0:T(128)S(1)} %pad_add_fusion.place_ref, ...), custom_call_target="tpu_custom_call" | custom-call | tf_op jit(solution)/shard_map/project/pallas_call | solution.py:103
  12.0 0.5 collective-permute-start
  12.6 1.2 %collective-permute-done.other_ref.refs_0_.refs_14_ = bf16[4,128,256]{2,1,0:T(8,128)(2,1)S(1)} collective-permute-done((bf16[4,128,256]{2,1,0:T(8,128)(2,1)S(1)}, bf16[4,128,256]{2,1,0:T(8,128)(2,1)S(1)}, u32[]{:S(2)}, u32[]{:S(2)}) %collective-permute-start) | collective-permute-done | bytes 262176 | tf_op jit(solution)/shard_map/ppermute | solution.py:852
  13.7 0.7 join_half.1
  14.4 3.9 %collective-permute-start.3 = (bf16[2,128,256]{2,1,0:T(8,128)(2,1)S(1)}, bf16[2,128,256]{2,1,0:T(8,128)(2,1)S(1)}, u32[]{:S(2)}, u32[]{:S(2)}) collective-permute-start(bf16[2,128,256]{2,1,0:T(8,128)(2,1)S(1)} %join_half.1), channel_id=1, source_target_pairs={{0,24},{4,28},{8,16},{12,20},{16,8},{20,12},{24,0},{28,4},{1,25},{... | collective-permute-start | bytes 393224 | tf_op jit(solution)/shard_map/ppermute | solution.py:852
  18.3 0.5 collective-permute-start.2
  19.0 4.8 %local_part.1 = (bf16[4,256,256]{2,1,0:T(8,128)(2,1)S(1)}, bf16[4,256,256]{2,1,0:T(8,128)(2,1)S(1)}, bf16[4,256,256]{2,1,0:T(8,128)(2,1)S(1)}, bf16[4,256,256]{2...) custom-call(f32[3,4,256,128]{3,2,1,0:T(8,128)S(1)} %get-tuple-elemen, ...), custom_call_target="tpu_custom_call", output_to_operand_aliasing={{10}: (0, {}), {11}: (1, {}), {12}: (11, {})} | custom-call | tf_op jit(solution)/shard_map/local_part/pallas_call | solution.py:103
  23.8 1.2 %collective-permute-done.2.refs_2_ = bf16[2,128,256]{2,1,0:T(8,128)(2,1)S(1)} collective-permute-done((bf16[2,128,256]{2,1,0:T(8,128)(2,1)S(1)}, bf16[2,128,256]{2,1,0:T(8,128)(2,1)S(1)}, u32[]{:S(2)}, u32[]{:S(2)}) %collective-permute-start.2) | collective-permute-done | bytes 131104 | tf_op jit(solution)/shard_map/ppermute | solution.py:852
  25.7 0.8 %collective-permute-done.4.refs_4_ = bf16[2,128,256]{2,1,0:T(8,128)(2,1)S(1)} collective-permute-done((bf16[2,128,256]{2,1,0:T(8,128)(2,1)S(1)}, bf16[2,128,256]{2,1,0:T(8,128)(2,1)S(1)}, u32[]{:S(2)}, u32[]{:S(2)}) %collective-permute-start.4) | collective-permute-done | bytes 131104 | tf_op jit(solution)/shard_map/ppermute | solution.py:852
  27.1 2.7 %reach.1 = (bf16[2,256,512]{2,1,0:T(8,128)(2,1)S(1)}, bf16[2,256,512]{2,1,0:T(8,128)(2,1)S(1)}, f32[4,256,128]{2,1,0:T(8,128)S(1)}, f32[256,128]{1,0:T(8,128)S(1...) custom-call(s32[2]{0:T(128)S(1)} %pad_add_fusion.place_ref, ...), custom_call_target="tpu_custom_call" | custom-call | tf_op jit(solution)/shard_map/reach/pallas_call | solution.py:103
  29.8 1.6 %collective-permute-start.7 = (bf16[2,256,512]{2,1,0:T(8,128)(2,1)S(1)}, bf16[2,256,512]{2,1,0:T(8,128)(2,1)S(1)}, u32[]{:S(2)}, u32[]{:S(2)}) collective-permute-start(bf16[2,256,512]{2,1,0:T(8,128)(2,1)S(1)} %get-tuple-element.95), channel_id=1, source_target_pairs={{0,1},{1,0},{2,3},{3,2},{4,5},{5,4},{6,7},{7,6},{8,9},{9,8},{10,11... | collective-permute-start | bytes 1572872 | tf_op jit(solution)/shard_map/ppermute | solution.py:852
  31.4 2.9 %return_states.1 = (f32[4,256,128]{2,1,0:T(8,128)S(1)}, f32[4,256,128]{2,1,0:T(8,128)S(1)}, bf16[4,128,256]{2,1,0:T(8,128)(2,1)S(1)}, bf16[4,128,256]{2,1,0:T(8,128)(2,1)S(1)}, bf16[4,128,128]{2,1,0:T(8,128)(2,1)S(1)}) custom-call(s32[2]{0:T(128)S(1)} %pad_add_fusion.place_ref, f32[1,128]{1,0:T(1,128)S(1)} %bitcast.12, ...), custom_call_target="tpu_custom_call" | custom-call | tf_op jit(solution)/shard_map/return_states/pallas_call | solution.py:103
  35.0 1.1 %collective-permute-done.10.refs_3_ = bf16[4,128,128]{2,1,0:T(8,128)(2,1)S(1)} collective-permute-done((bf16[4,128,128]{2,1,0:T(8,128)(2,1)S(1)}, bf16[4,128,128]{2,1,0:T(8,128)(2,1)S(1)}, u32[]{:S(2)}, u32[]{:S(2)}) %collective-permute-start.10) | collective-permute-done | bytes 131104 | tf_op jit(solution)/shard_map/ppermute | solution.py:852
  36.2 1.6 %collective-permute-start.11 = (bf16[4,128,256]{2,1,0:T(8,128)(2,1)S(1)}, bf16[4,128,256]{2,1,0:T(8,128)(2,1)S(1)}, u32[]{:S(2)}, u32[]{:S(2)}) collective-permute-start(bf16[4,128,256]{2,1,0:T(8,128)(2,1)S(1)} %get-tuple-element.128), channel_id=1, source_target_pairs={{0,8},{4,12},{8,0},{12,4},{16,24},{20,28},{24,16},{28,20},{1,9},{5... | collective-permute-start | bytes 786440 | tf_op jit(solution)/shard_map/ppermute | solution.py:852
  37.8 1.4 %collective-permute-start.13 = (bf16[4,128,128]{2,1,0:T(8,128)(2,1)S(1)}, bf16[4,128,128]{2,1,0:T(8,128)(2,1)S(1)}, u32[]{:S(2)}, u32[]{:S(2)}) collective-permute-start(bf16[4,128,128]{2,1,0:T(8,128)(2,1)S(1)} %get-tuple-element.129), channel_id=1, source_target_pairs={{0,24},{4,28},{8,16},{12,20},{16,8},{20,12},{24,0},{28,4},{1,25},{... | collective-permute-start | bytes 393224 | tf_op jit(solution)/shard_map/ppermute | solution.py:852
  39.2 0.6 collective-permute-start.12
  39.8 4.2 %pull_local.1 = (f32[3,4,256,128]{3,2,1,0:T(8,128)S(1)}, f32[4,256,128]{2,1,0:T(8,128)S(1)}, f32[256,128]{1,0:T(8,128)S(1)}, f32[8,256]{1,0:T(8,128)S(1)}, f32[256,128]{1,0:T(8,128)S(1)}) custom-call(f32[3,4,256,128]{3,2,1,0:T(8,128)S(1)} %get-tuple-element.97.refs_0_, f32[256,128]{1,0:T(8,128)S(1)} %get-tuple-element.85.pack_ref.refs_1_.refs_2_, ...), custom_call_target="tpu_custom_call" | custom-call | tf_op jit(solution)/shard_map/pull_local/pallas_call | solution.py:103
  44.2 2.7 %collective-permute-start.14 = (bf16[1,256,512]{2,1,0:T(8,128)(2,1)S(1)}, bf16[1,256,512]{2,1,0:T(8,128)(2,1)S(1)}, u32[]{:S(2)}, u32[]{:S(2)}) collective-permute-start(bf16[1,256,512]{2,1,0:T(8,128)(2,1)S(1)} %get-tuple-element.138), channel_id=1, source_target_pairs={{0,2},{1,3},{2,0},{3,1},{4,6},{5,7},{6,4},{7,5},{8,10},{9,11},{10,... | collective-permute-start | bytes 786440 | tf_op jit(solution)/shard_map/ppermute | solution.py:852
  46.9 1.5 %collective-permute-done.13.refs_20_ = bf16[4,128,128]{2,1,0:T(8,128)(2,1)S(1)} collective-permute-done((bf16[4,128,128]{2,1,0:T(8,128)(2,1)S(1)}, bf16[4,128,128]{2,1,0:T(8,128)(2,1)S(1)}, u32[]{:S(2)}, u32[]{:S(2)}) %collective-permute-start.13) | collective-permute-done | bytes 131104 | tf_op jit(solution)/shard_map/ppermute | solution.py:852
  48.3 5.4 %finish.1 = (bf16[256,1536]{1,0:T(8,128)(2,1)S(1)}, bf16[256,128]{1,0:T(8,128)(2,1)S(1)}) custom-call(s32[2]{0:T(128)S(1)} %pad_add_fusion.place_ref, f32[3,4,256,128]{3,2,1,0:T(8,128)S(1)} %get-tuple-element.97.refs_0_, f32[256,128]{1,0:T(8,128)S(1)} %get-tuple-element.98.refs_1_, f32[256,128]{1,0:T(8,128)S(1)} %get-tuple-element.85.pack_ref.refs_1_.refs_2_, ...), custom_call_target="tpu_custom_call" | custom-call | tf_op jit(solution)/shard_map/finish/pallas_call | solution.py:103
  53.8 2.6 %pull_tokens.1 = (bf16[2,256,256]{2,1,0:T(8,128)(2,1)S(1)}, bf16[2,256,256]{2,1,0:T(8,128)(2,1)S(1)}, bf16[256,256]{1,0:T(8,128)(2,1)S(1)}, bf16[256,256]{1,0:T(...) custom-call(s32[2]{0:T(128)S(1)} %pad_add_fusion.place_ref, ...), custom_call_target="tpu_custom_call" | custom-call | tf_op jit(solution)/shard_map/pull_tokens/pallas_call | solution.py:103
  56.4 0.5 collective-permute-start.15
  56.9 1.4 %collective-permute-done.14.refs_1_ = bf16[1,256,512]{2,1,0:T(8,128)(2,1)S(1)} collective-permute-done((bf16[1,256,512]{2,1,0:T(8,128)(2,1)S(1)}, bf16[1,256,512]{2,1,0:T(8,128)(2,1)S(1)}, u32[]{:S(2)}, u32[]{:S(2)}) %collective-permute-start.14) | collective-permute-done | bytes 262176 | tf_op jit(solution)/shard_map/ppermute | solution.py:852
  58.3 1.2 %collective-permute-start.17 = (bf16[256,256]{1,0:T(8,128)(2,1)S(1)}, bf16[256,256]{1,0:T(8,128)(2,1)S(1)}, u32[]{:S(2)}, u32[]{:S(2)}) collective-permute-start(bf16[256,256]{1,0:T(8,128)(2,1)S(1)} %get-tuple-element.147), channel_id=1, source_target_pairs={{0,2},{1,3},{2,0},{3,1},{4,6},{5,7},{6,4},{7,5},{8,10},{9,11},{10,... | collective-permute-start | bytes 393224 | tf_op jit(solution)/shard_map/ppermute | solution.py:852
  59.5 2.4 %collective-permute-start.18 = (bf16[256,256]{1,0:T(8,128)(2,1)S(1)}, bf16[256,256]{1,0:T(8,128)(2,1)S(1)}, u32[]{:S(2)}, u32[]{:S(2)}) collective-permute-start(bf16[256,256]{1,0:T(8,128)(2,1)S(1)} %get-tuple-element.148), channel_id=1, source_target_pairs={{0,3},{1,2},{2,1},{3,0},{4,7},{5,6},{6,5},{7,4},{8,11},{9,10},{10,... | collective-permute-start | bytes 393224 | tf_op jit(solution)/shard_map/ppermute | solution.py:852
  61.8 4.9 %collective-permute-done.15.got_ref = bf16[2,256,256]{2,1,0:T(8,128)(2,1)S(1)} collective-permute-done((bf16[2,256,256]{2,1,0:T(8,128)(2,1)S(1)}, bf16[2,256,256]{2,1,0:T(8,128)(2,1)S(1)}, u32[]{:S(2)}, u32[]{:S(2)}) %collective-permute-start.15) | collective-permute-done | bytes 262176 | tf_op jit(solution)/shard_map/ppermute | solution.py:852
  66.8 1.6 %collective-permute-start.16 = (bf16[1,256,256]{2,1,0:T(8,128)(2,1)S(1)}, bf16[1,256,256]{2,1,0:T(8,128)(2,1)S(1)}, u32[]{:S(2)}, u32[]{:S(2)}) collective-permute-start(bf16[1,256,256]{2,1,0:T(8,128)(2,1)S(1)} %get-tuple-element.145), channel_id=1, source_target_pairs={{0,2},{1,3},{2,0},{3,1},{4,6},{5,7},{6,4},{7,5},{8,10},{9,11},{10,... | collective-permute-start | bytes 393224 | tf_op jit(solution)/shard_map/ppermute | solution.py:852
  68.4 2.5 %collective-permute-start.19 = (bf16[256,256]{1,0:T(8,128)(2,1)S(1)}, bf16[256,256]{1,0:T(8,128)(2,1)S(1)}, u32[]{:S(2)}, u32[]{:S(2)}) collective-permute-start(bf16[256,256]{1,0:T(8,128)(2,1)S(1)} %get-tuple-element.149), channel_id=1, source_target_pairs={{0,1},{1,0},{2,3},{3,2},{4,5},{5,4},{6,7},{7,6},{8,9},{9,8},{10,11... | collective-permute-start | bytes 393224 | tf_op jit(solution)/shard_map/ppermute | solution.py:852
  70.9 0.7 head_sum.2
  71.7 1.7 %collective-permute-done.18.refs_4_ = bf16[256,256]{1,0:T(8,128)(2,1)S(1)} collective-permute-done((bf16[256,256]{1,0:T(8,128)(2,1)S(1)}, bf16[256,256]{1,0:T(8,128)(2,1)S(1)}, u32[]{:S(2)}, u32[]{:S(2)}) %collective-permute-start.18) | collective-permute-done | bytes 131104 | tf_op jit(solution)/shard_map/ppermute | solution.py:852
  73.4 4.8 %collective-permute-done.16.refs_1_ = bf16[1,256,256]{2,1,0:T(8,128)(2,1)S(1)} collective-permute-done((bf16[1,256,256]{2,1,0:T(8,128)(2,1)S(1)}, bf16[1,256,256]{2,1,0:T(8,128)(2,1)S(1)}, u32[]{:S(2)}, u32[]{:S(2)}) %collective-permute-start.16) | collective-permute-done | bytes 131104 | tf_op jit(solution)/shard_map/ppermute | solution.py:852
  78.2 0.8 %head_sum.3 = bf16[256,512]{1,0:T(8,128)(2,1)} custom-call(f32[1,256,256]{2,1,0:T(8,128)S(1)} %get-tuple-element.142.refs_0_, bf16[1,256,256]{2,1,0:T(8,128)(2,1)S(1)} %collective-permute-done.16.refs_1_, bf16[256,256]{1,0:T(8,128)(2,1)S(1)} %get-tuple-element.146.refs_2_, bf16[256,256]{1,0:T(8,128)(2,1)S(1)} %collective-permute-done.17.refs_3_, ...), custom_call_target="tpu_custom_call" | custom-call | tf_op jit(solution)/shard_map/head_sum/pallas_call | solution.py:103
  (35 shorter events, 2.5 us)
Async XLA Ops:
  0.7 18.3 %copy-start = (bf16[4,128,2048]{2,1,0:T(8,128)(2,1)S(1)}, bf16[4,128,2048]{2,1,0:T(8,128)(2,1)}, u32[]{:S(2)}) copy-start(bf16[4,128,2048]{2,1,0:T(8,128)(2,1)} %param.12) | copy-start | bytes 6291460
  0.7 18.3 %copy-start.1 = (bf16[256,2048]{1,0:T(8,128)(2,1)S(1)}, bf16[256,2048]{1,0:T(8,128)(2,1)}, u32[]{:S(2)}) copy-start(bf16[256,2048]{1,0:T(8,128)(2,1)} %tokens_ref.1) | copy-start | bytes 3145732
  0.7 18.3 %copy-start.2 = (bf16[256,2048]{1,0:T(8,128)(2,1)S(1)}, bf16[256,2048]{1,0:T(8,128)(2,1)}, u32[]{:S(2)}) copy-start(bf16[256,2048]{1,0:T(8,128)(2,1)} %grad_ref.1) | copy-start | bytes 3145732
  12.0 1.7 %collective-permute-start = (bf16[4,128,256]{2,1,0:T(8,128)(2,1)S(1)}, bf16[4,128,256]{2,1,0:T(8,128)(2,1)S(1)}, u32[]{:S(2)}, u32[]{:S(2)}) collective-permute-start(bf16[4,128,256]{2,1,0:T(8,128)(2,1)S(1)} %get-tuple-element.86.own_ref), channel_id=1, source_target_pairs={{0,4},{4,0},{8,12},{12,8},{16,20},{20,16},{24,28},{28,24},{1,5},{5... | collective-permute-start | bytes 786440 | tf_op jit(solution)/shard_map/ppermute | solution.py:852
  14.4 9.3 %collective-permute-start.3 = (bf16[2,128,256]{2,1,0:T(8,128)(2,1)S(1)}, bf16[2,128,256]{2,1,0:T(8,128)(2,1)S(1)}, u32[]{:S(2)}, u32[]{:S(2)}) collective-permute-start(bf16[2,128,256]{2,1,0:T(8,128)(2,1)S(1)} %join_half.1), channel_id=1, source_target_pairs={{0,24},{4,28},{8,16},{12,20},{16,8},{20,12},{24,0},{28,4},{1,25},{... | collective-permute-start | bytes 393224 | tf_op jit(solution)/shard_map/ppermute | solution.py:852
  18.3 6.6 %collective-permute-start.2 = (bf16[2,128,256]{2,1,0:T(8,128)(2,1)S(1)}, bf16[2,128,256]{2,1,0:T(8,128)(2,1)S(1)}, u32[]{:S(2)}, u32[]{:S(2)}) collective-permute-start(bf16[2,128,256]{2,1,0:T(8,128)(2,1)S(1)} %join_half.1), channel_id=1, source_target_pairs={{0,16},{4,20},{8,24},{12,28},{16,0},{20,4},{24,8},{28,12},{1,17},{... | collective-permute-start | bytes 393224 | tf_op jit(solution)/shard_map/ppermute | solution.py:852
  18.8 6.4 %collective-permute-start.1 = (bf16[2,128,256]{2,1,0:T(8,128)(2,1)S(1)}, bf16[2,128,256]{2,1,0:T(8,128)(2,1)S(1)}, u32[]{:S(2)}, u32[]{:S(2)}) collective-permute-start(bf16[2,128,256]{2,1,0:T(8,128)(2,1)S(1)} %join_half.1), channel_id=1, source_target_pairs={{0,8},{4,12},{8,0},{12,4},{16,24},{20,28},{24,16},{28,20},{1,9},{5... | collective-permute-start | bytes 393224 | tf_op jit(solution)/shard_map/ppermute | solution.py:852
  19.0 8.1 %copy-start.3 = (f32[128]{0:T(128)S(1)}, f32[128]{0:T(128)}, u32[]{:S(2)}) copy-start(f32[128]{0:T(128)} %param.11) | copy-start | bytes 1540
  25.2 1.3 %collective-permute-start.4 = (bf16[2,128,256]{2,1,0:T(8,128)(2,1)S(1)}, bf16[2,128,256]{2,1,0:T(8,128)(2,1)S(1)}, u32[]{:S(2)}, u32[]{:S(2)}) collective-permute-start(bf16[2,128,256]{2,1,0:T(8,128)(2,1)S(1)} %collective-permute-done.1.refs_1_), channel_id=1, source_target_pairs={{0,4},{4,0},{8,12},{12,8},{16,20},{20,16},{24,28},{28,24},{1,5},{5... | collective-permute-start | bytes 393224 | tf_op jit(solution)/shard_map/ppermute | solution.py:852
  25.2 1.5 %collective-permute-start.5 = (bf16[2,128,256]{2,1,0:T(8,128)(2,1)S(1)}, bf16[2,128,256]{2,1,0:T(8,128)(2,1)S(1)}, u32[]{:S(2)}, u32[]{:S(2)}) collective-permute-start(bf16[2,128,256]{2,1,0:T(8,128)(2,1)S(1)} %collective-permute-done.2.refs_2_), channel_id=1, source_target_pairs={{0,4},{4,0},{8,12},{12,8},{16,20},{20,16},{24,28},{28,24},{1,5},{5... | collective-permute-start | bytes 393224 | tf_op jit(solution)/shard_map/ppermute | solution.py:852
  25.7 1.3 %collective-permute-start.6 = (bf16[2,128,256]{2,1,0:T(8,128)(2,1)S(1)}, bf16[2,128,256]{2,1,0:T(8,128)(2,1)S(1)}, u32[]{:S(2)}, u32[]{:S(2)}) collective-permute-start(bf16[2,128,256]{2,1,0:T(8,128)(2,1)S(1)} %collective-permute-done.3.refs_3_), channel_id=1, source_target_pairs={{0,4},{4,0},{8,12},{12,8},{16,20},{20,16},{24,28},{28,24},{1,5},{5... | collective-permute-start | bytes 393224 | tf_op jit(solution)/shard_map/ppermute | solution.py:852
  29.8 14.3 %collective-permute-start.7 = (bf16[2,256,512]{2,1,0:T(8,128)(2,1)S(1)}, bf16[2,256,512]{2,1,0:T(8,128)(2,1)S(1)}, u32[]{:S(2)}, u32[]{:S(2)}) collective-permute-start(bf16[2,256,512]{2,1,0:T(8,128)(2,1)S(1)} %get-tuple-element.95), channel_id=1, source_target_pairs={{0,1},{1,0},{2,3},{3,2},{4,5},{5,4},{6,7},{7,6},{8,9},{9,8},{10,11... | collective-permute-start | bytes 1572872 | tf_op jit(solution)/shard_map/ppermute | solution.py:852
  34.3 1.8 %collective-permute-start.9 = (bf16[4,128,256]{2,1,0:T(8,128)(2,1)S(1)}, bf16[4,128,256]{2,1,0:T(8,128)(2,1)S(1)}, u32[]{:S(2)}, u32[]{:S(2)}) collective-permute-start(bf16[4,128,256]{2,1,0:T(8,128)(2,1)S(1)} %get-tuple-element.126.refs_0_), channel_id=1, source_target_pairs={{0,4},{4,0},{8,12},{12,8},{16,20},{20,16},{24,28},{28,24},{1,5},{5... | collective-permute-start | bytes 786440 | tf_op jit(solution)/shard_map/ppermute | solution.py:852
  34.4 1.7 %collective-permute-start.10 = (bf16[4,128,128]{2,1,0:T(8,128)(2,1)S(1)}, bf16[4,128,128]{2,1,0:T(8,128)(2,1)S(1)}, u32[]{:S(2)}, u32[]{:S(2)}) collective-permute-start(bf16[4,128,128]{2,1,0:T(8,128)(2,1)S(1)} %get-tuple-element.127.refs_1_), channel_id=1, source_target_pairs={{0,4},{4,0},{8,12},{12,8},{16,20},{20,16},{24,28},{28,24},{1,5},{5... | collective-permute-start | bytes 393224 | tf_op jit(solution)/shard_map/ppermute | solution.py:852
  34.9 11.9 %collective-permute-start.8 = (bf16[4,128,256]{2,1,0:T(8,128)(2,1)S(1)}, bf16[4,128,256]{2,1,0:T(8,128)(2,1)S(1)}, u32[]{:S(2)}, u32[]{:S(2)}) collective-permute-start(bf16[4,128,256]{2,1,0:T(8,128)(2,1)S(1)} %get-tuple-element.125), channel_id=1, source_target_pairs={{0,4},{4,0},{8,12},{12,8},{16,20},{20,16},{24,28},{28,24},{1,5},{5... | collective-permute-start | bytes 786440 | tf_op jit(solution)/shard_map/ppermute | solution.py:852
  36.2 12.1 %collective-permute-start.11 = (bf16[4,128,256]{2,1,0:T(8,128)(2,1)S(1)}, bf16[4,128,256]{2,1,0:T(8,128)(2,1)S(1)}, u32[]{:S(2)}, u32[]{:S(2)}) collective-permute-start(bf16[4,128,256]{2,1,0:T(8,128)(2,1)S(1)} %get-tuple-element.128), channel_id=1, source_target_pairs={{0,8},{4,12},{8,0},{12,4},{16,24},{20,28},{24,16},{28,20},{1,9},{5... | collective-permute-start | bytes 786440 | tf_op jit(solution)/shard_map/ppermute | solution.py:852
  37.8 10.5 %collective-permute-start.13 = (bf16[4,128,128]{2,1,0:T(8,128)(2,1)S(1)}, bf16[4,128,128]{2,1,0:T(8,128)(2,1)S(1)}, u32[]{:S(2)}, u32[]{:S(2)}) collective-permute-start(bf16[4,128,128]{2,1,0:T(8,128)(2,1)S(1)} %get-tuple-element.129), channel_id=1, source_target_pairs={{0,24},{4,28},{8,16},{12,20},{16,8},{20,12},{24,0},{28,4},{1,25},{... | collective-permute-start | bytes 393224 | tf_op jit(solution)/shard_map/ppermute | solution.py:852
  39.2 9.1 %collective-permute-start.12 = (bf16[4,128,128]{2,1,0:T(8,128)(2,1)S(1)}, bf16[4,128,128]{2,1,0:T(8,128)(2,1)S(1)}, u32[]{:S(2)}, u32[]{:S(2)}) collective-permute-start(bf16[4,128,128]{2,1,0:T(8,128)(2,1)S(1)} %get-tuple-element.129), channel_id=1, source_target_pairs={{0,16},{4,20},{8,24},{12,28},{16,0},{20,4},{24,8},{28,12},{1,17},{... | collective-permute-start | bytes 393224 | tf_op jit(solution)/shard_map/ppermute | solution.py:852
  39.8 13.9 %slice-start = ((s8[6291456]{0:T(1024)(128)(4,1)}), s8[2097152]{0:T(1024)(128)(4,1)S(1)}, s32[]{:S(2)}) async-start(s8[6291456]{0:T(1024)(128)(4,1)} %bitcast.7), calls=%async_computation | async-start | bytes 4194304
  44.0 9.7 %slice-start.1 = ((s8[6291456]{0:T(1024)(128)(4,1)}), s8[4194304]{0:T(1024)(128)(4,1)S(1)}, s32[]{:S(2)}) async-start(s8[6291456]{0:T(1024)(128)(4,1)} %bitcast.7), calls=%async_computation.1 | async-start | bytes 8388608
  44.2 14.1 %collective-permute-start.14 = (bf16[1,256,512]{2,1,0:T(8,128)(2,1)S(1)}, bf16[1,256,512]{2,1,0:T(8,128)(2,1)S(1)}, u32[]{:S(2)}, u32[]{:S(2)}) collective-permute-start(bf16[1,256,512]{2,1,0:T(8,128)(2,1)S(1)} %get-tuple-element.138), channel_id=1, source_target_pairs={{0,2},{1,3},{2,0},{3,1},{4,6},{5,7},{6,4},{7,5},{8,10},{9,11},{10,... | collective-permute-start | bytes 786440 | tf_op jit(solution)/shard_map/ppermute | solution.py:852
  56.4 10.4 %collective-permute-start.15 = (bf16[2,256,256]{2,1,0:T(8,128)(2,1)S(1)}, bf16[2,256,256]{2,1,0:T(8,128)(2,1)S(1)}, u32[]{:S(2)}, u32[]{:S(2)}) collective-permute-start(bf16[2,256,256]{2,1,0:T(8,128)(2,1)S(1)} %get-tuple-element.141), channel_id=1, source_target_pairs={{0,1},{1,0},{2,3},{3,2},{4,5},{5,4},{6,7},{7,6},{8,9},{9,8},{10,11... | collective-permute-start | bytes 786440 | tf_op jit(solution)/shard_map/ppermute | solution.py:852
  58.3 13.4 %collective-permute-start.17 = (bf16[256,256]{1,0:T(8,128)(2,1)S(1)}, bf16[256,256]{1,0:T(8,128)(2,1)S(1)}, u32[]{:S(2)}, u32[]{:S(2)}) collective-permute-start(bf16[256,256]{1,0:T(8,128)(2,1)S(1)} %get-tuple-element.147), channel_id=1, source_target_pairs={{0,2},{1,3},{2,0},{3,1},{4,6},{5,7},{6,4},{7,5},{8,10},{9,11},{10,... | collective-permute-start | bytes 393224 | tf_op jit(solution)/shard_map/ppermute | solution.py:852
  59.5 13.9 %collective-permute-start.18 = (bf16[256,256]{1,0:T(8,128)(2,1)S(1)}, bf16[256,256]{1,0:T(8,128)(2,1)S(1)}, u32[]{:S(2)}, u32[]{:S(2)}) collective-permute-start(bf16[256,256]{1,0:T(8,128)(2,1)S(1)} %get-tuple-element.148), channel_id=1, source_target_pairs={{0,3},{1,2},{2,1},{3,0},{4,7},{5,6},{6,5},{7,4},{8,11},{9,10},{10,... | collective-permute-start | bytes 393224 | tf_op jit(solution)/shard_map/ppermute | solution.py:852
  66.8 11.4 %collective-permute-start.16 = (bf16[1,256,256]{2,1,0:T(8,128)(2,1)S(1)}, bf16[1,256,256]{2,1,0:T(8,128)(2,1)S(1)}, u32[]{:S(2)}, u32[]{:S(2)}) collective-permute-start(bf16[1,256,256]{2,1,0:T(8,128)(2,1)S(1)} %get-tuple-element.145), channel_id=1, source_target_pairs={{0,2},{1,3},{2,0},{3,1},{4,6},{5,7},{6,4},{7,5},{8,10},{9,11},{10,... | collective-permute-start | bytes 393224 | tf_op jit(solution)/shard_map/ppermute | solution.py:852
  68.4 9.8 %collective-permute-start.19 = (bf16[256,256]{1,0:T(8,128)(2,1)S(1)}, bf16[256,256]{1,0:T(8,128)(2,1)S(1)}, u32[]{:S(2)}, u32[]{:S(2)}) collective-permute-start(bf16[256,256]{1,0:T(8,128)(2,1)S(1)} %get-tuple-element.149), channel_id=1, source_target_pairs={{0,1},{1,0},{2,3},{3,2},{4,5},{5,4},{6,7},{7,6},{8,9},{9,8},{10,11... | collective-permute-start | bytes 393224 | tf_op jit(solution)/shard_map/ppermute | solution.py:852

commit v16 on v15

--- a/solution.py
+++ b/solution.py
@@ -243,7 +243,7 @@
     gate_ref[...] = gate
     switch = jax.nn.sigmoid(gate + bias)
     lam = jnp.maximum(gate, 0.0) + jnp.log1p(jnp.exp(-jnp.abs(gate)))
-    cum = mm_full(inclusive.astype(F32), -rate * switch)
+    cum = mm_ones(inclusive.astype(F32), -rate * switch)
     pack = jnp.where(lane < decay_col, lam, jnp.where(lane < beta_col, cum, switch))
     pack_t = pack.T
     pack_t_ref[...] = pack_t
@@ -353,7 +353,7 @@
         here, col = ((query_ref, 0), (value_ref, 2 * size))[at // 2]
         there = wr_hbm.at[span, pl.ds(col, size)]
         keeps.append(pltpu.make_async_copy(here.at[span, :], there, sems.at[at]))
-        keeps[at].start()
+        keeps[at].start(priority=at % 2)
     rows = pack_ref.shape[0]
     decay_col = levels * heads
     beta_col = decay_col + heads

time: 79.1 us -> 79 us (level)
  transfers between devices with their start and end apart: 20 -> 20, of which waited for: 12 -> 12; matrix products, arithmetic and copies ran while one was open for 0% -> 0% of each run, Pallas kernels for 26% -> 27%
where the time goes in v16:
time: 79 us; the launch traced here: 78.8 us
  Pallas kernels  36.3 us (46%)
  starting transfers between devices  22.2 us (28%)
  waiting for transfers between devices  19.4 us (25%)
  between operations  0.79 us (1%)
    pallas_call x13, Pallas kernels, local_call(): pl.pallas_call(body, out_shape=tuple(out_shape), in_specs=[SCALARS] * len...  36.3 us
    ppermute x20, starting transfers between devices, swap(): return lax.ppermute(value, axis, [(at, at ^ mask) for at in range(size)])  22.2 us
    ppermute x20, waiting for transfers between devices, swap(): return lax.ppermute(value, axis, [(at, at ^ mask) for at in range(size)])  19.4 us
  transfers between devices with their start and end apart: 20, of which 12 were waited for; matrix products, arithmetic and copies ran while one was open for 0% of the time, Pallas kernels for 27%

profile of v16, /device:TPU:0, one launch (start us, length us, event | category | flops | bytes accessed | tf_op | source)
XLA Modules:
  0.0 78.8 jit_solution(1067779182528645592)
XLA Ops:
  0.7 11.1 %project.1 = (bf16[2048,1536]{1,0:T(8,128)(2,1)}, bf16[2048,512]{1,0:T(8,128)(2,1)S(1)}, bf16[2048,512]{1,0:T(8,128)(2,1)S(1)}, bf16[128,2048]{1,0:T(8,128)(2,1)...) custom-call(s32[2]{0:T(128)S(1)} %pad_add_fusion.place_ref, ...), custom_call_target="tpu_custom_call" | custom-call | tf_op jit(solution)/shard_map/project/pallas_call | solution.py:103
  11.9 0.5 collective-permute-start
  12.4 1.2 %collective-permute-done.other_ref.refs_0_.refs_14_ = bf16[4,128,256]{2,1,0:T(8,128)(2,1)S(1)} collective-permute-done((bf16[4,128,256]{2,1,0:T(8,128)(2,1)S(1)}, bf16[4,128,256]{2,1,0:T(8,128)(2,1)S(1)}, u32[]{:S(2)}, u32[]{:S(2)}) %collective-permute-start) | collective-permute-done | bytes 262176 | tf_op jit(solution)/shard_map/ppermute | solution.py:852
  13.6 0.7 join_half.1
  14.3 3.9 %collective-permute-start.3 = (bf16[2,128,256]{2,1,0:T(8,128)(2,1)S(1)}, bf16[2,128,256]{2,1,0:T(8,128)(2,1)S(1)}, u32[]{:S(2)}, u32[]{:S(2)}) collective-permute-start(bf16[2,128,256]{2,1,0:T(8,128)(2,1)S(1)} %join_half.1), channel_id=1, source_target_pairs={{0,24},{4,28},{8,16},{12,20},{16,8},{20,12},{24,0},{28,4},{1,25},{... | collective-permute-start | bytes 393224 | tf_op jit(solution)/shard_map/ppermute | solution.py:852
  18.2 0.5 collective-permute-start.2
  18.8 4.8 %local_part.1 = (bf16[4,256,256]{2,1,0:T(8,128)(2,1)S(1)}, bf16[4,256,256]{2,1,0:T(8,128)(2,1)S(1)}, bf16[4,256,256]{2,1,0:T(8,128)(2,1)S(1)}, bf16[4,256,256]{2...) custom-call(f32[3,4,256,128]{3,2,1,0:T(8,128)S(1)} %get-tuple-elemen, ...), custom_call_target="tpu_custom_call", output_to_operand_aliasing={{10}: (0, {}), {11}: (1, {}), {12}: (11, {})} | custom-call | tf_op jit(solution)/shard_map/local_part/pallas_call | solution.py:103
  23.6 1.2 %collective-permute-done.2.refs_2_ = bf16[2,128,256]{2,1,0:T(8,128)(2,1)S(1)} collective-permute-done((bf16[2,128,256]{2,1,0:T(8,128)(2,1)S(1)}, bf16[2,128,256]{2,1,0:T(8,128)(2,1)S(1)}, u32[]{:S(2)}, u32[]{:S(2)}) %collective-permute-start.2) | collective-permute-done | bytes 131104 | tf_op jit(solution)/shard_map/ppermute | solution.py:852
  25.6 0.8 %collective-permute-done.4.refs_4_ = bf16[2,128,256]{2,1,0:T(8,128)(2,1)S(1)} collective-permute-done((bf16[2,128,256]{2,1,0:T(8,128)(2,1)S(1)}, bf16[2,128,256]{2,1,0:T(8,128)(2,1)S(1)}, u32[]{:S(2)}, u32[]{:S(2)}) %collective-permute-start.4) | collective-permute-done | bytes 131104 | tf_op jit(solution)/shard_map/ppermute | solution.py:852
  26.9 2.7 %reach.1 = (bf16[2,256,512]{2,1,0:T(8,128)(2,1)S(1)}, bf16[2,256,512]{2,1,0:T(8,128)(2,1)S(1)}, f32[4,256,128]{2,1,0:T(8,128)S(1)}, f32[256,128]{1,0:T(8,128)S(1...) custom-call(s32[2]{0:T(128)S(1)} %pad_add_fusion.place_ref, ...), custom_call_target="tpu_custom_call" | custom-call | tf_op jit(solution)/shard_map/reach/pallas_call | solution.py:103
  29.6 1.6 %collective-permute-start.7 = (bf16[2,256,512]{2,1,0:T(8,128)(2,1)S(1)}, bf16[2,256,512]{2,1,0:T(8,128)(2,1)S(1)}, u32[]{:S(2)}, u32[]{:S(2)}) collective-permute-start(bf16[2,256,512]{2,1,0:T(8,128)(2,1)S(1)} %get-tuple-element.95), channel_id=1, source_target_pairs={{0,1},{1,0},{2,3},{3,2},{4,5},{5,4},{6,7},{7,6},{8,9},{9,8},{10,11... | collective-permute-start | bytes 1572872 | tf_op jit(solution)/shard_map/ppermute | solution.py:852
  31.2 2.9 %return_states.1 = (f32[4,256,128]{2,1,0:T(8,128)S(1)}, f32[4,256,128]{2,1,0:T(8,128)S(1)}, bf16[4,128,256]{2,1,0:T(8,128)(2,1)S(1)}, bf16[4,128,256]{2,1,0:T(8,128)(2,1)S(1)}, bf16[4,128,128]{2,1,0:T(8,128)(2,1)S(1)}) custom-call(s32[2]{0:T(128)S(1)} %pad_add_fusion.place_ref, f32[1,128]{1,0:T(1,128)S(1)} %bitcast.12, ...), custom_call_target="tpu_custom_call" | custom-call | tf_op jit(solution)/shard_map/return_states/pallas_call | solution.py:103
  34.8 1.1 %collective-permute-done.10.refs_3_ = bf16[4,128,128]{2,1,0:T(8,128)(2,1)S(1)} collective-permute-done((bf16[4,128,128]{2,1,0:T(8,128)(2,1)S(1)}, bf16[4,128,128]{2,1,0:T(8,128)(2,1)S(1)}, u32[]{:S(2)}, u32[]{:S(2)}) %collective-permute-start.10) | collective-permute-done | bytes 131104 | tf_op jit(solution)/shard_map/ppermute | solution.py:852
  36.1 1.6 %collective-permute-start.11 = (bf16[4,128,256]{2,1,0:T(8,128)(2,1)S(1)}, bf16[4,128,256]{2,1,0:T(8,128)(2,1)S(1)}, u32[]{:S(2)}, u32[]{:S(2)}) collective-permute-start(bf16[4,128,256]{2,1,0:T(8,128)(2,1)S(1)} %get-tuple-element.128), channel_id=1, source_target_pairs={{0,8},{4,12},{8,0},{12,4},{16,24},{20,28},{24,16},{28,20},{1,9},{5... | collective-permute-start | bytes 786440 | tf_op jit(solution)/shard_map/ppermute | solution.py:852
  37.6 1.4 %collective-permute-start.13 = (bf16[4,128,128]{2,1,0:T(8,128)(2,1)S(1)}, bf16[4,128,128]{2,1,0:T(8,128)(2,1)S(1)}, u32[]{:S(2)}, u32[]{:S(2)}) collective-permute-start(bf16[4,128,128]{2,1,0:T(8,128)(2,1)S(1)} %get-tuple-element.129), channel_id=1, source_target_pairs={{0,24},{4,28},{8,16},{12,20},{16,8},{20,12},{24,0},{28,4},{1,25},{... | collective-permute-start | bytes 393224 | tf_op jit(solution)/shard_map/ppermute | solution.py:852
  39.0 0.6 collective-permute-start.12
  39.6 4.2 %pull_local.1 = (f32[3,4,256,128]{3,2,1,0:T(8,128)S(1)}, f32[4,256,128]{2,1,0:T(8,128)S(1)}, f32[256,128]{1,0:T(8,128)S(1)}, f32[8,256]{1,0:T(8,128)S(1)}, f32[256,128]{1,0:T(8,128)S(1)}) custom-call(f32[3,4,256,128]{3,2,1,0:T(8,128)S(1)} %get-tuple-element.97.refs_0_, f32[256,128]{1,0:T(8,128)S(1)} %get-tuple-element.85.pack_ref.refs_1_.refs_2_, ...), custom_call_target="tpu_custom_call" | custom-call | tf_op jit(solution)/shard_map/pull_local/pallas_call | solution.py:103
  44.0 2.7 %collective-permute-start.14 = (bf16[1,256,512]{2,1,0:T(8,128)(2,1)S(1)}, bf16[1,256,512]{2,1,0:T(8,128)(2,1)S(1)}, u32[]{:S(2)}, u32[]{:S(2)}) collective-permute-start(bf16[1,256,512]{2,1,0:T(8,128)(2,1)S(1)} %get-tuple-element.138), channel_id=1, source_target_pairs={{0,2},{1,3},{2,0},{3,1},{4,6},{5,7},{6,4},{7,5},{8,10},{9,11},{10,... | collective-permute-start | bytes 786440 | tf_op jit(solution)/shard_map/ppermute | solution.py:852
  46.7 1.5 %collective-permute-done.13.refs_20_ = bf16[4,128,128]{2,1,0:T(8,128)(2,1)S(1)} collective-permute-done((bf16[4,128,128]{2,1,0:T(8,128)(2,1)S(1)}, bf16[4,128,128]{2,1,0:T(8,128)(2,1)S(1)}, u32[]{:S(2)}, u32[]{:S(2)}) %collective-permute-start.13) | collective-permute-done | bytes 131104 | tf_op jit(solution)/shard_map/ppermute | solution.py:852
  48.2 5.4 %finish.1 = (bf16[256,1536]{1,0:T(8,128)(2,1)S(1)}, bf16[256,128]{1,0:T(8,128)(2,1)S(1)}) custom-call(s32[2]{0:T(128)S(1)} %pad_add_fusion.place_ref, f32[3,4,256,128]{3,2,1,0:T(8,128)S(1)} %get-tuple-element.97.refs_0_, f32[256,128]{1,0:T(8,128)S(1)} %get-tuple-element.98.refs_1_, f32[256,128]{1,0:T(8,128)S(1)} %get-tuple-element.85.pack_ref.refs_1_.refs_2_, ...), custom_call_target="tpu_custom_call" | custom-call | tf_op jit(solution)/shard_map/finish/pallas_call | solution.py:103
  53.6 2.6 %pull_tokens.1 = (bf16[2,256,256]{2,1,0:T(8,128)(2,1)S(1)}, bf16[2,256,256]{2,1,0:T(8,128)(2,1)S(1)}, bf16[256,256]{1,0:T(8,128)(2,1)S(1)}, bf16[256,256]{1,0:T(...) custom-call(s32[2]{0:T(128)S(1)} %pad_add_fusion.place_ref, ...), custom_call_target="tpu_custom_call" | custom-call | tf_op jit(solution)/shard_map/pull_tokens/pallas_call | solution.py:103
  56.2 0.5 collective-permute-start.15
  56.7 1.4 %collective-permute-done.14.refs_1_ = bf16[1,256,512]{2,1,0:T(8,128)(2,1)S(1)} collective-permute-done((bf16[1,256,512]{2,1,0:T(8,128)(2,1)S(1)}, bf16[1,256,512]{2,1,0:T(8,128)(2,1)S(1)}, u32[]{:S(2)}, u32[]{:S(2)}) %collective-permute-start.14) | collective-permute-done | bytes 262176 | tf_op jit(solution)/shard_map/ppermute | solution.py:852
  58.1 1.2 %collective-permute-start.17 = (bf16[256,256]{1,0:T(8,128)(2,1)S(1)}, bf16[256,256]{1,0:T(8,128)(2,1)S(1)}, u32[]{:S(2)}, u32[]{:S(2)}) collective-permute-start(bf16[256,256]{1,0:T(8,128)(2,1)S(1)} %get-tuple-element.147), channel_id=1, source_target_pairs={{0,2},{1,3},{2,0},{3,1},{4,6},{5,7},{6,4},{7,5},{8,10},{9,11},{10,... | collective-permute-start | bytes 393224 | tf_op jit(solution)/shard_map/ppermute | solution.py:852
  59.3 2.4 %collective-permute-start.18 = (bf16[256,256]{1,0:T(8,128)(2,1)S(1)}, bf16[256,256]{1,0:T(8,128)(2,1)S(1)}, u32[]{:S(2)}, u32[]{:S(2)}) collective-permute-start(bf16[256,256]{1,0:T(8,128)(2,1)S(1)} %get-tuple-element.148), channel_id=1, source_target_pairs={{0,3},{1,2},{2,1},{3,0},{4,7},{5,6},{6,5},{7,4},{8,11},{9,10},{10,... | collective-permute-start | bytes 393224 | tf_op jit(solution)/shard_map/ppermute | solution.py:852
  61.7 4.9 %collective-permute-done.15.got_ref = bf16[2,256,256]{2,1,0:T(8,128)(2,1)S(1)} collective-permute-done((bf16[2,256,256]{2,1,0:T(8,128)(2,1)S(1)}, bf16[2,256,256]{2,1,0:T(8,128)(2,1)S(1)}, u32[]{:S(2)}, u32[]{:S(2)}) %collective-permute-start.15) | collective-permute-done | bytes 262176 | tf_op jit(solution)/shard_map/ppermute | solution.py:852
  66.7 1.6 %collective-permute-start.16 = (bf16[1,256,256]{2,1,0:T(8,128)(2,1)S(1)}, bf16[1,256,256]{2,1,0:T(8,128)(2,1)S(1)}, u32[]{:S(2)}, u32[]{:S(2)}) collective-permute-start(bf16[1,256,256]{2,1,0:T(8,128)(2,1)S(1)} %get-tuple-element.145), channel_id=1, source_target_pairs={{0,2},{1,3},{2,0},{3,1},{4,6},{5,7},{6,4},{7,5},{8,10},{9,11},{10,... | collective-permute-start | bytes 393224 | tf_op jit(solution)/shard_map/ppermute | solution.py:852
  68.2 2.5 %collective-permute-start.19 = (bf16[256,256]{1,0:T(8,128)(2,1)S(1)}, bf16[256,256]{1,0:T(8,128)(2,1)S(1)}, u32[]{:S(2)}, u32[]{:S(2)}) collective-permute-start(bf16[256,256]{1,0:T(8,128)(2,1)S(1)} %get-tuple-element.149), channel_id=1, source_target_pairs={{0,1},{1,0},{2,3},{3,2},{4,5},{5,4},{6,7},{7,6},{8,9},{9,8},{10,11... | collective-permute-start | bytes 393224 | tf_op jit(solution)/shard_map/ppermute | solution.py:852
  70.7 0.7 head_sum.2
  71.5 1.7 %collective-permute-done.18.refs_4_ = bf16[256,256]{1,0:T(8,128)(2,1)S(1)} collective-permute-done((bf16[256,256]{1,0:T(8,128)(2,1)S(1)}, bf16[256,256]{1,0:T(8,128)(2,1)S(1)}, u32[]{:S(2)}, u32[]{:S(2)}) %collective-permute-start.18) | collective-permute-done | bytes 131104 | tf_op jit(solution)/shard_map/ppermute | solution.py:852
  73.2 4.8 %collective-permute-done.16.refs_1_ = bf16[1,256,256]{2,1,0:T(8,128)(2,1)S(1)} collective-permute-done((bf16[1,256,256]{2,1,0:T(8,128)(2,1)S(1)}, bf16[1,256,256]{2,1,0:T(8,128)(2,1)S(1)}, u32[]{:S(2)}, u32[]{:S(2)}) %collective-permute-start.16) | collective-permute-done | bytes 131104 | tf_op jit(solution)/shard_map/ppermute | solution.py:852
  78.0 0.8 %head_sum.3 = bf16[256,512]{1,0:T(8,128)(2,1)} custom-call(f32[1,256,256]{2,1,0:T(8,128)S(1)} %get-tuple-element.142.refs_0_, bf16[1,256,256]{2,1,0:T(8,128)(2,1)S(1)} %collective-permute-done.16.refs_1_, bf16[256,256]{1,0:T(8,128)(2,1)S(1)} %get-tuple-element.146.refs_2_, bf16[256,256]{1,0:T(8,128)(2,1)S(1)} %collective-permute-done.17.refs_3_, ...), custom_call_target="tpu_custom_call" | custom-call | tf_op jit(solution)/shard_map/head_sum/pallas_call | solution.py:103
  (35 shorter events, 2.5 us)
Async XLA Ops:
  0.7 18.1 %copy-start = (bf16[4,128,2048]{2,1,0:T(8,128)(2,1)S(1)}, bf16[4,128,2048]{2,1,0:T(8,128)(2,1)}, u32[]{:S(2)}) copy-start(bf16[4,128,2048]{2,1,0:T(8,128)(2,1)} %param.12) | copy-start | bytes 6291460
  0.7 18.1 %copy-start.1 = (bf16[256,2048]{1,0:T(8,128)(2,1)S(1)}, bf16[256,2048]{1,0:T(8,128)(2,1)}, u32[]{:S(2)}) copy-start(bf16[256,2048]{1,0:T(8,128)(2,1)} %tokens_ref.1) | copy-start | bytes 3145732
  0.7 18.1 %copy-start.2 = (bf16[256,2048]{1,0:T(8,128)(2,1)S(1)}, bf16[256,2048]{1,0:T(8,128)(2,1)}, u32[]{:S(2)}) copy-start(bf16[256,2048]{1,0:T(8,128)(2,1)} %grad_ref.1) | copy-start | bytes 3145732
  11.9 1.7 %collective-permute-start = (bf16[4,128,256]{2,1,0:T(8,128)(2,1)S(1)}, bf16[4,128,256]{2,1,0:T(8,128)(2,1)S(1)}, u32[]{:S(2)}, u32[]{:S(2)}) collective-permute-start(bf16[4,128,256]{2,1,0:T(8,128)(2,1)S(1)} %get-tuple-element.86.own_ref), channel_id=1, source_target_pairs={{0,4},{4,0},{8,12},{12,8},{16,20},{20,16},{24,28},{28,24},{1,5},{5... | collective-permute-start | bytes 786440 | tf_op jit(solution)/shard_map/ppermute | solution.py:852
  14.3 9.3 %collective-permute-start.3 = (bf16[2,128,256]{2,1,0:T(8,128)(2,1)S(1)}, bf16[2,128,256]{2,1,0:T(8,128)(2,1)S(1)}, u32[]{:S(2)}, u32[]{:S(2)}) collective-permute-start(bf16[2,128,256]{2,1,0:T(8,128)(2,1)S(1)} %join_half.1), channel_id=1, source_target_pairs={{0,24},{4,28},{8,16},{12,20},{16,8},{20,12},{24,0},{28,4},{1,25},{... | collective-permute-start | bytes 393224 | tf_op jit(solution)/shard_map/ppermute | solution.py:852
  18.2 6.6 %collective-permute-start.2 = (bf16[2,128,256]{2,1,0:T(8,128)(2,1)S(1)}, bf16[2,128,256]{2,1,0:T(8,128)(2,1)S(1)}, u32[]{:S(2)}, u32[]{:S(2)}) collective-permute-start(bf16[2,128,256]{2,1,0:T(8,128)(2,1)S(1)} %join_half.1), channel_id=1, source_target_pairs={{0,16},{4,20},{8,24},{12,28},{16,0},{20,4},{24,8},{28,12},{1,17},{... | collective-permute-start | bytes 393224 | tf_op jit(solution)/shard_map/ppermute | solution.py:852
  18.7 6.4 %collective-permute-start.1 = (bf16[2,128,256]{2,1,0:T(8,128)(2,1)S(1)}, bf16[2,128,256]{2,1,0:T(8,128)(2,1)S(1)}, u32[]{:S(2)}, u32[]{:S(2)}) collective-permute-start(bf16[2,128,256]{2,1,0:T(8,128)(2,1)S(1)} %join_half.1), channel_id=1, source_target_pairs={{0,8},{4,12},{8,0},{12,4},{16,24},{20,28},{24,16},{28,20},{1,9},{5... | collective-permute-start | bytes 393224 | tf_op jit(solution)/shard_map/ppermute | solution.py:852
  18.8 8.1 %copy-start.3 = (f32[128]{0:T(128)S(1)}, f32[128]{0:T(128)}, u32[]{:S(2)}) copy-start(f32[128]{0:T(128)} %param.11) | copy-start | bytes 1540
  25.0 1.3 %collective-permute-start.4 = (bf16[2,128,256]{2,1,0:T(8,128)(2,1)S(1)}, bf16[2,128,256]{2,1,0:T(8,128)(2,1)S(1)}, u32[]{:S(2)}, u32[]{:S(2)}) collective-permute-start(bf16[2,128,256]{2,1,0:T(8,128)(2,1)S(1)} %collective-permute-done.1.refs_1_), channel_id=1, source_target_pairs={{0,4},{4,0},{8,12},{12,8},{16,20},{20,16},{24,28},{28,24},{1,5},{5... | collective-permute-start | bytes 393224 | tf_op jit(solution)/shard_map/ppermute | solution.py:852
  25.0 1.5 %collective-permute-start.5 = (bf16[2,128,256]{2,1,0:T(8,128)(2,1)S(1)}, bf16[2,128,256]{2,1,0:T(8,128)(2,1)S(1)}, u32[]{:S(2)}, u32[]{:S(2)}) collective-permute-start(bf16[2,128,256]{2,1,0:T(8,128)(2,1)S(1)} %collective-permute-done.2.refs_2_), channel_id=1, source_target_pairs={{0,4},{4,0},{8,12},{12,8},{16,20},{20,16},{24,28},{28,24},{1,5},{5... | collective-permute-start | bytes 393224 | tf_op jit(solution)/shard_map/ppermute | solution.py:852
  25.6 1.3 %collective-permute-start.6 = (bf16[2,128,256]{2,1,0:T(8,128)(2,1)S(1)}, bf16[2,128,256]{2,1,0:T(8,128)(2,1)S(1)}, u32[]{:S(2)}, u32[]{:S(2)}) collective-permute-start(bf16[2,128,256]{2,1,0:T(8,128)(2,1)S(1)} %collective-permute-done.3.refs_3_), channel_id=1, source_target_pairs={{0,4},{4,0},{8,12},{12,8},{16,20},{20,16},{24,28},{28,24},{1,5},{5... | collective-permute-start | bytes 393224 | tf_op jit(solution)/shard_map/ppermute | solution.py:852
  29.6 14.2 %collective-permute-start.7 = (bf16[2,256,512]{2,1,0:T(8,128)(2,1)S(1)}, bf16[2,256,512]{2,1,0:T(8,128)(2,1)S(1)}, u32[]{:S(2)}, u32[]{:S(2)}) collective-permute-start(bf16[2,256,512]{2,1,0:T(8,128)(2,1)S(1)} %get-tuple-element.95), channel_id=1, source_target_pairs={{0,1},{1,0},{2,3},{3,2},{4,5},{5,4},{6,7},{7,6},{8,9},{9,8},{10,11... | collective-permute-start | bytes 1572872 | tf_op jit(solution)/shard_map/ppermute | solution.py:852
  34.2 1.8 %collective-permute-start.9 = (bf16[4,128,256]{2,1,0:T(8,128)(2,1)S(1)}, bf16[4,128,256]{2,1,0:T(8,128)(2,1)S(1)}, u32[]{:S(2)}, u32[]{:S(2)}) collective-permute-start(bf16[4,128,256]{2,1,0:T(8,128)(2,1)S(1)} %get-tuple-element.126.refs_0_), channel_id=1, source_target_pairs={{0,4},{4,0},{8,12},{12,8},{16,20},{20,16},{24,28},{28,24},{1,5},{5... | collective-permute-start | bytes 786440 | tf_op jit(solution)/shard_map/ppermute | solution.py:852
  34.2 1.7 %collective-permute-start.10 = (bf16[4,128,128]{2,1,0:T(8,128)(2,1)S(1)}, bf16[4,128,128]{2,1,0:T(8,128)(2,1)S(1)}, u32[]{:S(2)}, u32[]{:S(2)}) collective-permute-start(bf16[4,128,128]{2,1,0:T(8,128)(2,1)S(1)} %get-tuple-element.127.refs_1_), channel_id=1, source_target_pairs={{0,4},{4,0},{8,12},{12,8},{16,20},{20,16},{24,28},{28,24},{1,5},{5... | collective-permute-start | bytes 393224 | tf_op jit(solution)/shard_map/ppermute | solution.py:852
  34.7 11.9 %collective-permute-start.8 = (bf16[4,128,256]{2,1,0:T(8,128)(2,1)S(1)}, bf16[4,128,256]{2,1,0:T(8,128)(2,1)S(1)}, u32[]{:S(2)}, u32[]{:S(2)}) collective-permute-start(bf16[4,128,256]{2,1,0:T(8,128)(2,1)S(1)} %get-tuple-element.125), channel_id=1, source_target_pairs={{0,4},{4,0},{8,12},{12,8},{16,20},{20,16},{24,28},{28,24},{1,5},{5... | collective-permute-start | bytes 786440 | tf_op jit(solution)/shard_map/ppermute | solution.py:852
  36.1 12.1 %collective-permute-start.11 = (bf16[4,128,256]{2,1,0:T(8,128)(2,1)S(1)}, bf16[4,128,256]{2,1,0:T(8,128)(2,1)S(1)}, u32[]{:S(2)}, u32[]{:S(2)}) collective-permute-start(bf16[4,128,256]{2,1,0:T(8,128)(2,1)S(1)} %get-tuple-element.128), channel_id=1, source_target_pairs={{0,8},{4,12},{8,0},{12,4},{16,24},{20,28},{24,16},{28,20},{1,9},{5... | collective-permute-start | bytes 786440 | tf_op jit(solution)/shard_map/ppermute | solution.py:852
  37.6 10.5 %collective-permute-start.13 = (bf16[4,128,128]{2,1,0:T(8,128)(2,1)S(1)}, bf16[4,128,128]{2,1,0:T(8,128)(2,1)S(1)}, u32[]{:S(2)}, u32[]{:S(2)}) collective-permute-start(bf16[4,128,128]{2,1,0:T(8,128)(2,1)S(1)} %get-tuple-element.129), channel_id=1, source_target_pairs={{0,24},{4,28},{8,16},{12,20},{16,8},{20,12},{24,0},{28,4},{1,25},{... | collective-permute-start | bytes 393224 | tf_op jit(solution)/shard_map/ppermute | solution.py:852
  39.0 9.1 %collective-permute-start.12 = (bf16[4,128,128]{2,1,0:T(8,128)(2,1)S(1)}, bf16[4,128,128]{2,1,0:T(8,128)(2,1)S(1)}, u32[]{:S(2)}, u32[]{:S(2)}) collective-permute-start(bf16[4,128,128]{2,1,0:T(8,128)(2,1)S(1)} %get-tuple-element.129), channel_id=1, source_target_pairs={{0,16},{4,20},{8,24},{12,28},{16,0},{20,4},{24,8},{28,12},{1,17},{... | collective-permute-start | bytes 393224 | tf_op jit(solution)/shard_map/ppermute | solution.py:852
  39.6 13.9 %slice-start = ((s8[6291456]{0:T(1024)(128)(4,1)}), s8[2097152]{0:T(1024)(128)(4,1)S(1)}, s32[]{:S(2)}) async-start(s8[6291456]{0:T(1024)(128)(4,1)} %bitcast.7), calls=%async_computation | async-start | bytes 4194304
  43.9 9.7 %slice-start.1 = ((s8[6291456]{0:T(1024)(128)(4,1)}), s8[4194304]{0:T(1024)(128)(4,1)S(1)}, s32[]{:S(2)}) async-start(s8[6291456]{0:T(1024)(128)(4,1)} %bitcast.7), calls=%async_computation.1 | async-start | bytes 8388608
  44.0 14.1 %collective-permute-start.14 = (bf16[1,256,512]{2,1,0:T(8,128)(2,1)S(1)}, bf16[1,256,512]{2,1,0:T(8,128)(2,1)S(1)}, u32[]{:S(2)}, u32[]{:S(2)}) collective-permute-start(bf16[1,256,512]{2,1,0:T(8,128)(2,1)S(1)} %get-tuple-element.138), channel_id=1, source_target_pairs={{0,2},{1,3},{2,0},{3,1},{4,6},{5,7},{6,4},{7,5},{8,10},{9,11},{10,... | collective-permute-start | bytes 786440 | tf_op jit(solution)/shard_map/ppermute | solution.py:852
  56.2 10.4 %collective-permute-start.15 = (bf16[2,256,256]{2,1,0:T(8,128)(2,1)S(1)}, bf16[2,256,256]{2,1,0:T(8,128)(2,1)S(1)}, u32[]{:S(2)}, u32[]{:S(2)}) collective-permute-start(bf16[2,256,256]{2,1,0:T(8,128)(2,1)S(1)} %get-tuple-element.141), channel_id=1, source_target_pairs={{0,1},{1,0},{2,3},{3,2},{4,5},{5,4},{6,7},{7,6},{8,9},{9,8},{10,11... | collective-permute-start | bytes 786440 | tf_op jit(solution)/shard_map/ppermute | solution.py:852
  58.1 13.4 %collective-permute-start.17 = (bf16[256,256]{1,0:T(8,128)(2,1)S(1)}, bf16[256,256]{1,0:T(8,128)(2,1)S(1)}, u32[]{:S(2)}, u32[]{:S(2)}) collective-permute-start(bf16[256,256]{1,0:T(8,128)(2,1)S(1)} %get-tuple-element.147), channel_id=1, source_target_pairs={{0,2},{1,3},{2,0},{3,1},{4,6},{5,7},{6,4},{7,5},{8,10},{9,11},{10,... | collective-permute-start | bytes 393224 | tf_op jit(solution)/shard_map/ppermute | solution.py:852
  59.3 13.9 %collective-permute-start.18 = (bf16[256,256]{1,0:T(8,128)(2,1)S(1)}, bf16[256,256]{1,0:T(8,128)(2,1)S(1)}, u32[]{:S(2)}, u32[]{:S(2)}) collective-permute-start(bf16[256,256]{1,0:T(8,128)(2,1)S(1)} %get-tuple-element.148), channel_id=1, source_target_pairs={{0,3},{1,2},{2,1},{3,0},{4,7},{5,6},{6,5},{7,4},{8,11},{9,10},{10,... | collective-permute-start | bytes 393224 | tf_op jit(solution)/shard_map/ppermute | solution.py:852
  66.7 11.4 %collective-permute-start.16 = (bf16[1,256,256]{2,1,0:T(8,128)(2,1)S(1)}, bf16[1,256,256]{2,1,0:T(8,128)(2,1)S(1)}, u32[]{:S(2)}, u32[]{:S(2)}) collective-permute-start(bf16[1,256,256]{2,1,0:T(8,128)(2,1)S(1)} %get-tuple-element.145), channel_id=1, source_target_pairs={{0,2},{1,3},{2,0},{3,1},{4,6},{5,7},{6,4},{7,5},{8,10},{9,11},{10,... | collective-permute-start | bytes 393224 | tf_op jit(solution)/shard_map/ppermute | solution.py:852
  68.2 9.8 %collective-permute-start.19 = (bf16[256,256]{1,0:T(8,128)(2,1)S(1)}, bf16[256,256]{1,0:T(8,128)(2,1)S(1)}, u32[]{:S(2)}, u32[]{:S(2)}) collective-permute-start(bf16[256,256]{1,0:T(8,128)(2,1)S(1)} %get-tuple-element.149), channel_id=1, source_target_pairs={{0,1},{1,0},{2,3},{3,2},{4,5},{5,4},{6,7},{7,6},{8,9},{9,8},{10,11... | collective-permute-start | bytes 393224 | tf_op jit(solution)/shard_map/ppermute | solution.py:852
